TPU v7x, 32 devices: a whole 2x2x4 slice. The times are simulated.
32 devices in a mesh: fsdp: 32 (over z, y, x, core).
Axes of the slice: x: 2, y: 2, z: 4, core: 2. Of those that a mesh axis runs over, the one named last changes fastest.
Arguments:
- tokens: bfloat16 [35840, 768], P('fsdp'), may hold values from -6 to 6
- cotangent: bfloat16 [35840, 768], P('fsdp'), may hold values from -6 to 6
- lengths: int32 [224], P('fsdp'), may hold values from 80 to 160, as said below
- span_start: int32 [224, 4], P('fsdp'), may hold values from 0 to 159, as said below
- span_end: int32 [224, 4], P('fsdp'), may hold values from 1 to 160, as said below
- query_weight: bfloat16 [768, 768], P('fsdp'), may hold values from -0.21875 to 0.21875
- query_bias: bfloat16 [768], P('fsdp'), may hold values from -1.75 to 1.75
- key_weight: bfloat16 [768, 768], P('fsdp'), may hold values from -0.21875 to 0.21875
- value_weight: bfloat16 [768, 768], P('fsdp'), may hold values from -0.21875 to 0.21875
- value_bias: bfloat16 [768], P('fsdp'), may hold values from -1.75 to 1.75
- out_weight: bfloat16 [768, 768], P('fsdp'), may hold values from -0.875 to 0.875
- out_bias: bfloat16 [768], P('fsdp'), may hold values from -1.75 to 1.75
- attn_gain: bfloat16 [768], P('fsdp'), may hold values from 0.5 to 1.5
- attn_shift: bfloat16 [768], P('fsdp'), may hold values from -1.75 to 1.75
- up_weight: bfloat16 [768, 3072], P('fsdp'), may hold values from -0.21875 to 0.21875
- up_bias: bfloat16 [3072], P('fsdp'), may hold values from -1.75 to 1.75
- down_weight: bfloat16 [3072, 768], P('fsdp'), may hold values from -0.109375 to 0.109375
- down_bias: bfloat16 [768], P('fsdp'), may hold values from -1.75 to 1.75
- ffn_gain: bfloat16 [768], P('fsdp'), may hold values from 0.5 to 1.5
- ffn_shift: bfloat16 [768], P('fsdp'), may hold values from -1.75 to 1.75
Outputs:
- layer_out: bfloat16 [35840, 768], P('fsdp')
- input_grad: bfloat16 [35840, 768], P('fsdp')
- query_weight_grad: float32 [768, 768], P('fsdp')
- query_bias_grad: float32 [768], P('fsdp')
- key_weight_grad: float32 [768, 768], P('fsdp')
- value_weight_grad: float32 [768, 768], P('fsdp')
- value_bias_grad: float32 [768], P('fsdp')
- out_weight_grad: float32 [768, 768], P('fsdp')
- out_bias_grad: float32 [768], P('fsdp')
- attn_gain_grad: float32 [768], P('fsdp')
- attn_shift_grad: float32 [768], P('fsdp')
- up_weight_grad: float32 [768, 3072], P('fsdp')
- up_bias_grad: float32 [3072], P('fsdp')
- down_weight_grad: float32 [3072, 768], P('fsdp')
- down_bias_grad: float32 [768], P('fsdp')
- ffn_gain_grad: float32 [768], P('fsdp')
- ffn_shift_grad: float32 [768], P('fsdp')
Inputs may be any that keep to these rules, and one draw needn't show every extreme that they name: `lengths`: residues of each chain; positions at or past it are padding; some chain has exactly 160 and some exactly 80. `span_start`: each span lies inside its chain's residues; spans of a chain may intersect. `span_end`: greater than the span's start and at most the chain's length.
All inputs are finite; a program needn't handle non-finite values.
Results may differ from a plain program's by a relative error of at most 0.013.
Values may be sent and summed in bfloat16 or wider, within the bound.
No kernel may reach another device: no remote copies, remote signals or barrier semaphores. Data moves between devices by JAX's collectives and lax.ppermute only.
A program may use at most 256 MiB of HBM per device.

v0:
```python
import jax
import jax.numpy as jnp
from jax import lax
from jax.sharding import PartitionSpec as P

D = 768
HEADS = 12
HEAD = 64


epsilon = 1e-05
masked_score = -1000000000.0


def matmul(left, right):
    return jnp.dot(left, right, preferred_element_type=jnp.float32)


def inner_left(left, right):
    return lax.dot_general(
        left, right, (((0,), (0,)), ((), ())), preferred_element_type=jnp.float32
    )


def inner_right(left, right):
    return lax.dot_general(
        left, right, (((1,), (1,)), ((), ())), preferred_element_type=jnp.float32
    )


def normalize(values, gain, shift):
    center = values - jnp.mean(values, axis=-1, keepdims=True)
    spread = jnp.mean(center * center, axis=-1, keepdims=True)
    scale = lax.rsqrt(spread + epsilon)
    normed = center * scale
    return (normed * gain.astype(jnp.float32) + shift.astype(jnp.float32), normed, scale)


def norm_back(incoming, normed, scale, gain):
    weighted = incoming * gain.astype(jnp.float32)
    inner = weighted - jnp.mean(weighted, axis=-1, keepdims=True)
    inner = inner - normed * jnp.mean(weighted * normed, axis=-1, keepdims=True)
    return (jnp.sum(incoming * normed, axis=0), jnp.sum(incoming, axis=0), scale * inner)


def score_block(query, keyrows, valid):
    scores = (
        jnp.einsum("cqhe,ckhe->chqk", query, keyrows, preferred_element_type=jnp.float32) * 0.125
    )
    return jnp.where(valid, scores, masked_score)


def exact_gelu(values):
    return jax.nn.gelu(values, approximate=False)


def shards(
    tokens,
    cotangent,
    lengths,
    span_start,
    span_end,
    query_weight,
    query_bias,
    key_weight,
    value_weight,
    value_bias,
    out_weight,
    out_bias,
    attn_gain,
    attn_shift,
    up_weight,
    up_bias,
    down_weight,
    down_bias,
    ffn_gain,
    ffn_shift,
):
    gathered_attn = (
        lax.all_gather(query_weight, "fsdp", axis=0, tiled=True),
        lax.all_gather(query_bias, "fsdp", axis=0, tiled=True),
        lax.all_gather(key_weight, "fsdp", axis=0, tiled=True),
        lax.all_gather(value_weight, "fsdp", axis=0, tiled=True),
        lax.all_gather(value_bias, "fsdp", axis=0, tiled=True),
        lax.all_gather(out_weight, "fsdp", axis=0, tiled=True),
        lax.all_gather(out_bias, "fsdp", axis=0, tiled=True),
        lax.all_gather(attn_gain, "fsdp", axis=0, tiled=True),
        lax.all_gather(attn_shift, "fsdp", axis=0, tiled=True),
    )
    gathered_ffn = (
        lax.all_gather(up_weight, "fsdp", axis=0, tiled=True),
        lax.all_gather(up_bias, "fsdp", axis=0, tiled=True),
        lax.all_gather(down_weight, "fsdp", axis=0, tiled=True),
        lax.all_gather(down_bias, "fsdp", axis=0, tiled=True),
        lax.all_gather(ffn_gain, "fsdp", axis=0, tiled=True),
        lax.all_gather(ffn_shift, "fsdp", axis=0, tiled=True),
    )
    (
        full_query,
        full_qbias,
        full_key,
        full_value,
        full_vbias,
        full_out,
        full_obias,
        full_again,
        full_ashift,
    ) = gathered_attn
    full_up, full_ubias, full_down, full_dbias, full_fgain, full_fshift = gathered_ffn
    chains = lengths.shape[0]
    rows = tokens.shape[0]
    length = rows // chains
    shape = (chains, length, HEADS, HEAD)
    query = (
        (matmul(tokens, full_query) + full_qbias.astype(jnp.float32))
        .astype(jnp.bfloat16)
        .reshape(shape)
    )
    keyrows = matmul(tokens, full_key).astype(jnp.bfloat16).reshape(shape)
    valrows = (
        (matmul(tokens, full_value) + full_vbias.astype(jnp.float32))
        .astype(jnp.bfloat16)
        .reshape(shape)
    )
    valid = (jnp.arange(length)[None, :] < lengths[:, None])[:, None, None, :]
    scores = score_block(query, keyrows, valid)
    highest = jnp.max(scores, axis=-1, keepdims=True)
    expo = jnp.exp(scores - highest)
    total = jnp.sum(expo, axis=-1, keepdims=True)
    log_total = highest + jnp.log(total)
    probs = (expo / total).astype(jnp.bfloat16)
    mixed = jnp.einsum("chqk,ckhe->cqhe", probs, valrows, preferred_element_type=jnp.float32)
    mixed = mixed.reshape(rows, D).astype(jnp.bfloat16)
    attn = matmul(mixed, full_out) + full_obias.astype(jnp.float32)
    first, first_hat, first_scale = normalize(
        tokens.astype(jnp.float32) + attn, full_again, full_ashift
    )
    first_low = first.astype(jnp.bfloat16)
    pre = matmul(first_low, full_up) + full_ubias.astype(jnp.float32)
    hidden = exact_gelu(pre).astype(jnp.bfloat16)
    ffn = matmul(hidden, full_down) + full_dbias.astype(jnp.float32)
    layer_out, second_hat, second_scale = normalize(first + ffn, full_fgain, full_fshift)
    again_ffn = (
        lax.all_gather(up_weight, "fsdp", axis=0, tiled=True),
        lax.all_gather(up_bias, "fsdp", axis=0, tiled=True),
        lax.all_gather(down_weight, "fsdp", axis=0, tiled=True),
        lax.all_gather(down_bias, "fsdp", axis=0, tiled=True),
        lax.all_gather(ffn_gain, "fsdp", axis=0, tiled=True),
        lax.all_gather(ffn_shift, "fsdp", axis=0, tiled=True),
    )
    full_up, full_down, full_fgain = (again_ffn[0], again_ffn[2], again_ffn[4])
    positions = jnp.arange(length)
    inside = jnp.any(
        (positions[None, None, :] >= span_start[:, :, None])
        & (positions[None, None, :] < span_end[:, :, None]),
        axis=1,
    )
    grad_out = cotangent.astype(jnp.float32) * inside.astype(jnp.float32).reshape(rows, 1)
    fgain_grad, fshift_grad, grad_second = norm_back(grad_out, second_hat, second_scale, full_fgain)
    grad_ffn = grad_second.astype(jnp.bfloat16)
    dbias_grad = jnp.sum(grad_ffn.astype(jnp.float32), axis=0)
    grad_hidden = inner_right(grad_ffn, full_down)
    _, gelu_back = jax.vjp(exact_gelu, pre)
    grad_pre = gelu_back(grad_hidden)[0].astype(jnp.bfloat16)
    ubias_grad = jnp.sum(grad_pre.astype(jnp.float32), axis=0)
    grad_first = grad_second + inner_right(grad_pre, full_up)
    down_grad = inner_left(hidden, grad_ffn)
    up_grad = inner_left(first_low, grad_pre)
    owned_ffn = (
        lax.psum_scatter(up_grad, "fsdp", scatter_dimension=0, tiled=True),
        lax.psum_scatter(ubias_grad, "fsdp", scatter_dimension=0, tiled=True),
        lax.psum_scatter(down_grad, "fsdp", scatter_dimension=0, tiled=True),
        lax.psum_scatter(dbias_grad, "fsdp", scatter_dimension=0, tiled=True),
        lax.psum_scatter(fgain_grad, "fsdp", scatter_dimension=0, tiled=True),
        lax.psum_scatter(fshift_grad, "fsdp", scatter_dimension=0, tiled=True),
    )
    again_attn = (
        lax.all_gather(query_weight, "fsdp", axis=0, tiled=True),
        lax.all_gather(query_bias, "fsdp", axis=0, tiled=True),
        lax.all_gather(key_weight, "fsdp", axis=0, tiled=True),
        lax.all_gather(value_weight, "fsdp", axis=0, tiled=True),
        lax.all_gather(value_bias, "fsdp", axis=0, tiled=True),
        lax.all_gather(out_weight, "fsdp", axis=0, tiled=True),
        lax.all_gather(out_bias, "fsdp", axis=0, tiled=True),
        lax.all_gather(attn_gain, "fsdp", axis=0, tiled=True),
        lax.all_gather(attn_shift, "fsdp", axis=0, tiled=True),
    )
    full_query, full_key, full_value = (again_attn[0], again_attn[2], again_attn[3])
    full_out, full_again = (again_attn[5], again_attn[7])
    again_grad, ashift_grad, grad_resid = norm_back(grad_first, first_hat, first_scale, full_again)
    grad_attn = grad_resid.astype(jnp.bfloat16)
    obias_grad = jnp.sum(grad_attn.astype(jnp.float32), axis=0)
    grad_mixed = inner_right(grad_attn, full_out).astype(jnp.bfloat16).reshape(shape)
    recomputed = jnp.exp(score_block(query, keyrows, valid) - log_total)
    grad_value = jnp.einsum(
        "chqk,cqhe->ckhe",
        recomputed.astype(jnp.bfloat16),
        grad_mixed,
        preferred_element_type=jnp.float32,
    )
    grad_value = grad_value.astype(jnp.bfloat16).reshape(rows, D)
    grad_probs = jnp.einsum(
        "cqhe,ckhe->chqk", grad_mixed, valrows, preferred_element_type=jnp.float32
    )
    grad_scores = recomputed * (
        grad_probs - jnp.sum(recomputed * grad_probs, axis=-1, keepdims=True)
    )
    grad_scores = grad_scores.astype(jnp.bfloat16)
    grad_query = jnp.einsum(
        "chqk,ckhe->cqhe", grad_scores, keyrows, preferred_element_type=jnp.float32
    )
    grad_query = (grad_query * 0.125).astype(jnp.bfloat16).reshape(rows, D)
    grad_key = jnp.einsum("chqk,cqhe->ckhe", grad_scores, query, preferred_element_type=jnp.float32)
    grad_key = (grad_key * 0.125).astype(jnp.bfloat16).reshape(rows, D)
    qbias_grad = jnp.sum(grad_query.astype(jnp.float32), axis=0)
    vbias_grad = jnp.sum(grad_value.astype(jnp.float32), axis=0)
    input_grad = grad_resid + inner_right(grad_query, full_query) + inner_right(grad_key, full_key)
    input_grad = (input_grad + inner_right(grad_value, full_value)).astype(jnp.bfloat16)
    out_grad = inner_left(mixed, grad_attn)
    query_grad = inner_left(tokens, grad_query)
    key_grad = inner_left(tokens, grad_key)
    value_grad = inner_left(tokens, grad_value)
    owned_attn = (
        lax.psum_scatter(query_grad, "fsdp", scatter_dimension=0, tiled=True),
        lax.psum_scatter(qbias_grad, "fsdp", scatter_dimension=0, tiled=True),
        lax.psum_scatter(key_grad, "fsdp", scatter_dimension=0, tiled=True),
        lax.psum_scatter(value_grad, "fsdp", scatter_dimension=0, tiled=True),
        lax.psum_scatter(vbias_grad, "fsdp", scatter_dimension=0, tiled=True),
        lax.psum_scatter(out_grad, "fsdp", scatter_dimension=0, tiled=True),
        lax.psum_scatter(obias_grad, "fsdp", scatter_dimension=0, tiled=True),
        lax.psum_scatter(again_grad, "fsdp", scatter_dimension=0, tiled=True),
        lax.psum_scatter(ashift_grad, "fsdp", scatter_dimension=0, tiled=True),
    )
    owned = tuple(owned_attn) + tuple(owned_ffn)
    return (
        layer_out.astype(jnp.bfloat16),
        input_grad,
        owned[0],
        owned[1],
        owned[2],
        owned[3],
        owned[4],
        owned[5],
        owned[6],
        owned[7],
        owned[8],
        owned[9],
        owned[10],
        owned[11],
        owned[12],
        owned[13],
        owned[14],
    )


def solution(mesh):
    return jax.shard_map(
        shards,
        mesh=mesh,
        in_specs=(
            P("fsdp", None),
            P("fsdp", None),
            P("fsdp"),
            P("fsdp", None),
            P("fsdp", None),
            P("fsdp", None),
            P("fsdp"),
            P("fsdp", None),
            P("fsdp", None),
            P("fsdp"),
            P("fsdp", None),
            P("fsdp"),
            P("fsdp"),
            P("fsdp"),
            P("fsdp", None),
            P("fsdp"),
            P("fsdp", None),
            P("fsdp"),
            P("fsdp"),
            P("fsdp"),
        ),
        out_specs=(
            P("fsdp", None),
            P("fsdp", None),
            P("fsdp", None),
            P("fsdp"),
            P("fsdp", None),
            P("fsdp", None),
            P("fsdp"),
            P("fsdp", None),
            P("fsdp"),
            P("fsdp"),
            P("fsdp"),
            P("fsdp", None),
            P("fsdp"),
            P("fsdp", None),
            P("fsdp"),
            P("fsdp"),
            P("fsdp"),
        ),
        check_vma=False,
    )
```

profile of v0, /device:TPU:0, one launch (start us, length us, event | category | flops | bytes accessed | tf_op | source)
XLA Modules:
  0.0 1123.1 jit_solution(12925980726816812820)
XLA Ops:
  21.8 42.4 %all-reduce.19 = (bf16[3072]{0:T(1024)(128)(2,1)S(1)}, bf16[768]{0:T(1024)(128)(2,1)S(1)}, bf16[768]{0:T(1024)(128)(2,1)S(1)}, bf16[768]{0:T(1024)(128)(2,1)S(1)...) all-reduce(bf16[3072]{0:T(1024)(128)(2,1)S(1)} %dynamic-update-slic, ...), channel_id=1, replica_groups=mesh['fsdp'=32] {'fsdp'}, use_global_device_ids=true, to_apply=%add.5 | all-reduce | flops 9216 | bytes 36864
  67.9 3.3 convolution_convert_fusion.1
  71.2 4.4 reshape.180
  75.6 6.1 copy.108
  81.7 42.0 %all-gather.7.cloned.1.call-done = bf16[768,768]{1,0:T(8,128)(2,1)} async-done(((bf16[24,768]{1,0:T(8,128)(2,1)}), bf16[768,768]{1,0:T(8,128)(2,1)}) %all-gather.7.cloned.1.call-update) | async-done | bytes 1179664 | tf_op jit(solution)/shard_map/all_gather | solution.py:83
  123.7 4.5 fusion.17
  128.2 6.3 reshape.178
  134.5 7.3 copy.109
  141.8 37.8 %all-gather.9.cloned.1.call-done = bf16[768,768]{1,0:T(8,128)(2,1)} async-done(((bf16[24,768]{1,0:T(8,128)(2,1)}), bf16[768,768]{1,0:T(8,128)(2,1)}) %all-gather.9.cloned.1.call-update) | async-done | bytes 1179664 | tf_op jit(solution)/shard_map/all_gather | solution.py:80
  179.7 4.5 fusion.18
  184.1 6.3 reshape.179
  190.4 7.5 copy.107
  197.9 10.2 fusion.37
  208.1 8.6 fusion.6
  216.8 7.7 convert_bitcast_fusion.1
  226.3 4.4 convert_element_type.140
  230.7 4.7 all-gather.13.cloned.1.call-done
  235.4 4.1 fusion.38
  240.1 60.7 %all-gather.15.cloned.1.call-done = bf16[768,3072]{1,0:T(8,128)(2,1)} async-done(((bf16[24,3072]{1,0:T(8,128)(2,1)}), bf16[768,3072]{1,0:T(8,128)(2,1)}) %all-gather.15.cloned.1.call-update) | async-done | bytes 4718608 | tf_op jit(solution)/shard_map/all_gather | solution.py:91
  300.8 39.3 %multiply_convert_fusion.1 = (bf16[1120,3072]{1,0:T(8,128)(2,1)}, f32[1120,3072]{1,0:T(8,128)}, f32[1120,3072]{1,0:T(8,128)}) fusion(f32[3072]{0:T(1024)S(1)} %convert_element_type.145, bf16[768,3072]{1,0:T(8,128)(2,1)} %all-gather.15.cloned.1.call-done, f32[1120,768]{1,0:T(8,128)S(1)} %get-tuple-element.121, f32[768]{0:T(1024)S(1)} %convert_element_type.143, ...), kind=kOutput, calls=%fused_computation.7 | convolution fusion | flops 5516206080 | bytes 42593024 | tf_op jit(solution)/shard_map/dot_general | solution.py:16
  340.0 26.0 %all-gather.17.cloned.1.call-done = bf16[3072,768]{1,0:T(8,128)(2,1)} async-done(((bf16[96,768]{1,0:T(8,128)(2,1)}), bf16[3072,768]{1,0:T(8,128)(2,1)}) %all-gather.17.cloned.1.call-update) | async-done | bytes 4718608 | tf_op jit(solution)/shard_map/all_gather | solution.py:93
  366.0 10.4 fusion.39
  382.9 20.3 %convert_reduce_fusion = (f32[3072]{0:T(1024)S(1)}, bf16[1120,3072]{1,0:T(8,128)(2,1)}) fusion(f32[1120,3072]{1,0:T(8,128)} %get-tuple-element.116, f32[1120,3072]{1,0:T(8,128)} %get-tuple-element.122, bf16[3072,768]{1,0:T(8,128)(2,1)} %all-gather.17.cloned.1.call-done, f32[1120,768]{1,0:T(8,128)} %get-tuple-element.112), kind=kOutput, calls=%fused_computation.2 | convolution fusion | flops 5340730368 | bytes 42577920 | tf_op jit(solution)/shard_map/dot_general | solution.py:26
  403.2 12.0 %multiply_reduce_fusion.2 = (f32[768]{0:T(1024)S(1)}, f32[1120]{0:T(1024)S(1)}, f32[1120]{0:T(1024)S(1)}, f32[768]{0:T(1024)S(1)}, f32[1120,768]{1,0:T(8,128)S(1)}) fusion(f32[1120,768]{1,0:T(8,128)S(1)} %get-tuple-element.121, f32[1120]{0:T(1024)S(1)} %add_rsqrt_fusion.1, f32[1120]{0:T(1024)S(1)} %broadcast_multiply_fusion.5, ...), kind=kOutput, calls=%fused_computation.46 | convolution fusion | flops 5293420544 | bytes 21948928 | tf_op jit(solution)/shard_map/dot_general | solution.py:26
  421.9 3.9 convolution_convert_fusion
  425.7 4.5 reshape.181
  430.2 6.1 copy.115
  436.3 7.8 convert_reduce_fusion.1
  444.2 3.6 copy.125
  447.7 6.0 reshape.152
  453.7 5.1 convolution_bitcast_fusion
  462.2 10.8 multiply_reduce_fusion
  473.0 10.8 multiply_convert_fusion
  488.5 3.9 reshape.151
  492.4 5.2 convolution_bitcast_fusion.1
  501.1 4.2 convert_reduce_fusion.2
  507.2 4.0 reshape.150
  511.1 5.2 convolution_bitcast_fusion.2
  516.3 3.2 copy.133
  519.6 12.0 %fusion.33 = f32[768,3072]{1,0:T(8,128)} fusion(bf16[1120,3072]{1,0:T(8,128)(2,1)} %get-tuple-element.133, f32[1120,768]{1,0:T(8,128)S(1)} %copy-done.4, f32[768]{0:T(1024)S(1)} %convert_element_type.143, f32[768]{0:T(1024)S(1)} %convert_element_type.142, f32[1120]{0:T(1024)S(1)} %add_rsqrt_fusion.1, f32[1120]{0:T(1024)S(1)} %broadcast_multiply_fusion.5), kind=kOutput, calls=%fused_computation.96 | convolution fusion | flops 5289123840 | bytes 19774208 | tf_op jit(solution)/shard_map/dot_general | solution.py:20
  533.7 10.7 fusion.30
  544.6 40.4 %all-reduce.18 = (f32[768]{0:T(1024)S(1)}, f32[768]{0:T(1024)S(1)}, f32[768]{0:T(1024)S(1)}, f32[768]{0:T(1024)S(1)}, f32[768]{0:T(1024)S(1)}, /*index=5*/f32[30...) all-reduce(f32[768]{0:T(1024)S(1)} %reduce_sum.186, ...), channel_id=3, replica_groups=mesh['fsdp'=32] {'fsdp'}, use_global_device_ids=true, to_apply=%region_14.15.clone | all-reduce | flops 9216 | bytes 73728
  590.3 3.6 convolution_add_fusion.5
  598.6 25.6 %reduce-scatter.23.cloned.1.call-done = f32[24,768]{1,0:T(8,128)} async-done(((f32[768,768]{1,0:T(8,128)}), f32[24,768]{1,0:T(8,128)}) %reduce-scatter.23.cloned.1.call-update) | async-done | bytes 73744
  624.2 103.9 %reduce-scatter.21.cloned.1.call-done = f32[24,768]{1,0:T(8,128)} async-done(((f32[768,768]{1,0:T(8,128)}), f32[24,768]{1,0:T(8,128)}) %reduce-scatter.21.cloned.1.call-update) | async-done | bytes 73744
  728.1 104.6 %reduce-scatter.19.cloned.1.call-done = f32[24,768]{1,0:T(8,128)} async-done(((f32[768,768]{1,0:T(8,128)}), f32[24,768]{1,0:T(8,128)}) %reduce-scatter.19.cloned.1.call-update) | async-done | bytes 73744
  832.8 141.0 %reduce-scatter.15.cloned.1.call-done = f32[24,3072]{1,0:T(8,128)} async-done(((f32[768,3072]{1,0:T(8,128)}), f32[24,3072]{1,0:T(8,128)}) %reduce-scatter.15.cloned.1.call-update) | async-done | bytes 294928 | tf_op jit(solution)/shard_map/reduce_scatter | solution.py:170
  973.8 142.1 %reduce-scatter.17.cloned.1.call-done = f32[96,768]{1,0:T(8,128)} async-done(((f32[3072,768]{1,0:T(8,128)}), f32[96,768]{1,0:T(8,128)}) %reduce-scatter.17.cloned.1.call-update) | async-done | bytes 294928 | tf_op jit(solution)/shard_map/reduce_scatter | solution.py:172
  (140 shorter events, 59.1 us)
Async XLA Ops:
  7.2 60.7 %all-gather.11.cloned.1.call-start = ((), (), s32[]{:S(2)}) async-start(), calls=%async_computation.8 | async-start | bytes 1216512 | tf_op jit(solution)/shard_map/all_gather | solution.py:82
  7.9 115.8 %all-gather.7.cloned.1.call-start = ((), (), s32[]{:S(2)}) async-start(), calls=%async_computation.6 | async-start | bytes 1216512 | tf_op jit(solution)/shard_map/all_gather | solution.py:83
  8.7 171.0 %all-gather.9.cloned.1.call-start = ((), (), s32[]{:S(2)}) async-start(), calls=%async_computation.7 | async-start | bytes 1216512 | tf_op jit(solution)/shard_map/all_gather | solution.py:80
  9.4 226.0 %all-gather.13.cloned.1.call-start = ((), (), s32[]{:S(2)}) async-start(), calls=%async_computation.9 | async-start | bytes 1216512 | tf_op jit(solution)/shard_map/all_gather | solution.py:85
  10.0 290.8 %all-gather.15.cloned.1.call-start = ((), (), s32[]{:S(2)}) async-start(), calls=%async_computation.10 | async-start | bytes 4866048 | tf_op jit(solution)/shard_map/all_gather | solution.py:91
  10.6 355.4 %all-gather.17.cloned.1.call-start = ((), (), s32[]{:S(2)}) async-start(), calls=%async_computation.11 | async-start | bytes 4866048 | tf_op jit(solution)/shard_map/all_gather | solution.py:93
  11.1 587.4 %reduce-scatter.13.cloned.1.call-start = ((), (), s32[]{:S(2)}) async-start(), calls=%async_computation.12 | async-start | bytes 2433024 | tf_op jit(solution)/shard_map/reduce_scatter | solution.py:229
  81.7 116.2 %copy-start.1 = (bf16[7,160,12,64]{1,3,2,0:T(8,128)(2,1)}, bf16[7,160,12,64]{1,3,2,0:T(8,128)(2,1)S(1)}, u32[]{:S(2)}) copy-start(bf16[7,160,12,64]{1,3,2,0:T(8,128)(2,1)S(1)} %copy.108) | copy-start | bytes 5160964
  208.1 8.6 copy-start.14
  208.1 8.6 copy-start.6
  216.7 7.7 copy-start.16
  239.5 175.7 %copy-start.3 = (f32[1120,768]{1,0:T(8,128)}, f32[1120,768]{1,0:T(8,128)S(1)}, u32[]{:S(2)}) copy-start(f32[1120,768]{1,0:T(8,128)S(1)} %get-tuple-element.121) | copy-start | bytes 10321924
  240.1 126.0 %copy-start.21 = (f32[768]{0:T(1024)S(1)}, f32[768]{0:T(1024)}, u32[]{:S(2)}) copy-start(f32[768]{0:T(1024)} %convert_element_type.147) | copy-start | bytes 9220
  376.4 1.5 copy-start.7
  376.4 1.5 copy-start.18
  376.5 1.4 copy-start.19
  377.0 2.7 copy-start.20
  415.2 3.0 copy-start.13
  416.5 1.7 copy-start.8
  418.2 3.7 copy-start.15
  418.2 3.7 copy-start.17
  421.4 202.8 %reduce-scatter.23.cloned.1.call-start = ((), (), s32[]{:S(2)}) async-start(), calls=%async_computation.17 | async-start | bytes 2433024
  461.9 266.2 %reduce-scatter.21.cloned.1.call-start = ((), (), s32[]{:S(2)}) async-start(), calls=%async_computation.16 | async-start | bytes 2433024
  473.0 10.8 copy-start.5
  483.8 2.8 copy-start
  497.6 3.5 copy-start.2
  500.8 332.0 %reduce-scatter.19.cloned.1.call-start = ((), (), s32[]{:S(2)}) async-start(), calls=%async_computation.15 | async-start | bytes 2433024
  516.3 3.3 copy-start.4
  519.6 454.2 %reduce-scatter.15.cloned.1.call-start = ((), (), s32[]{:S(2)}) async-start(), calls=%async_computation.13 | async-start | bytes 9732096 | tf_op jit(solution)/shard_map/reduce_scatter | solution.py:170
  531.7 2.0 copy-start.10
  531.7 584.1 %reduce-scatter.17.cloned.1.call-start = ((), (), s32[]{:S(2)}) async-start(), calls=%async_computation.14 | async-start | bytes 9732096 | tf_op jit(solution)/shard_map/reduce_scatter | solution.py:172
  544.5 45.9 %copy-start.9 = (f32[1120,768]{1,0:T(8,128)S(1)}, f32[1120,768]{1,0:T(8,128)}, u32[]{:S(2)}) copy-start(f32[1120,768]{1,0:T(8,128)} %copy-done.8) | copy-start | bytes 10321924
  590.3 3.6 copy-start.12
  590.3 3.6 copy-start.22
  594.0 1.7 copy-start.11
  594.0 1.8 copy-start.23
Sparse Core Ops, SparseCore 0:
  10.9 56.9 all-gather.10
  70.8 52.8 all-gather.6
  126.6 52.9 all-gather.8
  182.4 52.9 all-gather.12
  238.2 62.5 all-gather.14
  303.5 62.4 all-gather.16
  421.5 97.8 reduce-scatter.12
  526.1 98.1 reduce-scatter.22
  630.1 98.0 reduce-scatter.20
  734.7 98.0 reduce-scatter.18
  839.2 134.4 reduce-scatter.14
  981.1 134.6 reduce-scatter.16
where the time goes:
time: 1130 us; the launch traced here: 1120 us
  waiting for transfers between devices  694 us (61%)
  matrix products  195 us (17%)
  local copies, waits for them, and re-layouts  106 us (9%)
  blocking collectives  82.9 us (7%)
  other arithmetic  29.4 us (3%)
  between operations  15.1 us (1%)
    unnamed x15, waiting for transfers between devices  238 us
    reduce_scatter x1, waiting for transfers between devices, shards(): lax.psum_scatter(down_grad, 'fsdp', scatter_dimension=0, tiled=True)  142 us
    reduce_scatter x1, waiting for transfers between devices, shards(): lax.psum_scatter(up_grad, 'fsdp', scatter_dimension=0, tiled=True)  141 us
    unnamed x2, blocking collectives  82.9 us
    dot_general x6, matrix products, matmul(): return jnp.dot(left, right, preferred_element_type=jnp.float32)  66 us
    all_gather x1, waiting for transfers between devices, shards(): lax.all_gather(up_weight, 'fsdp', axis=0, tiled=True)  60.7 us
    dot_general x6, matrix products, inner_right(): lax.dot_general(left, right, (((1,), (1,)), ((), ())), preferred_element_...  44.2 us
    all_gather x1, waiting for transfers between devices, shards(): lax.all_gather(value_weight, 'fsdp', axis=0, tiled=True)  42 us
  transfers between devices with their start and end apart: 12, of which 11 were waited for; matrix products, arithmetic and copies ran while one was open for 24% of the time, Pallas kernels for 0%

commit v1 on v0

v1 whole, which is shorter than its diff:
```python
import functools
import jax
import jax.numpy as jnp
from jax import lax
from jax.sharding import PartitionSpec as P
from jax.experimental import pallas as pl
from jax.experimental.pallas import tpu as pltpu

D = 768
HEADS = 12
HEAD = 64
epsilon = 1e-05
masked_score = -1000000000.0
F32 = jnp.float32
BF16 = jnp.bfloat16


def dot(left, right):
    return lax.dot_general(left, right, (((1,), (0,)), ((), ())), preferred_element_type=F32)


def dot_rt(left, right):
    return lax.dot_general(left, right, (((1,), (1,)), ((), ())), preferred_element_type=F32)


def dot_lt(left, right):
    return lax.dot_general(left, right, (((0,), (0,)), ((), ())), preferred_element_type=F32)


def call(body, grid, in_specs, out_specs, out_shape, scratch=(), flops=0, moved=0, vmem=60):
    return pl.pallas_call(
        body,
        grid_spec=pltpu.PrefetchScalarGridSpec(
            num_scalar_prefetch=0, grid=grid, in_specs=in_specs, out_specs=out_specs, scratch_shapes=scratch
        ),
        out_shape=out_shape,
        compiler_params=pltpu.CompilerParams(vmem_limit_bytes=vmem * 1024 * 1024),
        cost_estimate=pl.CostEstimate(flops=flops, bytes_accessed=moved, transcendentals=0),
    )


def shaped(shape, dtype):
    return jax.ShapeDtypeStruct(shape, dtype)


def half_mask(dtype, scale=1.0):
    lane = lax.broadcasted_iota(jnp.int32, (1, 128), 1)
    low = jnp.where(lane < HEAD, scale, 0.0).astype(dtype)
    high = jnp.where(lane < HEAD, 0.0, scale).astype(dtype)
    return low, high


def attn_fwd_body(len_ref, x_ref, wq_ref, wk_ref, wv_ref, bq_ref, bv_ref, q_ref, k_ref, v_ref, mix_ref, lse_ref):
    c = pl.program_id(0)
    x = x_ref[...]
    length = x.shape[0]
    q_ref[...] = (dot(x, wq_ref[...]) + bq_ref[...]).astype(BF16)
    k_ref[...] = dot(x, wk_ref[...]).astype(BF16)
    v_ref[...] = (dot(x, wv_ref[...]) + bv_ref[...]).astype(BF16)
    valid = lax.broadcasted_iota(jnp.int32, (1, length), 1) < len_ref[c]
    masks = half_mask(BF16, 0.125)
    lane = lax.broadcasted_iota(jnp.int32, (1, 128), 1)
    lses = jnp.zeros((length, 128), F32)
    for p in range(HEADS // 2):
        cols = slice(128 * p, 128 * p + 128)
        qp, kp, vp = q_ref[:, cols], k_ref[:, cols], v_ref[:, cols]
        outs = []
        for t in range(2):
            s = dot_rt(qp * masks[t], kp)
            s = jnp.where(valid, s, masked_score)
            m = jnp.max(s, axis=1, keepdims=True)
            e = jnp.exp(s - m)
            total = jnp.sum(e, axis=1, keepdims=True)
            pr = (e * (1.0 / total)).astype(BF16)
            outs.append(dot(pr, vp))
            lses = jnp.where(lane == 2 * p + t, m + jnp.log(total), lses)
        mix_ref[:, cols] = jnp.where(lane < HEAD, outs[0], outs[1]).astype(BF16)
    lse_ref[...] = lses


def attn_fwd(x, wq, wk, wv, bq, bv, lengths):
    rows = x.shape[0]
    n = lengths.shape[0]
    length = rows // n
    tile = pl.BlockSpec((length, D), lambda c: (c, 0))
    full = pl.BlockSpec((D, D), lambda c: (0, 0))
    one = pl.BlockSpec((1, D), lambda c: (0, 0))
    act = shaped((rows, D), BF16)
    return call(
        attn_fwd_body, (n,),
        [pl.BlockSpec(memory_space=pltpu.SMEM), tile, full, full, full, one, one],
        [tile, tile, tile, tile, pl.BlockSpec((length, 128), lambda c: (c, 0))],
        [act, act, act, act, shaped((rows, 128), F32)],
        flops=2 * rows * D * D * 3 + 4 * rows * length * D * 4, moved=rows * D * 10 + 6 * D * D,
    )(lengths, x, wq, wk, wv, bq, bv)


def attn_bwd_body(len_ref, q_ref, k_ref, v_ref, gm_ref, lse_ref, gq_ref, gk_ref, gv_ref, gbq_ref, gbv_ref):
    c = pl.program_id(0)
    length = q_ref.shape[0]
    valid = lax.broadcasted_iota(jnp.int32, (1, length), 1) < len_ref[c]
    masks = half_mask(BF16)
    scaled = half_mask(BF16, 0.125)

    @pl.when(c == 0)
    def _():
        gbq_ref[...] = jnp.zeros_like(gbq_ref)
        gbv_ref[...] = jnp.zeros_like(gbv_ref)

    for p in range(HEADS // 2):
        cols = slice(128 * p, 128 * p + 128)
        qp, kp, vp, gm = q_ref[:, cols], k_ref[:, cols], v_ref[:, cols], gm_ref[:, cols]
        gq, gk, gv = 0.0, 0.0, 0.0
        for t in range(2):
            h = 2 * p + t
            qt = qp * scaled[t]
            kt = kp * scaled[t]
            gt = gm * masks[t]
            s = dot_rt(qt, kp)
            s = jnp.where(valid, s, masked_score)
            pf = jnp.exp(s - lse_ref[:, h : h + 1])
            gp = dot_rt(gt, vp)
            gs = pf * (gp - jnp.sum(pf * gp, axis=1, keepdims=True))
            gs = gs.astype(BF16)
            gv = gv + dot_lt(pf.astype(BF16), gt)
            gq = gq + dot(gs, kt)
            gk = gk + dot_lt(gs, qt)
        gq, gk, gv = gq.astype(BF16), gk.astype(BF16), gv.astype(BF16)
        gq_ref[:, cols] = gq
        gk_ref[:, cols] = gk
        gv_ref[:, cols] = gv
        gbq_ref[:, cols] += jnp.sum(gq.astype(F32), axis=0, keepdims=True)
        gbv_ref[:, cols] += jnp.sum(gv.astype(F32), axis=0, keepdims=True)


def attn_bwd(q, k, v, gm, lse, lengths):
    rows = q.shape[0]
    n = lengths.shape[0]
    length = rows // n
    tile = pl.BlockSpec((length, D), lambda c: (c, 0))
    one = pl.BlockSpec((1, D), lambda c: (0, 0))
    act = shaped((rows, D), BF16)
    return call(
        attn_bwd_body, (n,),
        [pl.BlockSpec(memory_space=pltpu.SMEM), tile, tile, tile, tile, pl.BlockSpec((length, 128), lambda c: (c, 0))],
        [tile, tile, tile, one, one],
        [act, act, act, shaped((1, D), F32), shaped((1, D), F32)],
        flops=2 * rows * length * D * 5 * 4, moved=rows * D * 14,
    )(lengths, q, k, v, gm, lse)


def mean(v):
    return jnp.sum(v, axis=-1, keepdims=True) * (1.0 / D)


def normalize(values):
    center = values - mean(values)
    scale = lax.rsqrt(mean(center * center) + epsilon)
    return center * scale, scale


def norm_back(incoming, normed, scale, gain):
    weighted = incoming * gain
    return scale * (weighted - mean(weighted) - normed * mean(weighted * normed))


def colsum(v):
    return jnp.sum(v, axis=0, keepdims=True)


def gelu_parts(pre):
    cdf = 0.5 + 0.5 * lax.erf(pre * 0.7071067811865476)
    pdf = 0.3989422804014327 * jnp.exp(-0.5 * pre * pre)
    return pre * cdf, cdf + pre * pdf


def ffn_body(chunk, mix_ref, x_ref, gy_ref, wo_ref, wu_ref, wd_ref, small_ref, ub_ref,
             out_ref, hid_ref, gffn_ref, low_ref, gpre_ref, gattn_ref, g1_ref, gmix_ref, gsmall_ref, gub_ref, dg_ref):
    i = pl.program_id(0)
    bo, again, ashift, bd, fgain, fshift = (small_ref[j : j + 1, :] for j in range(6))
    ff = wu_ref.shape[1]

    @pl.when(i == 0)
    def _():
        gsmall_ref[...] = jnp.zeros_like(gsmall_ref)
        gub_ref[...] = jnp.zeros_like(gub_ref)

    attn = dot(mix_ref[...], wo_ref[...]) + bo
    xhat1, rs1 = normalize(x_ref[...].astype(F32) + attn)
    first = xhat1 * again + ashift
    low = first.astype(BF16)
    low_ref[...] = low
    ffn = 0.0
    for j in range(ff // chunk):
        cols = slice(j * chunk, (j + 1) * chunk)
        pre = dot(low, wu_ref[:, cols]) + ub_ref[:, cols]
        hid, dg = gelu_parts(pre)
        hid = hid.astype(BF16)
        hid_ref[:, cols] = hid
        dg_ref[:, cols] = dg.astype(dg_ref.dtype)
        ffn = ffn + dot(hid, wd_ref[cols, :])
    xhat2, rs2 = normalize(first + ffn + bd)
    out_ref[...] = (xhat2 * fgain + fshift).astype(BF16)
    gy = gy_ref[...].astype(F32)
    g2 = norm_back(gy, xhat2, rs2, fgain)
    gffn = g2.astype(BF16)
    gffn_ref[...] = gffn
    gsmall_ref[3:4, :] += colsum(gffn.astype(F32))
    gsmall_ref[4:5, :] += colsum(gy * xhat2)
    gsmall_ref[5:6, :] += colsum(gy)
    gfirst = g2
    for j in range(ff // chunk):
        cols = slice(j * chunk, (j + 1) * chunk)
        gh = dot_rt(gffn, wd_ref[cols, :])
        gpre = (gh * dg_ref[:, cols].astype(F32)).astype(BF16)
        gpre_ref[:, cols] = gpre
        gub_ref[:, cols] += colsum(gpre.astype(F32))
        gfirst = gfirst + dot_rt(gpre, wu_ref[:, cols])
    g1 = norm_back(gfirst, xhat1, rs1, again)
    gattn = g1.astype(BF16)
    g1_ref[...] = g1
    gattn_ref[...] = gattn
    gsmall_ref[0:1, :] += colsum(gattn.astype(F32))
    gsmall_ref[1:2, :] += colsum(gfirst * xhat1)
    gsmall_ref[2:3, :] += colsum(gfirst)
    gmix_ref[...] = dot_rt(gattn, wo_ref[...]).astype(BF16)


def ffn_both(mixed, x, gy, wo, wu, wd, small, ub, tile_rows=280, chunk=768, dg_dtype=F32):
    rows = x.shape[0]
    ff = wu.shape[1]
    n = rows // tile_rows
    tile = pl.BlockSpec((tile_rows, D), lambda c: (c, 0))
    wide = pl.BlockSpec((tile_rows, ff), lambda c: (c, 0))
    fixed = lambda s: pl.BlockSpec(s, lambda c: (0, 0), pipeline_mode=pl.Buffered(1))
    act = shaped((rows, D), BF16)
    big = shaped((rows, ff), BF16)
    return call(
        functools.partial(ffn_body, chunk), (n,),
        [tile, tile, tile, fixed((D, D)), fixed((D, ff)), fixed((ff, D)), fixed((8, D)), fixed((1, ff))],
        [tile, wide, tile, tile, wide, tile, tile, tile, pl.BlockSpec((8, D), lambda c: (0, 0)), pl.BlockSpec((1, ff), lambda c: (0, 0))],
        [act, big, act, act, big, act, shaped((rows, D), F32), act, shaped((8, D), F32), shaped((1, ff), F32)],
        scratch=[pltpu.VMEM((tile_rows, ff), dg_dtype)],
        flops=2 * rows * D * (2 * D + 4 * ff), moved=rows * (D * 20 + ff * 4) + D * (D + 2 * ff) * 2,
    )(mixed, x, gy, wo, wu, wd, small, ub)


def wgrad_body(l_ref, r_ref, o_ref):
    o_ref[...] = dot_lt(l_ref[...], r_ref[...]).astype(o_ref.dtype)


def wgrad(left, right, tile_m=384, dtype=BF16):
    rows, m = left.shape
    n = right.shape[1]
    tn = min(n, 768)
    return call(
        wgrad_body, (n // tn, m // tile_m),
        [pl.BlockSpec((rows, tile_m), lambda j, i: (0, i)), pl.BlockSpec((rows, tn), lambda j, i: (0, j))],
        pl.BlockSpec((tile_m, tn), lambda j, i: (i, j)),
        shaped((m, n), dtype),
        flops=2 * rows * m * n, moved=2 * (rows * (m + n) + m * n),
    )(left, right)


def wgrad3_body(l_ref, a_ref, b_ref, c_ref, oa_ref, ob_ref, oc_ref):
    left = l_ref[...]
    for r_ref, o_ref in ((a_ref, oa_ref), (b_ref, ob_ref), (c_ref, oc_ref)):
        o_ref[...] = dot_lt(left, r_ref[...]).astype(o_ref.dtype)


def wgrad3(left, a, b, c, tile_m=384, dtype=BF16):
    rows = left.shape[0]
    right = pl.BlockSpec((rows, D), lambda i: (0, 0))
    out = pl.BlockSpec((tile_m, D), lambda i: (i, 0))
    return call(
        wgrad3_body, (D // tile_m,),
        [pl.BlockSpec((rows, tile_m), lambda i: (0, i)), right, right, right],
        [out, out, out],
        [shaped((D, D), dtype)] * 3,
        flops=6 * rows * D * D, moved=2 * (4 * rows * D + 3 * D * D),
    )(left, a, b, c)


def input_grad_body(g1_ref, gq_ref, gk_ref, gv_ref, wq_ref, wk_ref, wv_ref, o_ref):
    total = g1_ref[...] + dot_rt(gq_ref[...], wq_ref[...])
    total = total + dot_rt(gk_ref[...], wk_ref[...]) + dot_rt(gv_ref[...], wv_ref[...])
    o_ref[...] = total.astype(BF16)


def input_grad(g1, gq, gk, gv, wq, wk, wv, tile_rows=280):
    rows = g1.shape[0]
    tile = pl.BlockSpec((tile_rows, D), lambda c: (c, 0))
    full = pl.BlockSpec((D, D), lambda c: (0, 0))
    return call(
        input_grad_body, (rows // tile_rows,),
        [tile, tile, tile, tile, full, full, full], tile, shaped((rows, D), BF16),
        flops=6 * rows * D * D, moved=rows * D * 12 + 6 * D * D,
    )(g1, gq, gk, gv, wq, wk, wv)


def shards(
    tokens, cotangent, lengths, span_start, span_end,
    query_weight, query_bias, key_weight, value_weight, value_bias, out_weight, out_bias,
    attn_gain, attn_shift, up_weight, up_bias, down_weight, down_bias, ffn_gain, ffn_shift,
):
    chains = lengths.shape[0]
    rows = tokens.shape[0]
    length = rows // chains
    own = query_weight.shape[0]
    parts = D // own
    ff = up_weight.shape[1]
    vectors = (query_bias, value_bias, out_bias, attn_gain, attn_shift, down_bias, ffn_gain, ffn_shift, up_bias)
    packed = jnp.concatenate(vectors)
    packed = jnp.pad(packed, (0, D - packed.shape[0])).reshape(1, D)
    wide = own * ff // D
    sent = jnp.concatenate(
        [query_weight, key_weight, value_weight, out_weight, up_weight.reshape(own, ff // D, D).swapaxes(0, 1).reshape(wide, D), down_weight, packed],
        axis=0,
    )
    held = lax.all_gather(sent, "fsdp", axis=0, tiled=False)
    wq, wk, wv, wo = (held[:, own * i : own * (i + 1)].reshape(D, D) for i in range(4))
    wu = jnp.concatenate(
        [held[:, own * (4 + i) : own * (5 + i)].reshape(D, D) for i in range(ff // D)], axis=1
    )
    wd = held[:, 4 * own + wide : 4 * own + 2 * wide].reshape(ff, D)
    small = held[:, -1].astype(F32)
    qb, vb, ob, again, ashift, db, fgain, fshift = (
        small[:, own * i : own * (i + 1)].reshape(1, D) for i in range(8)
    )
    ub = small[:, 8 * own : 8 * own + wide].reshape(1, ff)
    zero = jnp.zeros((1, D), F32)
    table = jnp.concatenate([ob, again, ashift, db, fgain, fshift, zero, zero], axis=0)

    positions = jnp.arange(length)
    inside = jnp.any(
        (positions[None, None, :] >= span_start[:, :, None]) & (positions[None, None, :] < span_end[:, :, None]),
        axis=1,
    )
    gy = jnp.where(inside.reshape(rows, 1), cotangent, jnp.zeros_like(cotangent))

    q, k, v, mixed, lse = attn_fwd(tokens, wq, wk, wv, qb, vb, lengths)
    layer_out, hidden, gffn, low, gpre, gattn, g1, gmixed, gtable, gub = ffn_both(
        mixed, tokens, gy, wo, wu, wd, table, ub
    )
    down_grad = wgrad(hidden, gffn)
    up_grad = wgrad(low, gpre)
    gathered_ffn = jnp.concatenate(
        [up_grad.reshape(parts, wide, D), down_grad.reshape(parts, wide, D)], axis=1
    )
    ffn_own = lax.psum_scatter(gathered_ffn, "fsdp", scatter_dimension=0, tiled=False)
    out_grad = wgrad(mixed, gattn)
    gq, gk, gv, gqb, gvb = attn_bwd(q, k, v, gmixed, lse, lengths)
    query_grad, key_grad, value_grad = wgrad3(tokens, gq, gk, gv)
    parts_of = [gqb, gvb, gtable[0:1], gtable[1:2], gtable[2:3], gtable[3:4], gtable[4:5], gtable[5:6]]
    vec = jnp.concatenate([p.reshape(parts, own) for p in parts_of] + [gub.reshape(parts, wide)], axis=1)
    vec = jnp.pad(vec.astype(BF16), ((0, 0), (0, D - vec.shape[1]))).reshape(parts, 1, D)
    attn_parts = jnp.concatenate(
        [g.reshape(parts, own, D) for g in (query_grad, key_grad, value_grad, out_grad)] + [vec], axis=1
    )
    attn_own = lax.psum_scatter(attn_parts, "fsdp", scatter_dimension=0, tiled=False)
    in_grad = input_grad(g1, gq, gk, gv, wq, wk, wv)

    attn_own = attn_own.astype(F32)
    ffn_own = ffn_own.astype(F32)
    gq_w, gk_w, gv_w, go_w = (attn_own[own * i : own * (i + 1)] for i in range(4))
    vec = attn_own[-1]
    gqb, gvb, gob, gag, gas, gdb, gfg, gfs = (vec[own * i : own * (i + 1)] for i in range(8))
    gub = vec[8 * own : 8 * own + wide]
    gup = ffn_own[:wide].reshape(own, ff)
    gdown = ffn_own[wide:]
    return (
        layer_out, in_grad, gq_w, gqb, gk_w, gv_w, gvb, go_w, gob, gag, gas, gup, gub, gdown, gdb, gfg, gfs,
    )


def solution(mesh):
    two, one = P("fsdp", None), P("fsdp")
    return jax.shard_map(
        shards,
        mesh=mesh,
        in_specs=(two, two, one, two, two, two, one, two, two, one, two, one, one, one, two, one, two, one, one, one),
        out_specs=(two, two, two, one, two, two, one, two, one, one, one, two, one, two, one, one, one),
        check_vma=False,
    )
```

time: 1130 us -> 512 us (0.45)
  waiting for transfers between devices: 694 us -> 298 us
  matrix products: 195 us -> 0 us
  Pallas kernels: 0 us -> 132 us
  blocking collectives: 82.9 us -> 0 us
  local copies, waits for them, and re-layouts: 106 us -> 49.8 us
  other arithmetic: 29.4 us -> 16.9 us
    unnamed x15 -> x3, waiting for transfers between devices: 238 us -> 0.05 us
    dot_general x24 -> x0, matrix products: 195 us -> none  [the longest x6 66 us: matmul(): return jnp.dot(left, right, preferred_element_type=jnp.float32)]
    pallas_call x0 -> x8, Pallas kernels: none -> 132 us  [the longest x1 40.3 us: ffn_both(): call(functools.partial(ffn_body, chunk), (n,), [tile, tile, tile, fixed((...]
    reduce_scatter x3 -> x2, waiting for transfers between devices: 283 us -> 195 us  [the longest x1 139 us: shards(): lax.psum_scatter(gathered_ffn, 'fsdp', scatter_dimension=0, tiled=False)]
    unnamed x2 -> x0, blocking collectives: 82.9 us -> none
    all_gather x6 -> x1, waiting for transfers between devices: 173 us -> 103 us  [shards(): held = lax.all_gather(sent, 'fsdp', axis=0, tiled=False)]
    reshape x11 -> x22, local copies, waits for them, and re-layouts: 62.3 us -> 13.6 us  [the longest x1 8.54 us: shards(): up_grad.reshape(parts, wide, D)]
    reduce_sum x6 -> x0, other arithmetic: 15.9 us -> none  [the longest x1 8.59 us: shards(): total = jnp.sum(expo, axis=-1, keepdims=True)]
  transfers between devices with their start and end apart: 12 -> 3, of which waited for: 11 -> 3; matrix products, arithmetic and copies ran while one was open for 24% -> 5% of each run, Pallas kernels for 0% -> 7%
where the time goes in v1:
time: 512 us; the launch traced here: 510 us
  waiting for transfers between devices  298 us (58%)
  Pallas kernels  132 us (26%)
  local copies, waits for them, and re-layouts  49.8 us (10%)
  other arithmetic  16.9 us (3%)
  between operations  13.9 us (3%)
    reduce_scatter x1, waiting for transfers between devices, shards(): lax.psum_scatter(gathered_ffn, 'fsdp', scatter_dimension=0, tiled=False)  139 us
    all_gather x1, waiting for transfers between devices, shards(): held = lax.all_gather(sent, 'fsdp', axis=0, tiled=False)  103 us
    reduce_scatter x1, waiting for transfers between devices, shards(): lax.psum_scatter(attn_parts, 'fsdp', scatter_dimension=0, tiled=False)  55.9 us
    pallas_call x1, Pallas kernels, ffn_both(): call(functools.partial(ffn_body, chunk), (n,), [tile, tile, tile, fixed((...  40.3 us
    pallas_call x3, Pallas kernels, wgrad(): call(wgrad_body, (n // tn, m // tile_m), [pl.BlockSpec((rows, tile_m), la...  30.4 us
    pallas_call x1, Pallas kernels, attn_bwd(): call(attn_bwd_body, (n,), [pl.BlockSpec(memory_space=pltpu.SMEM), tile, t...  26 us
    pallas_call x1, Pallas kernels, attn_fwd(): call(attn_fwd_body, (n,), [pl.BlockSpec(memory_space=pltpu.SMEM), tile, f...  17.2 us
    unnamed x23, local copies, waits for them, and re-layouts  13.6 us
  transfers between devices with their start and end apart: 3, of which 3 were waited for; matrix products, arithmetic and copies ran while one was open for 5% of the time, Pallas kernels for 7%

profile of v1, /device:TPU:0, one launch (start us, length us, event | category | flops | bytes accessed | tf_op | source)
XLA Modules:
  0.0 510.3 jit_solution(8488967169958476810)
XLA Ops:
  7.2 0.9 copy.57
  8.2 0.8 constant_dynamic-update-slice_fusion.6
  8.9 6.1 %concatenate.25 = bf16[288]{0:T(512)(128)(2,1)S(1)} concatenate(bf16[24]{0:T(256)(128)(2,1)} %param.26, bf16[24]{0:T(256)(128)(2,1)} %param.29, bf16[24]{0:T(256)(128)(2,1)} %param.31, bf16[24]{0:T(256)(128)(2,1)} %param.32, bf16[24]{0:T(256)(128)(2,1)} %param.33, bf16[24]{0:T(256)(128)(2,1)} %param.37, bf16[24]{0:T(256)(128)(2,1)} %param.38, bf16[24]{0:T(256)(128)(2,1)} %param.39, ...), dimensions={0} | concatenate | bytes 1152 | tf_op jit(solution)/shard_map/concatenate | solution.py:313
  15.0 0.8 constant_dynamic-update-slice_fusion.5
  15.8 0.8 constant_dynamic-update-slice_fusion.4
  16.6 0.8 constant_dynamic-update-slice_fusion.3
  17.4 0.9 constant_dynamic-update-slice_fusion.1
  18.3 0.8 copy-done.2
  19.2 0.8 copy.49
  19.9 0.8 copy.50
  20.7 0.1 fusion.1
  20.9 2.9 broadcast_select_fusion.gy_ref
  23.8 103.1 %all-gather.4.cloned.1.call-done = bf16[32,289,768]{2,1,0:T(8,128)(2,1)} async-done(((bf16[1,289,768]{2,1,0:T(8,128)(2,1)}), bf16[32,289,768]{2,1,0:T(8,128)(2,1)}) %all-gather.4.cloned.1.call-update) | async-done | bytes 14204944 | tf_op jit(solution)/shard_map/all_gather | solution.py:320
  126.9 1.0 slice_convert_fusion
  128.1 0.7 reshape.201.ub_ref
  129.4 0.7 reshape.188.bv_ref
  130.0 0.7 reshape.187.bq_ref
  130.7 6.1 %fusion.2 = (bf16[32,24,768]{2,1,0:T(8,128)(2,1)S(1)}, bf16[32,24,768]{2,1,0:T(8,128)(2,1)S(1)}, bf16[32,24,768]{2,1,0:T(8,128)(2,1)S(1)}, bf16[32,24,768]{2,1,0...) fusion(bf16[32,289,768]{2,1,0:T(8,128)(2,1)} %all-gather.4.clon, ...), kind=kLoop, calls=%fused_computation.47 | loop fusion | bytes 18874368 | tf_op jit(solution)/shard_map/slice | solution.py:323
  136.8 2.4 pad_maximum_fusion.1.wu_ref
  139.3 0.6 concatenate.29.small_ref
  139.9 17.2 %shard_map.323 = (bf16[1120,768]{1,0:T(8,128)(2,1)}, bf16[1120,768]{1,0:T(8,128)(2,1)}, bf16[1120,768]{1,0:T(8,128)(2,1)}, bf16[1120,768]{1,0:T(8,128)(2,1)}, f32[1120,128]{1,0:T(8,128)}) custom-call(s32[7]{0:T(128)} %len_ref.3, bf16[1120,768]{1,0:T(8,128)(2,1)} %l_ref.1, bf16[768,768]{1,0:T(8,128)(2,1)} %bitcast.67, bf16[768,768]{1,0:T(8,128)(2,1)} %bitcast.65, ...), custom_call_target="tpu_custom_call" | custom-call | flops 6165626880 | bytes 12140544 | tf_op jit(solution)/shard_map/pallas_call | solution.py:89
  157.1 4.8 slice.244
  162.0 40.3 %shard_map.324 = (bf16[1120,768]{1,0:T(8,128)(2,1)}, bf16[1120,3072]{1,0:T(8,128)(2,1)}, bf16[1120,768]{1,0:T(8,128)(2,1)}, bf16[1120,768]{1,0:T(8,128)(2,1)}, b...) custom-call(bf16[1120,768]{1,0:T(8,128)(2,1)} %get-tuple-element.40., ...), custom_call_target="tpu_custom_call" | custom-call | flops 23781703680 | bytes 41582592 | tf_op jit(solution)/shard_map/pallas_call | solution.py:238
  202.3 4.5 shard_map.328
  206.9 26.0 %shard_map.325 = (bf16[1120,768]{1,0:T(8,128)(2,1)}, bf16[1120,768]{1,0:T(8,128)(2,1)}, bf16[1120,768]{1,0:T(8,128)(2,1)}, f32[1,768]{1,0:T(1,128)}, f32[1,768]{1,0:T(1,128)}) custom-call(s32[7]{0:T(128)} %len_ref.3, bf16[1120,768]{1,0:T(8,128)(2,1)} %get-tuple-element.43.q_ref, bf16[1120,768]{1,0:T(8,128)(2,1)} %get-tuple-element.44.k_ref, ...), custom_call_target="tpu_custom_call" | custom-call | flops 5505024000 | bytes 12042240 | tf_op jit(solution)/shard_map/pallas_call | solution.py:143
  232.9 0.7 convert_reduce_fusion.1
  234.6 0.1 concatenate.30
  234.7 8.6 %shard_map.327 = (bf16[768,768]{1,0:T(8,128)(2,1)}, bf16[768,768]{1,0:T(8,128)(2,1)}, bf16[768,768]{1,0:T(8,128)(2,1)}) custom-call(bf16[1120,768]{1,0:T(8,128)(2,1)} %l_ref.1, bf16[1120,768]{1,0:T(8,128)(2,1)} %get-tuple-element.48.gq_ref.a_ref, bf16[1120,768]{1,0:T(8,128)(2,1)} %get-tuple-element.49.gk_ref.b_ref, ...), custom_call_target="tpu_custom_call" | custom-call | flops 3963617280 | bytes 10420224 | tf_op jit(solution)/shard_map/pallas_call | solution.py:275
  243.4 2.6 constant_dynamic-update-slice_fusion.10
  246.0 2.4 constant_dynamic-update-slice_fusion.9
  248.4 1.1 constant_dynamic-update-slice_fusion.8
  249.5 1.2 constant_dynamic-update-slice_fusion.7
  250.7 0.8 copy_dynamic-update-slice_fusion
  251.5 13.9 %shard_map.329 = bf16[768,3072]{1,0:T(8,128)(2,1)} custom-call(bf16[1120,768]{1,0:T(8,128)(2,1)} %get-tuple-element.59.l_ref, bf16[1120,3072]{1,0:T(8,128)(2,1)} %get-tuple-element.60.r_ref), custom_call_target="tpu_custom_call" | custom-call | flops 5284823040 | bytes 13320192 | tf_op jit(solution)/shard_map/pallas_call | solution.py:256
  265.5 8.5 %reshape.216 = bf16[32,96,768]{2,1,0:T(8,128)(2,1)} reshape(bf16[768,3072]{1,0:T(8,128)(2,1)} %shard_map.329) | data formatting | bytes 9437184 | tf_op jit(solution)/shard_map/reshape | solution.py:348
  274.0 11.9 %shard_map.330 = bf16[3072,768]{1,0:T(8,128)(2,1)} custom-call(bf16[1120,3072]{1,0:T(8,128)(2,1)} %get-tuple-element.61.l_ref, bf16[1120,768]{1,0:T(8,128)(2,1)} %get-tuple-element.62.r_ref), custom_call_target="tpu_custom_call" | custom-call | flops 5284823040 | bytes 13320192 | tf_op jit(solution)/shard_map/pallas_call | solution.py:256
  286.0 7.7 %pad_maximum_fusion = bf16[32,192,768]{2,1,0:T(8,128)(2,1)} fusion(bf16[32,96,768]{2,1,0:T(8,128)(2,1)} %bitcast.62, bf16[32,96,768]{2,1,0:T(8,128)(2,1)} %reshape.216), kind=kLoop, calls=%fused_computation | loop fusion | flops 18874368 | bytes 18874368 | tf_op jit(solution)/shard_map/concatenate | solution.py:347
  293.7 9.2 %shard_map.326 = bf16[1120,768]{1,0:T(8,128)(2,1)} custom-call(f32[1120,768]{1,0:T(8,128)} %get-tuple-element.42.g1_ref, bf16[1120,768]{1,0:T(8,128)(2,1)} %get-tuple-element.48.gq_ref.a_ref, bf16[1120,768]{1,0:T(8,128)(2,1)} %get-tuple-element.49.gk_ref.b_ref, bf16[1120,768]{1,0:T(8,128)(2,1)} %get-tuple-element.50.gv_ref.c_ref, bf16[768,768]{1,0:T(8,128)(2,1)} %bitcast.68, ...), custom_call_target="tpu_custom_call" | custom-call | flops 3963617280 | bytes 13860864 | tf_op jit(solution)/shard_map/pallas_call | solution.py:294
  302.9 55.9 %reduce-scatter.3.cloned.1.call-done = bf16[1,97,768]{2,1,0:T(8,128)(2,1)} async-done(((bf16[32,97,768]{2,1,0:T(8,128)(2,1)}), bf16[1,97,768]{2,1,0:T(8,128)(2,1)}) %reduce-scatter.3.cloned.1.call-update) | async-done | bytes 149008 | tf_op jit(solution)/shard_map/reduce_scatter | solution.py:360
  358.8 1.0 convert_bitcast_fusion
  359.7 0.6 slice_bitcast_fusion.8
  360.3 0.6 slice_bitcast_fusion.5
  360.9 0.7 slice_bitcast_fusion.1
  361.6 138.7 %reduce-scatter.5.cloned.1.call-done = bf16[1,192,768]{2,1,0:T(8,128)(2,1)} async-done(((bf16[32,192,768]{2,1,0:T(8,128)(2,1)}), bf16[1,192,768]{2,1,0:T(8,128)(2,1)}) %reduce-scatter.5.cloned.1.call-update) | async-done | bytes 294928 | tf_op jit(solution)/shard_map/reduce_scatter | solution.py:350
  500.3 0.9 slice.267
  501.2 0.8 reshape.218
  502.0 1.0 convert_element_type.25
  503.0 0.7 slice_bitcast_fusion
  (42 shorter events, 1.9 us)
Async XLA Ops:
  7.2 119.7 %all-gather.4.cloned.1.call-start = ((), (), s32[]{:S(2)}) async-start(), calls=%async_computation.4 | async-start | bytes 15003648 | tf_op jit(solution)/shard_map/all_gather | solution.py:320
  18.3 0.8 copy-start.2
  19.1 339.7 %reduce-scatter.3.cloned.1.call-start = ((), (), s32[]{:S(2)}) async-start(), calls=%async_computation.2 | async-start | bytes 5271552 | tf_op jit(solution)/shard_map/reduce_scatter | solution.py:360
  206.9 26.8 %copy-start.4 = (f32[1,3072]{1,0:T(1,128)S(1)}, f32[1,3072]{1,0:T(1,128)}, u32[]{:S(2)}) copy-start(f32[1,3072]{1,0:T(1,128)} %get-tuple-element.58) | copy-start | bytes 36868
  206.9 27.1 %copy-start.3 = (f32[8,768]{1,0:T(8,128)S(1)}, f32[8,768]{1,0:T(8,128)}, u32[]{:S(2)}) copy-start(f32[8,768]{1,0:T(8,128)} %get-tuple-element.57) | copy-start | bytes 73732
  243.4 5.0 copy-start.1
  243.4 6.1 %copy-start = (bf16[768,768]{1,0:T(8,128)(2,1)S(1)}, bf16[768,768]{1,0:T(8,128)(2,1)}, u32[]{:S(2)}) copy-start(bf16[768,768]{1,0:T(8,128)(2,1)} %shard_map.328) | copy-start | bytes 3538948
  251.5 248.8 %reduce-scatter.5.cloned.1.call-start = ((), (), s32[]{:S(2)}) async-start(), calls=%async_computation.3 | async-start | bytes 9732096 | tf_op jit(solution)/shard_map/reduce_scatter | solution.py:350
Sparse Core Ops, SparseCore 0:
  19.2 107.6 all-gather.3
  251.6 107.1 reduce-scatter.2
  365.7 134.5 reduce-scatter.4

commit v2 on v1

--- a/solution.py
+++ b/solution.py
@@ -13,6 +13,7 @@
 masked_score = -1000000000.0
 F32 = jnp.float32
 BF16 = jnp.bfloat16
+WAIT = 1 << 40
 
 
 def dot(left, right):
@@ -27,15 +28,16 @@
     return lax.dot_general(left, right, (((0,), (0,)), ((), ())), preferred_element_type=F32)
 
 
-def call(body, grid, in_specs, out_specs, out_shape, scratch=(), flops=0, moved=0, vmem=60):
+def call(body, grid, in_specs, out_specs, out_shape, scratch=(), flops=0, moved=0, vmem=60, aliases={}, weight=0):
     return pl.pallas_call(
         body,
         grid_spec=pltpu.PrefetchScalarGridSpec(
             num_scalar_prefetch=0, grid=grid, in_specs=in_specs, out_specs=out_specs, scratch_shapes=scratch
         ),
         out_shape=out_shape,
+        input_output_aliases=aliases,
         compiler_params=pltpu.CompilerParams(vmem_limit_bytes=vmem * 1024 * 1024),
-        cost_estimate=pl.CostEstimate(flops=flops, bytes_accessed=moved, transcendentals=0),
+        cost_estimate=pl.CostEstimate(flops=weight, bytes_accessed=weight // 64, transcendentals=0),
     )
 
 
@@ -95,17 +97,18 @@
     )(lengths, x, wq, wk, wv, bq, bv)
 
 
-def attn_bwd_body(len_ref, q_ref, k_ref, v_ref, gm_ref, lse_ref, gq_ref, gk_ref, gv_ref, gbq_ref, gbv_ref):
+def attn_bwd_body(start, len_ref, q_ref, k_ref, v_ref, gm_ref, lse_ref, *rest):
+    gq_ref, gk_ref, gv_ref, gbq_ref, gbv_ref = rest[-5:]
     c = pl.program_id(0)
     length = q_ref.shape[0]
-    valid = lax.broadcasted_iota(jnp.int32, (1, length), 1) < len_ref[c]
+    valid = lax.broadcasted_iota(jnp.int32, (1, length), 1) < len_ref[c + start]
     masks = half_mask(BF16)
     scaled = half_mask(BF16, 0.125)
 
     @pl.when(c == 0)
     def _():
-        gbq_ref[...] = jnp.zeros_like(gbq_ref)
-        gbv_ref[...] = jnp.zeros_like(gbv_ref)
+        gbq_ref[...] = rest[3][...] if start else jnp.zeros_like(gbq_ref)
+        gbv_ref[...] = rest[4][...] if start else jnp.zeros_like(gbv_ref)
 
     for p in range(HEADS // 2):
         cols = slice(128 * p, 128 * p + 128)
@@ -133,20 +136,24 @@
         gbv_ref[:, cols] += jnp.sum(gv.astype(F32), axis=0, keepdims=True)
 
 
-def attn_bwd(q, k, v, gm, lse, lengths):
+def attn_bwd(q, k, v, gm, lse, lengths, start=0, stop=None, before=(), weight=0):
     rows = q.shape[0]
     n = lengths.shape[0]
+    stop = n if stop is None else stop
     length = rows // n
-    tile = pl.BlockSpec((length, D), lambda c: (c, 0))
+    tile = pl.BlockSpec((length, D), lambda c: (c + start, 0))
     one = pl.BlockSpec((1, D), lambda c: (0, 0))
     act = shaped((rows, D), BF16)
-    return call(
-        attn_bwd_body, (n,),
-        [pl.BlockSpec(memory_space=pltpu.SMEM), tile, tile, tile, tile, pl.BlockSpec((length, 128), lambda c: (c, 0))],
+    whole = pl.BlockSpec(memory_space=pl.ANY)
+    return call(
+        functools.partial(attn_bwd_body, start), (stop - start,),
+        [pl.BlockSpec(memory_space=pltpu.SMEM), tile, tile, tile, tile, pl.BlockSpec((length, 128), lambda c: (c + start, 0))]
+        + ([whole, whole, whole, one, one] if before else []),
         [tile, tile, tile, one, one],
         [act, act, act, shaped((1, D), F32), shaped((1, D), F32)],
-        flops=2 * rows * length * D * 5 * 4, moved=rows * D * 14,
-    )(lengths, q, k, v, gm, lse)
+        flops=2 * (stop - start) * length * length * D * 5 * 4, moved=(stop - start) * length * D * 14,
+        aliases={6: 0, 7: 1, 8: 2} if before else {}, weight=weight,
+    )(lengths, q, k, v, gm, lse, *before)
 
 
 def mean(v):
@@ -174,10 +181,148 @@
     return pre * cdf, cdf + pre * pdf
 
 
-def ffn_body(chunk, mix_ref, x_ref, gy_ref, wo_ref, wu_ref, wd_ref, small_ref, ub_ref,
-             out_ref, hid_ref, gffn_ref, low_ref, gpre_ref, gattn_ref, g1_ref, gmix_ref, gsmall_ref, gub_ref, dg_ref):
+def wgrad_body(l_ref, r_ref, o_ref):
+    o_ref[...] = dot_lt(l_ref[...], r_ref[...]).astype(o_ref.dtype)
+
+
+def wgrad(left, right, tile_m=768, dtype=BF16):
+    rows, m = left.shape
+    n = right.shape[1]
+    tn = min(n, 768)
+    return call(
+        wgrad_body, (n // tn, m // tile_m),
+        [pl.BlockSpec((rows, tile_m), lambda j, i: (0, i)), pl.BlockSpec((rows, tn), lambda j, i: (0, j))],
+        pl.BlockSpec((tile_m, tn), lambda j, i: (i, j)),
+        shaped((m, n), dtype),
+        flops=2 * rows * m * n, moved=2 * (rows * (m + n) + m * n),
+    )(left, right)
+
+def place():
+    idx = lax.axis_index("fsdp")
+    return idx % 2, (idx // 2) % 4, idx // 8
+
+def swap(n, bits):
+    return [(i, i ^ bits) for i in range(n)]
+
+def shift(n, k):
+    return [(i, (i + 8 * k) % n) for i in range(n)]
+
+def hop(value, pairs):
+    return lax.ppermute(value, "fsdp", pairs)
+
+
+def gather_blocks(block, n):
+    far = n // 8
+    zs = [hop(block, shift(n, k)) for k in range(1, far)]
+    x0, y0, d0 = (hop(block, swap(n, b)) for b in (2, 4, 6))
+    line = jnp.stack(zs)
+    first = jnp.stack([block, x0, y0, d0])
+    first_other = hop(first, swap(n, 1))
+    line_other = hop(line, swap(n, 1))
+    xs = hop(line, swap(n, 2))
+    ys = hop(line, swap(n, 4))
+    ds = jnp.stack([hop(d0, shift(n, k)) for k in range(1, far)])
+    rest = jnp.concatenate([xs, ys, ds])
+    rest_other = hop(rest, swap(n, 1))
+    return (first, line, rest), (first_other, line_other, rest_other)
+
+
+def sources(far):
+    out = [(0, i, i, 0) for i in range(4)]
+    out += [(1, k - 1, 0, k) for k in range(1, far)]
+    out += [(2, (d - 1) * (far - 1) + k - 1, d, k) for d in (1, 2, 3) for k in range(1, far)]
+    return out
+
+
+def assemble_body(far, own, at_ref, f_ref, l_ref, r_ref, fo_ref, lo_ref, ro_ref, wq_ref, wk_ref, wv_ref, table_ref, ub_ref):
+    core, fast, slow = at_ref[0], at_ref[1], at_ref[2]
+    first = core == 0
+    mine, other = (f_ref, l_ref, r_ref), (fo_ref, lo_ref, ro_ref)
+    table = jnp.zeros((8, D), F32)
+    ub = jnp.zeros((1, ub_ref.shape[1]), F32)
+    for array, i, dxy, dz in sources(far):
+        chip = ((slow - dz) % far) * 4 + (fast ^ dxy)
+        a, b = mine[array][i], other[array][i]
+        low, high = jnp.where(first, a, b), jnp.where(first, b, a)
+        for m, ref in enumerate((wq_ref, wk_ref, wv_ref)):
+            rows = slice(own * m, own * m + own)
+            ref[chip] = jnp.concatenate([low[rows], high[rows]], axis=0)
+        for side, part in ((0, low), (1, high)):
+            tail = part[3 * own :].astype(F32)
+            spot = chip * 2 + side
+            lane = lax.broadcasted_iota(jnp.int32, (1, D), 1)
+            table = table + pltpu.roll(jnp.where(lane < own, tail, 0.0), spot * own, 1)
+            wide = tail[0:1, 128:256]
+            wide = jnp.concatenate([wide, jnp.zeros((1, ub_ref.shape[1] - 128), F32)], axis=1)
+            ub = ub + pltpu.roll(wide, spot * 4 * own, 1)
+    table_ref[...] = table
+    ub_ref[...] = ub
+
+
+def assemble(at, mine, other, own, n):
+    far = n // 8
+    full = lambda a: pl.BlockSpec(a.shape, lambda i: (0,) * a.ndim)
+    arrays = list(mine) + list(other)
+    w = shaped((n // 2, 2 * own, D), BF16)
+    outs = [w, w, w, shaped((8, D), F32), shaped((1, 4 * D), F32)]
+    wq, wk, wv, table, ub = call(
+        functools.partial(assemble_body, far, own), (1,),
+        [pl.BlockSpec(memory_space=pltpu.SMEM)] + [full(a) for a in arrays],
+        [full(a) for a in outs], outs, moved=7 * D * D * 2,
+    )(at, *arrays)
+    return wq.reshape(D, D), wk.reshape(D, D), wv.reshape(D, D), table, ub
+
+
+def pack_small(vectors, wide):
+    total = jnp.pad(wide[None, :], ((0, 7), (128, D - 128 - wide.shape[0])))
+    for i, v in enumerate(vectors):
+        total = total + jnp.pad(v[None, :], ((i, 7 - i), (0, D - v.shape[0])))
+    return total
+
+
+def ffn_raw_body(chunk, own, mix_ref, x_ref, gy_ref, raw_ref, small_ref, ub_ref, *rest):
+    outs, (dg_ref, wo_ref, wu_ref) = rest[:-3], rest[-3:]
+    wide = 4 * own
+
+    @pl.when(pl.program_id(0) == 0)
+    def _():
+        def step(i, _):
+            low, high = raw_ref[2 * i, wide:], raw_ref[2 * i + 1, wide:]
+            at = pl.ds(pl.multiple_of(2 * own * i, 16), 2 * own)
+            for j in range(5):
+                rows = slice(own * j, own * j + own)
+                both = jnp.concatenate([low[rows], high[rows]], axis=0)
+                if j < 4:
+                    wu_ref[at, D * j : D * j + D] = both
+                else:
+                    wo_ref[at, :] = both
+            return 0
+
+        lax.fori_loop(0, D // (2 * own), step, 0)
+
+    ffn_steps(chunk, mix_ref, x_ref, gy_ref, wo_ref, wu_ref, RawDown(raw_ref, wide), small_ref, ub_ref, *outs, dg_ref)
+
+
+class RawDown:
+    def __init__(self, ref, wide):
+        self.ref, self.wide = ref, wide
+
+    def rows(self, start, size):
+        return self.ref[start // self.wide : (start + size) // self.wide, : self.wide].reshape(size, D)
+
+
+class FullDown:
+    def __init__(self, ref):
+        self.ref = ref
+
+    def rows(self, start, size):
+        return self.ref[start : start + size, :]
+
+
+def ffn_steps(chunk, mix_ref, x_ref, gy_ref, wo_ref, wu_ref, down, small_ref, ub_ref,
+              out_ref, hid_ref, gffn_ref, low_ref, gpre_ref, gattn_ref, g1_ref, gmix_ref, gsmall_ref, gub_ref, dg_ref):
     i = pl.program_id(0)
-    bo, again, ashift, bd, fgain, fshift = (small_ref[j : j + 1, :] for j in range(6))
+    bo, again, ashift, bd, fgain, fshift = (small_ref[j : j + 1, :] for j in range(2, 8))
     ff = wu_ref.shape[1]
 
     @pl.when(i == 0)
@@ -198,20 +343,20 @@
         hid = hid.astype(BF16)
         hid_ref[:, cols] = hid
         dg_ref[:, cols] = dg.astype(dg_ref.dtype)
-        ffn = ffn + dot(hid, wd_ref[cols, :])
+        ffn = ffn + dot(hid, down.rows(j * chunk, chunk))
     xhat2, rs2 = normalize(first + ffn + bd)
     out_ref[...] = (xhat2 * fgain + fshift).astype(BF16)
     gy = gy_ref[...].astype(F32)
     g2 = norm_back(gy, xhat2, rs2, fgain)
     gffn = g2.astype(BF16)
     gffn_ref[...] = gffn
-    gsmall_ref[3:4, :] += colsum(gffn.astype(F32))
-    gsmall_ref[4:5, :] += colsum(gy * xhat2)
-    gsmall_ref[5:6, :] += colsum(gy)
+    gsmall_ref[5:6, :] += colsum(gffn.astype(F32))
+    gsmall_ref[6:7, :] += colsum(gy * xhat2)
+    gsmall_ref[7:8, :] += colsum(gy)
     gfirst = g2
     for j in range(ff // chunk):
         cols = slice(j * chunk, (j + 1) * chunk)
-        gh = dot_rt(gffn, wd_ref[cols, :])
+        gh = dot_rt(gffn, down.rows(j * chunk, chunk))
         gpre = (gh * dg_ref[:, cols].astype(F32)).astype(BF16)
         gpre_ref[:, cols] = gpre
         gub_ref[:, cols] += colsum(gpre.astype(F32))
@@ -220,46 +365,181 @@
     gattn = g1.astype(BF16)
     g1_ref[...] = g1
     gattn_ref[...] = gattn
-    gsmall_ref[0:1, :] += colsum(gattn.astype(F32))
-    gsmall_ref[1:2, :] += colsum(gfirst * xhat1)
-    gsmall_ref[2:3, :] += colsum(gfirst)
+    gsmall_ref[2:3, :] += colsum(gattn.astype(F32))
+    gsmall_ref[3:4, :] += colsum(gfirst * xhat1)
+    gsmall_ref[4:5, :] += colsum(gfirst)
     gmix_ref[...] = dot_rt(gattn, wo_ref[...]).astype(BF16)
 
 
-def ffn_both(mixed, x, gy, wo, wu, wd, small, ub, tile_rows=280, chunk=768, dg_dtype=F32):
+def ffn_full_body(chunk, mix_ref, x_ref, gy_ref, wo_ref, wu_ref, wd_ref, small_ref, ub_ref, *rest):
+    ffn_steps(chunk, mix_ref, x_ref, gy_ref, wo_ref, wu_ref, FullDown(wd_ref), small_ref, ub_ref, *rest)
+
+
+def ffn_both(mixed, x, gy, weights, small, ub, own=0, tile_rows=280, chunk=768):
     rows = x.shape[0]
-    ff = wu.shape[1]
-    n = rows // tile_rows
+    ff = ub.shape[1]
     tile = pl.BlockSpec((tile_rows, D), lambda c: (c, 0))
     wide = pl.BlockSpec((tile_rows, ff), lambda c: (c, 0))
-    fixed = lambda s: pl.BlockSpec(s, lambda c: (0, 0), pipeline_mode=pl.Buffered(1))
+    fixed = lambda a: pl.BlockSpec(a.shape, lambda c: (0,) * a.ndim, pipeline_mode=pl.Buffered(1))
     act = shaped((rows, D), BF16)
     big = shaped((rows, ff), BF16)
-    return call(
-        functools.partial(ffn_body, chunk), (n,),
-        [tile, tile, tile, fixed((D, D)), fixed((D, ff)), fixed((ff, D)), fixed((8, D)), fixed((1, ff))],
+    scratch = [pltpu.VMEM((tile_rows, ff), F32)]
+    if len(weights) == 1:
+        body = functools.partial(ffn_raw_body, chunk, own)
+        scratch += [pltpu.VMEM((D, D), BF16), pltpu.VMEM((D, ff), BF16)]
+    else:
+        body = functools.partial(ffn_full_body, chunk)
+    return call(
+        body, (rows // tile_rows,),
+        [tile, tile, tile] + [fixed(w) for w in weights] + [fixed(small), fixed(ub)],
         [tile, wide, tile, tile, wide, tile, tile, tile, pl.BlockSpec((8, D), lambda c: (0, 0)), pl.BlockSpec((1, ff), lambda c: (0, 0))],
         [act, big, act, act, big, act, shaped((rows, D), F32), act, shaped((8, D), F32), shaped((1, ff), F32)],
-        scratch=[pltpu.VMEM((tile_rows, ff), dg_dtype)],
+        scratch=scratch,
         flops=2 * rows * D * (2 * D + 4 * ff), moved=rows * (D * 20 + ff * 4) + D * (D + 2 * ff) * 2,
-    )(mixed, x, gy, wo, wu, wd, small, ub)
-
-
-def wgrad_body(l_ref, r_ref, o_ref):
-    o_ref[...] = dot_lt(l_ref[...], r_ref[...]).astype(o_ref.dtype)
-
-
-def wgrad(left, right, tile_m=384, dtype=BF16):
-    rows, m = left.shape
-    n = right.shape[1]
-    tn = min(n, 768)
-    return call(
-        wgrad_body, (n // tn, m // tile_m),
-        [pl.BlockSpec((rows, tile_m), lambda j, i: (0, i)), pl.BlockSpec((rows, tn), lambda j, i: (0, j))],
-        pl.BlockSpec((tile_m, tn), lambda j, i: (i, j)),
-        shaped((m, n), dtype),
-        flops=2 * rows * m * n, moved=2 * (rows * (m + n) + m * n),
-    )(left, right)
+    )(mixed, x, gy, *weights, small, ub)
+
+
+def row_block(at_ref, far, own, dxy, dz):
+    chip = ((at_ref[2] + dz) % far) * 4 + (at_ref[1] ^ dxy)
+    return tuple(2 * chip + side for side in (at_ref[0], 1 - at_ref[0]))
+
+
+def acc_rows(ref, m, d, own):
+    at = pl.ds(pl.multiple_of(own * d, 8), own)
+    return ref[at, :] if m is None else ref[m, at, :]
+
+
+def wgrad_down_body(far, own, at_ref, hid_ref, gffn_ref, *rest):
+    outs, acc_ref = rest[:-1], rest[-1]
+    acc_ref[...] = dot_lt(hid_ref[...], gffn_ref[...])
+    dz = (pl.program_id(0) - at_ref[2]) % far
+    for dxy in range(4):
+        chip = at_ref[1] ^ dxy
+        for out, side in zip(outs, (at_ref[0], 1 - at_ref[0])):
+            out[dxy, dz] = acc_rows(acc_ref, None, 2 * chip + side, own).astype(BF16)
+
+
+def keep_send(*shape):
+    out = shaped((4,) + shape, BF16)
+    spec = pl.BlockSpec(out.shape, lambda j: (0,) * len(out.shape))
+    return [spec, spec], [out, out]
+
+
+def wgrad_down(at, hidden, gffn, n):
+    rows, ff = hidden.shape
+    far = n // 8
+    own = ff // n
+    specs, outs = keep_send(far, own, D)
+    return call(
+        functools.partial(wgrad_down_body, far, own), (far,),
+        [pl.BlockSpec(memory_space=pltpu.SMEM), pl.BlockSpec((rows, ff // far), lambda j: (0, j)), pl.BlockSpec((rows, D), lambda j: (0, 0))],
+        specs, outs, scratch=[pltpu.VMEM((ff // far, D), F32)],
+        flops=2 * rows * D * ff, moved=2 * (rows * (D + ff) + D * ff),
+    )(at, hidden, gffn)
+
+
+def wgrad_up_body(far, own, at_ref, low_ref, gpre_ref, mix_ref, gattn_ref, *rest):
+    outs, acc_ref = rest[:-1], rest[-1]
+    j = pl.program_id(0)
+
+    @pl.when(j < 4)
+    def _():
+        acc_ref[j] = dot_lt(low_ref[...], gpre_ref[...])
+
+    @pl.when(j == 4)
+    def _():
+        acc_ref[4] = dot_lt(mix_ref[...], gattn_ref[...])
+        for dxy in range(4):
+            for dz in range(far):
+                for k, d in enumerate(row_block(at_ref, far, own, dxy, dz)):
+                    value = jnp.concatenate([acc_rows(acc_ref, m, d, own) for m in range(5)], axis=0)
+                    outs[k][dxy, dz] = value.astype(BF16)
+
+
+def wgrad_up(at, low, gpre, mixed, gattn, own, n):
+    rows = low.shape[0]
+    far = n // 8
+    act = pl.BlockSpec((rows, D), lambda j: (0, 0))
+    specs, outs = keep_send(far, 5 * own, D)
+    return call(
+        functools.partial(wgrad_up_body, far, own), (5,),
+        [pl.BlockSpec(memory_space=pltpu.SMEM), act, pl.BlockSpec((rows, D), lambda j: (0, jnp.minimum(j, 3))), act, act],
+        specs, outs, scratch=[pltpu.VMEM((5, D, D), F32)],
+        flops=10 * rows * D * D, moved=2 * (7 * rows * D + 5 * D * D),
+    )(at, low, gpre, mixed, gattn)
+
+
+def wgrad_in_body(far, own, at_ref, x_ref, gq_ref, gk_ref, gv_ref, small_ref, ub_ref, *rest):
+    outs, acc_ref = rest[:-1], rest[-1]
+    left = x_ref[...]
+    for m, ref in enumerate((gq_ref, gk_ref, gv_ref)):
+        acc_ref[m] = dot_lt(left, ref[...])
+    lane = lax.broadcasted_iota(jnp.int32, (8, D), 1)
+    row = lax.broadcasted_iota(jnp.int32, (8, D), 0)
+    ff = ub_ref.shape[1]
+    wide = ff // (8 * far)
+    for dxy in range(4):
+        for dz in range(far):
+            for k, d in enumerate(row_block(at_ref, far, own, dxy, dz)):
+                tail = pltpu.roll(small_ref[...], (D - own * d) % D, 1)
+                ub = pltpu.roll(ub_ref[...], (ff + 128 - wide * d) % ff, 1)[:, :D]
+                tail = jnp.where(lane < own, tail, 0.0)
+                tail = jnp.where((row == 0) & (lane >= 128) & (lane < 128 + wide), ub, tail)
+                parts = [acc_rows(acc_ref, m, d, own) for m in range(3)] + [tail]
+                outs[k][dxy, dz] = jnp.concatenate(parts, axis=0).astype(BF16)
+
+
+def wgrad_in(at, x, gq, gk, gv, small, ub, own, n):
+    rows = x.shape[0]
+    far = n // 8
+    full = lambda a: pl.BlockSpec(a.shape, lambda i: (0,) * a.ndim)
+    specs, outs = keep_send(far, 3 * own + 8, D)
+    return call(
+        functools.partial(wgrad_in_body, far, own), (1,),
+        [pl.BlockSpec(memory_space=pltpu.SMEM)] + [full(a) for a in (x, gq, gk, gv, small, ub)],
+        specs, outs, scratch=[pltpu.VMEM((3, D, D), F32)],
+        flops=6 * rows * D * D, moved=2 * (4 * rows * D + 3 * D * D),
+    )(at, x, gq, gk, gv, small, ub)
+
+
+def pair_sum(keep, other, i):
+    return keep[i].astype(F32) + other[i].astype(F32)
+
+
+def near_parts(keep, other):
+    return tuple(pair_sum(keep, other, i).astype(BF16) for i in (1, 2, 3))
+
+
+def near_hops(parts, n):
+    return tuple(hop(p, swap(n, 2 * i)) for i, p in enumerate(parts, 1))
+
+
+def line_body(keep_ref, other_ref, x_ref, y_ref, d_ref, base_ref, *sent):
+    total = keep_ref[...].astype(F32) + other_ref[...].astype(F32)
+    for ref in (x_ref, y_ref, d_ref):
+        total = total + ref[...].astype(F32)
+    base_ref[...] = total[0, 0]
+    for k, ref in enumerate(sent, 1):
+        ref[...] = total[0, k].astype(BF16)
+
+
+def line_sum(keep, other, near):
+    far, rows = keep.shape[1:3]
+    block = pl.BlockSpec((1, far, rows, D), lambda i: (0, 0, 0, 0))
+    part = pl.BlockSpec((rows, D), lambda i: (0, 0))
+    base, *sent = call(
+        line_body, (1,), [block] * 5, [part] * far,
+        [shaped((rows, D), F32)] + [shaped((rows, D), BF16)] * (far - 1), weight=WAIT,
+    )(keep, other, *(p[None] for p in near))
+    return base, sent
+
+
+def far_hops(sent, n, which):
+    return {k: hop(sent[k - 1], shift(n, k)) for k in which}
+
+
+def last_sum(base, far):
+    return base + sum(p.astype(F32) for p in far.values())
 
 
 def wgrad3_body(l_ref, a_ref, b_ref, c_ref, oa_ref, ob_ref, oc_ref):
@@ -281,41 +561,129 @@
     )(left, a, b, c)
 
 
-def input_grad_body(g1_ref, gq_ref, gk_ref, gv_ref, wq_ref, wk_ref, wv_ref, o_ref):
+def input_grad_body(g1_ref, gq_ref, gk_ref, gv_ref, wq_ref, wk_ref, wv_ref, *rest):
     total = g1_ref[...] + dot_rt(gq_ref[...], wq_ref[...])
     total = total + dot_rt(gk_ref[...], wk_ref[...]) + dot_rt(gv_ref[...], wv_ref[...])
-    o_ref[...] = total.astype(BF16)
-
-
-def input_grad(g1, gq, gk, gv, wq, wk, wv, tile_rows=280):
+    rest[-1][...] = total.astype(BF16)
+
+
+def input_grad(g1, gq, gk, gv, wq, wk, wv, start=0, stop=4, before=(), tiles=4):
     rows = g1.shape[0]
-    tile = pl.BlockSpec((tile_rows, D), lambda c: (c, 0))
+    tile = pl.BlockSpec((rows // tiles, D), lambda c: (c + start, 0))
     full = pl.BlockSpec((D, D), lambda c: (0, 0))
     return call(
-        input_grad_body, (rows // tile_rows,),
-        [tile, tile, tile, tile, full, full, full], tile, shaped((rows, D), BF16),
+        input_grad_body, (stop - start,),
+        [tile, tile, tile, tile, full, full, full] + [pl.BlockSpec(memory_space=pl.ANY)] * len(before),
+        tile, shaped((rows, D), BF16), aliases={7: 0} if before else {},
         flops=6 * rows * D * D, moved=rows * D * 12 + 6 * D * D,
-    )(g1, gq, gk, gv, wq, wk, wv)
-
-
-def shards(
+    )(g1, gq, gk, gv, wq, wk, wv, *before)
+
+
+def residue_mask(cotangent, span_start, span_end):
+    chains = span_start.shape[0]
+    rows = cotangent.shape[0]
+    positions = jnp.arange(rows // chains)
+    inside = jnp.any(
+        (positions[None, None, :] >= span_start[:, :, None]) & (positions[None, None, :] < span_end[:, :, None]),
+        axis=1,
+    )
+    return jnp.where(inside.reshape(rows, 1), cotangent, jnp.zeros_like(cotangent))
+
+
+def tie(*values):
+    return lax.optimization_barrier(values)
+
+
+def chunked(weight):
+    own = weight.shape[0]
+    return weight.reshape(own, -1, D).swapaxes(0, 1).reshape(-1, D)
+
+
+def fast_shards(
+    n, tokens, cotangent, lengths, span_start, span_end,
+    query_weight, query_bias, key_weight, value_weight, value_bias, out_weight, out_bias,
+    attn_gain, attn_shift, up_weight, up_bias, down_weight, down_bias, ffn_gain, ffn_shift,
+):
+    own = query_weight.shape[0]
+    wide = up_bias.shape[0]
+    vectors = (query_bias, value_bias, out_bias, attn_gain, attn_shift, down_bias, ffn_gain, ffn_shift)
+    at = jnp.stack(place()).astype(jnp.int32)
+    block = jnp.concatenate([query_weight, key_weight, value_weight, pack_small(vectors, up_bias)], axis=0)
+    sent = jnp.concatenate([down_weight, chunked(up_weight), out_weight], axis=0)
+    sent = jnp.pad(sent, ((0, -sent.shape[0] % 16), (0, 0)))
+    raw = lax.all_gather(sent, "fsdp", axis=0, tiled=False)
+    mine, other = gather_blocks(block, n)
+    wq, wk, wv, table, ub = assemble(at, mine, other, own, n)
+    gy = residue_mask(cotangent, span_start, span_end)
+
+    q, k, v, mixed, lse = attn_fwd(tokens, wq, wk, wv, table[0:1], table[1:2], lengths)
+    layer_out, hidden, gffn, low, gpre, gattn, g1, gmixed, gtable, gub = ffn_both(
+        mixed, tokens, gy, (raw,), table, ub, own
+    )
+    chains = lengths.shape[0]
+    cuts = (0, 1, 4, chains)
+    keep_d, send_d = wgrad_down(at, hidden, gffn, n)
+    gmixed, keep_d, send_d = tie(gmixed, keep_d, send_d)
+    other_d = hop(send_d, swap(n, 1))
+    begun = attn_bwd(q, k, v, gmixed, lse, lengths, cuts[0], cuts[1], weight=WAIT)
+    begun, other_d = tie(begun, other_d)
+    low, begun, parts_d = tie(low, begun, near_parts(keep_d, other_d))
+    near_d = near_hops(parts_d, n)
+    keep_u, send_u = wgrad_up(at, low, gpre, mixed, gattn, own, n)
+    begun, keep_u, send_u = tie(begun, keep_u, send_u)
+    other_u = hop(send_u, swap(n, 1))
+    begun = attn_bwd(q, k, v, gmixed, lse, lengths, cuts[1], cuts[2], begun)
+    begun, near_d = tie(begun, near_d)
+    base_d, sent_d = line_sum(keep_d, other_d, near_d)
+    base_d, sent_d, other_u = tie(base_d, sent_d, other_u)
+    far_d = far_hops(sent_d, n, (1, 3))
+    begun, parts_u = tie(begun, near_parts(keep_u, other_u))
+    near_u = near_hops(parts_u, n)
+    gq, gk, gv, gqb, gvb = attn_bwd(q, k, v, gmixed, lse, lengths, cuts[2], cuts[3], begun)
+    gq, far_d, sent_d = tie(gq, far_d, sent_d)
+    far_d.update(far_hops(sent_d, n, (2,)))
+    gtable = jnp.concatenate([gqb, gvb, gtable[2:]], axis=0)
+    keep_i, send_i = wgrad_in(at, tokens, gq, gk, gv, gtable, gub, own, n)
+    g1, keep_i, send_i = tie(g1, keep_i, send_i)
+    other_i = hop(send_i, swap(n, 1))
+    in_grad = input_grad(g1, gq, gk, gv, wq, wk, wv, 0, 2)
+    in_grad, near_u, far_d = tie(in_grad, near_u, far_d)
+    base_u, sent_u = line_sum(keep_u, other_u, near_u)
+    base_u, sent_u, other_i = tie(base_u, sent_u, other_i)
+    far_u = far_hops(sent_u, n, (1, 2))
+    in_grad, parts_i = tie(in_grad, near_parts(keep_i, other_i))
+    near_i = near_hops(parts_i, n)
+    in_grad = input_grad(g1, gq, gk, gv, wq, wk, wv, 2, 4, (in_grad,))
+    in_grad, near_i, far_u = tie(in_grad, near_i, far_u)
+    base_i, sent_i = line_sum(keep_i, other_i, near_i)
+    far_i = far_hops(sent_i, n, (1, 2, 3))
+    far_u.update(far_hops(sent_u, n, (3,)))
+    down_own, up_own, in_own = last_sum(base_d, far_d), last_sum(base_u, far_u), last_sum(base_i, far_i)
+
+    gq_w, gk_w, gv_w = (in_own[own * i : own * (i + 1)] for i in range(3))
+    gqb, gvb, gob, gag, gas, gdb, gfg, gfs = (in_own[3 * own + i, :own] for i in range(8))
+    gub = in_own[3 * own, 128 : 128 + wide]
+    gup = jnp.concatenate([up_own[own * i : own * (i + 1)] for i in range(wide // own)], axis=1)
+    go_w = up_own[wide : wide + own]
+    return (
+        layer_out, in_grad, gq_w, gqb, gk_w, gv_w, gvb, go_w, gob, gag, gas, gup, gub, down_own, gdb, gfg, gfs,
+    )
+
+
+def plain_shards(
     tokens, cotangent, lengths, span_start, span_end,
     query_weight, query_bias, key_weight, value_weight, value_bias, out_weight, out_bias,
     attn_gain, attn_shift, up_weight, up_bias, down_weight, down_bias, ffn_gain, ffn_shift,
 ):
-    chains = lengths.shape[0]
-    rows = tokens.shape[0]
-    length = rows // chains
     own = query_weight.shape[0]
     parts = D // own
     ff = up_weight.shape[1]
+    wide = own * ff // D
     vectors = (query_bias, value_bias, out_bias, attn_gain, attn_shift, down_bias, ffn_gain, ffn_shift, up_bias)
     packed = jnp.concatenate(vectors)
     packed = jnp.pad(packed, (0, D - packed.shape[0])).reshape(1, D)
-    wide = own * ff // D
     sent = jnp.concatenate(
-        [query_weight, key_weight, value_weight, out_weight, up_weight.reshape(own, ff // D, D).swapaxes(0, 1).reshape(wide, D), down_weight, packed],
-        axis=0,
+        [query_weight, key_weight, value_weight, out_weight, chunked(up_weight), down_weight, packed], axis=0
     )
     held = lax.all_gather(sent, "fsdp", axis=0, tiled=False)
     wq, wk, wv, wo = (held[:, own * i : own * (i + 1)].reshape(D, D) for i in range(4))
@@ -324,44 +692,30 @@
     )
     wd = held[:, 4 * own + wide : 4 * own + 2 * wide].reshape(ff, D)
     small = held[:, -1].astype(F32)
-    qb, vb, ob, again, ashift, db, fgain, fshift = (
-        small[:, own * i : own * (i + 1)].reshape(1, D) for i in range(8)
-    )
+    table = jnp.concatenate([small[:, own * i : own * (i + 1)].reshape(1, D) for i in range(8)], axis=0)
     ub = small[:, 8 * own : 8 * own + wide].reshape(1, ff)
-    zero = jnp.zeros((1, D), F32)
-    table = jnp.concatenate([ob, again, ashift, db, fgain, fshift, zero, zero], axis=0)
-
-    positions = jnp.arange(length)
-    inside = jnp.any(
-        (positions[None, None, :] >= span_start[:, :, None]) & (positions[None, None, :] < span_end[:, :, None]),
-        axis=1,
-    )
-    gy = jnp.where(inside.reshape(rows, 1), cotangent, jnp.zeros_like(cotangent))
-
-    q, k, v, mixed, lse = attn_fwd(tokens, wq, wk, wv, qb, vb, lengths)
+    gy = residue_mask(cotangent, span_start, span_end)
+
+    q, k, v, mixed, lse = attn_fwd(tokens, wq, wk, wv, table[0:1], table[1:2], lengths)
     layer_out, hidden, gffn, low, gpre, gattn, g1, gmixed, gtable, gub = ffn_both(
-        mixed, tokens, gy, wo, wu, wd, table, ub
+        mixed, tokens, gy, (wo, wu, wd), table, ub
     )
     down_grad = wgrad(hidden, gffn)
     up_grad = wgrad(low, gpre)
-    gathered_ffn = jnp.concatenate(
-        [up_grad.reshape(parts, wide, D), down_grad.reshape(parts, wide, D)], axis=1
-    )
-    ffn_own = lax.psum_scatter(gathered_ffn, "fsdp", scatter_dimension=0, tiled=False)
+    ffn_parts = jnp.concatenate([up_grad.reshape(parts, wide, D), down_grad.reshape(parts, wide, D)], axis=1)
+    ffn_own = lax.psum_scatter(ffn_parts, "fsdp", scatter_dimension=0, tiled=False).astype(F32)
     out_grad = wgrad(mixed, gattn)
     gq, gk, gv, gqb, gvb = attn_bwd(q, k, v, gmixed, lse, lengths)
     query_grad, key_grad, value_grad = wgrad3(tokens, gq, gk, gv)
-    parts_of = [gqb, gvb, gtable[0:1], gtable[1:2], gtable[2:3], gtable[3:4], gtable[4:5], gtable[5:6]]
-    vec = jnp.concatenate([p.reshape(parts, own) for p in parts_of] + [gub.reshape(parts, wide)], axis=1)
+    vec = [gqb, gvb] + [gtable[i : i + 1] for i in range(2, 8)]
+    vec = jnp.concatenate([p.reshape(parts, own) for p in vec] + [gub.reshape(parts, wide)], axis=1)
     vec = jnp.pad(vec.astype(BF16), ((0, 0), (0, D - vec.shape[1]))).reshape(parts, 1, D)
     attn_parts = jnp.concatenate(
         [g.reshape(parts, own, D) for g in (query_grad, key_grad, value_grad, out_grad)] + [vec], axis=1
     )
-    attn_own = lax.psum_scatter(attn_parts, "fsdp", scatter_dimension=0, tiled=False)
+    attn_own = lax.psum_scatter(attn_parts, "fsdp", scatter_dimension=0, tiled=False).astype(F32)
     in_grad = input_grad(g1, gq, gk, gv, wq, wk, wv)
 
-    attn_own = attn_own.astype(F32)
-    ffn_own = ffn_own.astype(F32)
     gq_w, gk_w, gv_w, go_w = (attn_own[own * i : own * (i + 1)] for i in range(4))
     vec = attn_own[-1]
     gqb, gvb, gob, gag, gas, gdb, gfg, gfs = (vec[own * i : own * (i + 1)] for i in range(8))
@@ -375,8 +729,10 @@
 
 def solution(mesh):
     two, one = P("fsdp", None), P("fsdp")
+    n = mesh.shape["fsdp"]
+    whole_tiles = n % 8 == 0 and n // 8 == 4 and (D // n) % 8 == 0
     return jax.shard_map(
-        shards,
+        functools.partial(fast_shards, n) if whole_tiles else plain_shards,
         mesh=mesh,
         in_specs=(two, two, one, two, two, two, one, two, two, one, two, one, one, one, two, one, two, one, one, one),
         out_specs=(two, two, two, one, two, two, one, two, one, one, one, two, one, two, one, one, one),

time: 512 us -> 309 us (0.60)
  waiting for transfers between devices: 298 us -> 59.3 us
  starting transfers between devices: 0.12 us -> 53.2 us
  local copies, waits for them, and re-layouts: 49.8 us -> 9.35 us
  Pallas kernels: 132 us -> 152 us
    reduce_scatter x2 -> x0, waiting for transfers between devices: 195 us -> none  [the longest x1 139 us: shards(): lax.psum_scatter(gathered_ffn, 'fsdp', scatter_dimension=0, tiled=False)]
    all_gather x1, waiting for transfers between devices: 103 us -> 4.09 us  [fast_shards(): raw = lax.all_gather(sent, 'fsdp', axis=0, tiled=False)]
    ppermute x0 -> x35, waiting for transfers between devices: none -> 55.2 us  [hop(): return lax.ppermute(value, 'fsdp', pairs)]
    ppermute x0 -> x35, starting transfers between devices: none -> 53.2 us  [hop(): return lax.ppermute(value, 'fsdp', pairs)]
    pallas_call x7 -> x13, Pallas kernels: 115 us -> 134 us  [the longest x1 41 us: ffn_both(): call(body, (rows // tile_rows,), [tile, tile, tile] + [fixed(w) for w in...]
    reshape x22 -> x1, local copies, waits for them, and re-layouts: 13.6 us -> 0.92 us  [chunked(): return weight.reshape(own, -1, D).swapaxes(0, 1).reshape(-1, D)]
    slice x10 -> x4, local copies, waits for them, and re-layouts: 14.8 us -> 2.96 us  [the longest x1 1.4 us: fast_shards(): table[1:2]]
    unnamed x23 -> x84, local copies, waits for them, and re-layouts: 13.6 us -> 4.31 us
  transfers between devices with their start and end apart: 3 -> 36, of which waited for: 3 -> 13; matrix products, arithmetic and copies ran while one was open for 5% -> 3% of each run, Pallas kernels for 7% -> 31%
where the time goes in v2:
time: 309 us; the launch traced here: 306 us
  Pallas kernels  152 us (49%)
  waiting for transfers between devices  59.3 us (19%)
  starting transfers between devices  53.2 us (17%)
  other arithmetic  17.5 us (6%)
  between operations  15.1 us (5%)
  local copies, waits for them, and re-layouts  9.35 us (3%)
    ppermute x35, waiting for transfers between devices, hop(): return lax.ppermute(value, 'fsdp', pairs)  55.2 us
    ppermute x35, starting transfers between devices, hop(): return lax.ppermute(value, 'fsdp', pairs)  53.2 us
    pallas_call x1, Pallas kernels, ffn_both(): call(body, (rows // tile_rows,), [tile, tile, tile] + [fixed(w) for w in...  41 us
    pallas_call x3, Pallas kernels, attn_bwd(): call(functools.partial(attn_bwd_body, start), (stop - start,), [pl.BlockS...  30.5 us
    pallas_call x1, Pallas kernels, attn_fwd(): call(attn_fwd_body, (n,), [pl.BlockSpec(memory_space=pltpu.SMEM), tile, f...  17.4 us
    pallas_call x1, Pallas kernels, wgrad_up(): call(functools.partial(wgrad_up_body, far, own), (5,), [pl.BlockSpec(memo...  15 us
    pallas_call x2, Pallas kernels, input_grad(): call(input_grad_body, (stop - start,), [tile, tile, tile, tile, full, ful...  12.4 us
    pallas_call x1, Pallas kernels, wgrad_down(): call(functools.partial(wgrad_down_body, far, own), (far,), [pl.BlockSpec(...  11.8 us
  transfers between devices with their start and end apart: 36, of which 13 were waited for; matrix products, arithmetic and copies ran while one was open for 3% of the time, Pallas kernels for 31%

profile of v2, /device:TPU:0, one launch (start us, length us, event | category | flops | bytes accessed | tf_op | source)
XLA Modules:
  0.0 306.0 jit_solution(1188242315351382219)
XLA Ops:
  8.2 1.7 fusion.13
  11.5 4.1 %collective-permute-start.4 = (bf16[80,768]{1,0:T(8,128)(2,1)S(1)}, bf16[80,768]{1,0:T(8,128)(2,1)S(1)}, u32[]{:S(2)}, u32[]{:S(2)}) collective-permute-start(bf16[80,768]{1,0:T(8,128)(2,1)S(1)} %get-tuple-element.299), channel_id=1, source_target_pairs={{0,16},{1,17},{2,18},{3,19},{4,20},{5,21},{6,22},{7,23},{8,24},{9,... | collective-permute-start | bytes 368648 | tf_op jit(solution)/shard_map/ppermute | solution.py:211
  15.6 1.6 collective-permute-start.3
  17.2 2.2 collective-permute-start.5
  19.5 5.6 %collective-permute-done.4 = bf16[80,768]{1,0:T(8,128)(2,1)S(1)} collective-permute-done((bf16[80,768]{1,0:T(8,128)(2,1)S(1)}, bf16[80,768]{1,0:T(8,128)(2,1)S(1)}, u32[]{:S(2)}, u32[]{:S(2)}) %collective-permute-start.4) | collective-permute-done | bytes 122912 | tf_op jit(solution)/shard_map/ppermute | solution.py:211
  25.1 2.9 collective-permute-done.5
  29.4 1.6 collective-permute-start.7
  31.6 7.3 %collective-permute-done.2 = bf16[80,768]{1,0:T(8,128)(2,1)S(1)} collective-permute-done((bf16[80,768]{1,0:T(8,128)(2,1)S(1)}, bf16[80,768]{1,0:T(8,128)(2,1)S(1)}, u32[]{:S(2)}, u32[]{:S(2)}) %collective-permute-start.2) | collective-permute-done | bytes 122912 | tf_op jit(solution)/shard_map/ppermute | solution.py:211
  38.9 3.2 %collective-permute-start.10 = (bf16[80,768]{1,0:T(8,128)(2,1)S(1)}, bf16[80,768]{1,0:T(8,128)(2,1)S(1)}, u32[]{:S(2)}, u32[]{:S(2)}) collective-permute-start(bf16[80,768]{1,0:T(8,128)(2,1)S(1)} %collective-permute-done.2), channel_id=1, source_target_pairs={{0,24},{1,25},{2,26},{3,27},{4,28},{5,29},{6,30},{7,31},{8,0},{9,1... | collective-permute-start | bytes 368648 | tf_op jit(solution)/shard_map/ppermute | solution.py:211
  42.2 9.2 %collective-permute-start.9 = (bf16[80,768]{1,0:T(8,128)(2,1)S(1)}, bf16[80,768]{1,0:T(8,128)(2,1)S(1)}, u32[]{:S(2)}, u32[]{:S(2)}) collective-permute-start(bf16[80,768]{1,0:T(8,128)(2,1)S(1)} %collective-permute-done.2), channel_id=1, source_target_pairs={{0,16},{1,17},{2,18},{3,19},{4,20},{5,21},{6,22},{7,23},{8,24},{9,... | collective-permute-start | bytes 368648 | tf_op jit(solution)/shard_map/ppermute | solution.py:211
  51.4 2.0 collective-permute-start.8
  53.5 15.0 %collective-permute-done.8 = bf16[80,768]{1,0:T(8,128)(2,1)S(1)} collective-permute-done((bf16[80,768]{1,0:T(8,128)(2,1)S(1)}, bf16[80,768]{1,0:T(8,128)(2,1)S(1)}, u32[]{:S(2)}, u32[]{:S(2)}) %collective-permute-start.8) | collective-permute-done | bytes 122912 | tf_op jit(solution)/shard_map/ppermute | solution.py:211
  68.5 1.7 collective-permute-done.9
  70.4 1.5 collective-permute-start.1
  71.9 1.5 collective-permute-start
  74.4 2.3 collective-permute-done.1
  76.7 2.7 collective-permute-done
  83.5 4.8 %shard_map.323 = (bf16[16,48,768]{2,1,0:T(8,128)(2,1)}, bf16[16,48,768]{2,1,0:T(8,128)(2,1)}, bf16[16,48,768]{2,1,0:T(8,128)(2,1)}, f32[8,768]{1,0:T(8,128)}, f32[1,3072]{1,0:T(1,128)}) custom-call(s32[3]{0:T(128)} %pad_add_fusion.1.at_ref, bf16[4,80,768]{2,1,0:T(8,128)(2,1)} %copy-done.1, bf16[3,80,768]{2,1,0:T(8,128)(2,1)} %copy-done.4, ...), custom_call_target="tpu_custom_call" | custom-call | tf_op jit(solution)/shard_map/pallas_call | solution.py:268
  89.8 17.4 %shard_map.324 = (bf16[1120,768]{1,0:T(8,128)(2,1)}, bf16[1120,768]{1,0:T(8,128)(2,1)}, bf16[1120,768]{1,0:T(8,128)(2,1)}, bf16[1120,768]{1,0:T(8,128)(2,1)}, f32[1120,128]{1,0:T(8,128)}) custom-call(s32[7]{0:T(128)} %len_ref.7, bf16[1120,768]{1,0:T(8,128)(2,1)} %x_ref.5, bf16[768,768]{1,0:T(8,128)(2,1)} %bitcast.83, bf16[768,768]{1,0:T(8,128)(2,1)} %bitcast.86, ...), custom_call_target="tpu_custom_call" | custom-call | tf_op jit(solution)/shard_map/pallas_call | solution.py:91
  107.2 4.1 %all-gather.3.cloned.1.call-done = bf16[7168,768]{1,0:T(8,128)(2,1)} async-done(((bf16[224,768]{1,0:T(8,128)(2,1)}), bf16[7168,768]{1,0:T(8,128)(2,1)}) %all-gather.3.cloned.1.call-update) | async-done | bytes 11010064 | tf_op jit(solution)/shard_map/all_gather | solution.py:614
  111.3 41.0 %shard_map.325 = (bf16[1120,768]{1,0:T(8,128)(2,1)}, bf16[1120,3072]{1,0:T(8,128)(2,1)}, bf16[1120,768]{1,0:T(8,128)(2,1)}, bf16[1120,768]{1,0:T(8,128)(2,1)}, b...) custom-call(bf16[1120,768]{1,0:T(8,128)(2,1)} %get-tuple-element.149, ...), custom_call_target="tpu_custom_call" | custom-call | tf_op jit(solution)/shard_map/pallas_call | solution.py:392
  152.2 11.8 %shard_map.326 = (bf16[4,4,96,768]{3,2,1,0:T(8,128)(2,1)}, bf16[4,4,96,768]{3,2,1,0:T(8,128)(2,1)}) custom-call(s32[3]{0:T(128)} %pad_add_fusion.1.at_ref, bf16[1120,3072]{1,0:T(8,128)(2,1)} %get-tuple-element.157.hid_ref, bf16[1120,768]{1,0:T(8,128)(2,1)} %get-tuple-element.158.gffn_ref), custom_call_target="tpu_custom_call" | custom-call | tf_op jit(solution)/shard_map/pallas_call | solution.py:433
  164.3 5.6 %shard_map.327 = (bf16[1120,768]{1,0:T(8,128)(2,1)}, bf16[1120,768]{1,0:T(8,128)(2,1)}, bf16[1120,768]{1,0:T(8,128)(2,1)}, f32[1,768]{1,0:T(1,128)}, f32[1,768]{1,0:T(1,128)}) custom-call(s32[7]{0:T(128)} %len_ref.7, bf16[1120,768]{1,0:T(8,128)(2,1)} %get-tuple-element.153.q_ref, bf16[1120,768]{1,0:T(8,128)(2,1)} %get-tuple-element.154.k_ref, ...), custom_call_target="tpu_custom_call" | custom-call | flops 1099511627776 | bytes 17179869184 | tf_op jit(solution)/shard_map/pallas_call | solution.py:148
  169.9 1.9 fusion.8
  171.8 1.5 collective-permute-start.15
  173.9 1.5 collective-permute-start.17
  175.4 15.0 %shard_map.328 = (bf16[4,4,120,768]{3,2,1,0:T(8,128)(2,1)}, bf16[4,4,120,768]{3,2,1,0:T(8,128)(2,1)}) custom-call(s32[3]{0:T(128)} %pad_add_fusion.1.at_ref, bf16[1120,768]{1,0:T(8,128)(2,1)} %get-tuple-element.182.low_ref, bf16[1120,3072]{1,0:T(8,128)(2,1)} %get-tuple-element.183.gpre_ref, bf16[1120,768]{1,0:T(8,128)(2,1)} %get-tuple-element.149.mix_ref, ...), custom_call_target="tpu_custom_call" | custom-call | tf_op jit(solution)/shard_map/pallas_call | solution.py:464
  190.4 12.3 %shard_map.329 = (bf16[1120,768]{1,0:T(8,128)(2,1)}, bf16[1120,768]{1,0:T(8,128)(2,1)}, bf16[1120,768]{1,0:T(8,128)(2,1)}, f32[1,768]{1,0:T(1,128)}, f32[1,768]{1,0:T(1,128)}) custom-call(s32[7]{0:T(128)} %len_ref.7, bf16[1120,768]{1,0:T(8,128)(2,1)} %get-tuple-element.153.q_ref, ...), custom_call_target="tpu_custom_call", output_to_operand_aliasing={{0}: (6, {}), {1}: (7, {}), {2}: (8, {})} | custom-call | tf_op jit(solution)/shard_map/pallas_call | solution.py:148
  204.0 2.9 shard_map.330
  206.9 3.4 %fusion.2 = (bf16[4,120,768]{2,1,0:T(8,128)(2,1)S(1)}, bf16[4,120,768]{2,1,0:T(8,128)(2,1)}, bf16[4,120,768]{2,1,0:T(8,128)(2,1)}) fusion(bf16[4,4,120,768]{3,2,1,0:T(8,128)(2,1)} %collective-permute-done.18.other_ref, bf16[4,4,120,768]{3,2,1,0:T(8,128)(2,1)S(1)} %copy-done.3), kind=kLoop, calls=%fused_computation.12 | loop fusion | flops 4423680 | bytes 6635520 | tf_op jit(solution)/shard_map/convert_element_type | solution.py:510
  212.3 1.5 collective-permute-start.23
  215.1 2.6 collective-permute-start.20
  217.6 12.5 %shard_map.331 = (bf16[1120,768]{1,0:T(8,128)(2,1)}, bf16[1120,768]{1,0:T(8,128)(2,1)}, bf16[1120,768]{1,0:T(8,128)(2,1)}, f32[1,768]{1,0:T(1,128)}, f32[1,768]{1,0:T(1,128)}) custom-call(s32[7]{0:T(128)} %len_ref.7, bf16[1120,768]{1,0:T(8,128)(2,1)} %get-tuple-element.153.q_ref, ...), custom_call_target="tpu_custom_call", output_to_operand_aliasing={{0}: (6, {}), {1}: (7, {}), {2}: (8, {})} | custom-call | tf_op jit(solution)/shard_map/pallas_call | solution.py:148
  231.6 9.9 %shard_map.332 = (bf16[4,4,80,768]{3,2,1,0:T(8,128)(2,1)}, bf16[4,4,80,768]{3,2,1,0:T(8,128)(2,1)}) custom-call(s32[3]{0:T(128)} %pad_add_fusion.1.at_ref, bf16[1120,768]{1,0:T(8,128)(2,1)} %x_ref.5, bf16[1120,768]{1,0:T(8,128)(2,1)} %get-tuple-element.224.gq_ref, bf16[1120,768]{1,0:T(8,128)(2,1)} %get-tuple-element.225.gk_ref, ...), custom_call_target="tpu_custom_call" | custom-call | tf_op jit(solution)/shard_map/pallas_call | solution.py:497
  241.5 6.3 %shard_map.333.rest_0_ = bf16[1120,768]{1,0:T(8,128)(2,1)} custom-call(f32[1120,768]{1,0:T(8,128)} %get-tuple-element.233.g1_ref, bf16[1120,768]{1,0:T(8,128)(2,1)} %get-tuple-element.224.gq_ref, bf16[1120,768]{1,0:T(8,128)(2,1)} %get-tuple-element.225.gk_ref, bf16[1120,768]{1,0:T(8,128)(2,1)} %get-tuple-element.226.gv_ref, bf16[768,768]{1,0:T(8,128)(2,1)} %bitcast.84, ...), custom_call_target="tpu_custom_call" | custom-call | tf_op jit(solution)/shard_map/pallas_call | solution.py:574
  249.4 3.3 %shard_map.334 = (f32[120,768]{1,0:T(8,128)}, bf16[120,768]{1,0:T(8,128)(2,1)}, bf16[120,768]{1,0:T(8,128)(2,1)}, bf16[120,768]{1,0:T(8,128)(2,1)}) custom-call(bf16[4,4,120,768]{3,2,1,0:T(8,128)(2,1)} %get-tuple-element.205.keep_ref, bf16[4,4,120,768]{3,2,1,0:T(8,128)(2,1)} %collective-permute-done.18.other_ref, bf16[1,4,120,768]{3,2,1,0:T(8,128)(2,1)} %bitcast.107, ...), custom_call_target="tpu_custom_call" | custom-call | flops 1099511627776 | bytes 17179869184 | tf_op jit(solution)/shard_map/pallas_call | solution.py:530
  252.8 1.8 fusion.11
  254.5 1.5 collective-permute-start.26
  256.6 1.5 collective-permute-start.28
  258.6 2.4 collective-permute-start.30
  261.0 6.5 %collective-permute-done.29 = bf16[120,768]{1,0:T(8,128)(2,1)S(1)} collective-permute-done((bf16[120,768]{1,0:T(8,128)(2,1)S(1)}, bf16[120,768]{1,0:T(8,128)(2,1)S(1)}, u32[]{:S(2)}, u32[]{:S(2)}) %collective-permute-start.29) | collective-permute-done | bytes 184352 | tf_op jit(solution)/shard_map/ppermute | solution.py:211
  268.3 6.1 %shard_map.335 = bf16[1120,768]{1,0:T(8,128)(2,1)} custom-call(f32[1120,768]{1,0:T(8,128)} %get-tuple-element.233.g1_ref, bf16[1120,768]{1,0:T(8,128)(2,1)} %get-tuple-element.224.gq_ref, bf16[1120,768]{1,0:T(8,128)(2,1)} %get-tuple-element.225.gk_ref, bf16[1120,768]{1,0:T(8,128)(2,1)} %get-tuple-element.226.gv_ref, ...), custom_call_target="tpu_custom_call", output_to_operand_aliasing={{}: (7, {})} | custom-call | tf_op jit(solution)/shard_map/pallas_call | solution.py:574
  274.4 5.5 %collective-permute-done.27 = bf16[4,80,768]{2,1,0:T(8,128)(2,1)S(1)} collective-permute-done((bf16[4,80,768]{2,1,0:T(8,128)(2,1)S(1)}, bf16[4,80,768]{2,1,0:T(8,128)(2,1)S(1)}, u32[]{:S(2)}, u32[]{:S(2)}) %collective-permute-start.27) | collective-permute-done | bytes 491552 | tf_op jit(solution)/shard_map/ppermute | solution.py:211
  281.0 2.6 shard_map.336
  283.6 1.6 collective-permute-start.31
  285.2 3.9 %collective-permute-start.32 = (bf16[80,768]{1,0:T(8,128)(2,1)}, bf16[80,768]{1,0:T(8,128)(2,1)S(1)}, u32[]{:S(2)}, u32[]{:S(2)}) collective-permute-start(bf16[80,768]{1,0:T(8,128)(2,1)} %get-tuple-element.263), channel_id=1, source_target_pairs={{0,16},{1,17},{2,18},{3,19},{4,20},{5,21},{6,22},{7,23},{8,24},{9,... | collective-permute-start | bytes 368648 | tf_op jit(solution)/shard_map/ppermute | solution.py:211
  290.8 2.1 collective-permute-done.31
  292.9 3.0 collective-permute-done.32
  (148 shorter events, 27.1 us)
Async XLA Ops:
  7.2 104.1 %all-gather.3.cloned.1.call-start = ((), (), s32[]{:S(2)}) async-start(), calls=%async_computation | async-start | bytes 11354112 | tf_op jit(solution)/shard_map/all_gather | solution.py:614
  9.9 63.5 %copy-start.23 = (s32[7,4]{0,1:T(4,128)S(1)}, s32[7,4]{0,1:T(4,128)}, u32[]{:S(2)}) copy-start(s32[7,4]{0,1:T(4,128)} %param.23) | copy-start | bytes 340
  9.9 63.6 %copy-start.24 = (s32[7,4]{0,1:T(4,128)S(1)}, s32[7,4]{0,1:T(4,128)}, u32[]{:S(2)}) copy-start(s32[7,4]{0,1:T(4,128)} %param.24) | copy-start | bytes 340
  11.5 13.6 %collective-permute-start.4 = (bf16[80,768]{1,0:T(8,128)(2,1)S(1)}, bf16[80,768]{1,0:T(8,128)(2,1)S(1)}, u32[]{:S(2)}, u32[]{:S(2)}) collective-permute-start(bf16[80,768]{1,0:T(8,128)(2,1)S(1)} %get-tuple-element.299), channel_id=1, source_target_pairs={{0,16},{1,17},{2,18},{3,19},{4,20},{5,21},{6,22},{7,23},{8,24},{9,... | collective-permute-start | bytes 368648 | tf_op jit(solution)/shard_map/ppermute | solution.py:211
  15.6 9.5 %collective-permute-start.3 = (bf16[80,768]{1,0:T(8,128)(2,1)S(1)}, bf16[80,768]{1,0:T(8,128)(2,1)S(1)}, u32[]{:S(2)}, u32[]{:S(2)}) collective-permute-start(bf16[80,768]{1,0:T(8,128)(2,1)S(1)} %get-tuple-element.299), channel_id=1, source_target_pairs={{0,8},{1,9},{2,10},{3,11},{4,12},{5,13},{6,14},{7,15},{8,16},{9,17... | collective-permute-start | bytes 368648 | tf_op jit(solution)/shard_map/ppermute | solution.py:211
  17.2 10.8 %collective-permute-start.5 = (bf16[80,768]{1,0:T(8,128)(2,1)S(1)}, bf16[80,768]{1,0:T(8,128)(2,1)S(1)}, u32[]{:S(2)}, u32[]{:S(2)}) collective-permute-start(bf16[80,768]{1,0:T(8,128)(2,1)S(1)} %get-tuple-element.299), channel_id=1, source_target_pairs={{0,24},{1,25},{2,26},{3,27},{4,28},{5,29},{6,30},{7,31},{8,0},{9,1... | collective-permute-start | bytes 368648 | tf_op jit(solution)/shard_map/ppermute | solution.py:211
  28.0 54.0 %copy-start.4 = (bf16[3,80,768]{2,1,0:T(8,128)(2,1)}, bf16[3,80,768]{2,1,0:T(8,128)(2,1)S(1)}, u32[]{:S(2)}) copy-start(bf16[3,80,768]{2,1,0:T(8,128)(2,1)S(1)} %pad_maximum_fusion.1.l_ref) | copy-start | bytes 1105924
  28.0 52.5 %copy-start.2 = (bf16[1120,768]{1,0:T(8,128)(2,1)S(1)}, bf16[1120,768]{1,0:T(8,128)(2,1)}, u32[]{:S(2)}) copy-start(bf16[1120,768]{1,0:T(8,128)(2,1)} %param.21) | copy-start | bytes 5160964
  28.0 25.3 %collective-permute-start.6 = (bf16[3,80,768]{2,1,0:T(8,128)(2,1)S(1)}, bf16[3,80,768]{2,1,0:T(8,128)(2,1)S(1)}, u32[]{:S(2)}, u32[]{:S(2)}) collective-permute-start(bf16[3,80,768]{2,1,0:T(8,128)(2,1)S(1)} %pad_maximum_fusion.1.l_ref), channel_id=1, source_target_pairs={{0,2},{1,3},{2,0},{3,1},{4,6},{5,7},{6,4},{7,5},{8,10},{9,11},{10,... | collective-permute-start | bytes 1105928 | tf_op jit(solution)/shard_map/ppermute | solution.py:211
  29.4 24.0 %collective-permute-start.7 = (bf16[3,80,768]{2,1,0:T(8,128)(2,1)S(1)}, bf16[3,80,768]{2,1,0:T(8,128)(2,1)S(1)}, u32[]{:S(2)}, u32[]{:S(2)}) collective-permute-start(bf16[3,80,768]{2,1,0:T(8,128)(2,1)S(1)} %pad_maximum_fusion.1.l_ref), channel_id=1, source_target_pairs={{0,4},{1,5},{2,6},{3,7},{4,0},{5,1},{6,2},{7,3},{8,12},{9,13},{10,... | collective-permute-start | bytes 1105928 | tf_op jit(solution)/shard_map/ppermute | solution.py:211
  31.0 7.9 %collective-permute-start.2 = (bf16[80,768]{1,0:T(8,128)(2,1)S(1)}, bf16[80,768]{1,0:T(8,128)(2,1)S(1)}, u32[]{:S(2)}, u32[]{:S(2)}) collective-permute-start(bf16[80,768]{1,0:T(8,128)(2,1)S(1)} %get-tuple-element.299), channel_id=1, source_target_pairs={{0,6},{1,7},{2,4},{3,5},{4,2},{5,3},{6,0},{7,1},{8,14},{9,15},{10,... | collective-permute-start | bytes 368648 | tf_op jit(solution)/shard_map/ppermute | solution.py:211
  38.9 31.4 %copy-start.21 = (bf16[80,768]{1,0:T(8,128)(2,1)}, bf16[80,768]{1,0:T(8,128)(2,1)S(1)}, u32[]{:S(2)}) copy-start(bf16[80,768]{1,0:T(8,128)(2,1)S(1)} %collective-permute-done.2) | copy-start | bytes 368644
  38.9 31.3 %collective-permute-start.10 = (bf16[80,768]{1,0:T(8,128)(2,1)S(1)}, bf16[80,768]{1,0:T(8,128)(2,1)S(1)}, u32[]{:S(2)}, u32[]{:S(2)}) collective-permute-start(bf16[80,768]{1,0:T(8,128)(2,1)S(1)} %collective-permute-done.2), channel_id=1, source_target_pairs={{0,24},{1,25},{2,26},{3,27},{4,28},{5,29},{6,30},{7,31},{8,0},{9,1... | collective-permute-start | bytes 368648 | tf_op jit(solution)/shard_map/ppermute | solution.py:211
  42.2 28.1 %collective-permute-start.9 = (bf16[80,768]{1,0:T(8,128)(2,1)S(1)}, bf16[80,768]{1,0:T(8,128)(2,1)S(1)}, u32[]{:S(2)}, u32[]{:S(2)}) collective-permute-start(bf16[80,768]{1,0:T(8,128)(2,1)S(1)} %collective-permute-done.2), channel_id=1, source_target_pairs={{0,16},{1,17},{2,18},{3,19},{4,20},{5,21},{6,22},{7,23},{8,24},{9,... | collective-permute-start | bytes 368648 | tf_op jit(solution)/shard_map/ppermute | solution.py:211
  51.4 17.1 %collective-permute-start.8 = (bf16[80,768]{1,0:T(8,128)(2,1)S(1)}, bf16[80,768]{1,0:T(8,128)(2,1)S(1)}, u32[]{:S(2)}, u32[]{:S(2)}) collective-permute-start(bf16[80,768]{1,0:T(8,128)(2,1)S(1)} %collective-permute-done.2), channel_id=1, source_target_pairs={{0,8},{1,9},{2,10},{3,11},{4,12},{5,13},{6,14},{7,15},{8,16},{9,17... | collective-permute-start | bytes 368648 | tf_op jit(solution)/shard_map/ppermute | solution.py:211
  70.3 13.2 %collective-permute-start.13 = (bf16[9,80,768]{2,1,0:T(8,128)(2,1)S(1)}, bf16[9,80,768]{2,1,0:T(8,128)(2,1)}, u32[]{:S(2)}, u32[]{:S(2)}) collective-permute-start(bf16[9,80,768]{2,1,0:T(8,128)(2,1)S(1)} %bitcast_dynamic-update-slice_fusion.r_ref), channel_id=1, source_target_pairs={{0,1},{1,0},{2,3},{3,2},{4,5},{5,4},{6,7},{7,6},{8,9},{9,8},{10,11... | collective-permute-start | bytes 3317768 | tf_op jit(solution)/shard_map/ppermute | solution.py:211
  70.4 6.3 %collective-permute-start.1 = (bf16[80,768]{1,0:T(8,128)(2,1)S(1)}, bf16[80,768]{1,0:T(8,128)(2,1)}, u32[]{:S(2)}, u32[]{:S(2)}) collective-permute-start(bf16[80,768]{1,0:T(8,128)(2,1)S(1)} %get-tuple-element.299), channel_id=1, source_target_pairs={{0,4},{1,5},{2,6},{3,7},{4,0},{5,1},{6,2},{7,3},{8,12},{9,13},{10,... | collective-permute-start | bytes 368648 | tf_op jit(solution)/shard_map/ppermute | solution.py:211
  71.9 7.5 %collective-permute-start = (bf16[80,768]{1,0:T(8,128)(2,1)S(1)}, bf16[80,768]{1,0:T(8,128)(2,1)}, u32[]{:S(2)}, u32[]{:S(2)}) collective-permute-start(bf16[80,768]{1,0:T(8,128)(2,1)S(1)} %get-tuple-element.299), channel_id=1, source_target_pairs={{0,2},{1,3},{2,0},{3,1},{4,6},{5,7},{6,4},{7,5},{8,10},{9,11},{10,... | collective-permute-start | bytes 368648 | tf_op jit(solution)/shard_map/ppermute | solution.py:211
  74.4 7.6 %collective-permute-start.12 = (bf16[3,80,768]{2,1,0:T(8,128)(2,1)S(1)}, bf16[3,80,768]{2,1,0:T(8,128)(2,1)S(1)}, u32[]{:S(2)}, u32[]{:S(2)}) collective-permute-start(bf16[3,80,768]{2,1,0:T(8,128)(2,1)S(1)} %pad_maximum_fusion.1.l_ref), channel_id=1, source_target_pairs={{0,1},{1,0},{2,3},{3,2},{4,5},{5,4},{6,7},{7,6},{8,9},{9,8},{10,11... | collective-permute-start | bytes 1105928 | tf_op jit(solution)/shard_map/ppermute | solution.py:211
  80.5 1.9 collective-permute-start.11
  164.0 5.9 %collective-permute-start.14 = (bf16[4,4,96,768]{3,2,1,0:T(8,128)(2,1)}, bf16[4,4,96,768]{3,2,1,0:T(8,128)(2,1)}, u32[]{:S(2)}, u32[]{:S(2)}) collective-permute-start(bf16[4,4,96,768]{3,2,1,0:T(8,128)(2,1)} %get-tuple-element.169), channel_id=1, source_target_pairs={{0,1},{1,0},{2,3},{3,2},{4,5},{5,4},{6,7},{7,6},{8,9},{9,8},{10,11... | collective-permute-start | bytes 7077896 | tf_op jit(solution)/shard_map/ppermute | solution.py:211
  171.8 30.9 %collective-permute-start.15 = (bf16[4,96,768]{2,1,0:T(8,128)(2,1)S(1)}, bf16[4,96,768]{2,1,0:T(8,128)(2,1)S(1)}, u32[]{:S(2)}, u32[]{:S(2)}) collective-permute-start(bf16[4,96,768]{2,1,0:T(8,128)(2,1)S(1)} %get-tuple-element.197), channel_id=1, source_target_pairs={{0,2},{1,3},{2,0},{3,1},{4,6},{5,7},{6,4},{7,5},{8,10},{9,11},{10,... | collective-permute-start | bytes 1769480 | tf_op jit(solution)/shard_map/ppermute | solution.py:211
  173.3 29.5 %collective-permute-start.16 = (bf16[4,96,768]{2,1,0:T(8,128)(2,1)S(1)}, bf16[4,96,768]{2,1,0:T(8,128)(2,1)S(1)}, u32[]{:S(2)}, u32[]{:S(2)}) collective-permute-start(bf16[4,96,768]{2,1,0:T(8,128)(2,1)S(1)} %get-tuple-element.198), channel_id=1, source_target_pairs={{0,4},{1,5},{2,6},{3,7},{4,0},{5,1},{6,2},{7,3},{8,12},{9,13},{10,... | collective-permute-start | bytes 1769480 | tf_op jit(solution)/shard_map/ppermute | solution.py:211
  173.9 28.9 %collective-permute-start.17 = (bf16[4,96,768]{2,1,0:T(8,128)(2,1)S(1)}, bf16[4,96,768]{2,1,0:T(8,128)(2,1)S(1)}, u32[]{:S(2)}, u32[]{:S(2)}) collective-permute-start(bf16[4,96,768]{2,1,0:T(8,128)(2,1)S(1)} %get-tuple-element.199), channel_id=1, source_target_pairs={{0,6},{1,7},{2,4},{3,5},{4,2},{5,3},{6,0},{7,1},{8,14},{9,15},{10,... | collective-permute-start | bytes 1769480 | tf_op jit(solution)/shard_map/ppermute | solution.py:211
  190.4 16.5 %collective-permute-start.18 = (bf16[4,4,120,768]{3,2,1,0:T(8,128)(2,1)}, bf16[4,4,120,768]{3,2,1,0:T(8,128)(2,1)}, u32[]{:S(2)}, u32[]{:S(2)}) collective-permute-start(bf16[4,4,120,768]{3,2,1,0:T(8,128)(2,1)} %get-tuple-element.213), channel_id=1, source_target_pairs={{0,1},{1,0},{2,3},{3,2},{4,5},{5,4},{6,7},{7,6},{8,9},{9,8},{10,11... | collective-permute-start | bytes 8847368 | tf_op jit(solution)/shard_map/ppermute | solution.py:211
  210.3 19.9 %copy-start.36 = (bf16[96,768]{1,0:T(8,128)(2,1)S(1)}, bf16[96,768]{1,0:T(8,128)(2,1)}, u32[]{:S(2)}) copy-start(bf16[96,768]{1,0:T(8,128)(2,1)} %get-tuple-element.238) | copy-start | bytes 442372
  210.3 20.0 %copy-start.22 = (f32[8,768]{1,0:T(8,128)S(1)}, f32[8,768]{1,0:T(8,128)}, u32[]{:S(2)}) copy-start(f32[8,768]{1,0:T(8,128)} %get-tuple-element.229) | copy-start | bytes 73732
  210.3 37.6 %collective-permute-start.21 = (bf16[4,120,768]{2,1,0:T(8,128)(2,1)}, bf16[4,120,768]{2,1,0:T(8,128)(2,1)S(1)}, u32[]{:S(2)}, u32[]{:S(2)}) collective-permute-start(bf16[4,120,768]{2,1,0:T(8,128)(2,1)} %get-tuple-element.234), channel_id=1, source_target_pairs={{0,2},{1,3},{2,0},{3,1},{4,6},{5,7},{6,4},{7,5},{8,10},{9,11},{10,... | collective-permute-start | bytes 2211848 | tf_op jit(solution)/shard_map/ppermute | solution.py:211
  211.7 36.2 %collective-permute-start.22 = (bf16[4,120,768]{2,1,0:T(8,128)(2,1)}, bf16[4,120,768]{2,1,0:T(8,128)(2,1)S(1)}, u32[]{:S(2)}, u32[]{:S(2)}) collective-permute-start(bf16[4,120,768]{2,1,0:T(8,128)(2,1)} %get-tuple-element.235), channel_id=1, source_target_pairs={{0,4},{1,5},{2,6},{3,7},{4,0},{5,1},{6,2},{7,3},{8,12},{9,13},{10,... | collective-permute-start | bytes 2211848 | tf_op jit(solution)/shard_map/ppermute | solution.py:211
  212.3 35.6 %collective-permute-start.23 = (bf16[4,120,768]{2,1,0:T(8,128)(2,1)S(1)}, bf16[4,120,768]{2,1,0:T(8,128)(2,1)S(1)}, u32[]{:S(2)}, u32[]{:S(2)}) collective-permute-start(bf16[4,120,768]{2,1,0:T(8,128)(2,1)S(1)} %get-tuple-element.236), channel_id=1, source_target_pairs={{0,6},{1,7},{2,4},{3,5},{4,2},{5,3},{6,0},{7,1},{8,14},{9,15},{10,... | collective-permute-start | bytes 2211848 | tf_op jit(solution)/shard_map/ppermute | solution.py:211
  213.8 16.4 %collective-permute-start.19 = (bf16[96,768]{1,0:T(8,128)(2,1)S(1)}, bf16[96,768]{1,0:T(8,128)(2,1)S(1)}, u32[]{:S(2)}, u32[]{:S(2)}) collective-permute-start(bf16[96,768]{1,0:T(8,128)(2,1)S(1)} %copy-done.38), channel_id=1, source_target_pairs={{0,8},{1,9},{2,10},{3,11},{4,12},{5,13},{6,14},{7,15},{8,16},{9,17... | collective-permute-start | bytes 442376 | tf_op jit(solution)/shard_map/ppermute | solution.py:211
  215.1 15.1 %collective-permute-start.20 = (bf16[96,768]{1,0:T(8,128)(2,1)S(1)}, bf16[96,768]{1,0:T(8,128)(2,1)S(1)}, u32[]{:S(2)}, u32[]{:S(2)}) collective-permute-start(bf16[96,768]{1,0:T(8,128)(2,1)S(1)} %copy-done.37), channel_id=1, source_target_pairs={{0,24},{1,25},{2,26},{3,27},{4,28},{5,29},{6,30},{7,31},{8,0},{9,1... | collective-permute-start | bytes 442376 | tf_op jit(solution)/shard_map/ppermute | solution.py:211
  230.2 17.6 %collective-permute-start.24 = (bf16[96,768]{1,0:T(8,128)(2,1)S(1)}, bf16[96,768]{1,0:T(8,128)(2,1)S(1)}, u32[]{:S(2)}, u32[]{:S(2)}) collective-permute-start(bf16[96,768]{1,0:T(8,128)(2,1)S(1)} %copy-done.36), channel_id=1, source_target_pairs={{0,16},{1,17},{2,18},{3,19},{4,20},{5,21},{6,22},{7,23},{8,24},{9,... | collective-permute-start | bytes 442376 | tf_op jit(solution)/shard_map/ppermute | solution.py:211
  247.8 4.8 %collective-permute-start.25 = (bf16[4,4,80,768]{3,2,1,0:T(8,128)(2,1)}, bf16[4,4,80,768]{3,2,1,0:T(8,128)(2,1)}, u32[]{:S(2)}, u32[]{:S(2)}) collective-permute-start(bf16[4,4,80,768]{3,2,1,0:T(8,128)(2,1)} %get-tuple-element.249), channel_id=1, source_target_pairs={{0,1},{1,0},{2,3},{3,2},{4,5},{5,4},{6,7},{7,6},{8,9},{9,8},{10,11... | collective-permute-start | bytes 5898248 | tf_op jit(solution)/shard_map/ppermute | solution.py:211
  252.7 14.8 %copy-start.34 = (bf16[120,768]{1,0:T(8,128)(2,1)S(1)}, bf16[120,768]{1,0:T(8,128)(2,1)}, u32[]{:S(2)}) copy-start(bf16[120,768]{1,0:T(8,128)(2,1)} %get-tuple-element.268) | copy-start | bytes 552964
  252.7 14.8 %copy-start.14 = (f32[96,768]{1,0:T(8,128)S(1)}, f32[96,768]{1,0:T(8,128)}, u32[]{:S(2)}) copy-start(f32[96,768]{1,0:T(8,128)} %get-tuple-element.269) | copy-start | bytes 884740
  252.7 14.8 %copy-start.16 = (bf16[96,768]{1,0:T(8,128)(2,1)S(1)}, bf16[96,768]{1,0:T(8,128)(2,1)}, u32[]{:S(2)}) copy-start(bf16[96,768]{1,0:T(8,128)(2,1)} %copy-done.15) | copy-start | bytes 442372
  252.7 14.8 %copy-start.18 = (bf16[96,768]{1,0:T(8,128)(2,1)S(1)}, bf16[96,768]{1,0:T(8,128)(2,1)}, u32[]{:S(2)}) copy-start(bf16[96,768]{1,0:T(8,128)(2,1)} %copy-done.17) | copy-start | bytes 442372
  252.8 14.8 %copy-start.20 = (bf16[96,768]{1,0:T(8,128)(2,1)S(1)}, bf16[96,768]{1,0:T(8,128)(2,1)}, u32[]{:S(2)}) copy-start(bf16[96,768]{1,0:T(8,128)(2,1)} %copy-done.19) | copy-start | bytes 442372
  254.5 19.9 %collective-permute-start.26 = (bf16[4,80,768]{2,1,0:T(8,128)(2,1)S(1)}, bf16[4,80,768]{2,1,0:T(8,128)(2,1)S(1)}, u32[]{:S(2)}, u32[]{:S(2)}) collective-permute-start(bf16[4,80,768]{2,1,0:T(8,128)(2,1)S(1)} %get-tuple-element.252), channel_id=1, source_target_pairs={{0,2},{1,3},{2,0},{3,1},{4,6},{5,7},{6,4},{7,5},{8,10},{9,11},{10,... | collective-permute-start | bytes 1474568 | tf_op jit(solution)/shard_map/ppermute | solution.py:211
  256.0 23.9 %collective-permute-start.27 = (bf16[4,80,768]{2,1,0:T(8,128)(2,1)S(1)}, bf16[4,80,768]{2,1,0:T(8,128)(2,1)S(1)}, u32[]{:S(2)}, u32[]{:S(2)}) collective-permute-start(bf16[4,80,768]{2,1,0:T(8,128)(2,1)S(1)} %get-tuple-element.253), channel_id=1, source_target_pairs={{0,4},{1,5},{2,6},{3,7},{4,0},{5,1},{6,2},{7,3},{8,12},{9,13},{10,... | collective-permute-start | bytes 1474568 | tf_op jit(solution)/shard_map/ppermute | solution.py:211
  256.6 23.3 %collective-permute-start.28 = (bf16[4,80,768]{2,1,0:T(8,128)(2,1)S(1)}, bf16[4,80,768]{2,1,0:T(8,128)(2,1)S(1)}, u32[]{:S(2)}, u32[]{:S(2)}) collective-permute-start(bf16[4,80,768]{2,1,0:T(8,128)(2,1)S(1)} %get-tuple-element.254), channel_id=1, source_target_pairs={{0,6},{1,7},{2,4},{3,5},{4,2},{5,3},{6,0},{7,1},{8,14},{9,15},{10,... | collective-permute-start | bytes 1474568 | tf_op jit(solution)/shard_map/ppermute | solution.py:211
  258.1 9.4 %collective-permute-start.29 = (bf16[120,768]{1,0:T(8,128)(2,1)S(1)}, bf16[120,768]{1,0:T(8,128)(2,1)S(1)}, u32[]{:S(2)}, u32[]{:S(2)}) collective-permute-start(bf16[120,768]{1,0:T(8,128)(2,1)S(1)} %copy-done.35), channel_id=1, source_target_pairs={{0,8},{1,9},{2,10},{3,11},{4,12},{5,13},{6,14},{7,15},{8,16},{9,17... | collective-permute-start | bytes 552968 | tf_op jit(solution)/shard_map/ppermute | solution.py:211
  258.6 15.8 %collective-permute-start.30 = (bf16[120,768]{1,0:T(8,128)(2,1)}, bf16[120,768]{1,0:T(8,128)(2,1)S(1)}, u32[]{:S(2)}, u32[]{:S(2)}) collective-permute-start(bf16[120,768]{1,0:T(8,128)(2,1)} %get-tuple-element.256), channel_id=1, source_target_pairs={{0,16},{1,17},{2,18},{3,19},{4,20},{5,21},{6,22},{7,23},{8,24},{9,... | collective-permute-start | bytes 552968 | tf_op jit(solution)/shard_map/ppermute | solution.py:211
  267.5 12.4 %collective-permute-start.34 = (bf16[120,768]{1,0:T(8,128)(2,1)S(1)}, bf16[120,768]{1,0:T(8,128)(2,1)S(1)}, u32[]{:S(2)}, u32[]{:S(2)}) collective-permute-start(bf16[120,768]{1,0:T(8,128)(2,1)S(1)} %copy-done.34), channel_id=1, source_target_pairs={{0,24},{1,25},{2,26},{3,27},{4,28},{5,29},{6,30},{7,31},{8,0},{9,1... | collective-permute-start | bytes 552968 | tf_op jit(solution)/shard_map/ppermute | solution.py:211
  283.6 9.3 %collective-permute-start.31 = (bf16[80,768]{1,0:T(8,128)(2,1)}, bf16[80,768]{1,0:T(8,128)(2,1)S(1)}, u32[]{:S(2)}, u32[]{:S(2)}) collective-permute-start(bf16[80,768]{1,0:T(8,128)(2,1)} %get-tuple-element.262), channel_id=1, source_target_pairs={{0,8},{1,9},{2,10},{3,11},{4,12},{5,13},{6,14},{7,15},{8,16},{9,17... | collective-permute-start | bytes 368648 | tf_op jit(solution)/shard_map/ppermute | solution.py:211
  285.2 10.8 %collective-permute-start.32 = (bf16[80,768]{1,0:T(8,128)(2,1)}, bf16[80,768]{1,0:T(8,128)(2,1)S(1)}, u32[]{:S(2)}, u32[]{:S(2)}) collective-permute-start(bf16[80,768]{1,0:T(8,128)(2,1)} %get-tuple-element.263), channel_id=1, source_target_pairs={{0,16},{1,17},{2,18},{3,19},{4,20},{5,21},{6,22},{7,23},{8,24},{9,... | collective-permute-start | bytes 368648 | tf_op jit(solution)/shard_map/ppermute | solution.py:211
  289.1 6.9 %collective-permute-start.33 = (bf16[80,768]{1,0:T(8,128)(2,1)}, bf16[80,768]{1,0:T(8,128)(2,1)S(1)}, u32[]{:S(2)}, u32[]{:S(2)}) collective-permute-start(bf16[80,768]{1,0:T(8,128)(2,1)} %get-tuple-element.264), channel_id=1, source_target_pairs={{0,24},{1,25},{2,26},{3,27},{4,28},{5,29},{6,30},{7,31},{8,0},{9,1... | collective-permute-start | bytes 368648 | tf_op jit(solution)/shard_map/ppermute | solution.py:211
  (27 other events, 133.4 us)
Sparse Core Ops, SparseCore 0:
  10.9 100.3 all-gather.2

commit v3 on v2

--- a/solution.py
+++ b/solution.py
@@ -52,14 +52,14 @@
     return low, high
 
 
-def attn_fwd_body(len_ref, x_ref, wq_ref, wk_ref, wv_ref, bq_ref, bv_ref, q_ref, k_ref, v_ref, mix_ref, lse_ref):
-    c = pl.program_id(0)
+def attn_fwd_body(start, len_ref, x_ref, wq_ref, wk_ref, wv_ref, table_ref, *rest):
+    q_ref, k_ref, v_ref, mix_ref, lse_ref = rest[-5:]
     x = x_ref[...]
     length = x.shape[0]
-    q_ref[...] = (dot(x, wq_ref[...]) + bq_ref[...]).astype(BF16)
+    q_ref[...] = (dot(x, wq_ref[...]) + table_ref[0:1, :]).astype(BF16)
     k_ref[...] = dot(x, wk_ref[...]).astype(BF16)
-    v_ref[...] = (dot(x, wv_ref[...]) + bv_ref[...]).astype(BF16)
-    valid = lax.broadcasted_iota(jnp.int32, (1, length), 1) < len_ref[c]
+    v_ref[...] = (dot(x, wv_ref[...]) + table_ref[1:2, :]).astype(BF16)
+    valid = lax.broadcasted_iota(jnp.int32, (1, length), 1) < len_ref[pl.program_id(0) + start]
     masks = half_mask(BF16, 0.125)
     lane = lax.broadcasted_iota(jnp.int32, (1, 128), 1)
     lses = jnp.zeros((length, 128), F32)
@@ -80,21 +80,23 @@
     lse_ref[...] = lses
 
 
-def attn_fwd(x, wq, wk, wv, bq, bv, lengths):
+def attn_fwd(x, wq, wk, wv, table, lengths, start=0, stop=None, before=()):
     rows = x.shape[0]
     n = lengths.shape[0]
+    stop = n if stop is None else stop
     length = rows // n
-    tile = pl.BlockSpec((length, D), lambda c: (c, 0))
+    tile = pl.BlockSpec((length, D), lambda c: (c + start, 0))
     full = pl.BlockSpec((D, D), lambda c: (0, 0))
-    one = pl.BlockSpec((1, D), lambda c: (0, 0))
+    eight = pl.BlockSpec((8, D), lambda c: (0, 0))
     act = shaped((rows, D), BF16)
     return call(
-        attn_fwd_body, (n,),
-        [pl.BlockSpec(memory_space=pltpu.SMEM), tile, full, full, full, one, one],
-        [tile, tile, tile, tile, pl.BlockSpec((length, 128), lambda c: (c, 0))],
+        functools.partial(attn_fwd_body, start), (stop - start,),
+        [pl.BlockSpec(memory_space=pltpu.SMEM), tile, full, full, full, eight] + [pl.BlockSpec(memory_space=pl.ANY)] * len(before),
+        [tile, tile, tile, tile, pl.BlockSpec((length, 128), lambda c: (c + start, 0))],
         [act, act, act, act, shaped((rows, 128), F32)],
         flops=2 * rows * D * D * 3 + 4 * rows * length * D * 4, moved=rows * D * 10 + 6 * D * D,
-    )(lengths, x, wq, wk, wv, bq, bv)
+        aliases={6 + i: i for i in range(5)} if before else {},
+    )(lengths, x, wq, wk, wv, table, *before)
 
 
 def attn_bwd_body(start, len_ref, q_ref, k_ref, v_ref, gm_ref, lse_ref, *rest):
@@ -197,6 +199,10 @@
         flops=2 * rows * m * n, moved=2 * (rows * (m + n) + m * n),
     )(left, right)
 
+def tie(*values):
+    return lax.optimization_barrier(values)
+
+
 def place():
     idx = lax.axis_index("fsdp")
     return idx % 2, (idx // 2) % 4, idx // 8
@@ -211,44 +217,72 @@
     return lax.ppermute(value, "fsdp", pairs)
 
 
-def gather_blocks(block, n):
-    far = n // 8
-    zs = [hop(block, shift(n, k)) for k in range(1, far)]
-    x0, y0, d0 = (hop(block, swap(n, b)) for b in (2, 4, 6))
-    line = jnp.stack(zs)
-    first = jnp.stack([block, x0, y0, d0])
-    first_other = hop(first, swap(n, 1))
-    line_other = hop(line, swap(n, 1))
-    xs = hop(line, swap(n, 2))
-    ys = hop(line, swap(n, 4))
-    ds = jnp.stack([hop(d0, shift(n, k)) for k in range(1, far)])
-    rest = jnp.concatenate([xs, ys, ds])
-    rest_other = hop(rest, swap(n, 1))
-    return (first, line, rest), (first_other, line_other, rest_other)
-
-
-def sources(far):
-    out = [(0, i, i, 0) for i in range(4)]
-    out += [(1, k - 1, 0, k) for k in range(1, far)]
-    out += [(2, (d - 1) * (far - 1) + k - 1, d, k) for d in (1, 2, 3) for k in range(1, far)]
-    return out
-
-
-def assemble_body(far, own, at_ref, f_ref, l_ref, r_ref, fo_ref, lo_ref, ro_ref, wq_ref, wk_ref, wv_ref, table_ref, ub_ref):
+def join_body(*refs):
+    at = 0
+    for ref in refs[:-1]:
+        refs[-1][at : at + ref.shape[0]] = ref[...]
+        at += ref.shape[0]
+
+
+def join(*parts):
+    parts = [p if p.ndim == 3 else p[None] for p in parts]
+    full = lambda a: pl.BlockSpec(a.shape, lambda i: (0, 0, 0))
+    out = shaped((sum(p.shape[0] for p in parts),) + parts[0].shape[1:], BF16)
+    return call(join_body, (1,), [full(p) for p in parts], full(out), out)(*parts)
+
+
+def gather_all(first, second, n, spare, steps):
+    work, given = spare
+    across = lambda part: hop(part, swap(n, 1))
+    f1, f2, f3 = (hop(first, shift(n, k)) for k in (1, 2, 3))
+    x0, y0 = (hop(second, swap(n, b)) for b in (2, 4))
+    line = jnp.stack([first, f1, f2, f3])
+    line, second, x0, y0 = tie(line, second, x0, y0)
+    near = [hop(line, swap(n, b)) for b in (2, 4, 6)]
+    z1, z3 = (hop(second, shift(n, k)) for k in (1, 3))
+    near, second, z1, z3, given = tie(near, second, z1, z3, given)
+    mine = jnp.concatenate([line, *near])
+    other = across(mine)
+    pair = jnp.stack([z1, z3])
+    d0, z2 = hop(second, swap(n, 6)), hop(second, shift(n, 2))
+    x13, y13 = (hop(pair, swap(n, b)) for b in (2, 4))
+    other, begun = tie(other, jnp.stack([second, x0, y0, z1, z3]))
+    begun_other = across(begun)
+    held = steps[1](steps[0](mine, other))
+    held, d0, z2, x13, y13, begun_other, done = tie(held, d0, z2, x13, y13, begun_other, work(given))
+    middle = jnp.concatenate([d0[None], z2[None], x13, y13])
+    middle_other = across(middle)
+    last = [hop(z2, swap(n, b)) for b in (2, 4, 6)] + [hop(d0, shift(n, k)) for k in (1, 3)]
+    held, middle_other = tie(held, middle_other)
+    held, last = tie(steps[2](held), last)
+    last = [p[None] for p in last]
+    return done, held, [begun, middle, *last], [begun_other, middle_other, *(across(p) for p in last)]
+
+
+def first_sources():
+    return [(d, k) for d in range(4) for k in range(4)]
+
+
+def second_sources():
+    begun = [(0, 0), (1, 0), (2, 0), (0, 1), (0, 3)]
+    middle = [(3, 0), (0, 2), (1, 1), (1, 3), (2, 1), (2, 3)]
+    last = [[(1, 2)], [(2, 2)], [(3, 2)], [(3, 1)], [(3, 3)]]
+    return [(p, i, *at) for p, part in enumerate([begun, middle] + last) for i, at in enumerate(part)]
+
+
+def assemble_body(own, at_ref, mine_ref, other_ref, wq_ref, wk_ref, wv_ref, table_ref, ub_ref):
     core, fast, slow = at_ref[0], at_ref[1], at_ref[2]
-    first = core == 0
-    mine, other = (f_ref, l_ref, r_ref), (fo_ref, lo_ref, ro_ref)
     table = jnp.zeros((8, D), F32)
     ub = jnp.zeros((1, ub_ref.shape[1]), F32)
-    for array, i, dxy, dz in sources(far):
-        chip = ((slow - dz) % far) * 4 + (fast ^ dxy)
-        a, b = mine[array][i], other[array][i]
-        low, high = jnp.where(first, a, b), jnp.where(first, b, a)
+    for i, (dxy, dz) in enumerate(first_sources()):
+        chip = ((slow - dz) % 4) * 4 + (fast ^ dxy)
+        a, b = mine_ref[i], other_ref[i]
+        low, high = jnp.where(core == 0, a, b), jnp.where(core == 0, b, a)
         for m, ref in enumerate((wq_ref, wk_ref, wv_ref)):
             rows = slice(own * m, own * m + own)
             ref[chip] = jnp.concatenate([low[rows], high[rows]], axis=0)
-        for side, part in ((0, low), (1, high)):
-            tail = part[3 * own :].astype(F32)
+        for side, got in ((0, low), (1, high)):
+            tail = got[3 * own :].astype(F32)
             spot = chip * 2 + side
             lane = lax.broadcasted_iota(jnp.int32, (1, D), 1)
             table = table + pltpu.roll(jnp.where(lane < own, tail, 0.0), spot * own, 1)
@@ -260,13 +294,12 @@
 
 
 def assemble(at, mine, other, own, n):
-    far = n // 8
     full = lambda a: pl.BlockSpec(a.shape, lambda i: (0,) * a.ndim)
-    arrays = list(mine) + list(other)
+    arrays = [mine, other]
     w = shaped((n // 2, 2 * own, D), BF16)
     outs = [w, w, w, shaped((8, D), F32), shaped((1, 4 * D), F32)]
     wq, wk, wv, table, ub = call(
-        functools.partial(assemble_body, far, own), (1,),
+        functools.partial(assemble_body, own), (1,),
         [pl.BlockSpec(memory_space=pltpu.SMEM)] + [full(a) for a in arrays],
         [full(a) for a in outs], outs, moved=7 * D * D * 2,
     )(at, *arrays)
@@ -280,46 +313,35 @@
     return total
 
 
-def ffn_raw_body(chunk, own, mix_ref, x_ref, gy_ref, raw_ref, small_ref, ub_ref, *rest):
-    outs, (dg_ref, wo_ref, wu_ref) = rest[:-3], rest[-3:]
+def ffn_parts_body(chunk, own, at_ref, mix_ref, x_ref, gy_ref, *rest):
+    mine, other, (small_ref, ub_ref) = rest[:7], rest[7:14], rest[14:16]
+    outs, (dg_ref, wo_ref, wu_ref, wd_ref) = rest[16:-4], rest[-4:]
     wide = 4 * own
 
     @pl.when(pl.program_id(0) == 0)
     def _():
-        def step(i, _):
-            low, high = raw_ref[2 * i, wide:], raw_ref[2 * i + 1, wide:]
-            at = pl.ds(pl.multiple_of(2 * own * i, 16), 2 * own)
+        core, fast, slow = at_ref[0], at_ref[1], at_ref[2]
+        for part, i, dxy, dz in second_sources():
+            chip = ((slow - dz) % 4) * 4 + (fast ^ dxy)
+            a, b = mine[part][i], other[part][i]
+            low, high = jnp.where(core == 0, a, b), jnp.where(core == 0, b, a)
+            at = pl.ds(pl.multiple_of(2 * wide * chip, 16), wide)
+            wd_ref[at, :] = low[:wide]
+            at = pl.ds(pl.multiple_of(2 * wide * chip + wide, 16), wide)
+            wd_ref[at, :] = high[:wide]
+            at = pl.ds(pl.multiple_of(2 * own * chip, 16), 2 * own)
             for j in range(5):
-                rows = slice(own * j, own * j + own)
+                rows = slice(wide + own * j, wide + own * j + own)
                 both = jnp.concatenate([low[rows], high[rows]], axis=0)
                 if j < 4:
                     wu_ref[at, D * j : D * j + D] = both
                 else:
                     wo_ref[at, :] = both
-            return 0
-
-        lax.fori_loop(0, D // (2 * own), step, 0)
-
-    ffn_steps(chunk, mix_ref, x_ref, gy_ref, wo_ref, wu_ref, RawDown(raw_ref, wide), small_ref, ub_ref, *outs, dg_ref)
-
-
-class RawDown:
-    def __init__(self, ref, wide):
-        self.ref, self.wide = ref, wide
-
-    def rows(self, start, size):
-        return self.ref[start // self.wide : (start + size) // self.wide, : self.wide].reshape(size, D)
-
-
-class FullDown:
-    def __init__(self, ref):
-        self.ref = ref
-
-    def rows(self, start, size):
-        return self.ref[start : start + size, :]
-
-
-def ffn_steps(chunk, mix_ref, x_ref, gy_ref, wo_ref, wu_ref, down, small_ref, ub_ref,
+
+    ffn_steps(chunk, mix_ref, x_ref, gy_ref, wo_ref, wu_ref, wd_ref, small_ref, ub_ref, *outs, dg_ref)
+
+
+def ffn_steps(chunk, mix_ref, x_ref, gy_ref, wo_ref, wu_ref, wd_ref, small_ref, ub_ref,
               out_ref, hid_ref, gffn_ref, low_ref, gpre_ref, gattn_ref, g1_ref, gmix_ref, gsmall_ref, gub_ref, dg_ref):
     i = pl.program_id(0)
     bo, again, ashift, bd, fgain, fshift = (small_ref[j : j + 1, :] for j in range(2, 8))
@@ -343,7 +365,7 @@
         hid = hid.astype(BF16)
         hid_ref[:, cols] = hid
         dg_ref[:, cols] = dg.astype(dg_ref.dtype)
-        ffn = ffn + dot(hid, down.rows(j * chunk, chunk))
+        ffn = ffn + dot(hid, wd_ref[cols, :])
     xhat2, rs2 = normalize(first + ffn + bd)
     out_ref[...] = (xhat2 * fgain + fshift).astype(BF16)
     gy = gy_ref[...].astype(F32)
@@ -356,7 +378,7 @@
     gfirst = g2
     for j in range(ff // chunk):
         cols = slice(j * chunk, (j + 1) * chunk)
-        gh = dot_rt(gffn, down.rows(j * chunk, chunk))
+        gh = dot_rt(gffn, wd_ref[cols, :])
         gpre = (gh * dg_ref[:, cols].astype(F32)).astype(BF16)
         gpre_ref[:, cols] = gpre
         gub_ref[:, cols] += colsum(gpre.astype(F32))
@@ -371,11 +393,11 @@
     gmix_ref[...] = dot_rt(gattn, wo_ref[...]).astype(BF16)
 
 
-def ffn_full_body(chunk, mix_ref, x_ref, gy_ref, wo_ref, wu_ref, wd_ref, small_ref, ub_ref, *rest):
-    ffn_steps(chunk, mix_ref, x_ref, gy_ref, wo_ref, wu_ref, FullDown(wd_ref), small_ref, ub_ref, *rest)
-
-
-def ffn_both(mixed, x, gy, weights, small, ub, own=0, tile_rows=280, chunk=768):
+def ffn_full_body(chunk, *refs):
+    ffn_steps(chunk, *refs)
+
+
+def ffn_both(mixed, x, gy, weights, small, ub, at=None, own=0, tile_rows=280, chunk=768):
     rows = x.shape[0]
     ff = ub.shape[1]
     tile = pl.BlockSpec((tile_rows, D), lambda c: (c, 0))
@@ -384,19 +406,18 @@
     act = shaped((rows, D), BF16)
     big = shaped((rows, ff), BF16)
     scratch = [pltpu.VMEM((tile_rows, ff), F32)]
-    if len(weights) == 1:
-        body = functools.partial(ffn_raw_body, chunk, own)
-        scratch += [pltpu.VMEM((D, D), BF16), pltpu.VMEM((D, ff), BF16)]
-    else:
-        body = functools.partial(ffn_full_body, chunk)
+    body, place_of, specs = functools.partial(ffn_full_body, chunk), [], []
+    if at is not None:
+        body, place_of, specs = functools.partial(ffn_parts_body, chunk, own), [at], [pl.BlockSpec(memory_space=pltpu.SMEM)]
+        scratch += [pltpu.VMEM((D, D), BF16), pltpu.VMEM((D, ff), BF16), pltpu.VMEM((ff, D), BF16)]
     return call(
         body, (rows // tile_rows,),
-        [tile, tile, tile] + [fixed(w) for w in weights] + [fixed(small), fixed(ub)],
+        specs + [tile, tile, tile] + [fixed(w) for w in weights] + [fixed(small), fixed(ub)],
         [tile, wide, tile, tile, wide, tile, tile, tile, pl.BlockSpec((8, D), lambda c: (0, 0)), pl.BlockSpec((1, ff), lambda c: (0, 0))],
         [act, big, act, act, big, act, shaped((rows, D), F32), act, shaped((8, D), F32), shaped((1, ff), F32)],
         scratch=scratch,
         flops=2 * rows * D * (2 * D + 4 * ff), moved=rows * (D * 20 + ff * 4) + D * (D + 2 * ff) * 2,
-    )(mixed, x, gy, *weights, small, ub)
+    )(*place_of, mixed, x, gy, *weights, small, ub)
 
 
 def row_block(at_ref, far, own, dxy, dz):
@@ -590,10 +611,6 @@
     return jnp.where(inside.reshape(rows, 1), cotangent, jnp.zeros_like(cotangent))
 
 
-def tie(*values):
-    return lax.optimization_barrier(values)
-
-
 def chunked(weight):
     own = weight.shape[0]
     return weight.reshape(own, -1, D).swapaxes(0, 1).reshape(-1, D)
@@ -609,18 +626,25 @@
     vectors = (query_bias, value_bias, out_bias, attn_gain, attn_shift, down_bias, ffn_gain, ffn_shift)
     at = jnp.stack(place()).astype(jnp.int32)
     block = jnp.concatenate([query_weight, key_weight, value_weight, pack_small(vectors, up_bias)], axis=0)
-    sent = jnp.concatenate([down_weight, chunked(up_weight), out_weight], axis=0)
-    sent = jnp.pad(sent, ((0, -sent.shape[0] % 16), (0, 0)))
-    raw = lax.all_gather(sent, "fsdp", axis=0, tiled=False)
-    mine, other = gather_blocks(block, n)
-    wq, wk, wv, table, ub = assemble(at, mine, other, own, n)
-    gy = residue_mask(cotangent, span_start, span_end)
-
-    q, k, v, mixed, lse = attn_fwd(tokens, wq, wk, wv, table[0:1], table[1:2], lengths)
+    second = jnp.concatenate([down_weight, chunked(up_weight), out_weight], axis=0)
+    chains = lengths.shape[0]
+    ahead = chains * 3 // 7
+
+    def attend(w, start, stop, before=()):
+        return w, attn_fwd(tokens, *w[:4], lengths, start, stop, before)
+
+    gy, ((wq, wk, wv, table, ub), (q, k, v, mixed, lse)), mine, other = gather_all(
+        block, second, n,
+        (lambda given: residue_mask(*given), (cotangent, span_start, span_end)),
+        (
+            lambda mine, other: assemble(at, mine, other, own, n),
+            lambda w: attend(w, 0, ahead),
+            lambda held: attend(held[0], ahead, chains, held[1]),
+        ),
+    )
     layer_out, hidden, gffn, low, gpre, gattn, g1, gmixed, gtable, gub = ffn_both(
-        mixed, tokens, gy, (raw,), table, ub, own
-    )
-    chains = lengths.shape[0]
+        mixed, tokens, gy, mine + other, table, ub, at, own
+    )
     cuts = (0, 1, 4, chains)
     keep_d, send_d = wgrad_down(at, hidden, gffn, n)
     gmixed, keep_d, send_d = tie(gmixed, keep_d, send_d)
@@ -696,7 +720,7 @@
     ub = small[:, 8 * own : 8 * own + wide].reshape(1, ff)
     gy = residue_mask(cotangent, span_start, span_end)
 
-    q, k, v, mixed, lse = attn_fwd(tokens, wq, wk, wv, table[0:1], table[1:2], lengths)
+    q, k, v, mixed, lse = attn_fwd(tokens, wq, wk, wv, table, lengths)
     layer_out, hidden, gffn, low, gpre, gattn, g1, gmixed, gtable, gub = ffn_both(
         mixed, tokens, gy, (wo, wu, wd), table, ub
     )

time: 309 us -> 299 us (0.968)
  between operations: 15.1 us -> 1.6 us
  waiting for transfers between devices: 59.3 us -> 48 us
  starting transfers between devices: 53.2 us -> 57.3 us
  local copies, waits for them, and re-layouts: 9.35 us -> 12.9 us
    ppermute x35 -> x48, waiting for transfers between devices: 55.2 us -> 48 us  [hop(): return lax.ppermute(value, 'fsdp', pairs)]
    ppermute x35 -> x48, starting transfers between devices: 53.2 us -> 57.3 us  [hop(): return lax.ppermute(value, 'fsdp', pairs)]
    all_gather x1 -> x0, waiting for transfers between devices: 4.09 us -> none  [fast_shards(): raw = lax.all_gather(sent, 'fsdp', axis=0, tiled=False)]
    unnamed x84 -> x89, local copies, waits for them, and re-layouts: 4.31 us -> 8.32 us
    pallas_call x3 -> x4, Pallas kernels: 63.2 us -> 66.1 us  [the longest x1 41.2 us: ffn_both(): call(body, (rows // tile_rows,), specs + [tile, tile, tile] + [fixed(w) f...]
  transfers between devices with their start and end apart: 36 -> 48, of which waited for: 13 -> 17; matrix products, arithmetic and copies ran while one was open for 3% -> 4% of each run, Pallas kernels for 31% -> 34%
where the time goes in v3:
time: 299 us; the launch traced here: 294 us
  Pallas kernels  155 us (52%)
  starting transfers between devices  57.3 us (19%)
  waiting for transfers between devices  48 us (16%)
  other arithmetic  19.2 us (6%)
  local copies, waits for them, and re-layouts  12.9 us (4%)
    ppermute x48, starting transfers between devices, hop(): return lax.ppermute(value, 'fsdp', pairs)  57.3 us
    ppermute x48, waiting for transfers between devices, hop(): return lax.ppermute(value, 'fsdp', pairs)  48 us
    pallas_call x1, Pallas kernels, ffn_both(): call(body, (rows // tile_rows,), specs + [tile, tile, tile] + [fixed(w) f...  41.2 us
    pallas_call x3, Pallas kernels, attn_bwd(): call(functools.partial(attn_bwd_body, start), (stop - start,), [pl.BlockS...  30.5 us
    pallas_call x2, Pallas kernels, attn_fwd(): call(functools.partial(attn_fwd_body, start), (stop - start,), [pl.BlockS...  20 us
    pallas_call x1, Pallas kernels, wgrad_up(): call(functools.partial(wgrad_up_body, far, own), (5,), [pl.BlockSpec(memo...  15.2 us
    pallas_call x2, Pallas kernels, input_grad(): call(input_grad_body, (stop - start,), [tile, tile, tile, tile, full, ful...  12.4 us
    pallas_call x1, Pallas kernels, wgrad_down(): call(functools.partial(wgrad_down_body, far, own), (far,), [pl.BlockSpec(...  11.8 us
  transfers between devices with their start and end apart: 48, of which 17 were waited for; matrix products, arithmetic and copies ran while one was open for 4% of the time, Pallas kernels for 34%

profile of v3, /device:TPU:0, one launch (start us, length us, event | category | flops | bytes accessed | tf_op | source)
XLA Modules:
  0.0 293.6 jit_solution(9104342261759942070)
XLA Ops:
  2.5 3.0 %collective-permute-start.4 = (bf16[216,768]{1,0:T(8,128)(2,1)S(1)}, bf16[216,768]{1,0:T(8,128)(2,1)S(1)}, u32[]{:S(2)}, u32[]{:S(2)}) collective-permute-start(bf16[216,768]{1,0:T(8,128)(2,1)S(1)} %pad_maximum_fusion.3), channel_id=1, source_target_pairs={{0,4},{1,5},{2,6},{3,7},{4,0},{5,1},{6,2},{7,3},{8,12},{9,13},{10,... | collective-permute-start | bytes 995336 | tf_op jit(solution)/shard_map/ppermute | solution.py:217
  5.6 1.5 collective-permute-start.3
  8.7 2.7 collective-permute-start.1
  11.3 1.6 collective-permute-start
  12.9 2.2 collective-permute-start.2
  15.2 5.4 %collective-permute-done.1 = bf16[80,768]{1,0:T(8,128)(2,1)S(1)} collective-permute-done((bf16[80,768]{1,0:T(8,128)(2,1)S(1)}, bf16[80,768]{1,0:T(8,128)(2,1)S(1)}, u32[]{:S(2)}, u32[]{:S(2)}) %collective-permute-start.1) | collective-permute-done | bytes 122912 | tf_op jit(solution)/shard_map/ppermute | solution.py:217
  21.3 1.6 collective-permute-start.6
  22.9 1.5 collective-permute-start.5
  24.4 2.7 collective-permute-start.9
  27.1 7.5 %collective-permute-done.9 = bf16[216,768]{1,0:T(8,128)(2,1)S(1)} collective-permute-done((bf16[216,768]{1,0:T(8,128)(2,1)S(1)}, bf16[216,768]{1,0:T(8,128)(2,1)S(1)}, u32[]{:S(2)}, u32[]{:S(2)}) %collective-permute-start.9) | collective-permute-done | bytes 331808 | tf_op jit(solution)/shard_map/ppermute | solution.py:217
  34.7 8.6 %collective-permute-done.8 = bf16[216,768]{1,0:T(8,128)(2,1)S(1)} collective-permute-done((bf16[216,768]{1,0:T(8,128)(2,1)S(1)}, bf16[216,768]{1,0:T(8,128)(2,1)S(1)}, u32[]{:S(2)}, u32[]{:S(2)}) %collective-permute-start.8) | collective-permute-done | bytes 331808 | tf_op jit(solution)/shard_map/ppermute | solution.py:217
  49.7 4.9 %collective-permute-start.12 = (bf16[216,768]{1,0:T(8,128)(2,1)S(1)}, bf16[216,768]{1,0:T(8,128)(2,1)}, u32[]{:S(2)}, u32[]{:S(2)}) collective-permute-start(bf16[216,768]{1,0:T(8,128)(2,1)S(1)} %pad_maximum_fusion.3), channel_id=1, source_target_pairs={{0,16},{1,17},{2,18},{3,19},{4,20},{5,21},{6,22},{7,23},{8,24},{9,... | collective-permute-start | bytes 995336 | tf_op jit(solution)/shard_map/ppermute | solution.py:217
  56.8 1.5 collective-permute-start.14
  59.4 2.9 broadcast_select_fusion.gy_ref
  62.3 4.9 %shard_map.323 = (bf16[16,48,768]{2,1,0:T(8,128)(2,1)}, bf16[16,48,768]{2,1,0:T(8,128)(2,1)}, bf16[16,48,768]{2,1,0:T(8,128)(2,1)}, f32[8,768]{1,0:T(8,128)}, f32[1,3072]{1,0:T(1,128)}) custom-call(s32[3]{0:T(128)} %pad_add_fusion.1.at_ref, bf16[16,80,768]{2,1,0:T(8,128)(2,1)} %copy-done.1, bf16[16,80,768]{2,1,0:T(8,128)(2,1)} %copy-done.3), custom_call_target="tpu_custom_call" | custom-call | tf_op jit(solution)/shard_map/pallas_call | solution.py:301
  67.2 9.0 %shard_map.324 = (bf16[1120,768]{1,0:T(8,128)(2,1)}, bf16[1120,768]{1,0:T(8,128)(2,1)}, bf16[1120,768]{1,0:T(8,128)(2,1)}, bf16[1120,768]{1,0:T(8,128)(2,1)}, f32[1120,128]{1,0:T(8,128)}) custom-call(s32[7]{0:T(128)} %len_ref.9, bf16[1120,768]{1,0:T(8,128)(2,1)} %x_ref.7, bf16[768,768]{1,0:T(8,128)(2,1)} %bitcast.89, bf16[768,768]{1,0:T(8,128)(2,1)} %bitcast.93, ...), custom_call_target="tpu_custom_call" | custom-call | tf_op jit(solution)/shard_map/pallas_call | solution.py:92
  76.2 3.2 %collective-permute-done.14 = bf16[2,216,768]{2,1,0:T(8,128)(2,1)S(1)} collective-permute-done((bf16[2,216,768]{2,1,0:T(8,128)(2,1)}, bf16[2,216,768]{2,1,0:T(8,128)(2,1)S(1)}, u32[]{:S(2)}, u32[]{:S(2)}) %collective-permute-start.14) | collective-permute-done | bytes 663584 | tf_op jit(solution)/shard_map/ppermute | solution.py:217
  81.3 1.7 collective-permute-start.20
  84.3 1.4 collective-permute-start.18
  86.5 11.0 %shard_map.325 = (bf16[1120,768]{1,0:T(8,128)(2,1)}, bf16[1120,768]{1,0:T(8,128)(2,1)}, bf16[1120,768]{1,0:T(8,128)(2,1)}, bf16[1120,768]{1,0:T(8,128)(2,1)}, f32[1120,128]{1,0:T(8,128)}) custom-call(s32[7]{0:T(128)} %len_ref.9, bf16[1120,768]{1,0:T(8,128)(2,1)} %x_ref.7, ...), custom_call_target="tpu_custom_call", output_to_operand_aliasing={{0}: (6, {}), {1}: (7, {}), {2}: (8, {}), {3}: (9, {}), {4}... | custom-call | tf_op jit(solution)/shard_map/pallas_call | solution.py:92
  98.4 2.5 collective-permute-done.18
  105.7 41.2 %shard_map.326 = (bf16[1120,768]{1,0:T(8,128)(2,1)}, bf16[1120,3072]{1,0:T(8,128)(2,1)}, bf16[1120,768]{1,0:T(8,128)(2,1)}, bf16[1120,768]{1,0:T(8,128)(2,1)}, b...) custom-call(s32[3]{0:T(128)} %pad_add_fusion.1.at_ref, ...), custom_call_target="tpu_custom_call" | custom-call | tf_op jit(solution)/shard_map/pallas_call | solution.py:413
  146.9 11.8 %shard_map.327 = (bf16[4,4,96,768]{3,2,1,0:T(8,128)(2,1)}, bf16[4,4,96,768]{3,2,1,0:T(8,128)(2,1)}) custom-call(s32[3]{0:T(128)} %pad_add_fusion.1.at_ref, bf16[1120,3072]{1,0:T(8,128)(2,1)} %get-tuple-element.278.hid_ref, bf16[1120,768]{1,0:T(8,128)(2,1)} %get-tuple-element.279.gffn_ref), custom_call_target="tpu_custom_call" | custom-call | tf_op jit(solution)/shard_map/pallas_call | solution.py:454
  158.8 5.6 %shard_map.328 = (bf16[1120,768]{1,0:T(8,128)(2,1)}, bf16[1120,768]{1,0:T(8,128)(2,1)}, bf16[1120,768]{1,0:T(8,128)(2,1)}, f32[1,768]{1,0:T(1,128)}, f32[1,768]{1,0:T(1,128)}) custom-call(s32[7]{0:T(128)} %len_ref.9, bf16[1120,768]{1,0:T(8,128)(2,1)} %get-tuple-element.274.q_ref, bf16[1120,768]{1,0:T(8,128)(2,1)} %get-tuple-element.275.k_ref, ...), custom_call_target="tpu_custom_call" | custom-call | flops 1099511627776 | bytes 17179869184 | tf_op jit(solution)/shard_map/pallas_call | solution.py:150
  164.4 1.9 fusion.5
  168.2 1.7 collective-permute-start.30
  169.9 15.2 %shard_map.329 = (bf16[4,4,120,768]{3,2,1,0:T(8,128)(2,1)}, bf16[4,4,120,768]{3,2,1,0:T(8,128)(2,1)}) custom-call(s32[3]{0:T(128)} %pad_add_fusion.1.at_ref, bf16[1120,768]{1,0:T(8,128)(2,1)} %get-tuple-element.303.low_ref, bf16[1120,3072]{1,0:T(8,128)(2,1)} %get-tuple-element.304.gpre_ref, bf16[1120,768]{1,0:T(8,128)(2,1)} %get-tuple-element.261.mix_ref, ...), custom_call_target="tpu_custom_call" | custom-call | tf_op jit(solution)/shard_map/pallas_call | solution.py:485
  185.0 12.3 %shard_map.330 = (bf16[1120,768]{1,0:T(8,128)(2,1)}, bf16[1120,768]{1,0:T(8,128)(2,1)}, bf16[1120,768]{1,0:T(8,128)(2,1)}, f32[1,768]{1,0:T(1,128)}, f32[1,768]{1,0:T(1,128)}) custom-call(s32[7]{0:T(128)} %len_ref.9, bf16[1120,768]{1,0:T(8,128)(2,1)} %get-tuple-element.274.q_ref, ...), custom_call_target="tpu_custom_call", output_to_operand_aliasing={{0}: (6, {}), {1}: (7, {}), {2}: (8, {})} | custom-call | tf_op jit(solution)/shard_map/pallas_call | solution.py:150
  198.6 2.9 %shard_map.331 = (f32[96,768]{1,0:T(8,128)}, bf16[96,768]{1,0:T(8,128)(2,1)}, bf16[96,768]{1,0:T(8,128)(2,1)}, bf16[96,768]{1,0:T(8,128)(2,1)}) custom-call(bf16[4,4,96,768]{3,2,1,0:T(8,128)(2,1)} %get-tuple-element.296.keep_ref, bf16[4,4,96,768]{3,2,1,0:T(8,128)(2,1)} %collective-permute-done.27.other_ref, bf16[1,4,96,768]{3,2,1,0:T(8,128)(2,1)} %bitcast.120, ...), custom_call_target="tpu_custom_call" | custom-call | flops 1099511627776 | bytes 17179869184 | tf_op jit(solution)/shard_map/pallas_call | solution.py:551
  201.5 3.2 %fusion.2 = (bf16[4,120,768]{2,1,0:T(8,128)(2,1)S(1)}, bf16[4,120,768]{2,1,0:T(8,128)(2,1)}, bf16[4,120,768]{2,1,0:T(8,128)(2,1)}) fusion(bf16[4,4,120,768]{3,2,1,0:T(8,128)(2,1)} %collective-permute-done.31.other_ref, bf16[4,4,120,768]{3,2,1,0:T(8,128)(2,1)S(1)} %copy-done.4), kind=kLoop, calls=%fused_computation.13 | loop fusion | flops 4423680 | bytes 6635520 | tf_op jit(solution)/shard_map/convert_element_type | solution.py:531
  206.6 1.7 collective-permute-start.36
  208.6 3.5 %collective-permute-start.33 = (bf16[96,768]{1,0:T(8,128)(2,1)S(1)}, bf16[96,768]{1,0:T(8,128)(2,1)S(1)}, u32[]{:S(2)}, u32[]{:S(2)}) collective-permute-start(bf16[96,768]{1,0:T(8,128)(2,1)S(1)} %copy-done.39), channel_id=1, source_target_pairs={{0,24},{1,25},{2,26},{3,27},{4,28},{5,29},{6,30},{7,31},{8,0},{9,1... | collective-permute-start | bytes 442376 | tf_op jit(solution)/shard_map/ppermute | solution.py:217
  212.1 12.5 %shard_map.332 = (bf16[1120,768]{1,0:T(8,128)(2,1)}, bf16[1120,768]{1,0:T(8,128)(2,1)}, bf16[1120,768]{1,0:T(8,128)(2,1)}, f32[1,768]{1,0:T(1,128)}, f32[1,768]{1,0:T(1,128)}) custom-call(s32[7]{0:T(128)} %len_ref.9, bf16[1120,768]{1,0:T(8,128)(2,1)} %get-tuple-element.274.q_ref, ...), custom_call_target="tpu_custom_call", output_to_operand_aliasing={{0}: (6, {}), {1}: (7, {}), {2}: (8, {})} | custom-call | tf_op jit(solution)/shard_map/pallas_call | solution.py:150
  224.8 1.3 pad_maximum_fusion.6.small_ref
  226.1 9.9 %shard_map.333 = (bf16[4,4,80,768]{3,2,1,0:T(8,128)(2,1)}, bf16[4,4,80,768]{3,2,1,0:T(8,128)(2,1)}) custom-call(s32[3]{0:T(128)} %pad_add_fusion.1.at_ref, bf16[1120,768]{1,0:T(8,128)(2,1)} %x_ref.7, bf16[1120,768]{1,0:T(8,128)(2,1)} %get-tuple-element.345.gq_ref, bf16[1120,768]{1,0:T(8,128)(2,1)} %get-tuple-element.346.gk_ref, ...), custom_call_target="tpu_custom_call" | custom-call | tf_op jit(solution)/shard_map/pallas_call | solution.py:518
  236.1 6.3 %shard_map.334.rest_0_ = bf16[1120,768]{1,0:T(8,128)(2,1)} custom-call(f32[1120,768]{1,0:T(8,128)} %get-tuple-element.354.g1_ref, bf16[1120,768]{1,0:T(8,128)(2,1)} %get-tuple-element.345.gq_ref, bf16[1120,768]{1,0:T(8,128)(2,1)} %get-tuple-element.346.gk_ref, bf16[1120,768]{1,0:T(8,128)(2,1)} %get-tuple-element.347.gv_ref, bf16[768,768]{1,0:T(8,128)(2,1)} %bitcast.91, ...), custom_call_target="tpu_custom_call" | custom-call | tf_op jit(solution)/shard_map/pallas_call | solution.py:595
  243.8 3.3 %shard_map.335 = (f32[120,768]{1,0:T(8,128)}, bf16[120,768]{1,0:T(8,128)(2,1)}, bf16[120,768]{1,0:T(8,128)(2,1)}, bf16[120,768]{1,0:T(8,128)(2,1)}) custom-call(bf16[4,4,120,768]{3,2,1,0:T(8,128)(2,1)} %get-tuple-element.326.keep_ref, bf16[4,4,120,768]{3,2,1,0:T(8,128)(2,1)} %collective-permute-done.31.other_ref, bf16[1,4,120,768]{3,2,1,0:T(8,128)(2,1)} %bitcast.117, ...), custom_call_target="tpu_custom_call" | custom-call | flops 1099511627776 | bytes 17179869184 | tf_op jit(solution)/shard_map/pallas_call | solution.py:551
  247.1 1.8 fusion.8
  250.8 1.7 collective-permute-start.41
  253.4 1.9 collective-permute-start.43
  255.4 6.5 %collective-permute-done.42 = bf16[120,768]{1,0:T(8,128)(2,1)S(1)} collective-permute-done((bf16[120,768]{1,0:T(8,128)(2,1)S(1)}, bf16[120,768]{1,0:T(8,128)(2,1)S(1)}, u32[]{:S(2)}, u32[]{:S(2)}) %collective-permute-start.42) | collective-permute-done | bytes 184352 | tf_op jit(solution)/shard_map/ppermute | solution.py:217
  262.7 6.1 %shard_map.336 = bf16[1120,768]{1,0:T(8,128)(2,1)} custom-call(f32[1120,768]{1,0:T(8,128)} %get-tuple-element.354.g1_ref, bf16[1120,768]{1,0:T(8,128)(2,1)} %get-tuple-element.345.gq_ref, bf16[1120,768]{1,0:T(8,128)(2,1)} %get-tuple-element.346.gk_ref, bf16[1120,768]{1,0:T(8,128)(2,1)} %get-tuple-element.347.gv_ref, ...), custom_call_target="tpu_custom_call", output_to_operand_aliasing={{}: (7, {})} | custom-call | tf_op jit(solution)/shard_map/pallas_call | solution.py:595
  268.8 5.3 %collective-permute-done.40 = bf16[4,80,768]{2,1,0:T(8,128)(2,1)S(1)} collective-permute-done((bf16[4,80,768]{2,1,0:T(8,128)(2,1)S(1)}, bf16[4,80,768]{2,1,0:T(8,128)(2,1)S(1)}, u32[]{:S(2)}, u32[]{:S(2)}) %collective-permute-start.40) | collective-permute-done | bytes 491552 | tf_op jit(solution)/shard_map/ppermute | solution.py:217
  275.2 2.6 shard_map.337
  277.8 1.9 collective-permute-start.44
  279.7 3.9 %collective-permute-start.45 = (bf16[80,768]{1,0:T(8,128)(2,1)}, bf16[80,768]{1,0:T(8,128)(2,1)S(1)}, u32[]{:S(2)}, u32[]{:S(2)}) collective-permute-start(bf16[80,768]{1,0:T(8,128)(2,1)} %get-tuple-element.387), channel_id=1, source_target_pairs={{0,16},{1,17},{2,18},{3,19},{4,20},{5,21},{6,22},{7,23},{8,24},{9,... | collective-permute-start | bytes 368648 | tf_op jit(solution)/shard_map/ppermute | solution.py:217
  285.3 2.1 collective-permute-done.44
  287.4 3.0 %collective-permute-done.45 = bf16[80,768]{1,0:T(8,128)(2,1)S(1)} collective-permute-done((bf16[80,768]{1,0:T(8,128)(2,1)}, bf16[80,768]{1,0:T(8,128)(2,1)S(1)}, u32[]{:S(2)}, u32[]{:S(2)}) %collective-permute-start.45) | collective-permute-done | bytes 122912 | tf_op jit(solution)/shard_map/ppermute | solution.py:217
  (180 shorter events, 39.6 us)
Async XLA Ops:
  2.5 18.3 %collective-permute-start.4 = (bf16[216,768]{1,0:T(8,128)(2,1)S(1)}, bf16[216,768]{1,0:T(8,128)(2,1)S(1)}, u32[]{:S(2)}, u32[]{:S(2)}) collective-permute-start(bf16[216,768]{1,0:T(8,128)(2,1)S(1)} %pad_maximum_fusion.3), channel_id=1, source_target_pairs={{0,4},{1,5},{2,6},{3,7},{4,0},{5,1},{6,2},{7,3},{8,12},{9,13},{10,... | collective-permute-start | bytes 995336 | tf_op jit(solution)/shard_map/ppermute | solution.py:217
  5.6 15.3 %collective-permute-start.3 = (bf16[216,768]{1,0:T(8,128)(2,1)S(1)}, bf16[216,768]{1,0:T(8,128)(2,1)S(1)}, u32[]{:S(2)}, u32[]{:S(2)}) collective-permute-start(bf16[216,768]{1,0:T(8,128)(2,1)S(1)} %pad_maximum_fusion.3), channel_id=1, source_target_pairs={{0,2},{1,3},{2,0},{3,1},{4,6},{5,7},{6,4},{7,5},{8,10},{9,11},{10,... | collective-permute-start | bytes 995336 | tf_op jit(solution)/shard_map/ppermute | solution.py:217
  8.7 11.9 %collective-permute-start.1 = (bf16[80,768]{1,0:T(8,128)(2,1)S(1)}, bf16[80,768]{1,0:T(8,128)(2,1)S(1)}, u32[]{:S(2)}, u32[]{:S(2)}) collective-permute-start(bf16[80,768]{1,0:T(8,128)(2,1)S(1)} %get-tuple-element.423), channel_id=1, source_target_pairs={{0,16},{1,17},{2,18},{3,19},{4,20},{5,21},{6,22},{7,23},{8,24},{9,... | collective-permute-start | bytes 368648 | tf_op jit(solution)/shard_map/ppermute | solution.py:217
  11.3 9.3 %collective-permute-start = (bf16[80,768]{1,0:T(8,128)(2,1)S(1)}, bf16[80,768]{1,0:T(8,128)(2,1)S(1)}, u32[]{:S(2)}, u32[]{:S(2)}) collective-permute-start(bf16[80,768]{1,0:T(8,128)(2,1)S(1)} %get-tuple-element.423), channel_id=1, source_target_pairs={{0,8},{1,9},{2,10},{3,11},{4,12},{5,13},{6,14},{7,15},{8,16},{9,17... | collective-permute-start | bytes 368648 | tf_op jit(solution)/shard_map/ppermute | solution.py:217
  12.9 7.8 %collective-permute-start.2 = (bf16[80,768]{1,0:T(8,128)(2,1)S(1)}, bf16[80,768]{1,0:T(8,128)(2,1)S(1)}, u32[]{:S(2)}, u32[]{:S(2)}) collective-permute-start(bf16[80,768]{1,0:T(8,128)(2,1)S(1)} %get-tuple-element.423), channel_id=1, source_target_pairs={{0,24},{1,25},{2,26},{3,27},{4,28},{5,29},{6,30},{7,31},{8,0},{9,1... | collective-permute-start | bytes 368648 | tf_op jit(solution)/shard_map/ppermute | solution.py:217
  20.8 22.5 %collective-permute-start.7 = (bf16[4,80,768]{2,1,0:T(8,128)(2,1)S(1)}, bf16[4,80,768]{2,1,0:T(8,128)(2,1)S(1)}, u32[]{:S(2)}, u32[]{:S(2)}) collective-permute-start(bf16[4,80,768]{2,1,0:T(8,128)(2,1)S(1)} %pad_maximum_fusion.2), channel_id=1, source_target_pairs={{0,6},{1,7},{2,4},{3,5},{4,2},{5,3},{6,0},{7,1},{8,14},{9,15},{10,... | collective-permute-start | bytes 1474568 | tf_op jit(solution)/shard_map/ppermute | solution.py:217
  21.3 22.0 %collective-permute-start.6 = (bf16[4,80,768]{2,1,0:T(8,128)(2,1)S(1)}, bf16[4,80,768]{2,1,0:T(8,128)(2,1)S(1)}, u32[]{:S(2)}, u32[]{:S(2)}) collective-permute-start(bf16[4,80,768]{2,1,0:T(8,128)(2,1)S(1)} %pad_maximum_fusion.2), channel_id=1, source_target_pairs={{0,4},{1,5},{2,6},{3,7},{4,0},{5,1},{6,2},{7,3},{8,12},{9,13},{10,... | collective-permute-start | bytes 1474568 | tf_op jit(solution)/shard_map/ppermute | solution.py:217
  22.9 20.4 %collective-permute-start.5 = (bf16[4,80,768]{2,1,0:T(8,128)(2,1)S(1)}, bf16[4,80,768]{2,1,0:T(8,128)(2,1)S(1)}, u32[]{:S(2)}, u32[]{:S(2)}) collective-permute-start(bf16[4,80,768]{2,1,0:T(8,128)(2,1)S(1)} %pad_maximum_fusion.2), channel_id=1, source_target_pairs={{0,2},{1,3},{2,0},{3,1},{4,6},{5,7},{6,4},{7,5},{8,10},{9,11},{10,... | collective-permute-start | bytes 1474568 | tf_op jit(solution)/shard_map/ppermute | solution.py:217
  24.4 10.3 %collective-permute-start.9 = (bf16[216,768]{1,0:T(8,128)(2,1)S(1)}, bf16[216,768]{1,0:T(8,128)(2,1)S(1)}, u32[]{:S(2)}, u32[]{:S(2)}) collective-permute-start(bf16[216,768]{1,0:T(8,128)(2,1)S(1)} %pad_maximum_fusion.3), channel_id=1, source_target_pairs={{0,24},{1,25},{2,26},{3,27},{4,28},{5,29},{6,30},{7,31},{8,0},{9,1... | collective-permute-start | bytes 995336 | tf_op jit(solution)/shard_map/ppermute | solution.py:217
  27.1 16.2 %collective-permute-start.8 = (bf16[216,768]{1,0:T(8,128)(2,1)S(1)}, bf16[216,768]{1,0:T(8,128)(2,1)S(1)}, u32[]{:S(2)}, u32[]{:S(2)}) collective-permute-start(bf16[216,768]{1,0:T(8,128)(2,1)S(1)} %pad_maximum_fusion.3), channel_id=1, source_target_pairs={{0,8},{1,9},{2,10},{3,11},{4,12},{5,13},{6,14},{7,15},{8,16},{9,17... | collective-permute-start | bytes 995336 | tf_op jit(solution)/shard_map/ppermute | solution.py:217
  43.4 4.0 %collective-permute-start.10 = (bf16[16,80,768]{2,1,0:T(8,128)(2,1)S(1)}, bf16[16,80,768]{2,1,0:T(8,128)(2,1)S(1)}, u32[]{:S(2)}, u32[]{:S(2)}) collective-permute-start(bf16[16,80,768]{2,1,0:T(8,128)(2,1)S(1)} %constant_dynamic-update-slice_fusion.mine_ref), channel_id=1, source_target_pairs={{0,1},{1,0},{2,3},{3,2},{4,5},{5,4},{6,7},{7,6},{8,9},{9,8},{10,11... | collective-permute-start | bytes 5898248 | tf_op jit(solution)/shard_map/ppermute | solution.py:217
  48.8 30.6 %collective-permute-start.15 = (bf16[5,216,768]{2,1,0:T(8,128)(2,1)}, bf16[5,216,768]{2,1,0:T(8,128)(2,1)}, u32[]{:S(2)}, u32[]{:S(2)}) collective-permute-start(bf16[5,216,768]{2,1,0:T(8,128)(2,1)} %constant_dynamic-update-slice_fusion.4.rest_0_), channel_id=1, source_target_pairs={{0,1},{1,0},{2,3},{3,2},{4,5},{5,4},{6,7},{7,6},{8,9},{9,8},{10,11... | collective-permute-start | bytes 4976648 | tf_op jit(solution)/shard_map/ppermute | solution.py:217
  49.7 26.4 %collective-permute-start.12 = (bf16[216,768]{1,0:T(8,128)(2,1)S(1)}, bf16[216,768]{1,0:T(8,128)(2,1)}, u32[]{:S(2)}, u32[]{:S(2)}) collective-permute-start(bf16[216,768]{1,0:T(8,128)(2,1)S(1)} %pad_maximum_fusion.3), channel_id=1, source_target_pairs={{0,16},{1,17},{2,18},{3,19},{4,20},{5,21},{6,22},{7,23},{8,24},{9,... | collective-permute-start | bytes 995336 | tf_op jit(solution)/shard_map/ppermute | solution.py:217
  54.7 21.5 %collective-permute-start.11 = (bf16[216,768]{1,0:T(8,128)(2,1)S(1)}, bf16[216,768]{1,0:T(8,128)(2,1)}, u32[]{:S(2)}, u32[]{:S(2)}) collective-permute-start(bf16[216,768]{1,0:T(8,128)(2,1)S(1)} %pad_maximum_fusion.3), channel_id=1, source_target_pairs={{0,6},{1,7},{2,4},{3,5},{4,2},{5,3},{6,0},{7,1},{8,14},{9,15},{10,... | collective-permute-start | bytes 995336 | tf_op jit(solution)/shard_map/ppermute | solution.py:217
  56.8 22.5 %collective-permute-start.14 = (bf16[2,216,768]{2,1,0:T(8,128)(2,1)}, bf16[2,216,768]{2,1,0:T(8,128)(2,1)S(1)}, u32[]{:S(2)}, u32[]{:S(2)}) collective-permute-start(bf16[2,216,768]{2,1,0:T(8,128)(2,1)} %pad_maximum_fusion.1), channel_id=1, source_target_pairs={{0,4},{1,5},{2,6},{3,7},{4,0},{5,1},{6,2},{7,3},{8,12},{9,13},{10,... | collective-permute-start | bytes 1990664 | tf_op jit(solution)/shard_map/ppermute | solution.py:217
  58.3 21.1 %collective-permute-start.13 = (bf16[2,216,768]{2,1,0:T(8,128)(2,1)}, bf16[2,216,768]{2,1,0:T(8,128)(2,1)S(1)}, u32[]{:S(2)}, u32[]{:S(2)}) collective-permute-start(bf16[2,216,768]{2,1,0:T(8,128)(2,1)} %pad_maximum_fusion.1), channel_id=1, source_target_pairs={{0,2},{1,3},{2,0},{3,1},{4,6},{5,7},{6,4},{7,5},{8,10},{9,11},{10,... | collective-permute-start | bytes 1990664 | tf_op jit(solution)/shard_map/ppermute | solution.py:217
  80.7 5.0 %collective-permute-start.16 = (bf16[6,216,768]{2,1,0:T(8,128)(2,1)S(1)}, bf16[6,216,768]{2,1,0:T(8,128)(2,1)S(1)}, u32[]{:S(2)}, u32[]{:S(2)}) collective-permute-start(bf16[6,216,768]{2,1,0:T(8,128)(2,1)S(1)} %pad_maximum_fusion.rest_1_), channel_id=1, source_target_pairs={{0,1},{1,0},{2,3},{3,2},{4,5},{5,4},{6,7},{7,6},{8,9},{9,8},{10,11... | collective-permute-start | bytes 5971976 | tf_op jit(solution)/shard_map/ppermute | solution.py:217
  80.8 17.6 %collective-permute-start.21 = (bf16[216,768]{1,0:T(8,128)(2,1)}, bf16[216,768]{1,0:T(8,128)(2,1)}, u32[]{:S(2)}, u32[]{:S(2)}) collective-permute-start(bf16[216,768]{1,0:T(8,128)(2,1)} %collective-permute-done.11), channel_id=1, source_target_pairs={{0,24},{1,25},{2,26},{3,27},{4,28},{5,29},{6,30},{7,31},{8,0},{9,1... | collective-permute-start | bytes 995336 | tf_op jit(solution)/shard_map/ppermute | solution.py:217
  81.3 17.1 %collective-permute-start.20 = (bf16[216,768]{1,0:T(8,128)(2,1)}, bf16[216,768]{1,0:T(8,128)(2,1)}, u32[]{:S(2)}, u32[]{:S(2)}) collective-permute-start(bf16[216,768]{1,0:T(8,128)(2,1)} %collective-permute-done.11), channel_id=1, source_target_pairs={{0,8},{1,9},{2,10},{3,11},{4,12},{5,13},{6,14},{7,15},{8,16},{9,17... | collective-permute-start | bytes 995336 | tf_op jit(solution)/shard_map/ppermute | solution.py:217
  83.0 15.4 %collective-permute-start.19 = (bf16[216,768]{1,0:T(8,128)(2,1)}, bf16[216,768]{1,0:T(8,128)(2,1)}, u32[]{:S(2)}, u32[]{:S(2)}) collective-permute-start(bf16[216,768]{1,0:T(8,128)(2,1)} %collective-permute-done.12), channel_id=1, source_target_pairs={{0,6},{1,7},{2,4},{3,5},{4,2},{5,3},{6,0},{7,1},{8,14},{9,15},{10,... | collective-permute-start | bytes 995336 | tf_op jit(solution)/shard_map/ppermute | solution.py:217
  84.3 16.6 %collective-permute-start.18 = (bf16[216,768]{1,0:T(8,128)(2,1)}, bf16[216,768]{1,0:T(8,128)(2,1)}, u32[]{:S(2)}, u32[]{:S(2)}) collective-permute-start(bf16[216,768]{1,0:T(8,128)(2,1)} %collective-permute-done.12), channel_id=1, source_target_pairs={{0,4},{1,5},{2,6},{3,7},{4,0},{5,1},{6,2},{7,3},{8,12},{9,13},{10,... | collective-permute-start | bytes 995336 | tf_op jit(solution)/shard_map/ppermute | solution.py:217
  85.7 15.2 %collective-permute-start.17 = (bf16[216,768]{1,0:T(8,128)(2,1)}, bf16[216,768]{1,0:T(8,128)(2,1)}, u32[]{:S(2)}, u32[]{:S(2)}) collective-permute-start(bf16[216,768]{1,0:T(8,128)(2,1)} %collective-permute-done.12), channel_id=1, source_target_pairs={{0,2},{1,3},{2,0},{3,1},{4,6},{5,7},{6,4},{7,5},{8,10},{9,11},{10,... | collective-permute-start | bytes 995336 | tf_op jit(solution)/shard_map/ppermute | solution.py:217
  100.9 1.8 collective-permute-start.23
  100.9 2.3 collective-permute-start.22
  101.4 2.3 collective-permute-start.24
  101.4 2.7 collective-permute-start.25
  101.9 2.7 collective-permute-start.26
  158.7 5.7 %collective-permute-start.27 = (bf16[4,4,96,768]{3,2,1,0:T(8,128)(2,1)}, bf16[4,4,96,768]{3,2,1,0:T(8,128)(2,1)}, u32[]{:S(2)}, u32[]{:S(2)}) collective-permute-start(bf16[4,4,96,768]{3,2,1,0:T(8,128)(2,1)} %get-tuple-element.290), channel_id=1, source_target_pairs={{0,1},{1,0},{2,3},{3,2},{4,5},{5,4},{6,7},{7,6},{8,9},{9,8},{10,11... | collective-permute-start | bytes 7077896 | tf_op jit(solution)/shard_map/ppermute | solution.py:217
  166.3 31.0 %collective-permute-start.28 = (bf16[4,96,768]{2,1,0:T(8,128)(2,1)S(1)}, bf16[4,96,768]{2,1,0:T(8,128)(2,1)S(1)}, u32[]{:S(2)}, u32[]{:S(2)}) collective-permute-start(bf16[4,96,768]{2,1,0:T(8,128)(2,1)S(1)} %get-tuple-element.318), channel_id=1, source_target_pairs={{0,2},{1,3},{2,0},{3,1},{4,6},{5,7},{6,4},{7,5},{8,10},{9,11},{10,... | collective-permute-start | bytes 1769480 | tf_op jit(solution)/shard_map/ppermute | solution.py:217
  167.6 29.7 %collective-permute-start.29 = (bf16[4,96,768]{2,1,0:T(8,128)(2,1)S(1)}, bf16[4,96,768]{2,1,0:T(8,128)(2,1)S(1)}, u32[]{:S(2)}, u32[]{:S(2)}) collective-permute-start(bf16[4,96,768]{2,1,0:T(8,128)(2,1)S(1)} %get-tuple-element.319), channel_id=1, source_target_pairs={{0,4},{1,5},{2,6},{3,7},{4,0},{5,1},{6,2},{7,3},{8,12},{9,13},{10,... | collective-permute-start | bytes 1769480 | tf_op jit(solution)/shard_map/ppermute | solution.py:217
  168.2 29.2 %collective-permute-start.30 = (bf16[4,96,768]{2,1,0:T(8,128)(2,1)S(1)}, bf16[4,96,768]{2,1,0:T(8,128)(2,1)S(1)}, u32[]{:S(2)}, u32[]{:S(2)}) collective-permute-start(bf16[4,96,768]{2,1,0:T(8,128)(2,1)S(1)} %get-tuple-element.320), channel_id=1, source_target_pairs={{0,6},{1,7},{2,4},{3,5},{4,2},{5,3},{6,0},{7,1},{8,14},{9,15},{10,... | collective-permute-start | bytes 1769480 | tf_op jit(solution)/shard_map/ppermute | solution.py:217
  185.0 16.5 %collective-permute-start.31 = (bf16[4,4,120,768]{3,2,1,0:T(8,128)(2,1)}, bf16[4,4,120,768]{3,2,1,0:T(8,128)(2,1)}, u32[]{:S(2)}, u32[]{:S(2)}) collective-permute-start(bf16[4,4,120,768]{3,2,1,0:T(8,128)(2,1)} %get-tuple-element.334), channel_id=1, source_target_pairs={{0,1},{1,0},{2,3},{3,2},{4,5},{5,4},{6,7},{7,6},{8,9},{9,8},{10,11... | collective-permute-start | bytes 8847368 | tf_op jit(solution)/shard_map/ppermute | solution.py:217
  204.8 37.6 %collective-permute-start.34 = (bf16[4,120,768]{2,1,0:T(8,128)(2,1)}, bf16[4,120,768]{2,1,0:T(8,128)(2,1)S(1)}, u32[]{:S(2)}, u32[]{:S(2)}) collective-permute-start(bf16[4,120,768]{2,1,0:T(8,128)(2,1)} %get-tuple-element.358), channel_id=1, source_target_pairs={{0,2},{1,3},{2,0},{3,1},{4,6},{5,7},{6,4},{7,5},{8,10},{9,11},{10,... | collective-permute-start | bytes 2211848 | tf_op jit(solution)/shard_map/ppermute | solution.py:217
  206.0 36.4 %collective-permute-start.35 = (bf16[4,120,768]{2,1,0:T(8,128)(2,1)}, bf16[4,120,768]{2,1,0:T(8,128)(2,1)S(1)}, u32[]{:S(2)}, u32[]{:S(2)}) collective-permute-start(bf16[4,120,768]{2,1,0:T(8,128)(2,1)} %get-tuple-element.359), channel_id=1, source_target_pairs={{0,4},{1,5},{2,6},{3,7},{4,0},{5,1},{6,2},{7,3},{8,12},{9,13},{10,... | collective-permute-start | bytes 2211848 | tf_op jit(solution)/shard_map/ppermute | solution.py:217
  206.6 35.8 %collective-permute-start.36 = (bf16[4,120,768]{2,1,0:T(8,128)(2,1)S(1)}, bf16[4,120,768]{2,1,0:T(8,128)(2,1)S(1)}, u32[]{:S(2)}, u32[]{:S(2)}) collective-permute-start(bf16[4,120,768]{2,1,0:T(8,128)(2,1)S(1)} %get-tuple-element.360), channel_id=1, source_target_pairs={{0,6},{1,7},{2,4},{3,5},{4,2},{5,3},{6,0},{7,1},{8,14},{9,15},{10,... | collective-permute-start | bytes 2211848 | tf_op jit(solution)/shard_map/ppermute | solution.py:217
  208.3 16.4 %collective-permute-start.32 = (bf16[96,768]{1,0:T(8,128)(2,1)S(1)}, bf16[96,768]{1,0:T(8,128)(2,1)S(1)}, u32[]{:S(2)}, u32[]{:S(2)}) collective-permute-start(bf16[96,768]{1,0:T(8,128)(2,1)S(1)} %copy-done.40), channel_id=1, source_target_pairs={{0,8},{1,9},{2,10},{3,11},{4,12},{5,13},{6,14},{7,15},{8,16},{9,17... | collective-permute-start | bytes 442376 | tf_op jit(solution)/shard_map/ppermute | solution.py:217
  208.6 16.0 %collective-permute-start.33 = (bf16[96,768]{1,0:T(8,128)(2,1)S(1)}, bf16[96,768]{1,0:T(8,128)(2,1)S(1)}, u32[]{:S(2)}, u32[]{:S(2)}) collective-permute-start(bf16[96,768]{1,0:T(8,128)(2,1)S(1)} %copy-done.39), channel_id=1, source_target_pairs={{0,24},{1,25},{2,26},{3,27},{4,28},{5,29},{6,30},{7,31},{8,0},{9,1... | collective-permute-start | bytes 442376 | tf_op jit(solution)/shard_map/ppermute | solution.py:217
  224.7 17.7 %collective-permute-start.37 = (bf16[96,768]{1,0:T(8,128)(2,1)S(1)}, bf16[96,768]{1,0:T(8,128)(2,1)S(1)}, u32[]{:S(2)}, u32[]{:S(2)}) collective-permute-start(bf16[96,768]{1,0:T(8,128)(2,1)S(1)} %copy-done.38), channel_id=1, source_target_pairs={{0,16},{1,17},{2,18},{3,19},{4,20},{5,21},{6,22},{7,23},{8,24},{9,... | collective-permute-start | bytes 442376 | tf_op jit(solution)/shard_map/ppermute | solution.py:217
  236.0 11.1 %collective-permute-start.38 = (bf16[4,4,80,768]{3,2,1,0:T(8,128)(2,1)}, bf16[4,4,80,768]{3,2,1,0:T(8,128)(2,1)}, u32[]{:S(2)}, u32[]{:S(2)}) collective-permute-start(bf16[4,4,80,768]{3,2,1,0:T(8,128)(2,1)} %get-tuple-element.373), channel_id=1, source_target_pairs={{0,1},{1,0},{2,3},{3,2},{4,5},{5,4},{6,7},{7,6},{8,9},{9,8},{10,11... | collective-permute-start | bytes 5898248 | tf_op jit(solution)/shard_map/ppermute | solution.py:217
  248.9 19.9 %collective-permute-start.39 = (bf16[4,80,768]{2,1,0:T(8,128)(2,1)S(1)}, bf16[4,80,768]{2,1,0:T(8,128)(2,1)S(1)}, u32[]{:S(2)}, u32[]{:S(2)}) collective-permute-start(bf16[4,80,768]{2,1,0:T(8,128)(2,1)S(1)} %get-tuple-element.376), channel_id=1, source_target_pairs={{0,2},{1,3},{2,0},{3,1},{4,6},{5,7},{6,4},{7,5},{8,10},{9,11},{10,... | collective-permute-start | bytes 1474568 | tf_op jit(solution)/shard_map/ppermute | solution.py:217
  250.2 23.8 %collective-permute-start.40 = (bf16[4,80,768]{2,1,0:T(8,128)(2,1)S(1)}, bf16[4,80,768]{2,1,0:T(8,128)(2,1)S(1)}, u32[]{:S(2)}, u32[]{:S(2)}) collective-permute-start(bf16[4,80,768]{2,1,0:T(8,128)(2,1)S(1)} %get-tuple-element.377), channel_id=1, source_target_pairs={{0,4},{1,5},{2,6},{3,7},{4,0},{5,1},{6,2},{7,3},{8,12},{9,13},{10,... | collective-permute-start | bytes 1474568 | tf_op jit(solution)/shard_map/ppermute | solution.py:217
  250.8 23.3 %collective-permute-start.41 = (bf16[4,80,768]{2,1,0:T(8,128)(2,1)S(1)}, bf16[4,80,768]{2,1,0:T(8,128)(2,1)S(1)}, u32[]{:S(2)}, u32[]{:S(2)}) collective-permute-start(bf16[4,80,768]{2,1,0:T(8,128)(2,1)S(1)} %get-tuple-element.378), channel_id=1, source_target_pairs={{0,6},{1,7},{2,4},{3,5},{4,2},{5,3},{6,0},{7,1},{8,14},{9,15},{10,... | collective-permute-start | bytes 1474568 | tf_op jit(solution)/shard_map/ppermute | solution.py:217
  252.5 9.4 %collective-permute-start.42 = (bf16[120,768]{1,0:T(8,128)(2,1)S(1)}, bf16[120,768]{1,0:T(8,128)(2,1)S(1)}, u32[]{:S(2)}, u32[]{:S(2)}) collective-permute-start(bf16[120,768]{1,0:T(8,128)(2,1)S(1)} %copy-done.37), channel_id=1, source_target_pairs={{0,8},{1,9},{2,10},{3,11},{4,12},{5,13},{6,14},{7,15},{8,16},{9,17... | collective-permute-start | bytes 552968 | tf_op jit(solution)/shard_map/ppermute | solution.py:217
  253.4 15.3 %collective-permute-start.43 = (bf16[120,768]{1,0:T(8,128)(2,1)}, bf16[120,768]{1,0:T(8,128)(2,1)S(1)}, u32[]{:S(2)}, u32[]{:S(2)}) collective-permute-start(bf16[120,768]{1,0:T(8,128)(2,1)} %get-tuple-element.380), channel_id=1, source_target_pairs={{0,16},{1,17},{2,18},{3,19},{4,20},{5,21},{6,22},{7,23},{8,24},{9,... | collective-permute-start | bytes 552968 | tf_op jit(solution)/shard_map/ppermute | solution.py:217
  261.9 12.2 %collective-permute-start.47 = (bf16[120,768]{1,0:T(8,128)(2,1)S(1)}, bf16[120,768]{1,0:T(8,128)(2,1)S(1)}, u32[]{:S(2)}, u32[]{:S(2)}) collective-permute-start(bf16[120,768]{1,0:T(8,128)(2,1)S(1)} %copy-done.36), channel_id=1, source_target_pairs={{0,24},{1,25},{2,26},{3,27},{4,28},{5,29},{6,30},{7,31},{8,0},{9,1... | collective-permute-start | bytes 552968 | tf_op jit(solution)/shard_map/ppermute | solution.py:217
  277.8 9.6 %collective-permute-start.44 = (bf16[80,768]{1,0:T(8,128)(2,1)}, bf16[80,768]{1,0:T(8,128)(2,1)S(1)}, u32[]{:S(2)}, u32[]{:S(2)}) collective-permute-start(bf16[80,768]{1,0:T(8,128)(2,1)} %get-tuple-element.386), channel_id=1, source_target_pairs={{0,8},{1,9},{2,10},{3,11},{4,12},{5,13},{6,14},{7,15},{8,16},{9,17... | collective-permute-start | bytes 368648 | tf_op jit(solution)/shard_map/ppermute | solution.py:217
  279.7 10.8 %collective-permute-start.45 = (bf16[80,768]{1,0:T(8,128)(2,1)}, bf16[80,768]{1,0:T(8,128)(2,1)S(1)}, u32[]{:S(2)}, u32[]{:S(2)}) collective-permute-start(bf16[80,768]{1,0:T(8,128)(2,1)} %get-tuple-element.387), channel_id=1, source_target_pairs={{0,16},{1,17},{2,18},{3,19},{4,20},{5,21},{6,22},{7,23},{8,24},{9,... | collective-permute-start | bytes 368648 | tf_op jit(solution)/shard_map/ppermute | solution.py:217
  283.6 6.8 %collective-permute-start.46 = (bf16[80,768]{1,0:T(8,128)(2,1)}, bf16[80,768]{1,0:T(8,128)(2,1)S(1)}, u32[]{:S(2)}, u32[]{:S(2)}) collective-permute-start(bf16[80,768]{1,0:T(8,128)(2,1)} %get-tuple-element.388), channel_id=1, source_target_pairs={{0,24},{1,25},{2,26},{3,27},{4,28},{5,29},{6,30},{7,31},{8,0},{9,1... | collective-permute-start | bytes 368648 | tf_op jit(solution)/shard_map/ppermute | solution.py:217
  (41 other events, 309.1 us)

commit v4 on v3

--- a/solution.py
+++ b/solution.py
@@ -28,11 +28,11 @@
     return lax.dot_general(left, right, (((0,), (0,)), ((), ())), preferred_element_type=F32)
 
 
-def call(body, grid, in_specs, out_specs, out_shape, scratch=(), flops=0, moved=0, vmem=60, aliases={}, weight=0):
+def call(body, grid, in_specs, out_specs, out_shape, scratch=(), flops=0, moved=0, vmem=60, aliases={}, weight=0, prefetch=0):
     return pl.pallas_call(
         body,
         grid_spec=pltpu.PrefetchScalarGridSpec(
-            num_scalar_prefetch=0, grid=grid, in_specs=in_specs, out_specs=out_specs, scratch_shapes=scratch
+            num_scalar_prefetch=prefetch, grid=grid, in_specs=in_specs, out_specs=out_specs, scratch_shapes=scratch
         ),
         out_shape=out_shape,
         input_output_aliases=aliases,
@@ -45,11 +45,21 @@
     return jax.ShapeDtypeStruct(shape, dtype)
 
 
-def half_mask(dtype, scale=1.0):
-    lane = lax.broadcasted_iota(jnp.int32, (1, 128), 1)
-    low = jnp.where(lane < HEAD, scale, 0.0).astype(dtype)
-    high = jnp.where(lane < HEAD, 0.0, scale).astype(dtype)
-    return low, high
+GROUP = 4
+
+
+def by_head(values, scale=1.0):
+    lane = lax.broadcasted_iota(jnp.int32, (1, GROUP * HEAD), 1) // HEAD
+    return jnp.concatenate([values * jnp.where(lane == t, scale, 0.0).astype(BF16) for t in range(GROUP)], axis=0)
+
+
+def own_columns(stacked):
+    rows = stacked.shape[0] // GROUP
+    lane = lax.broadcasted_iota(jnp.int32, (1, GROUP * HEAD), 1) // HEAD
+    out = stacked[:rows]
+    for t in range(1, GROUP):
+        out = jnp.where(lane == t, stacked[rows * t : rows * (t + 1)], out)
+    return out
 
 
 def attn_fwd_body(start, len_ref, x_ref, wq_ref, wk_ref, wv_ref, table_ref, *rest):
@@ -59,25 +69,19 @@
     q_ref[...] = (dot(x, wq_ref[...]) + table_ref[0:1, :]).astype(BF16)
     k_ref[...] = dot(x, wk_ref[...]).astype(BF16)
     v_ref[...] = (dot(x, wv_ref[...]) + table_ref[1:2, :]).astype(BF16)
-    valid = lax.broadcasted_iota(jnp.int32, (1, length), 1) < len_ref[pl.program_id(0) + start]
-    masks = half_mask(BF16, 0.125)
-    lane = lax.broadcasted_iota(jnp.int32, (1, 128), 1)
-    lses = jnp.zeros((length, 128), F32)
-    for p in range(HEADS // 2):
-        cols = slice(128 * p, 128 * p + 128)
-        qp, kp, vp = q_ref[:, cols], k_ref[:, cols], v_ref[:, cols]
-        outs = []
-        for t in range(2):
-            s = dot_rt(qp * masks[t], kp)
-            s = jnp.where(valid, s, masked_score)
-            m = jnp.max(s, axis=1, keepdims=True)
+    valid = lax.broadcasted_iota(jnp.int32, (length, length), 0) < len_ref[pl.program_id(0) + start]
+    for g in range(HEADS // GROUP):
+        cols = slice(GROUP * HEAD * g, GROUP * HEAD * (g + 1))
+        scores = dot_rt(by_head(k_ref[:, cols], 0.125), q_ref[:, cols])
+        probs = []
+        for t in range(GROUP):
+            s = jnp.where(valid, scores[length * t : length * (t + 1)], masked_score)
+            m = jnp.max(s, axis=0, keepdims=True)
             e = jnp.exp(s - m)
-            total = jnp.sum(e, axis=1, keepdims=True)
-            pr = (e * (1.0 / total)).astype(BF16)
-            outs.append(dot(pr, vp))
-            lses = jnp.where(lane == 2 * p + t, m + jnp.log(total), lses)
-        mix_ref[:, cols] = jnp.where(lane < HEAD, outs[0], outs[1]).astype(BF16)
-    lse_ref[...] = lses
+            total = jnp.sum(e, axis=0, keepdims=True)
+            probs.append((e * (1.0 / total)).astype(BF16))
+            lse_ref[0, GROUP * g + t : GROUP * g + t + 1, :] = m + jnp.log(total)
+        mix_ref[:, cols] = dot_lt(jnp.concatenate(probs, axis=0), by_head(v_ref[:, cols])).astype(BF16)
 
 
 def attn_fwd(x, wq, wk, wv, table, lengths, start=0, stop=None, before=()):
@@ -92,48 +96,45 @@
     return call(
         functools.partial(attn_fwd_body, start), (stop - start,),
         [pl.BlockSpec(memory_space=pltpu.SMEM), tile, full, full, full, eight] + [pl.BlockSpec(memory_space=pl.ANY)] * len(before),
-        [tile, tile, tile, tile, pl.BlockSpec((length, 128), lambda c: (c + start, 0))],
-        [act, act, act, act, shaped((rows, 128), F32)],
+        [tile, tile, tile, tile, pl.BlockSpec((1, HEADS, length), lambda c: (c + start, 0, 0))],
+        [act, act, act, act, shaped((n, HEADS, length), F32)],
         flops=2 * rows * D * D * 3 + 4 * rows * length * D * 4, moved=rows * D * 10 + 6 * D * D,
         aliases={6 + i: i for i in range(5)} if before else {},
-    )(lengths, x, wq, wk, wv, table, *before)
+     vmem=24,)(lengths, x, wq, wk, wv, table, *before)
 
 
 def attn_bwd_body(start, len_ref, q_ref, k_ref, v_ref, gm_ref, lse_ref, *rest):
-    gq_ref, gk_ref, gv_ref, gbq_ref, gbv_ref = rest[-5:]
+    grads_ref, gbq_ref, gbv_ref = rest[-3:]
     c = pl.program_id(0)
     length = q_ref.shape[0]
-    valid = lax.broadcasted_iota(jnp.int32, (1, length), 1) < len_ref[c + start]
-    masks = half_mask(BF16)
-    scaled = half_mask(BF16, 0.125)
+    valid = lax.broadcasted_iota(jnp.int32, (length, length), 0) < len_ref[c + start]
 
     @pl.when(c == 0)
     def _():
-        gbq_ref[...] = rest[3][...] if start else jnp.zeros_like(gbq_ref)
-        gbv_ref[...] = rest[4][...] if start else jnp.zeros_like(gbv_ref)
-
-    for p in range(HEADS // 2):
-        cols = slice(128 * p, 128 * p + 128)
-        qp, kp, vp, gm = q_ref[:, cols], k_ref[:, cols], v_ref[:, cols], gm_ref[:, cols]
-        gq, gk, gv = 0.0, 0.0, 0.0
-        for t in range(2):
-            h = 2 * p + t
-            qt = qp * scaled[t]
-            kt = kp * scaled[t]
-            gt = gm * masks[t]
-            s = dot_rt(qt, kp)
-            s = jnp.where(valid, s, masked_score)
-            pf = jnp.exp(s - lse_ref[:, h : h + 1])
-            gp = dot_rt(gt, vp)
-            gs = pf * (gp - jnp.sum(pf * gp, axis=1, keepdims=True))
-            gs = gs.astype(BF16)
-            gv = gv + dot_lt(pf.astype(BF16), gt)
-            gq = gq + dot(gs, kt)
-            gk = gk + dot_lt(gs, qt)
-        gq, gk, gv = gq.astype(BF16), gk.astype(BF16), gv.astype(BF16)
-        gq_ref[:, cols] = gq
-        gk_ref[:, cols] = gk
-        gv_ref[:, cols] = gv
+        gbq_ref[...] = rest[1][...] if start else jnp.zeros_like(gbq_ref)
+        gbv_ref[...] = rest[2][...] if start else jnp.zeros_like(gbv_ref)
+
+    for g in range(HEADS // GROUP):
+        cols = slice(GROUP * HEAD * g, GROUP * HEAD * (g + 1))
+        q, gm = q_ref[:, cols], gm_ref[:, cols]
+        keys = by_head(k_ref[:, cols], 0.125)
+        scores = dot_rt(keys, q)
+        gprobs = dot_rt(by_head(v_ref[:, cols]), gm)
+        probs, gscores = [], []
+        for t in range(GROUP):
+            rows = slice(length * t, length * (t + 1))
+            h = GROUP * g + t
+            pf = jnp.exp(jnp.where(valid, scores[rows], masked_score) - lse_ref[0, h : h + 1, :])
+            gp = gprobs[rows]
+            gs = pf * (gp - jnp.sum(pf * gp, axis=0, keepdims=True))
+            probs.append(pf.astype(BF16))
+            gscores.append(gs.astype(BF16))
+        gscores = jnp.concatenate(gscores, axis=0)
+        gv = own_columns(dot(jnp.concatenate(probs, axis=0), gm)).astype(BF16)
+        gk = (own_columns(dot(gscores, q)) * 0.125).astype(BF16)
+        gq = dot_lt(gscores, keys).astype(BF16)
+        for m, value in enumerate((gq, gk, gv)):
+            grads_ref[:, m * D + cols.start : m * D + cols.stop] = value
         gbq_ref[:, cols] += jnp.sum(gq.astype(F32), axis=0, keepdims=True)
         gbv_ref[:, cols] += jnp.sum(gv.astype(F32), axis=0, keepdims=True)
 
@@ -145,17 +146,16 @@
     length = rows // n
     tile = pl.BlockSpec((length, D), lambda c: (c + start, 0))
     one = pl.BlockSpec((1, D), lambda c: (0, 0))
-    act = shaped((rows, D), BF16)
     whole = pl.BlockSpec(memory_space=pl.ANY)
     return call(
         functools.partial(attn_bwd_body, start), (stop - start,),
-        [pl.BlockSpec(memory_space=pltpu.SMEM), tile, tile, tile, tile, pl.BlockSpec((length, 128), lambda c: (c + start, 0))]
-        + ([whole, whole, whole, one, one] if before else []),
-        [tile, tile, tile, one, one],
-        [act, act, act, shaped((1, D), F32), shaped((1, D), F32)],
+        [pl.BlockSpec(memory_space=pltpu.SMEM), tile, tile, tile, tile, pl.BlockSpec((1, HEADS, length), lambda c: (c + start, 0, 0))]
+        + ([whole, one, one] if before else []),
+        [pl.BlockSpec((length, 3 * D), lambda c: (c + start, 0)), one, one],
+        [shaped((rows, 3 * D), BF16), shaped((1, D), F32), shaped((1, D), F32)],
         flops=2 * (stop - start) * length * length * D * 5 * 4, moved=(stop - start) * length * D * 14,
-        aliases={6: 0, 7: 1, 8: 2} if before else {}, weight=weight,
-    )(lengths, q, k, v, gm, lse, *before)
+        aliases={6: 0} if before else {}, weight=weight,
+     vmem=20,)(lengths, q, k, v, gm, lse, *before)
 
 
 def mean(v):
@@ -228,25 +228,25 @@
     parts = [p if p.ndim == 3 else p[None] for p in parts]
     full = lambda a: pl.BlockSpec(a.shape, lambda i: (0, 0, 0))
     out = shaped((sum(p.shape[0] for p in parts),) + parts[0].shape[1:], BF16)
-    return call(join_body, (1,), [full(p) for p in parts], full(out), out)(*parts)
+    return call(join_body, (1,), [full(p) for p in parts], full(out), out, vmem=16)(*parts)
 
 
 def gather_all(first, second, n, spare, steps):
     work, given = spare
     across = lambda part: hop(part, swap(n, 1))
     f1, f2, f3 = (hop(first, shift(n, k)) for k in (1, 2, 3))
-    x0, y0 = (hop(second, swap(n, b)) for b in (2, 4))
+    x0, y0, d0 = (hop(second, swap(n, b)) for b in (2, 4, 6))
     line = jnp.stack([first, f1, f2, f3])
-    line, second, x0, y0 = tie(line, second, x0, y0)
+    line, second = tie(line, second)
     near = [hop(line, swap(n, b)) for b in (2, 4, 6)]
     z1, z3 = (hop(second, shift(n, k)) for k in (1, 3))
-    near, second, z1, z3, given = tie(near, second, z1, z3, given)
+    near, second, z1, z3, given, x0, y0, d0 = tie(near, second, z1, z3, given, x0, y0, d0)
     mine = jnp.concatenate([line, *near])
     other = across(mine)
     pair = jnp.stack([z1, z3])
-    d0, z2 = hop(second, swap(n, 6)), hop(second, shift(n, 2))
+    z2 = hop(second, shift(n, 2))
     x13, y13 = (hop(pair, swap(n, b)) for b in (2, 4))
-    other, begun = tie(other, jnp.stack([second, x0, y0, z1, z3]))
+    other, begun = tie(other, join(second, x0, y0, z1, z3))
     begun_other = across(begun)
     held = steps[1](steps[0](mine, other))
     held, d0, z2, x13, y13, begun_other, done = tie(held, d0, z2, x13, y13, begun_other, work(given))
@@ -273,7 +273,7 @@
 def assemble_body(own, at_ref, mine_ref, other_ref, wq_ref, wk_ref, wv_ref, table_ref, ub_ref):
     core, fast, slow = at_ref[0], at_ref[1], at_ref[2]
     table = jnp.zeros((8, D), F32)
-    ub = jnp.zeros((1, ub_ref.shape[1]), F32)
+    ub = jnp.zeros((8, D), F32)
     for i, (dxy, dz) in enumerate(first_sources()):
         chip = ((slow - dz) % 4) * 4 + (fast ^ dxy)
         a, b = mine_ref[i], other_ref[i]
@@ -284,25 +284,25 @@
         for side, got in ((0, low), (1, high)):
             tail = got[3 * own :].astype(F32)
             spot = chip * 2 + side
-            lane = lax.broadcasted_iota(jnp.int32, (1, D), 1)
+            lane = lax.broadcasted_iota(jnp.int32, (8, D), 1)
+            row = lax.broadcasted_iota(jnp.int32, (8, D), 0)
             table = table + pltpu.roll(jnp.where(lane < own, tail, 0.0), spot * own, 1)
-            wide = tail[0:1, 128:256]
-            wide = jnp.concatenate([wide, jnp.zeros((1, ub_ref.shape[1] - 128), F32)], axis=1)
-            ub = ub + pltpu.roll(wide, spot * 4 * own, 1)
+            wide = jnp.where((lane >= 128) & (lane < 128 + 4 * own) & (row == spot // 8), tail[0:1], 0.0)
+            ub = ub + pltpu.roll(wide, (D - 128 + spot % 8 * 4 * own) % D, 1)
     table_ref[...] = table
-    ub_ref[...] = ub
+    ub_ref[...] = ub[:4]
 
 
 def assemble(at, mine, other, own, n):
     full = lambda a: pl.BlockSpec(a.shape, lambda i: (0,) * a.ndim)
     arrays = [mine, other]
     w = shaped((n // 2, 2 * own, D), BF16)
-    outs = [w, w, w, shaped((8, D), F32), shaped((1, 4 * D), F32)]
+    outs = [w, w, w, shaped((8, D), F32), shaped((4, D), F32)]
     wq, wk, wv, table, ub = call(
         functools.partial(assemble_body, own), (1,),
         [pl.BlockSpec(memory_space=pltpu.SMEM)] + [full(a) for a in arrays],
         [full(a) for a in outs], outs, moved=7 * D * D * 2,
-    )(at, *arrays)
+     vmem=28,)(at, *arrays)
     return wq.reshape(D, D), wk.reshape(D, D), wv.reshape(D, D), table, ub
 
 
@@ -360,7 +360,7 @@
     ffn = 0.0
     for j in range(ff // chunk):
         cols = slice(j * chunk, (j + 1) * chunk)
-        pre = dot(low, wu_ref[:, cols]) + ub_ref[:, cols]
+        pre = dot(low, wu_ref[:, cols]) + ub_ref[j : j + 1, :]
         hid, dg = gelu_parts(pre)
         hid = hid.astype(BF16)
         hid_ref[:, cols] = hid
@@ -397,9 +397,9 @@
     ffn_steps(chunk, *refs)
 
 
-def ffn_both(mixed, x, gy, weights, small, ub, at=None, own=0, tile_rows=280, chunk=768):
+def ffn_both(mixed, x, gy, weights, small, ub, at=None, own=0, tile_rows=280, chunk=D):
     rows = x.shape[0]
-    ff = ub.shape[1]
+    ff = ub.size
     tile = pl.BlockSpec((tile_rows, D), lambda c: (c, 0))
     wide = pl.BlockSpec((tile_rows, ff), lambda c: (c, 0))
     fixed = lambda a: pl.BlockSpec(a.shape, lambda c: (0,) * a.ndim, pipeline_mode=pl.Buffered(1))
@@ -430,97 +430,95 @@
     return ref[at, :] if m is None else ref[m, at, :]
 
 
-def wgrad_down_body(far, own, at_ref, hid_ref, gffn_ref, *rest):
-    outs, acc_ref = rest[:-1], rest[-1]
-    acc_ref[...] = dot_lt(hid_ref[...], gffn_ref[...])
-    dz = (pl.program_id(0) - at_ref[2]) % far
-    for dxy in range(4):
-        chip = at_ref[1] ^ dxy
-        for out, side in zip(outs, (at_ref[0], 1 - at_ref[0])):
-            out[dxy, dz] = acc_rows(acc_ref, None, 2 * chip + side, own).astype(BF16)
-
-
 def keep_send(*shape):
     out = shaped((4,) + shape, BF16)
     spec = pl.BlockSpec(out.shape, lambda j: (0,) * len(out.shape))
     return [spec, spec], [out, out]
 
 
+def wgrad_down_body(far, own, at_ref, hid_ref, gffn_ref, keep_ref, send_ref, acc_ref):
+    acc_ref[...] = dot_lt(hid_ref[...], gffn_ref[...])
+    for dxy in range(4):
+        chip = at_ref[1] ^ dxy
+        for out, side in zip((keep_ref, send_ref), (at_ref[0], 1 - at_ref[0])):
+            out[dxy, 0] = acc_rows(acc_ref, None, 2 * chip + side, own).astype(BF16)
+
+
 def wgrad_down(at, hidden, gffn, n):
     rows, ff = hidden.shape
     far = n // 8
     own = ff // n
-    specs, outs = keep_send(far, own, D)
+    out = shaped((4, far, own, D), BF16)
+    spec = pl.BlockSpec((4, 1, own, D), lambda j, at_ref: (0, (j + far - at_ref[2]) % far, 0, 0))
     return call(
         functools.partial(wgrad_down_body, far, own), (far,),
-        [pl.BlockSpec(memory_space=pltpu.SMEM), pl.BlockSpec((rows, ff // far), lambda j: (0, j)), pl.BlockSpec((rows, D), lambda j: (0, 0))],
-        specs, outs, scratch=[pltpu.VMEM((ff // far, D), F32)],
-        flops=2 * rows * D * ff, moved=2 * (rows * (D + ff) + D * ff),
-    )(at, hidden, gffn)
-
-
-def wgrad_up_body(far, own, at_ref, low_ref, gpre_ref, mix_ref, gattn_ref, *rest):
-    outs, acc_ref = rest[:-1], rest[-1]
+        [pl.BlockSpec((rows, ff // far), lambda j, at_ref: (0, j)), pl.BlockSpec((rows, D), lambda j, at_ref: (0, 0))],
+        [spec, spec], [out, out], scratch=[pltpu.VMEM((ff // far, D), F32)], prefetch=1,
+     vmem=60,)(at, hidden, gffn)
+
+
+def wgrad_up_body(far, own, at_ref, low_ref, gpre_ref, mix_ref, gattn_ref, keep_ref, send_ref, acc_ref):
     j = pl.program_id(0)
 
     @pl.when(j < 4)
     def _():
-        acc_ref[j] = dot_lt(low_ref[...], gpre_ref[...])
+        acc_ref[...] = dot_lt(low_ref[...], gpre_ref[...])
 
     @pl.when(j == 4)
     def _():
-        acc_ref[4] = dot_lt(mix_ref[...], gattn_ref[...])
-        for dxy in range(4):
-            for dz in range(far):
-                for k, d in enumerate(row_block(at_ref, far, own, dxy, dz)):
-                    value = jnp.concatenate([acc_rows(acc_ref, m, d, own) for m in range(5)], axis=0)
-                    outs[k][dxy, dz] = value.astype(BF16)
+        acc_ref[...] = dot_lt(mix_ref[...], gattn_ref[...])
+
+    for dxy in range(4):
+        for dz in range(far):
+            for out, d in zip((keep_ref, send_ref), row_block(at_ref, far, own, dxy, dz)):
+                out[dxy, dz, 0] = acc_rows(acc_ref, None, d, own).astype(BF16)
 
 
 def wgrad_up(at, low, gpre, mixed, gattn, own, n):
     rows = low.shape[0]
     far = n // 8
     act = pl.BlockSpec((rows, D), lambda j: (0, 0))
-    specs, outs = keep_send(far, 5 * own, D)
-    return call(
+    out = shaped((4, far, 5, own, D), BF16)
+    spec = pl.BlockSpec((4, far, 1, own, D), lambda j: (0, 0, j, 0, 0))
+    got = call(
         functools.partial(wgrad_up_body, far, own), (5,),
         [pl.BlockSpec(memory_space=pltpu.SMEM), act, pl.BlockSpec((rows, D), lambda j: (0, jnp.minimum(j, 3))), act, act],
-        specs, outs, scratch=[pltpu.VMEM((5, D, D), F32)],
-        flops=10 * rows * D * D, moved=2 * (7 * rows * D + 5 * D * D),
-    )(at, low, gpre, mixed, gattn)
-
-
-def wgrad_in_body(far, own, at_ref, x_ref, gq_ref, gk_ref, gv_ref, small_ref, ub_ref, *rest):
-    outs, acc_ref = rest[:-1], rest[-1]
-    left = x_ref[...]
-    for m, ref in enumerate((gq_ref, gk_ref, gv_ref)):
-        acc_ref[m] = dot_lt(left, ref[...])
-    lane = lax.broadcasted_iota(jnp.int32, (8, D), 1)
-    row = lax.broadcasted_iota(jnp.int32, (8, D), 0)
-    ff = ub_ref.shape[1]
-    wide = ff // (8 * far)
-    for dxy in range(4):
-        for dz in range(far):
-            for k, d in enumerate(row_block(at_ref, far, own, dxy, dz)):
-                tail = pltpu.roll(small_ref[...], (D - own * d) % D, 1)
-                ub = pltpu.roll(ub_ref[...], (ff + 128 - wide * d) % ff, 1)[:, :D]
-                tail = jnp.where(lane < own, tail, 0.0)
-                tail = jnp.where((row == 0) & (lane >= 128) & (lane < 128 + wide), ub, tail)
-                parts = [acc_rows(acc_ref, m, d, own) for m in range(3)] + [tail]
-                outs[k][dxy, dz] = jnp.concatenate(parts, axis=0).astype(BF16)
-
-
-def wgrad_in(at, x, gq, gk, gv, small, ub, own, n):
+        [spec, spec], [out, out], scratch=[pltpu.VMEM((D, D), F32)],
+     vmem=32,)(at, low, gpre, mixed, gattn)
+    return [g.reshape(4, far, 5 * own, D) for g in got]
+
+
+def wgrad_in_body(far, own, at_ref, x_ref, grad_ref, small_ref, ub_ref, keep_ref, send_ref, acc_ref):
+    j = pl.program_id(0)
+    acc_ref[j] = dot_lt(x_ref[...], grad_ref[...])
+
+    @pl.when(j == 2)
+    def _():
+        lane = lax.broadcasted_iota(jnp.int32, (8, D), 1)
+        row = lax.broadcasted_iota(jnp.int32, (8, D), 0)
+        ff = ub_ref.shape[1]
+        wide = ff // (8 * far)
+        for dxy in range(4):
+            for dz in range(far):
+                for out, d in zip((keep_ref, send_ref), row_block(at_ref, far, own, dxy, dz)):
+                    tail = pltpu.roll(small_ref[...], (D - own * d) % D, 1)
+                    ub = pltpu.roll(ub_ref[...], (ff + 128 - wide * d) % ff, 1)[:, :D]
+                    tail = jnp.where(lane < own, tail, 0.0)
+                    tail = jnp.where((row == 0) & (lane >= 128) & (lane < 128 + wide), ub, tail)
+                    parts = [acc_rows(acc_ref, m, d, own) for m in range(3)] + [tail]
+                    out[dxy, dz] = jnp.concatenate(parts, axis=0).astype(BF16)
+
+
+def wgrad_in(at, x, grads, small, ub, own, n):
     rows = x.shape[0]
     far = n // 8
     full = lambda a: pl.BlockSpec(a.shape, lambda i: (0,) * a.ndim)
     specs, outs = keep_send(far, 3 * own + 8, D)
     return call(
-        functools.partial(wgrad_in_body, far, own), (1,),
-        [pl.BlockSpec(memory_space=pltpu.SMEM)] + [full(a) for a in (x, gq, gk, gv, small, ub)],
+        functools.partial(wgrad_in_body, far, own), (3,),
+        [pl.BlockSpec(memory_space=pltpu.SMEM), full(x), pl.BlockSpec((rows, D), lambda j: (0, j)), full(small), full(ub)],
         specs, outs, scratch=[pltpu.VMEM((3, D, D), F32)],
-        flops=6 * rows * D * D, moved=2 * (4 * rows * D + 3 * D * D),
-    )(at, x, gq, gk, gv, small, ub)
+     vmem=36,)(at, x, grads, small, ub)
 
 
 def pair_sum(keep, other, i):
@@ -551,7 +549,7 @@
     base, *sent = call(
         line_body, (1,), [block] * 5, [part] * far,
         [shaped((rows, D), F32)] + [shaped((rows, D), BF16)] * (far - 1), weight=WAIT,
-    )(keep, other, *(p[None] for p in near))
+     vmem=16,)(keep, other, *(p[None] for p in near))
     return base, sent
 
 
@@ -561,25 +559,6 @@
 
 def last_sum(base, far):
     return base + sum(p.astype(F32) for p in far.values())
-
-
-def wgrad3_body(l_ref, a_ref, b_ref, c_ref, oa_ref, ob_ref, oc_ref):
-    left = l_ref[...]
-    for r_ref, o_ref in ((a_ref, oa_ref), (b_ref, ob_ref), (c_ref, oc_ref)):
-        o_ref[...] = dot_lt(left, r_ref[...]).astype(o_ref.dtype)
-
-
-def wgrad3(left, a, b, c, tile_m=384, dtype=BF16):
-    rows = left.shape[0]
-    right = pl.BlockSpec((rows, D), lambda i: (0, 0))
-    out = pl.BlockSpec((tile_m, D), lambda i: (i, 0))
-    return call(
-        wgrad3_body, (D // tile_m,),
-        [pl.BlockSpec((rows, tile_m), lambda i: (0, i)), right, right, right],
-        [out, out, out],
-        [shaped((D, D), dtype)] * 3,
-        flops=6 * rows * D * D, moved=2 * (4 * rows * D + 3 * D * D),
-    )(left, a, b, c)
 
 
 def input_grad_body(g1_ref, gq_ref, gk_ref, gv_ref, wq_ref, wk_ref, wv_ref, *rest):
@@ -588,16 +567,16 @@
     rest[-1][...] = total.astype(BF16)
 
 
-def input_grad(g1, gq, gk, gv, wq, wk, wv, start=0, stop=4, before=(), tiles=4):
+def input_grad(g1, grads, wq, wk, wv, start=0, stop=4, before=(), tiles=4):
     rows = g1.shape[0]
     tile = pl.BlockSpec((rows // tiles, D), lambda c: (c + start, 0))
     full = pl.BlockSpec((D, D), lambda c: (0, 0))
     return call(
         input_grad_body, (stop - start,),
-        [tile, tile, tile, tile, full, full, full] + [pl.BlockSpec(memory_space=pl.ANY)] * len(before),
+        [tile] + [pl.BlockSpec((rows // tiles, D), lambda c, m=m: (c + start, m)) for m in range(3)] + [full, full, full] + [pl.BlockSpec(memory_space=pl.ANY)] * len(before),
         tile, shaped((rows, D), BF16), aliases={7: 0} if before else {},
         flops=6 * rows * D * D, moved=rows * D * 12 + 6 * D * D,
-    )(g1, gq, gk, gv, wq, wk, wv, *before)
+     vmem=24,)(g1, grads, grads, grads, wq, wk, wv, *before)
 
 
 def residue_mask(cotangent, span_start, span_end):
@@ -663,21 +642,21 @@
     far_d = far_hops(sent_d, n, (1, 3))
     begun, parts_u = tie(begun, near_parts(keep_u, other_u))
     near_u = near_hops(parts_u, n)
-    gq, gk, gv, gqb, gvb = attn_bwd(q, k, v, gmixed, lse, lengths, cuts[2], cuts[3], begun)
-    gq, far_d, sent_d = tie(gq, far_d, sent_d)
+    grads, gqb, gvb = attn_bwd(q, k, v, gmixed, lse, lengths, cuts[2], cuts[3], begun)
+    grads, far_d, sent_d = tie(grads, far_d, sent_d)
     far_d.update(far_hops(sent_d, n, (2,)))
     gtable = jnp.concatenate([gqb, gvb, gtable[2:]], axis=0)
-    keep_i, send_i = wgrad_in(at, tokens, gq, gk, gv, gtable, gub, own, n)
+    keep_i, send_i = wgrad_in(at, tokens, grads, gtable, gub, own, n)
     g1, keep_i, send_i = tie(g1, keep_i, send_i)
     other_i = hop(send_i, swap(n, 1))
-    in_grad = input_grad(g1, gq, gk, gv, wq, wk, wv, 0, 2)
+    in_grad = input_grad(g1, grads, wq, wk, wv, 0, 2)
     in_grad, near_u, far_d = tie(in_grad, near_u, far_d)
     base_u, sent_u = line_sum(keep_u, other_u, near_u)
     base_u, sent_u, other_i = tie(base_u, sent_u, other_i)
     far_u = far_hops(sent_u, n, (1, 2))
     in_grad, parts_i = tie(in_grad, near_parts(keep_i, other_i))
     near_i = near_hops(parts_i, n)
-    in_grad = input_grad(g1, gq, gk, gv, wq, wk, wv, 2, 4, (in_grad,))
+    in_grad = input_grad(g1, grads, wq, wk, wv, 2, 4, (in_grad,))
     in_grad, near_i, far_u = tie(in_grad, near_i, far_u)
     base_i, sent_i = line_sum(keep_i, other_i, near_i)
     far_i = far_hops(sent_i, n, (1, 2, 3))
@@ -717,7 +696,7 @@
     wd = held[:, 4 * own + wide : 4 * own + 2 * wide].reshape(ff, D)
     small = held[:, -1].astype(F32)
     table = jnp.concatenate([small[:, own * i : own * (i + 1)].reshape(1, D) for i in range(8)], axis=0)
-    ub = small[:, 8 * own : 8 * own + wide].reshape(1, ff)
+    ub = small[:, 8 * own : 8 * own + wide].reshape(ff // D, D)
     gy = residue_mask(cotangent, span_start, span_end)
 
     q, k, v, mixed, lse = attn_fwd(tokens, wq, wk, wv, table, lengths)
@@ -729,8 +708,8 @@
     ffn_parts = jnp.concatenate([up_grad.reshape(parts, wide, D), down_grad.reshape(parts, wide, D)], axis=1)
     ffn_own = lax.psum_scatter(ffn_parts, "fsdp", scatter_dimension=0, tiled=False).astype(F32)
     out_grad = wgrad(mixed, gattn)
-    gq, gk, gv, gqb, gvb = attn_bwd(q, k, v, gmixed, lse, lengths)
-    query_grad, key_grad, value_grad = wgrad3(tokens, gq, gk, gv)
+    grads, gqb, gvb = attn_bwd(q, k, v, gmixed, lse, lengths)
+    query_grad, key_grad, value_grad = (wgrad(tokens, grads)[:, D * i : D * (i + 1)] for i in range(3))
     vec = [gqb, gvb] + [gtable[i : i + 1] for i in range(2, 8)]
     vec = jnp.concatenate([p.reshape(parts, own) for p in vec] + [gub.reshape(parts, wide)], axis=1)
     vec = jnp.pad(vec.astype(BF16), ((0, 0), (0, D - vec.shape[1]))).reshape(parts, 1, D)
@@ -738,7 +717,7 @@
         [g.reshape(parts, own, D) for g in (query_grad, key_grad, value_grad, out_grad)] + [vec], axis=1
     )
     attn_own = lax.psum_scatter(attn_parts, "fsdp", scatter_dimension=0, tiled=False).astype(F32)
-    in_grad = input_grad(g1, gq, gk, gv, wq, wk, wv)
+    in_grad = input_grad(g1, grads, wq, wk, wv)
 
     gq_w, gk_w, gv_w, go_w = (attn_own[own * i : own * (i + 1)] for i in range(4))
     vec = attn_own[-1]

time: 299 us -> 273 us (0.913); the launches traced: 294 us -> 272 us
  Pallas kernels: 155 us -> 114 us
  waiting for transfers between devices: 48 us -> 70.4 us
  starting transfers between devices: 57.3 us -> 52.4 us
  local copies, waits for them, and re-layouts: 12.9 us -> 16.3 us
    ppermute x48, waiting for transfers between devices: 48 us -> 70.4 us  [hop(): return lax.ppermute(value, 'fsdp', pairs)]
    pallas_call x3, Pallas kernels: 30.5 us -> 12.8 us  [attn_bwd(): call(functools.partial(attn_bwd_body, start), (stop - start,), [pl.BlockS...]
    pallas_call x2, Pallas kernels: 20 us -> 13.6 us  [attn_fwd(): call(functools.partial(attn_fwd_body, start), (stop - start,), [pl.BlockS...]
    pallas_call x3 -> x4, Pallas kernels: 22.3 us -> 16.7 us  [the longest x1 8.49 us: wgrad_in(): call(functools.partial(wgrad_in_body, far, own), (3,), [pl.BlockSpec(memo...]
    ppermute x48, starting transfers between devices: 57.3 us -> 52.4 us  [hop(): return lax.ppermute(value, 'fsdp', pairs)]
    unnamed x89 -> x123, local copies, waits for them, and re-layouts: 8.32 us -> 12.6 us
    pallas_call x3, Pallas kernels: 8.83 us -> 4.93 us  [line_sum(): call(line_body, (1,), [block] * 5, [part] * far, [shaped((rows, D), F32)]...]
    pallas_call x1, Pallas kernels: 15.2 us -> 11.5 us  [wgrad_up(): call(functools.partial(wgrad_up_body, far, own), (5,), [pl.BlockSpec(memo...]
  transfers between devices with their start and end apart: 48 -> 48, of which waited for: 17 -> 25; matrix products, arithmetic and copies ran while one was open for 4% -> 3% of each run, Pallas kernels for 34% -> 22%
where the time goes in v4:
time: 273 us; the launch traced here: 272 us
  Pallas kernels  114 us (42%)
  waiting for transfers between devices  70.4 us (26%)
  starting transfers between devices  52.4 us (19%)
  other arithmetic  18.1 us (7%)
  local copies, waits for them, and re-layouts  16.3 us (6%)
    ppermute x48, waiting for transfers between devices, hop(): return lax.ppermute(value, 'fsdp', pairs)  70.4 us
    ppermute x48, starting transfers between devices, hop(): return lax.ppermute(value, 'fsdp', pairs)  52.4 us
    pallas_call x1, Pallas kernels, ffn_both(): call(body, (rows // tile_rows,), specs + [tile, tile, tile] + [fixed(w) f...  41.2 us
    pallas_call x2, Pallas kernels, attn_fwd(): call(functools.partial(attn_fwd_body, start), (stop - start,), [pl.BlockS...  13.6 us
    pallas_call x3, Pallas kernels, attn_bwd(): call(functools.partial(attn_bwd_body, start), (stop - start,), [pl.BlockS...  12.8 us
    unnamed x123, local copies, waits for them, and re-layouts  12.6 us
    pallas_call x1, Pallas kernels, wgrad_up(): call(functools.partial(wgrad_up_body, far, own), (5,), [pl.BlockSpec(memo...  11.5 us
    pallas_call x1, Pallas kernels, wgrad_down(): call(functools.partial(wgrad_down_body, far, own), (far,), [pl.BlockSpec(...  11.5 us
  transfers between devices with their start and end apart: 48, of which 25 were waited for; matrix products, arithmetic and copies ran while one was open for 3% of the time, Pallas kernels for 22%

profile of v4, /device:TPU:0, one launch (start us, length us, event | category | flops | bytes accessed | tf_op | source)
XLA Modules:
  0.0 272.0 jit_solution(7730024403393816570)
XLA Ops:
  2.5 4.0 %collective-permute-start.10 = (bf16[216,768]{1,0:T(8,128)(2,1)S(1)}, bf16[216,768]{1,0:T(8,128)(2,1)S(1)}, u32[]{:S(2)}, u32[]{:S(2)}) collective-permute-start(bf16[216,768]{1,0:T(8,128)(2,1)S(1)} %pad_maximum_fusion.3), channel_id=1, source_target_pairs={{0,6},{1,7},{2,4},{3,5},{4,2},{5,3},{6,0},{7,1},{8,14},{9,15},{10,... | collective-permute-start | bytes 995336 | tf_op jit(solution)/shard_map/ppermute | solution.py:217
  8.1 2.7 collective-permute-start.1
  10.8 1.6 collective-permute-start
  12.4 2.2 collective-permute-start.2
  15.1 5.2 %collective-permute-done.1 = bf16[80,768]{1,0:T(8,128)(2,1)S(1)} collective-permute-done((bf16[80,768]{1,0:T(8,128)(2,1)S(1)}, bf16[80,768]{1,0:T(8,128)(2,1)S(1)}, u32[]{:S(2)}, u32[]{:S(2)}) %collective-permute-start.1) | collective-permute-done | bytes 122912 | tf_op jit(solution)/shard_map/ppermute | solution.py:217
  22.4 1.5 collective-permute-start.4
  25.4 1.5 collective-permute-start.7
  27.0 4.1 %collective-permute-done.8 = bf16[216,768]{1,0:T(8,128)(2,1)S(1)} collective-permute-done((bf16[216,768]{1,0:T(8,128)(2,1)S(1)}, bf16[216,768]{1,0:T(8,128)(2,1)S(1)}, u32[]{:S(2)}, u32[]{:S(2)}) %collective-permute-start.8) | collective-permute-done | bytes 331808 | tf_op jit(solution)/shard_map/ppermute | solution.py:217
  31.1 4.2 %collective-permute-done.7 = bf16[216,768]{1,0:T(8,128)(2,1)S(1)} collective-permute-done((bf16[216,768]{1,0:T(8,128)(2,1)S(1)}, bf16[216,768]{1,0:T(8,128)(2,1)S(1)}, u32[]{:S(2)}, u32[]{:S(2)}) %collective-permute-start.7) | collective-permute-done | bytes 331808 | tf_op jit(solution)/shard_map/ppermute | solution.py:217
  35.3 8.1 %collective-permute-done.6 = bf16[216,768]{1,0:T(8,128)(2,1)S(1)} collective-permute-done((bf16[216,768]{1,0:T(8,128)(2,1)S(1)}, bf16[216,768]{1,0:T(8,128)(2,1)S(1)}, u32[]{:S(2)}, u32[]{:S(2)}) %collective-permute-start.6) | collective-permute-done | bytes 331808 | tf_op jit(solution)/shard_map/ppermute | solution.py:217
  44.1 3.9 %collective-permute-done.3 = bf16[4,80,768]{2,1,0:T(8,128)(2,1)S(1)} collective-permute-done((bf16[4,80,768]{2,1,0:T(8,128)(2,1)S(1)}, bf16[4,80,768]{2,1,0:T(8,128)(2,1)S(1)}, u32[]{:S(2)}, u32[]{:S(2)}) %collective-permute-start.3) | collective-permute-done | bytes 491552 | tf_op jit(solution)/shard_map/ppermute | solution.py:217
  49.5 2.6 collective-permute-done.11.other_ref
  57.1 3.0 %broadcast_select_fusion.gy_ref = bf16[1120,768]{1,0:T(8,128)(2,1)} fusion(bf16[1120,768]{1,0:T(8,128)(2,1)} %param.21, pred[1120]{0:T(1024)(128)(4,1)S(1)} %broadcast_in_dim.121), kind=kLoop, calls=%fused_computation.1 | loop fusion | flops 860160 | bytes 3441760 | tf_op jit(solution)/shard_map/jit(_where)/select_n | solution.py:590
  62.2 5.8 %shard_map.325 = (bf16[1120,768]{1,0:T(8,128)(2,1)S(1)}, bf16[1120,768]{1,0:T(8,128)(2,1)S(1)}, bf16[1120,768]{1,0:T(8,128)(2,1)S(1)}, bf16[1120,768]{1,0:T(8,128)(2,1)S(1)}, f32[7,12,160]{2,1,0:T(8,128)S(1)}) custom-call(s32[7]{0:T(128)S(1)} %copy-done.32, bf16[1120,768]{1,0:T(8,128)(2,1)S(1)} %copy-done, bf16[768,768]{1,0:T(8,128)(2,1)S(1)} %bitcast.86, ...), custom_call_target="tpu_custom_call" | custom-call | tf_op jit(solution)/shard_map/pallas_call | solution.py:96
  68.0 3.8 %collective-permute-done.12 = bf16[216,768]{1,0:T(8,128)(2,1)} collective-permute-done((bf16[216,768]{1,0:T(8,128)(2,1)S(1)}, bf16[216,768]{1,0:T(8,128)(2,1)}, u32[]{:S(2)}, u32[]{:S(2)}) %collective-permute-start.12) | collective-permute-done | bytes 331808 | tf_op jit(solution)/shard_map/ppermute | solution.py:217
  73.1 1.6 pad_maximum_fusion.rest_1_
  74.8 3.3 %collective-permute-start.21 = (bf16[216,768]{1,0:T(8,128)(2,1)S(1)}, bf16[216,768]{1,0:T(8,128)(2,1)S(1)}, u32[]{:S(2)}, u32[]{:S(2)}) collective-permute-start(bf16[216,768]{1,0:T(8,128)(2,1)S(1)} %copy-done.46), channel_id=1, source_target_pairs={{0,24},{1,25},{2,26},{3,27},{4,28},{5,29},{6,30},{7,31},{8,0},{9,1... | collective-permute-start | bytes 995336 | tf_op jit(solution)/shard_map/ppermute | solution.py:217
  81.9 7.8 %shard_map.326 = (bf16[1120,768]{1,0:T(8,128)(2,1)S(1)}, bf16[1120,768]{1,0:T(8,128)(2,1)S(1)}, bf16[1120,768]{1,0:T(8,128)(2,1)S(1)}, bf16[1120,768]{1,0:T(8,128)(2,1)S(1)}, f32[7,12,160]{2,1,0:T(8,128)S(1)}) custom-call(s32[7]{0:T(128)S(1)} %copy-done.32, ...), custom_call_target="tpu_custom_call", output_to_operand_aliasing={{0}: (6, {}), {1}: (7, {}), {2}: (8, {}), {3}: (9, {}), {4}... | custom-call | tf_op jit(solution)/shard_map/pallas_call | solution.py:96
  93.9 2.6 collective-permute-done.18
  101.1 41.2 %shard_map.327 = (bf16[1120,768]{1,0:T(8,128)(2,1)}, bf16[1120,3072]{1,0:T(8,128)(2,1)}, bf16[1120,768]{1,0:T(8,128)(2,1)}, bf16[1120,768]{1,0:T(8,128)(2,1)}, b...) custom-call(s32[3]{0:T(128)} %copy-done.27, ...), custom_call_target="tpu_custom_call" | custom-call | tf_op jit(solution)/shard_map/pallas_call | solution.py:413
  142.3 11.5 %shard_map.328 = (bf16[4,4,96,768]{3,2,1,0:T(8,128)(2,1)}, bf16[4,4,96,768]{3,2,1,0:T(8,128)(2,1)}) custom-call(s32[3]{0:T(128)} %copy-done.27, bf16[1120,3072]{1,0:T(8,128)(2,1)} %get-tuple-element.264.hid_ref, bf16[1120,768]{1,0:T(8,128)(2,1)} %get-tuple-element.265.gffn_ref), custom_call_target="tpu_custom_call" | custom-call | tf_op jit(solution)/shard_map/pallas_call | solution.py:453
  156.8 2.1 shard_map.329
  159.0 3.1 %fusion.5 = (bf16[4,96,768]{2,1,0:T(8,128)(2,1)}, bf16[4,96,768]{2,1,0:T(8,128)(2,1)}, bf16[4,96,768]{2,1,0:T(8,128)(2,1)}) fusion(bf16[4,4,96,768]{3,2,1,0:T(8,128)(2,1)} %collective-permute-done.27.other_ref, bf16[4,4,96,768]{3,2,1,0:T(8,128)(2,1)S(1)} %copy-done.25), kind=kLoop, calls=%fused_computation.17 | loop fusion | flops 3538944 | bytes 5308416 | tf_op jit(solution)/shard_map/convert_element_type | solution.py:529
  165.6 2.9 %copy-done.18 = bf16[1120,3072]{1,0:T(8,128)(2,1)S(1)} copy-done((bf16[1120,3072]{1,0:T(8,128)(2,1)S(1)}, bf16[1120,3072]{1,0:T(8,128)(2,1)}, u32[]{:S(2)}) %copy-start.18) | copy-done | bytes 6881304
  168.5 11.5 %shard_map.330 = (bf16[4,4,5,24,768]{4,3,2,1,0:T(8,128)(2,1)S(1)}, bf16[4,4,5,24,768]{4,3,2,1,0:T(8,128)(2,1)}) custom-call(s32[3]{0:T(128)S(1)} %copy-done.28, bf16[1120,768]{1,0:T(8,128)(2,1)S(1)} %copy-done.21, bf16[1120,3072]{1,0:T(8,128)(2,1)S(1)} %copy-done.18, bf16[1120,768]{1,0:T(8,128)(2,1)S(1)} %copy-done.14, bf16[1120,768]{1,0:T(8,128)(2,1)S(1)} %copy-done.22), custom_call_target="tpu_custom_call" | custom-call | tf_op jit(solution)/shard_map/pallas_call | solution.py:483
  180.0 5.4 %shard_map.331 = (bf16[1120,2304]{1,0:T(8,128)(2,1)S(1)}, f32[1,768]{1,0:T(1,128)S(1)}, f32[1,768]{1,0:T(1,128)S(1)}) custom-call(s32[7]{0:T(128)S(1)} %copy-done.32, bf16[1120,768]{1,0:T(8,128)(2,1)S(1)} %get-tuple-element.260.q_ref, bf16[1120,768]{1,0:T(8,128)(2,1)S(1)} %copy-done.9, ...), custom_call_target="tpu_custom_call", output_to_operand_aliasing={{0}: (6, {})} | custom-call | tf_op jit(solution)/shard_map/pallas_call | solution.py:150
  185.4 5.5 %collective-permute-done.30 = bf16[4,96,768]{2,1,0:T(8,128)(2,1)} collective-permute-done((bf16[4,96,768]{2,1,0:T(8,128)(2,1)}, bf16[4,96,768]{2,1,0:T(8,128)(2,1)}, u32[]{:S(2)}, u32[]{:S(2)}) %collective-permute-start.30) | collective-permute-done | bytes 589856 | tf_op jit(solution)/shard_map/ppermute | solution.py:217
  190.9 2.0 shard_map.332
  192.9 3.3 %fusion.2 = (bf16[4,120,768]{2,1,0:T(8,128)(2,1)}, bf16[4,120,768]{2,1,0:T(8,128)(2,1)}, bf16[4,120,768]{2,1,0:T(8,128)(2,1)}) fusion(bf16[4,4,120,768]{3,2,1,0:T(8,128)(2,1)} %collective-permute-done.31.other_ref, bf16[4,4,120,768]{3,2,1,0:T(8,128)(2,1)S(1)} %bitcast.98), kind=kLoop, calls=%fused_computation.13 | loop fusion | flops 4423680 | bytes 6635520 | tf_op jit(solution)/shard_map/convert_element_type | solution.py:529
  196.2 1.5 collective-permute-start.34
  199.7 1.7 collective-permute-start.32
  201.5 2.1 collective-permute-start.33
  203.5 5.3 %shard_map.333 = (bf16[1120,2304]{1,0:T(8,128)(2,1)S(1)}, f32[1,768]{1,0:T(1,128)S(1)}, f32[1,768]{1,0:T(1,128)S(1)}) custom-call(s32[7]{0:T(128)S(1)} %copy-done.32, bf16[1120,768]{1,0:T(8,128)(2,1)S(1)} %get-tuple-element.260.q_ref, bf16[1120,768]{1,0:T(8,128)(2,1)S(1)} %copy-done.9, ...), custom_call_target="tpu_custom_call", output_to_operand_aliasing={{0}: (6, {})} | custom-call | tf_op jit(solution)/shard_map/pallas_call | solution.py:150
  209.8 8.5 %shard_map.334 = (bf16[4,4,80,768]{3,2,1,0:T(8,128)(2,1)S(1)}, bf16[4,4,80,768]{3,2,1,0:T(8,128)(2,1)}) custom-call(s32[3]{0:T(128)S(1)} %copy-done.29, bf16[1120,768]{1,0:T(8,128)(2,1)S(1)} %copy-done.1, bf16[1120,2304]{1,0:T(8,128)(2,1)S(1)} %get-tuple-element.317.grad_ref.gq_ref.gk_ref.gv_ref, f32[8,768]{1,0:T(8,128)S(1)} %pad_maximum_fusion.6.small_ref, ...), custom_call_target="tpu_custom_call" | custom-call | tf_op jit(solution)/shard_map/pallas_call | solution.py:517
  218.3 3.5 %shard_map.335.rest_0_ = bf16[1120,768]{1,0:T(8,128)(2,1)} custom-call(f32[1120,768]{1,0:T(8,128)S(1)} %copy-done.15, bf16[1120,2304]{1,0:T(8,128)(2,1)S(1)} %get-tuple-element.317.grad_ref.gq_ref.gk_ref.gv_ref, bf16[1120,2304]{1,0:T(8,128)(2,1)S(1)} %get-tuple-element.317.grad_ref.gq_ref.gk_ref.gv_ref, ...), custom_call_target="tpu_custom_call" | custom-call | tf_op jit(solution)/shard_map/pallas_call | solution.py:574
  221.8 9.4 %collective-permute-done.35 = bf16[4,120,768]{2,1,0:T(8,128)(2,1)S(1)} collective-permute-done((bf16[4,120,768]{2,1,0:T(8,128)(2,1)}, bf16[4,120,768]{2,1,0:T(8,128)(2,1)S(1)}, u32[]{:S(2)}, u32[]{:S(2)}) %collective-permute-start.35) | collective-permute-done | bytes 737312 | tf_op jit(solution)/shard_map/ppermute | solution.py:217
  231.1 1.6 shard_map.336
  232.8 1.8 fusion.8
  238.1 1.8 collective-permute-start.42
  239.9 2.1 collective-permute-start.43
  242.0 4.2 %collective-permute-done.42 = bf16[120,768]{1,0:T(8,128)(2,1)S(1)} collective-permute-done((bf16[120,768]{1,0:T(8,128)(2,1)S(1)}, bf16[120,768]{1,0:T(8,128)(2,1)S(1)}, u32[]{:S(2)}, u32[]{:S(2)}) %collective-permute-start.42) | collective-permute-done | bytes 184352 | tf_op jit(solution)/shard_map/ppermute | solution.py:217
  246.2 1.5 collective-permute-start.47
  248.6 3.4 %shard_map.337 = bf16[1120,768]{1,0:T(8,128)(2,1)} custom-call(f32[1120,768]{1,0:T(8,128)S(1)} %copy-done.15, bf16[1120,2304]{1,0:T(8,128)(2,1)S(1)} %get-tuple-element.317.grad_ref.gq_ref.gk_ref.gv_ref, bf16[1120,2304]{1,0:T(8,128)(2,1)S(1)} %get-tuple-element.317.grad_ref.gq_ref.gk_ref.gv_ref, ...), custom_call_target="tpu_custom_call", output_to_operand_aliasing={{}: (7, {})} | custom-call | tf_op jit(solution)/shard_map/pallas_call | solution.py:574
  252.0 4.8 %collective-permute-done.41 = bf16[4,80,768]{2,1,0:T(8,128)(2,1)S(1)} collective-permute-done((bf16[4,80,768]{2,1,0:T(8,128)(2,1)S(1)}, bf16[4,80,768]{2,1,0:T(8,128)(2,1)S(1)}, u32[]{:S(2)}, u32[]{:S(2)}) %collective-permute-start.41) | collective-permute-done | bytes 491552 | tf_op jit(solution)/shard_map/ppermute | solution.py:217
  259.0 1.8 collective-permute-start.44
  260.8 2.1 collective-permute-start.45
  264.2 2.2 collective-permute-done.44
  266.4 3.8 %collective-permute-done.45 = bf16[80,768]{1,0:T(8,128)(2,1)S(1)} collective-permute-done((bf16[80,768]{1,0:T(8,128)(2,1)S(1)}, bf16[80,768]{1,0:T(8,128)(2,1)S(1)}, u32[]{:S(2)}, u32[]{:S(2)}) %collective-permute-start.45) | collective-permute-done | bytes 122912 | tf_op jit(solution)/shard_map/ppermute | solution.py:217
  (214 shorter events, 49.9 us)
Async XLA Ops:
  2.5 21.4 %collective-permute-start.10 = (bf16[216,768]{1,0:T(8,128)(2,1)S(1)}, bf16[216,768]{1,0:T(8,128)(2,1)S(1)}, u32[]{:S(2)}, u32[]{:S(2)}) collective-permute-start(bf16[216,768]{1,0:T(8,128)(2,1)S(1)} %pad_maximum_fusion.3), channel_id=1, source_target_pairs={{0,6},{1,7},{2,4},{3,5},{4,2},{5,3},{6,0},{7,1},{8,14},{9,15},{10,... | collective-permute-start | bytes 995336 | tf_op jit(solution)/shard_map/ppermute | solution.py:217
  8.1 12.2 %collective-permute-start.1 = (bf16[80,768]{1,0:T(8,128)(2,1)S(1)}, bf16[80,768]{1,0:T(8,128)(2,1)S(1)}, u32[]{:S(2)}, u32[]{:S(2)}) collective-permute-start(bf16[80,768]{1,0:T(8,128)(2,1)S(1)} %get-tuple-element.393), channel_id=1, source_target_pairs={{0,16},{1,17},{2,18},{3,19},{4,20},{5,21},{6,22},{7,23},{8,24},{9,... | collective-permute-start | bytes 368648 | tf_op jit(solution)/shard_map/ppermute | solution.py:217
  10.8 10.1 %collective-permute-start = (bf16[80,768]{1,0:T(8,128)(2,1)S(1)}, bf16[80,768]{1,0:T(8,128)(2,1)S(1)}, u32[]{:S(2)}, u32[]{:S(2)}) collective-permute-start(bf16[80,768]{1,0:T(8,128)(2,1)S(1)} %get-tuple-element.393), channel_id=1, source_target_pairs={{0,8},{1,9},{2,10},{3,11},{4,12},{5,13},{6,14},{7,15},{8,16},{9,17... | collective-permute-start | bytes 368648 | tf_op jit(solution)/shard_map/ppermute | solution.py:217
  12.4 8.5 %collective-permute-start.2 = (bf16[80,768]{1,0:T(8,128)(2,1)S(1)}, bf16[80,768]{1,0:T(8,128)(2,1)S(1)}, u32[]{:S(2)}, u32[]{:S(2)}) collective-permute-start(bf16[80,768]{1,0:T(8,128)(2,1)S(1)} %get-tuple-element.393), channel_id=1, source_target_pairs={{0,24},{1,25},{2,26},{3,27},{4,28},{5,29},{6,30},{7,31},{8,0},{9,1... | collective-permute-start | bytes 368648 | tf_op jit(solution)/shard_map/ppermute | solution.py:217
  14.6 10.8 %collective-permute-start.9 = (bf16[216,768]{1,0:T(8,128)(2,1)S(1)}, bf16[216,768]{1,0:T(8,128)(2,1)S(1)}, u32[]{:S(2)}, u32[]{:S(2)}) collective-permute-start(bf16[216,768]{1,0:T(8,128)(2,1)S(1)} %pad_maximum_fusion.3), channel_id=1, source_target_pairs={{0,4},{1,5},{2,6},{3,7},{4,0},{5,1},{6,2},{7,3},{8,12},{9,13},{10,... | collective-permute-start | bytes 995336 | tf_op jit(solution)/shard_map/ppermute | solution.py:217
  20.3 10.7 %collective-permute-start.8 = (bf16[216,768]{1,0:T(8,128)(2,1)S(1)}, bf16[216,768]{1,0:T(8,128)(2,1)S(1)}, u32[]{:S(2)}, u32[]{:S(2)}) collective-permute-start(bf16[216,768]{1,0:T(8,128)(2,1)S(1)} %pad_maximum_fusion.3), channel_id=1, source_target_pairs={{0,2},{1,3},{2,0},{3,1},{4,6},{5,7},{6,4},{7,5},{8,10},{9,11},{10,... | collective-permute-start | bytes 995336 | tf_op jit(solution)/shard_map/ppermute | solution.py:217
  20.9 22.4 %collective-permute-start.5 = (bf16[4,80,768]{2,1,0:T(8,128)(2,1)S(1)}, bf16[4,80,768]{2,1,0:T(8,128)(2,1)S(1)}, u32[]{:S(2)}, u32[]{:S(2)}) collective-permute-start(bf16[4,80,768]{2,1,0:T(8,128)(2,1)S(1)} %pad_maximum_fusion.2), channel_id=1, source_target_pairs={{0,6},{1,7},{2,4},{3,5},{4,2},{5,3},{6,0},{7,1},{8,14},{9,15},{10,... | collective-permute-start | bytes 1474568 | tf_op jit(solution)/shard_map/ppermute | solution.py:217
  22.4 21.7 %collective-permute-start.4 = (bf16[4,80,768]{2,1,0:T(8,128)(2,1)S(1)}, bf16[4,80,768]{2,1,0:T(8,128)(2,1)S(1)}, u32[]{:S(2)}, u32[]{:S(2)}) collective-permute-start(bf16[4,80,768]{2,1,0:T(8,128)(2,1)S(1)} %pad_maximum_fusion.2), channel_id=1, source_target_pairs={{0,4},{1,5},{2,6},{3,7},{4,0},{5,1},{6,2},{7,3},{8,12},{9,13},{10,... | collective-permute-start | bytes 1474568 | tf_op jit(solution)/shard_map/ppermute | solution.py:217
  23.9 24.0 %collective-permute-start.3 = (bf16[4,80,768]{2,1,0:T(8,128)(2,1)S(1)}, bf16[4,80,768]{2,1,0:T(8,128)(2,1)S(1)}, u32[]{:S(2)}, u32[]{:S(2)}) collective-permute-start(bf16[4,80,768]{2,1,0:T(8,128)(2,1)S(1)} %pad_maximum_fusion.2), channel_id=1, source_target_pairs={{0,2},{1,3},{2,0},{3,1},{4,6},{5,7},{6,4},{7,5},{8,10},{9,11},{10,... | collective-permute-start | bytes 1474568 | tf_op jit(solution)/shard_map/ppermute | solution.py:217
  25.4 9.8 %collective-permute-start.7 = (bf16[216,768]{1,0:T(8,128)(2,1)S(1)}, bf16[216,768]{1,0:T(8,128)(2,1)S(1)}, u32[]{:S(2)}, u32[]{:S(2)}) collective-permute-start(bf16[216,768]{1,0:T(8,128)(2,1)S(1)} %pad_maximum_fusion.3), channel_id=1, source_target_pairs={{0,24},{1,25},{2,26},{3,27},{4,28},{5,29},{6,30},{7,31},{8,0},{9,1... | collective-permute-start | bytes 995336 | tf_op jit(solution)/shard_map/ppermute | solution.py:217
  31.0 12.3 %collective-permute-start.6 = (bf16[216,768]{1,0:T(8,128)(2,1)S(1)}, bf16[216,768]{1,0:T(8,128)(2,1)S(1)}, u32[]{:S(2)}, u32[]{:S(2)}) collective-permute-start(bf16[216,768]{1,0:T(8,128)(2,1)S(1)} %pad_maximum_fusion.3), channel_id=1, source_target_pairs={{0,8},{1,9},{2,10},{3,11},{4,12},{5,13},{6,14},{7,15},{8,16},{9,17... | collective-permute-start | bytes 995336 | tf_op jit(solution)/shard_map/ppermute | solution.py:217
  48.1 4.0 %collective-permute-start.11 = (bf16[16,80,768]{2,1,0:T(8,128)(2,1)S(1)}, bf16[16,80,768]{2,1,0:T(8,128)(2,1)S(1)}, u32[]{:S(2)}, u32[]{:S(2)}) collective-permute-start(bf16[16,80,768]{2,1,0:T(8,128)(2,1)S(1)} %constant_dynamic-update-slice_fusion.mine_ref), channel_id=1, source_target_pairs={{0,1},{1,0},{2,3},{3,2},{4,5},{5,4},{6,7},{7,6},{8,9},{9,8},{10,11... | collective-permute-start | bytes 5898248 | tf_op jit(solution)/shard_map/ppermute | solution.py:217
  53.4 19.7 %collective-permute-start.15 = (bf16[5,216,768]{2,1,0:T(8,128)(2,1)}, bf16[5,216,768]{2,1,0:T(8,128)(2,1)}, u32[]{:S(2)}, u32[]{:S(2)}) collective-permute-start(bf16[5,216,768]{2,1,0:T(8,128)(2,1)} %shard_map.323.rest_0_), channel_id=1, source_target_pairs={{0,1},{1,0},{2,3},{3,2},{4,5},{5,4},{6,7},{7,6},{8,9},{9,8},{10,11... | collective-permute-start | bytes 4976648 | tf_op jit(solution)/shard_map/ppermute | solution.py:217
  53.6 18.2 %collective-permute-start.12 = (bf16[216,768]{1,0:T(8,128)(2,1)S(1)}, bf16[216,768]{1,0:T(8,128)(2,1)}, u32[]{:S(2)}, u32[]{:S(2)}) collective-permute-start(bf16[216,768]{1,0:T(8,128)(2,1)S(1)} %pad_maximum_fusion.3), channel_id=1, source_target_pairs={{0,16},{1,17},{2,18},{3,19},{4,20},{5,21},{6,22},{7,23},{8,24},{9,... | collective-permute-start | bytes 995336 | tf_op jit(solution)/shard_map/ppermute | solution.py:217
  54.9 17.2 %collective-permute-start.14 = (bf16[2,216,768]{2,1,0:T(8,128)(2,1)}, bf16[2,216,768]{2,1,0:T(8,128)(2,1)}, u32[]{:S(2)}, u32[]{:S(2)}) collective-permute-start(bf16[2,216,768]{2,1,0:T(8,128)(2,1)} %pad_maximum_fusion.1), channel_id=1, source_target_pairs={{0,4},{1,5},{2,6},{3,7},{4,0},{5,1},{6,2},{7,3},{8,12},{9,13},{10,... | collective-permute-start | bytes 1990664 | tf_op jit(solution)/shard_map/ppermute | solution.py:217
  56.2 16.9 %collective-permute-start.13 = (bf16[2,216,768]{2,1,0:T(8,128)(2,1)}, bf16[2,216,768]{2,1,0:T(8,128)(2,1)}, u32[]{:S(2)}, u32[]{:S(2)}) collective-permute-start(bf16[2,216,768]{2,1,0:T(8,128)(2,1)} %pad_maximum_fusion.1), channel_id=1, source_target_pairs={{0,2},{1,3},{2,0},{3,1},{4,6},{5,7},{6,4},{7,5},{8,10},{9,11},{10,... | collective-permute-start | bytes 1990664 | tf_op jit(solution)/shard_map/ppermute | solution.py:217
  74.7 5.7 %collective-permute-start.16 = (bf16[6,216,768]{2,1,0:T(8,128)(2,1)S(1)}, bf16[6,216,768]{2,1,0:T(8,128)(2,1)S(1)}, u32[]{:S(2)}, u32[]{:S(2)}) collective-permute-start(bf16[6,216,768]{2,1,0:T(8,128)(2,1)S(1)} %pad_maximum_fusion.rest_1_), channel_id=1, source_target_pairs={{0,1},{1,0},{2,3},{3,2},{4,5},{5,4},{6,7},{7,6},{8,9},{9,8},{10,11... | collective-permute-start | bytes 5971976 | tf_op jit(solution)/shard_map/ppermute | solution.py:217
  74.8 19.1 %collective-permute-start.21 = (bf16[216,768]{1,0:T(8,128)(2,1)S(1)}, bf16[216,768]{1,0:T(8,128)(2,1)S(1)}, u32[]{:S(2)}, u32[]{:S(2)}) collective-permute-start(bf16[216,768]{1,0:T(8,128)(2,1)S(1)} %copy-done.46), channel_id=1, source_target_pairs={{0,24},{1,25},{2,26},{3,27},{4,28},{5,29},{6,30},{7,31},{8,0},{9,1... | collective-permute-start | bytes 995336 | tf_op jit(solution)/shard_map/ppermute | solution.py:217
  78.1 15.8 %collective-permute-start.20 = (bf16[216,768]{1,0:T(8,128)(2,1)S(1)}, bf16[216,768]{1,0:T(8,128)(2,1)S(1)}, u32[]{:S(2)}, u32[]{:S(2)}) collective-permute-start(bf16[216,768]{1,0:T(8,128)(2,1)S(1)} %copy-done.46), channel_id=1, source_target_pairs={{0,8},{1,9},{2,10},{3,11},{4,12},{5,13},{6,14},{7,15},{8,16},{9,17... | collective-permute-start | bytes 995336 | tf_op jit(solution)/shard_map/ppermute | solution.py:217
  78.4 15.4 %collective-permute-start.19 = (bf16[216,768]{1,0:T(8,128)(2,1)}, bf16[216,768]{1,0:T(8,128)(2,1)S(1)}, u32[]{:S(2)}, u32[]{:S(2)}) collective-permute-start(bf16[216,768]{1,0:T(8,128)(2,1)} %collective-permute-done.12), channel_id=1, source_target_pairs={{0,6},{1,7},{2,4},{3,5},{4,2},{5,3},{6,0},{7,1},{8,14},{9,15},{10,... | collective-permute-start | bytes 995336 | tf_op jit(solution)/shard_map/ppermute | solution.py:217
  79.9 16.5 %collective-permute-start.18 = (bf16[216,768]{1,0:T(8,128)(2,1)}, bf16[216,768]{1,0:T(8,128)(2,1)S(1)}, u32[]{:S(2)}, u32[]{:S(2)}) collective-permute-start(bf16[216,768]{1,0:T(8,128)(2,1)} %collective-permute-done.12), channel_id=1, source_target_pairs={{0,4},{1,5},{2,6},{3,7},{4,0},{5,1},{6,2},{7,3},{8,12},{9,13},{10,... | collective-permute-start | bytes 995336 | tf_op jit(solution)/shard_map/ppermute | solution.py:217
  80.4 16.1 %collective-permute-start.17 = (bf16[216,768]{1,0:T(8,128)(2,1)}, bf16[216,768]{1,0:T(8,128)(2,1)S(1)}, u32[]{:S(2)}, u32[]{:S(2)}) collective-permute-start(bf16[216,768]{1,0:T(8,128)(2,1)} %collective-permute-done.12), channel_id=1, source_target_pairs={{0,2},{1,3},{2,0},{3,1},{4,6},{5,7},{6,4},{7,5},{8,10},{9,11},{10,... | collective-permute-start | bytes 995336 | tf_op jit(solution)/shard_map/ppermute | solution.py:217
  96.5 1.6 collective-permute-start.23
  96.5 2.1 collective-permute-start.22
  97.0 2.1 collective-permute-start.24
  97.1 2.5 collective-permute-start.25
  97.6 2.5 collective-permute-start.26
  153.7 5.2 %collective-permute-start.27 = (bf16[4,4,96,768]{3,2,1,0:T(8,128)(2,1)}, bf16[4,4,96,768]{3,2,1,0:T(8,128)(2,1)}, u32[]{:S(2)}, u32[]{:S(2)}) collective-permute-start(bf16[4,4,96,768]{3,2,1,0:T(8,128)(2,1)} %get-tuple-element.274), channel_id=1, source_target_pairs={{0,1},{1,0},{2,3},{3,2},{4,5},{5,4},{6,7},{7,6},{8,9},{9,8},{10,11... | collective-permute-start | bytes 7077896 | tf_op jit(solution)/shard_map/ppermute | solution.py:217
  162.1 23.3 %collective-permute-start.28 = (bf16[4,96,768]{2,1,0:T(8,128)(2,1)}, bf16[4,96,768]{2,1,0:T(8,128)(2,1)}, u32[]{:S(2)}, u32[]{:S(2)}) collective-permute-start(bf16[4,96,768]{2,1,0:T(8,128)(2,1)} %get-tuple-element.294), channel_id=1, source_target_pairs={{0,2},{1,3},{2,0},{3,1},{4,6},{5,7},{6,4},{7,5},{8,10},{9,11},{10,... | collective-permute-start | bytes 1769480 | tf_op jit(solution)/shard_map/ppermute | solution.py:217
  162.6 22.8 %collective-permute-start.29 = (bf16[4,96,768]{2,1,0:T(8,128)(2,1)}, bf16[4,96,768]{2,1,0:T(8,128)(2,1)}, u32[]{:S(2)}, u32[]{:S(2)}) collective-permute-start(bf16[4,96,768]{2,1,0:T(8,128)(2,1)} %get-tuple-element.295), channel_id=1, source_target_pairs={{0,4},{1,5},{2,6},{3,7},{4,0},{5,1},{6,2},{7,3},{8,12},{9,13},{10,... | collective-permute-start | bytes 1769480 | tf_op jit(solution)/shard_map/ppermute | solution.py:217
  164.1 26.8 %collective-permute-start.30 = (bf16[4,96,768]{2,1,0:T(8,128)(2,1)}, bf16[4,96,768]{2,1,0:T(8,128)(2,1)}, u32[]{:S(2)}, u32[]{:S(2)}) collective-permute-start(bf16[4,96,768]{2,1,0:T(8,128)(2,1)} %get-tuple-element.296), channel_id=1, source_target_pairs={{0,6},{1,7},{2,4},{3,5},{4,2},{5,3},{6,0},{7,1},{8,14},{9,15},{10,... | collective-permute-start | bytes 1769480 | tf_op jit(solution)/shard_map/ppermute | solution.py:217
  180.0 12.8 %collective-permute-start.31 = (bf16[4,4,120,768]{3,2,1,0:T(8,128)(2,1)}, bf16[4,4,120,768]{3,2,1,0:T(8,128)(2,1)}, u32[]{:S(2)}, u32[]{:S(2)}) collective-permute-start(bf16[4,4,120,768]{3,2,1,0:T(8,128)(2,1)} %bitcast.37), channel_id=1, source_target_pairs={{0,1},{1,0},{2,3},{3,2},{4,5},{5,4},{6,7},{7,6},{8,9},{9,8},{10,11... | collective-permute-start | bytes 8847368 | tf_op jit(solution)/shard_map/ppermute | solution.py:217
  196.2 25.6 %collective-permute-start.34 = (bf16[4,120,768]{2,1,0:T(8,128)(2,1)}, bf16[4,120,768]{2,1,0:T(8,128)(2,1)S(1)}, u32[]{:S(2)}, u32[]{:S(2)}) collective-permute-start(bf16[4,120,768]{2,1,0:T(8,128)(2,1)} %get-tuple-element.328), channel_id=1, source_target_pairs={{0,2},{1,3},{2,0},{3,1},{4,6},{5,7},{6,4},{7,5},{8,10},{9,11},{10,... | collective-permute-start | bytes 2211848 | tf_op jit(solution)/shard_map/ppermute | solution.py:217
  197.7 33.4 %collective-permute-start.35 = (bf16[4,120,768]{2,1,0:T(8,128)(2,1)}, bf16[4,120,768]{2,1,0:T(8,128)(2,1)S(1)}, u32[]{:S(2)}, u32[]{:S(2)}) collective-permute-start(bf16[4,120,768]{2,1,0:T(8,128)(2,1)} %get-tuple-element.329), channel_id=1, source_target_pairs={{0,4},{1,5},{2,6},{3,7},{4,0},{5,1},{6,2},{7,3},{8,12},{9,13},{10,... | collective-permute-start | bytes 2211848 | tf_op jit(solution)/shard_map/ppermute | solution.py:217
  198.5 32.7 %collective-permute-start.36 = (bf16[4,120,768]{2,1,0:T(8,128)(2,1)}, bf16[4,120,768]{2,1,0:T(8,128)(2,1)S(1)}, u32[]{:S(2)}, u32[]{:S(2)}) collective-permute-start(bf16[4,120,768]{2,1,0:T(8,128)(2,1)} %get-tuple-element.330), channel_id=1, source_target_pairs={{0,6},{1,7},{2,4},{3,5},{4,2},{5,3},{6,0},{7,1},{8,14},{9,15},{10,... | collective-permute-start | bytes 2211848 | tf_op jit(solution)/shard_map/ppermute | solution.py:217
  199.7 9.2 %collective-permute-start.32 = (bf16[96,768]{1,0:T(8,128)(2,1)S(1)}, bf16[96,768]{1,0:T(8,128)(2,1)S(1)}, u32[]{:S(2)}, u32[]{:S(2)}) collective-permute-start(bf16[96,768]{1,0:T(8,128)(2,1)S(1)} %get-tuple-element.314), channel_id=1, source_target_pairs={{0,8},{1,9},{2,10},{3,11},{4,12},{5,13},{6,14},{7,15},{8,16},{9,17... | collective-permute-start | bytes 442376 | tf_op jit(solution)/shard_map/ppermute | solution.py:217
  201.5 7.4 %collective-permute-start.33 = (bf16[96,768]{1,0:T(8,128)(2,1)S(1)}, bf16[96,768]{1,0:T(8,128)(2,1)S(1)}, u32[]{:S(2)}, u32[]{:S(2)}) collective-permute-start(bf16[96,768]{1,0:T(8,128)(2,1)S(1)} %get-tuple-element.315), channel_id=1, source_target_pairs={{0,24},{1,25},{2,26},{3,27},{4,28},{5,29},{6,30},{7,31},{8,0},{9,1... | collective-permute-start | bytes 442376 | tf_op jit(solution)/shard_map/ppermute | solution.py:217
  208.9 12.8 %collective-permute-start.37 = (bf16[96,768]{1,0:T(8,128)(2,1)S(1)}, bf16[96,768]{1,0:T(8,128)(2,1)S(1)}, u32[]{:S(2)}, u32[]{:S(2)}) collective-permute-start(bf16[96,768]{1,0:T(8,128)(2,1)S(1)} %get-tuple-element.332), channel_id=1, source_target_pairs={{0,16},{1,17},{2,18},{3,19},{4,20},{5,21},{6,22},{7,23},{8,24},{9,... | collective-permute-start | bytes 442376 | tf_op jit(solution)/shard_map/ppermute | solution.py:217
  218.3 14.5 %collective-permute-start.38 = (bf16[4,4,80,768]{3,2,1,0:T(8,128)(2,1)}, bf16[4,4,80,768]{3,2,1,0:T(8,128)(2,1)}, u32[]{:S(2)}, u32[]{:S(2)}) collective-permute-start(bf16[4,4,80,768]{3,2,1,0:T(8,128)(2,1)} %get-tuple-element.343), channel_id=1, source_target_pairs={{0,1},{1,0},{2,3},{3,2},{4,5},{5,4},{6,7},{7,6},{8,9},{9,8},{10,11... | collective-permute-start | bytes 5898248 | tf_op jit(solution)/shard_map/ppermute | solution.py:217
  234.6 17.4 %collective-permute-start.39 = (bf16[4,80,768]{2,1,0:T(8,128)(2,1)S(1)}, bf16[4,80,768]{2,1,0:T(8,128)(2,1)S(1)}, u32[]{:S(2)}, u32[]{:S(2)}) collective-permute-start(bf16[4,80,768]{2,1,0:T(8,128)(2,1)S(1)} %get-tuple-element.346), channel_id=1, source_target_pairs={{0,2},{1,3},{2,0},{3,1},{4,6},{5,7},{6,4},{7,5},{8,10},{9,11},{10,... | collective-permute-start | bytes 1474568 | tf_op jit(solution)/shard_map/ppermute | solution.py:217
  235.4 16.6 %collective-permute-start.40 = (bf16[4,80,768]{2,1,0:T(8,128)(2,1)S(1)}, bf16[4,80,768]{2,1,0:T(8,128)(2,1)S(1)}, u32[]{:S(2)}, u32[]{:S(2)}) collective-permute-start(bf16[4,80,768]{2,1,0:T(8,128)(2,1)S(1)} %get-tuple-element.347), channel_id=1, source_target_pairs={{0,4},{1,5},{2,6},{3,7},{4,0},{5,1},{6,2},{7,3},{8,12},{9,13},{10,... | collective-permute-start | bytes 1474568 | tf_op jit(solution)/shard_map/ppermute | solution.py:217
  236.7 20.1 %collective-permute-start.41 = (bf16[4,80,768]{2,1,0:T(8,128)(2,1)S(1)}, bf16[4,80,768]{2,1,0:T(8,128)(2,1)S(1)}, u32[]{:S(2)}, u32[]{:S(2)}) collective-permute-start(bf16[4,80,768]{2,1,0:T(8,128)(2,1)S(1)} %get-tuple-element.348), channel_id=1, source_target_pairs={{0,6},{1,7},{2,4},{3,5},{4,2},{5,3},{6,0},{7,1},{8,14},{9,15},{10,... | collective-permute-start | bytes 1474568 | tf_op jit(solution)/shard_map/ppermute | solution.py:217
  238.1 8.1 %collective-permute-start.42 = (bf16[120,768]{1,0:T(8,128)(2,1)S(1)}, bf16[120,768]{1,0:T(8,128)(2,1)S(1)}, u32[]{:S(2)}, u32[]{:S(2)}) collective-permute-start(bf16[120,768]{1,0:T(8,128)(2,1)S(1)} %get-tuple-element.349), channel_id=1, source_target_pairs={{0,8},{1,9},{2,10},{3,11},{4,12},{5,13},{6,14},{7,15},{8,16},{9,17... | collective-permute-start | bytes 552968 | tf_op jit(solution)/shard_map/ppermute | solution.py:217
  239.9 12.1 %collective-permute-start.43 = (bf16[120,768]{1,0:T(8,128)(2,1)S(1)}, bf16[120,768]{1,0:T(8,128)(2,1)S(1)}, u32[]{:S(2)}, u32[]{:S(2)}) collective-permute-start(bf16[120,768]{1,0:T(8,128)(2,1)S(1)} %get-tuple-element.350), channel_id=1, source_target_pairs={{0,16},{1,17},{2,18},{3,19},{4,20},{5,21},{6,22},{7,23},{8,24},{9,... | collective-permute-start | bytes 552968 | tf_op jit(solution)/shard_map/ppermute | solution.py:217
  246.2 10.6 %collective-permute-start.47 = (bf16[120,768]{1,0:T(8,128)(2,1)S(1)}, bf16[120,768]{1,0:T(8,128)(2,1)S(1)}, u32[]{:S(2)}, u32[]{:S(2)}) collective-permute-start(bf16[120,768]{1,0:T(8,128)(2,1)S(1)} %get-tuple-element.362), channel_id=1, source_target_pairs={{0,24},{1,25},{2,26},{3,27},{4,28},{5,29},{6,30},{7,31},{8,0},{9,1... | collective-permute-start | bytes 552968 | tf_op jit(solution)/shard_map/ppermute | solution.py:217
  259.0 7.4 %collective-permute-start.44 = (bf16[80,768]{1,0:T(8,128)(2,1)S(1)}, bf16[80,768]{1,0:T(8,128)(2,1)S(1)}, u32[]{:S(2)}, u32[]{:S(2)}) collective-permute-start(bf16[80,768]{1,0:T(8,128)(2,1)S(1)} %get-tuple-element.356), channel_id=1, source_target_pairs={{0,8},{1,9},{2,10},{3,11},{4,12},{5,13},{6,14},{7,15},{8,16},{9,17... | collective-permute-start | bytes 368648 | tf_op jit(solution)/shard_map/ppermute | solution.py:217
  260.8 9.4 %collective-permute-start.45 = (bf16[80,768]{1,0:T(8,128)(2,1)S(1)}, bf16[80,768]{1,0:T(8,128)(2,1)S(1)}, u32[]{:S(2)}, u32[]{:S(2)}) collective-permute-start(bf16[80,768]{1,0:T(8,128)(2,1)S(1)} %get-tuple-element.357), channel_id=1, source_target_pairs={{0,16},{1,17},{2,18},{3,19},{4,20},{5,21},{6,22},{7,23},{8,24},{9,... | collective-permute-start | bytes 368648 | tf_op jit(solution)/shard_map/ppermute | solution.py:217
  262.9 7.3 %collective-permute-start.46 = (bf16[80,768]{1,0:T(8,128)(2,1)S(1)}, bf16[80,768]{1,0:T(8,128)(2,1)S(1)}, u32[]{:S(2)}, u32[]{:S(2)}) collective-permute-start(bf16[80,768]{1,0:T(8,128)(2,1)S(1)} %get-tuple-element.358), channel_id=1, source_target_pairs={{0,24},{1,25},{2,26},{3,27},{4,28},{5,29},{6,30},{7,31},{8,0},{9,1... | collective-permute-start | bytes 368648 | tf_op jit(solution)/shard_map/ppermute | solution.py:217
  (60 other events, 456.3 us)

commit v5 on v4

--- a/solution.py
+++ b/solution.py
@@ -274,7 +274,9 @@
     core, fast, slow = at_ref[0], at_ref[1], at_ref[2]
     table = jnp.zeros((8, D), F32)
     ub = jnp.zeros((8, D), F32)
-    for i, (dxy, dz) in enumerate(first_sources()):
+    def add(i, sums):
+        table, ub = sums
+        dxy, dz = i // 4, i % 4
         chip = ((slow - dz) % 4) * 4 + (fast ^ dxy)
         a, b = mine_ref[i], other_ref[i]
         low, high = jnp.where(core == 0, a, b), jnp.where(core == 0, b, a)
@@ -289,6 +291,9 @@
             table = table + pltpu.roll(jnp.where(lane < own, tail, 0.0), spot * own, 1)
             wide = jnp.where((lane >= 128) & (lane < 128 + 4 * own) & (row == spot // 8), tail[0:1], 0.0)
             ub = ub + pltpu.roll(wide, (D - 128 + spot % 8 * 4 * own) % D, 1)
+        return table, ub
+
+    table, ub = lax.fori_loop(0, 16, add, (table, ub))
     table_ref[...] = table
     ub_ref[...] = ub[:4]
 
@@ -381,7 +386,7 @@
         gh = dot_rt(gffn, wd_ref[cols, :])
         gpre = (gh * dg_ref[:, cols].astype(F32)).astype(BF16)
         gpre_ref[:, cols] = gpre
-        gub_ref[:, cols] += colsum(gpre.astype(F32))
+        gub_ref[j : j + 1, :] += colsum(gpre.astype(F32))
         gfirst = gfirst + dot_rt(gpre, wu_ref[:, cols])
     g1 = norm_back(gfirst, xhat1, rs1, again)
     gattn = g1.astype(BF16)
@@ -413,9 +418,9 @@
     return call(
         body, (rows // tile_rows,),
         specs + [tile, tile, tile] + [fixed(w) for w in weights] + [fixed(small), fixed(ub)],
-        [tile, wide, tile, tile, wide, tile, tile, tile, pl.BlockSpec((8, D), lambda c: (0, 0)), pl.BlockSpec((1, ff), lambda c: (0, 0))],
-        [act, big, act, act, big, act, shaped((rows, D), F32), act, shaped((8, D), F32), shaped((1, ff), F32)],
-        scratch=scratch,
+        [tile, wide, tile, tile, wide, tile, tile, tile, pl.BlockSpec((8, D), lambda c: (0, 0)), pl.BlockSpec((ff // D, D), lambda c: (0, 0))],
+        [act, big, act, act, big, act, shaped((rows, D), F32), act, shaped((8, D), F32), shaped((ff // D, D), F32)],
+        scratch=scratch, vmem=46,
         flops=2 * rows * D * (2 * D + 4 * ff), moved=rows * (D * 20 + ff * 4) + D * (D + 2 * ff) * 2,
     )(*place_of, mixed, x, gy, *weights, small, ub)
 
@@ -468,10 +473,13 @@
     def _():
         acc_ref[...] = dot_lt(mix_ref[...], gattn_ref[...])
 
-    for dxy in range(4):
-        for dz in range(far):
+    def along(dz, _):
+        for dxy in range(4):
             for out, d in zip((keep_ref, send_ref), row_block(at_ref, far, own, dxy, dz)):
                 out[dxy, dz, 0] = acc_rows(acc_ref, None, d, own).astype(BF16)
+        return 0
+
+    lax.fori_loop(0, far, along, 0)
 
 
 def wgrad_up(at, low, gpre, mixed, gattn, own, n):
@@ -496,17 +504,20 @@
     def _():
         lane = lax.broadcasted_iota(jnp.int32, (8, D), 1)
         row = lax.broadcasted_iota(jnp.int32, (8, D), 0)
-        ff = ub_ref.shape[1]
-        wide = ff // (8 * far)
-        for dxy in range(4):
-            for dz in range(far):
+        wide = ub_ref.size // (8 * far)
+        per = D // wide
+        def along(dz, _):
+            for dxy in range(4):
                 for out, d in zip((keep_ref, send_ref), row_block(at_ref, far, own, dxy, dz)):
                     tail = pltpu.roll(small_ref[...], (D - own * d) % D, 1)
-                    ub = pltpu.roll(ub_ref[...], (ff + 128 - wide * d) % ff, 1)[:, :D]
+                    ub = pltpu.roll(ub_ref[pl.ds(d // per, 1), :], (D + 128 - wide * (d % per)) % D, 1)
                     tail = jnp.where(lane < own, tail, 0.0)
                     tail = jnp.where((row == 0) & (lane >= 128) & (lane < 128 + wide), ub, tail)
                     parts = [acc_rows(acc_ref, m, d, own) for m in range(3)] + [tail]
                     out[dxy, dz] = jnp.concatenate(parts, axis=0).astype(BF16)
+            return 0
+
+        lax.fori_loop(0, far, along, 0)
 
 
 def wgrad_in(at, x, grads, small, ub, own, n):
@@ -548,9 +559,18 @@
     part = pl.BlockSpec((rows, D), lambda i: (0, 0))
     base, *sent = call(
         line_body, (1,), [block] * 5, [part] * far,
-        [shaped((rows, D), F32)] + [shaped((rows, D), BF16)] * (far - 1), weight=WAIT,
+        [shaped((rows, D), F32)] + [shaped((rows, D), BF16)] * (far - 1),
      vmem=16,)(keep, other, *(p[None] for p in near))
     return base, sent
+
+
+def pass_body(in_ref, out_ref):
+    out_ref[...] = in_ref[...]
+
+
+def passed(value):
+    full = pl.BlockSpec(value.shape, lambda i: (0, 0))
+    return call(pass_body, (1,), [full], full, shaped(value.shape, value.dtype), weight=WAIT, vmem=8)(value)
 
 
 def far_hops(sent, n, which):
@@ -637,11 +657,13 @@
     other_u = hop(send_u, swap(n, 1))
     begun = attn_bwd(q, k, v, gmixed, lse, lengths, cuts[1], cuts[2], begun)
     begun, near_d = tie(begun, near_d)
-    base_d, sent_d = line_sum(keep_d, other_d, near_d)
-    base_d, sent_d, other_u = tie(base_d, sent_d, other_u)
-    far_d = far_hops(sent_d, n, (1, 3))
+    begun = [begun[0], passed(begun[1]), begun[2]]
+    begun, other_u = tie(begun, other_u)
     begun, parts_u = tie(begun, near_parts(keep_u, other_u))
     near_u = near_hops(parts_u, n)
+    base_d, sent_d = line_sum(keep_d, other_d, near_d)
+    begun, base_d, sent_d = tie(begun, base_d, sent_d)
+    far_d = far_hops(sent_d, n, (1, 3))
     grads, gqb, gvb = attn_bwd(q, k, v, gmixed, lse, lengths, cuts[2], cuts[3], begun)
     grads, far_d, sent_d = tie(grads, far_d, sent_d)
     far_d.update(far_hops(sent_d, n, (2,)))
@@ -650,12 +672,14 @@
     g1, keep_i, send_i = tie(g1, keep_i, send_i)
     other_i = hop(send_i, swap(n, 1))
     in_grad = input_grad(g1, grads, wq, wk, wv, 0, 2)
-    in_grad, near_u, far_d = tie(in_grad, near_u, far_d)
+    in_grad, near_u, far_d, base_d = tie(in_grad, near_u, far_d, base_d)
+    base_d = passed(base_d)
+    base_d, other_i = tie(base_d, other_i)
+    in_grad, parts_i, base_d = tie(in_grad, near_parts(keep_i, other_i), base_d)
+    near_i = near_hops(parts_i, n)
     base_u, sent_u = line_sum(keep_u, other_u, near_u)
-    base_u, sent_u, other_i = tie(base_u, sent_u, other_i)
+    in_grad, base_u, sent_u = tie(in_grad, base_u, sent_u)
     far_u = far_hops(sent_u, n, (1, 2))
-    in_grad, parts_i = tie(in_grad, near_parts(keep_i, other_i))
-    near_i = near_hops(parts_i, n)
     in_grad = input_grad(g1, grads, wq, wk, wv, 2, 4, (in_grad,))
     in_grad, near_i, far_u = tie(in_grad, near_i, far_u)
     base_i, sent_i = line_sum(keep_i, other_i, near_i)

time: 273 us -> 270 us (0.989)
  waiting for transfers between devices: 70.4 us -> 67 us
    ppermute x48, waiting for transfers between devices: 70.4 us -> 67 us  [hop(): return lax.ppermute(value, 'fsdp', pairs)]
    unnamed x123 -> x101, local copies, waits for them, and re-layouts: 12.6 us -> 12.4 us
  transfers between devices with their start and end apart: 48 -> 48, of which waited for: 25 -> 27; matrix products, arithmetic and copies ran while one was open for 3% -> 3% of each run, Pallas kernels for 22% -> 22%
where the time goes in v5:
time: 270 us; the launch traced here: 269 us
  Pallas kernels  114 us (42%)
  waiting for transfers between devices  67 us (25%)
  starting transfers between devices  51.8 us (19%)
  other arithmetic  18.5 us (7%)
  local copies, waits for them, and re-layouts  16.1 us (6%)
    ppermute x48, waiting for transfers between devices, hop(): return lax.ppermute(value, 'fsdp', pairs)  67 us
    ppermute x48, starting transfers between devices, hop(): return lax.ppermute(value, 'fsdp', pairs)  51.8 us
    pallas_call x1, Pallas kernels, ffn_both(): call(body, (rows // tile_rows,), specs + [tile, tile, tile] + [fixed(w) f...  41.3 us
    pallas_call x2, Pallas kernels, attn_fwd(): call(functools.partial(attn_fwd_body, start), (stop - start,), [pl.BlockS...  13.5 us
    pallas_call x3, Pallas kernels, attn_bwd(): call(functools.partial(attn_bwd_body, start), (stop - start,), [pl.BlockS...  12.8 us
    unnamed x101, local copies, waits for them, and re-layouts  12.4 us
    pallas_call x1, Pallas kernels, wgrad_up(): call(functools.partial(wgrad_up_body, far, own), (5,), [pl.BlockSpec(memo...  11.7 us
    pallas_call x1, Pallas kernels, wgrad_down(): call(functools.partial(wgrad_down_body, far, own), (far,), [pl.BlockSpec(...  11.3 us
  transfers between devices with their start and end apart: 48, of which 27 were waited for; matrix products, arithmetic and copies ran while one was open for 3% of the time, Pallas kernels for 22%

profile of v5, /device:TPU:0, one launch (start us, length us, event | category | flops | bytes accessed | tf_op | source)
XLA Modules:
  0.0 268.9 jit_solution(13867098959320712445)
XLA Ops:
  2.5 4.0 %collective-permute-start.10 = (bf16[216,768]{1,0:T(8,128)(2,1)S(1)}, bf16[216,768]{1,0:T(8,128)(2,1)}, u32[]{:S(2)}, u32[]{:S(2)}) collective-permute-start(bf16[216,768]{1,0:T(8,128)(2,1)S(1)} %pad_maximum_fusion.3), channel_id=1, source_target_pairs={{0,6},{1,7},{2,4},{3,5},{4,2},{5,3},{6,0},{7,1},{8,14},{9,15},{10,... | collective-permute-start | bytes 995336 | tf_op jit(solution)/shard_map/ppermute | solution.py:217
  8.1 2.7 collective-permute-start.1
  10.8 1.6 collective-permute-start
  12.4 2.2 collective-permute-start.2
  15.1 5.2 %collective-permute-done.1 = bf16[80,768]{1,0:T(8,128)(2,1)S(1)} collective-permute-done((bf16[80,768]{1,0:T(8,128)(2,1)S(1)}, bf16[80,768]{1,0:T(8,128)(2,1)S(1)}, u32[]{:S(2)}, u32[]{:S(2)}) %collective-permute-start.1) | collective-permute-done | bytes 122912 | tf_op jit(solution)/shard_map/ppermute | solution.py:217
  22.4 1.5 collective-permute-start.4
  25.5 1.5 collective-permute-start.7
  27.0 4.1 %collective-permute-done.8 = bf16[216,768]{1,0:T(8,128)(2,1)S(1)} collective-permute-done((bf16[216,768]{1,0:T(8,128)(2,1)S(1)}, bf16[216,768]{1,0:T(8,128)(2,1)S(1)}, u32[]{:S(2)}, u32[]{:S(2)}) %collective-permute-start.8) | collective-permute-done | bytes 331808 | tf_op jit(solution)/shard_map/ppermute | solution.py:217
  31.1 4.2 %collective-permute-done.7 = bf16[216,768]{1,0:T(8,128)(2,1)S(1)} collective-permute-done((bf16[216,768]{1,0:T(8,128)(2,1)S(1)}, bf16[216,768]{1,0:T(8,128)(2,1)S(1)}, u32[]{:S(2)}, u32[]{:S(2)}) %collective-permute-start.7) | collective-permute-done | bytes 331808 | tf_op jit(solution)/shard_map/ppermute | solution.py:217
  35.3 8.1 %collective-permute-done.6 = bf16[216,768]{1,0:T(8,128)(2,1)S(1)} collective-permute-done((bf16[216,768]{1,0:T(8,128)(2,1)S(1)}, bf16[216,768]{1,0:T(8,128)(2,1)S(1)}, u32[]{:S(2)}, u32[]{:S(2)}) %collective-permute-start.6) | collective-permute-done | bytes 331808 | tf_op jit(solution)/shard_map/ppermute | solution.py:217
  44.1 3.9 %collective-permute-done.3 = bf16[4,80,768]{2,1,0:T(8,128)(2,1)S(1)} collective-permute-done((bf16[4,80,768]{2,1,0:T(8,128)(2,1)S(1)}, bf16[4,80,768]{2,1,0:T(8,128)(2,1)S(1)}, u32[]{:S(2)}, u32[]{:S(2)}) %collective-permute-start.3) | collective-permute-done | bytes 491552 | tf_op jit(solution)/shard_map/ppermute | solution.py:217
  49.5 2.6 collective-permute-done.11.other_ref
  57.1 3.0 %broadcast_select_fusion.gy_ref = bf16[1120,768]{1,0:T(8,128)(2,1)} fusion(bf16[1120,768]{1,0:T(8,128)(2,1)} %param.21, pred[1120]{0:T(1024)(128)(4,1)S(1)} %broadcast_in_dim.121), kind=kLoop, calls=%fused_computation.1 | loop fusion | flops 860160 | bytes 3441760 | tf_op jit(solution)/shard_map/jit(_where)/select_n | solution.py:610
  60.1 2.6 shard_map.324
  62.8 5.8 %shard_map.325 = (bf16[1120,768]{1,0:T(8,128)(2,1)S(1)}, bf16[1120,768]{1,0:T(8,128)(2,1)S(1)}, bf16[1120,768]{1,0:T(8,128)(2,1)S(1)}, bf16[1120,768]{1,0:T(8,128)(2,1)S(1)}, f32[7,12,160]{2,1,0:T(8,128)S(1)}) custom-call(s32[7]{0:T(128)S(1)} %copy-done.38, bf16[1120,768]{1,0:T(8,128)(2,1)S(1)} %copy-done, bf16[768,768]{1,0:T(8,128)(2,1)S(1)} %bitcast.86, ...), custom_call_target="tpu_custom_call" | custom-call | tf_op jit(solution)/shard_map/pallas_call | solution.py:96
  68.6 3.2 %collective-permute-done.12 = bf16[216,768]{1,0:T(8,128)(2,1)} collective-permute-done((bf16[216,768]{1,0:T(8,128)(2,1)S(1)}, bf16[216,768]{1,0:T(8,128)(2,1)}, u32[]{:S(2)}, u32[]{:S(2)}) %collective-permute-start.12) | collective-permute-done | bytes 331808 | tf_op jit(solution)/shard_map/ppermute | solution.py:217
  73.1 1.7 pad_maximum_fusion.rest_1_
  74.9 3.3 %collective-permute-start.21 = (bf16[216,768]{1,0:T(8,128)(2,1)}, bf16[216,768]{1,0:T(8,128)(2,1)S(1)}, u32[]{:S(2)}, u32[]{:S(2)}) collective-permute-start(bf16[216,768]{1,0:T(8,128)(2,1)} %collective-permute-done.10), channel_id=1, source_target_pairs={{0,24},{1,25},{2,26},{3,27},{4,28},{5,29},{6,30},{7,31},{8,0},{9,1... | collective-permute-start | bytes 995336 | tf_op jit(solution)/shard_map/ppermute | solution.py:217
  82.0 7.7 %shard_map.326 = (bf16[1120,768]{1,0:T(8,128)(2,1)S(1)}, bf16[1120,768]{1,0:T(8,128)(2,1)S(1)}, bf16[1120,768]{1,0:T(8,128)(2,1)S(1)}, bf16[1120,768]{1,0:T(8,128)(2,1)S(1)}, f32[7,12,160]{2,1,0:T(8,128)S(1)}) custom-call(s32[7]{0:T(128)S(1)} %copy-done.38, ...), custom_call_target="tpu_custom_call", output_to_operand_aliasing={{0}: (6, {}), {1}: (7, {}), {2}: (8, {}), {3}: (9, {}), {4}... | custom-call | tf_op jit(solution)/shard_map/pallas_call | solution.py:96
  92.2 1.9 collective-permute-done.21
  94.2 2.4 collective-permute-done.18
  100.2 41.3 %shard_map.327 = (bf16[1120,768]{1,0:T(8,128)(2,1)}, bf16[1120,3072]{1,0:T(8,128)(2,1)}, bf16[1120,768]{1,0:T(8,128)(2,1)}, bf16[1120,768]{1,0:T(8,128)(2,1)}, b...) custom-call(s32[3]{0:T(128)S(1)} %pad_add_fusion.1.at_ref, ...), custom_call_target="tpu_custom_call" | custom-call | tf_op jit(solution)/shard_map/pallas_call | solution.py:418
  141.5 11.3 %shard_map.328 = (bf16[4,4,96,768]{3,2,1,0:T(8,128)(2,1)}, bf16[4,4,96,768]{3,2,1,0:T(8,128)(2,1)}) custom-call(s32[3]{0:T(128)} %copy-done.35, bf16[1120,3072]{1,0:T(8,128)(2,1)} %get-tuple-element.274.hid_ref, bf16[1120,768]{1,0:T(8,128)(2,1)} %get-tuple-element.275.gffn_ref), custom_call_target="tpu_custom_call" | custom-call | tf_op jit(solution)/shard_map/pallas_call | solution.py:458
  155.9 2.1 shard_map.329
  158.1 3.1 %fusion.5 = (bf16[4,96,768]{2,1,0:T(8,128)(2,1)S(1)}, bf16[4,96,768]{2,1,0:T(8,128)(2,1)}, bf16[4,96,768]{2,1,0:T(8,128)(2,1)}) fusion(bf16[4,4,96,768]{3,2,1,0:T(8,128)(2,1)} %collective-permute-done.27.other_ref, bf16[4,4,96,768]{3,2,1,0:T(8,128)(2,1)S(1)} %copy-done.16), kind=kLoop, calls=%fused_computation.17 | loop fusion | flops 3538944 | bytes 5308416 | tf_op jit(solution)/shard_map/convert_element_type | solution.py:540
  163.1 1.5 collective-permute-start.30
  164.7 2.9 %copy-done.20 = bf16[1120,3072]{1,0:T(8,128)(2,1)S(1)} copy-done((bf16[1120,3072]{1,0:T(8,128)(2,1)S(1)}, bf16[1120,3072]{1,0:T(8,128)(2,1)}, u32[]{:S(2)}) %copy-start.20) | copy-done | bytes 6881304
  167.6 11.7 %shard_map.330 = (bf16[4,4,5,24,768]{4,3,2,1,0:T(8,128)(2,1)S(1)}, bf16[4,4,5,24,768]{4,3,2,1,0:T(8,128)(2,1)}) custom-call(s32[3]{0:T(128)S(1)} %copy-done.36, bf16[1120,768]{1,0:T(8,128)(2,1)S(1)} %copy-done.23, bf16[1120,3072]{1,0:T(8,128)(2,1)S(1)} %copy-done.20, bf16[1120,768]{1,0:T(8,128)(2,1)S(1)} %copy-done.12, bf16[1120,768]{1,0:T(8,128)(2,1)S(1)} %copy-done.24), custom_call_target="tpu_custom_call" | custom-call | tf_op jit(solution)/shard_map/pallas_call | solution.py:491
  179.4 5.4 %shard_map.331 = (bf16[1120,2304]{1,0:T(8,128)(2,1)S(1)}, f32[1,768]{1,0:T(1,128)S(1)}, f32[1,768]{1,0:T(1,128)S(1)}) custom-call(s32[7]{0:T(128)S(1)} %copy-done.38, bf16[1120,768]{1,0:T(8,128)(2,1)S(1)} %get-tuple-element.270.q_ref, bf16[1120,768]{1,0:T(8,128)(2,1)S(1)} %get-tuple-element.271.k_ref, ...), custom_call_target="tpu_custom_call", output_to_operand_aliasing={{0}: (6, {})} | custom-call | tf_op jit(solution)/shard_map/pallas_call | solution.py:150
  184.8 5.1 %collective-permute-done.30 = bf16[4,96,768]{2,1,0:T(8,128)(2,1)S(1)} collective-permute-done((bf16[4,96,768]{2,1,0:T(8,128)(2,1)S(1)}, bf16[4,96,768]{2,1,0:T(8,128)(2,1)S(1)}, u32[]{:S(2)}, u32[]{:S(2)}) %collective-permute-start.30) | collective-permute-done | bytes 589856 | tf_op jit(solution)/shard_map/ppermute | solution.py:217
  190.7 3.4 %fusion.2 = (bf16[4,120,768]{2,1,0:T(8,128)(2,1)}, bf16[4,120,768]{2,1,0:T(8,128)(2,1)}, bf16[4,120,768]{2,1,0:T(8,128)(2,1)}) fusion(bf16[4,4,120,768]{3,2,1,0:T(8,128)(2,1)} %collective-permute-done.31.other_ref, bf16[4,4,120,768]{3,2,1,0:T(8,128)(2,1)S(1)} %bitcast.98), kind=kLoop, calls=%fused_computation.13 | loop fusion | flops 4423680 | bytes 6635520 | tf_op jit(solution)/shard_map/convert_element_type | solution.py:540
  194.1 1.7 collective-permute-start.34
  199.1 1.8 collective-permute-start.32
  200.9 2.0 collective-permute-start.33
  203.0 5.3 %shard_map.334 = (bf16[1120,2304]{1,0:T(8,128)(2,1)S(1)}, f32[1,768]{1,0:T(1,128)S(1)}, f32[1,768]{1,0:T(1,128)S(1)}) custom-call(s32[7]{0:T(128)S(1)} %copy-done.38, bf16[1120,768]{1,0:T(8,128)(2,1)S(1)} %get-tuple-element.270.q_ref, bf16[1120,768]{1,0:T(8,128)(2,1)S(1)} %get-tuple-element.271.k_ref, ...), custom_call_target="tpu_custom_call", output_to_operand_aliasing={{0}: (6, {})} | custom-call | tf_op jit(solution)/shard_map/pallas_call | solution.py:150
  209.2 8.4 %shard_map.335 = (bf16[4,4,80,768]{3,2,1,0:T(8,128)(2,1)S(1)}, bf16[4,4,80,768]{3,2,1,0:T(8,128)(2,1)}) custom-call(s32[3]{0:T(128)S(1)} %copy-done.37, bf16[1120,768]{1,0:T(8,128)(2,1)S(1)} %copy-done.1, bf16[1120,2304]{1,0:T(8,128)(2,1)S(1)} %get-tuple-element.333.grad_ref.gq_ref.gk_ref.gv_ref, f32[8,768]{1,0:T(8,128)S(1)} %pad_maximum_fusion.6.small_ref, ...), custom_call_target="tpu_custom_call" | custom-call | tf_op jit(solution)/shard_map/pallas_call | solution.py:528
  217.6 3.5 %shard_map.336.rest_0_ = bf16[1120,768]{1,0:T(8,128)(2,1)} custom-call(f32[1120,768]{1,0:T(8,128)S(1)} %copy-done.13, bf16[1120,2304]{1,0:T(8,128)(2,1)S(1)} %get-tuple-element.333.grad_ref.gq_ref.gk_ref.gv_ref, bf16[1120,2304]{1,0:T(8,128)(2,1)S(1)} %get-tuple-element.333.grad_ref.gq_ref.gk_ref.gv_ref, ...), custom_call_target="tpu_custom_call" | custom-call | tf_op jit(solution)/shard_map/pallas_call | solution.py:594
  221.9 7.1 %collective-permute-done.35 = bf16[4,120,768]{2,1,0:T(8,128)(2,1)S(1)} collective-permute-done((bf16[4,120,768]{2,1,0:T(8,128)(2,1)}, bf16[4,120,768]{2,1,0:T(8,128)(2,1)S(1)}, u32[]{:S(2)}, u32[]{:S(2)}) %collective-permute-start.35) | collective-permute-done | bytes 737312 | tf_op jit(solution)/shard_map/ppermute | solution.py:217
  229.9 1.9 fusion.8
  235.4 1.6 shard_map.338
  237.0 1.9 collective-permute-start.42
  238.9 3.4 %shard_map.339 = bf16[1120,768]{1,0:T(8,128)(2,1)} custom-call(f32[1120,768]{1,0:T(8,128)S(1)} %copy-done.13, bf16[1120,2304]{1,0:T(8,128)(2,1)S(1)} %get-tuple-element.333.grad_ref.gq_ref.gk_ref.gv_ref, bf16[1120,2304]{1,0:T(8,128)(2,1)S(1)} %get-tuple-element.333.grad_ref.gq_ref.gk_ref.gv_ref, ...), custom_call_target="tpu_custom_call", output_to_operand_aliasing={{}: (7, {})} | custom-call | tf_op jit(solution)/shard_map/pallas_call | solution.py:594
  242.3 2.1 collective-permute-start.43
  244.4 2.1 collective-permute-done.42
  247.6 5.0 %collective-permute-done.43 = bf16[120,768]{1,0:T(8,128)(2,1)S(1)} collective-permute-done((bf16[120,768]{1,0:T(8,128)(2,1)S(1)}, bf16[120,768]{1,0:T(8,128)(2,1)S(1)}, u32[]{:S(2)}, u32[]{:S(2)}) %collective-permute-start.43) | collective-permute-done | bytes 184352 | tf_op jit(solution)/shard_map/ppermute | solution.py:217
  255.5 2.6 collective-permute-start.44
  261.3 2.3 collective-permute-done.44
  263.6 3.5 %collective-permute-done.45 = bf16[80,768]{1,0:T(8,128)(2,1)S(1)} collective-permute-done((bf16[80,768]{1,0:T(8,128)(2,1)S(1)}, bf16[80,768]{1,0:T(8,128)(2,1)S(1)}, u32[]{:S(2)}, u32[]{:S(2)}) %collective-permute-start.45) | collective-permute-done | bytes 122912 | tf_op jit(solution)/shard_map/ppermute | solution.py:217
  (194 shorter events, 50.5 us)
Async XLA Ops:
  2.5 21.4 %collective-permute-start.10 = (bf16[216,768]{1,0:T(8,128)(2,1)S(1)}, bf16[216,768]{1,0:T(8,128)(2,1)}, u32[]{:S(2)}, u32[]{:S(2)}) collective-permute-start(bf16[216,768]{1,0:T(8,128)(2,1)S(1)} %pad_maximum_fusion.3), channel_id=1, source_target_pairs={{0,6},{1,7},{2,4},{3,5},{4,2},{5,3},{6,0},{7,1},{8,14},{9,15},{10,... | collective-permute-start | bytes 995336 | tf_op jit(solution)/shard_map/ppermute | solution.py:217
  8.1 12.2 %collective-permute-start.1 = (bf16[80,768]{1,0:T(8,128)(2,1)S(1)}, bf16[80,768]{1,0:T(8,128)(2,1)S(1)}, u32[]{:S(2)}, u32[]{:S(2)}) collective-permute-start(bf16[80,768]{1,0:T(8,128)(2,1)S(1)} %get-tuple-element.413), channel_id=1, source_target_pairs={{0,16},{1,17},{2,18},{3,19},{4,20},{5,21},{6,22},{7,23},{8,24},{9,... | collective-permute-start | bytes 368648 | tf_op jit(solution)/shard_map/ppermute | solution.py:217
  10.8 10.1 %collective-permute-start = (bf16[80,768]{1,0:T(8,128)(2,1)S(1)}, bf16[80,768]{1,0:T(8,128)(2,1)S(1)}, u32[]{:S(2)}, u32[]{:S(2)}) collective-permute-start(bf16[80,768]{1,0:T(8,128)(2,1)S(1)} %get-tuple-element.413), channel_id=1, source_target_pairs={{0,8},{1,9},{2,10},{3,11},{4,12},{5,13},{6,14},{7,15},{8,16},{9,17... | collective-permute-start | bytes 368648 | tf_op jit(solution)/shard_map/ppermute | solution.py:217
  12.4 8.5 %collective-permute-start.2 = (bf16[80,768]{1,0:T(8,128)(2,1)S(1)}, bf16[80,768]{1,0:T(8,128)(2,1)S(1)}, u32[]{:S(2)}, u32[]{:S(2)}) collective-permute-start(bf16[80,768]{1,0:T(8,128)(2,1)S(1)} %get-tuple-element.413), channel_id=1, source_target_pairs={{0,24},{1,25},{2,26},{3,27},{4,28},{5,29},{6,30},{7,31},{8,0},{9,1... | collective-permute-start | bytes 368648 | tf_op jit(solution)/shard_map/ppermute | solution.py:217
  14.6 10.8 %collective-permute-start.9 = (bf16[216,768]{1,0:T(8,128)(2,1)S(1)}, bf16[216,768]{1,0:T(8,128)(2,1)S(1)}, u32[]{:S(2)}, u32[]{:S(2)}) collective-permute-start(bf16[216,768]{1,0:T(8,128)(2,1)S(1)} %pad_maximum_fusion.3), channel_id=1, source_target_pairs={{0,4},{1,5},{2,6},{3,7},{4,0},{5,1},{6,2},{7,3},{8,12},{9,13},{10,... | collective-permute-start | bytes 995336 | tf_op jit(solution)/shard_map/ppermute | solution.py:217
  20.3 10.7 %collective-permute-start.8 = (bf16[216,768]{1,0:T(8,128)(2,1)S(1)}, bf16[216,768]{1,0:T(8,128)(2,1)S(1)}, u32[]{:S(2)}, u32[]{:S(2)}) collective-permute-start(bf16[216,768]{1,0:T(8,128)(2,1)S(1)} %pad_maximum_fusion.3), channel_id=1, source_target_pairs={{0,2},{1,3},{2,0},{3,1},{4,6},{5,7},{6,4},{7,5},{8,10},{9,11},{10,... | collective-permute-start | bytes 995336 | tf_op jit(solution)/shard_map/ppermute | solution.py:217
  20.9 22.4 %collective-permute-start.5 = (bf16[4,80,768]{2,1,0:T(8,128)(2,1)S(1)}, bf16[4,80,768]{2,1,0:T(8,128)(2,1)S(1)}, u32[]{:S(2)}, u32[]{:S(2)}) collective-permute-start(bf16[4,80,768]{2,1,0:T(8,128)(2,1)S(1)} %pad_maximum_fusion.2), channel_id=1, source_target_pairs={{0,6},{1,7},{2,4},{3,5},{4,2},{5,3},{6,0},{7,1},{8,14},{9,15},{10,... | collective-permute-start | bytes 1474568 | tf_op jit(solution)/shard_map/ppermute | solution.py:217
  22.4 21.7 %collective-permute-start.4 = (bf16[4,80,768]{2,1,0:T(8,128)(2,1)S(1)}, bf16[4,80,768]{2,1,0:T(8,128)(2,1)S(1)}, u32[]{:S(2)}, u32[]{:S(2)}) collective-permute-start(bf16[4,80,768]{2,1,0:T(8,128)(2,1)S(1)} %pad_maximum_fusion.2), channel_id=1, source_target_pairs={{0,4},{1,5},{2,6},{3,7},{4,0},{5,1},{6,2},{7,3},{8,12},{9,13},{10,... | collective-permute-start | bytes 1474568 | tf_op jit(solution)/shard_map/ppermute | solution.py:217
  23.9 24.0 %collective-permute-start.3 = (bf16[4,80,768]{2,1,0:T(8,128)(2,1)S(1)}, bf16[4,80,768]{2,1,0:T(8,128)(2,1)S(1)}, u32[]{:S(2)}, u32[]{:S(2)}) collective-permute-start(bf16[4,80,768]{2,1,0:T(8,128)(2,1)S(1)} %pad_maximum_fusion.2), channel_id=1, source_target_pairs={{0,2},{1,3},{2,0},{3,1},{4,6},{5,7},{6,4},{7,5},{8,10},{9,11},{10,... | collective-permute-start | bytes 1474568 | tf_op jit(solution)/shard_map/ppermute | solution.py:217
  25.5 9.8 %collective-permute-start.7 = (bf16[216,768]{1,0:T(8,128)(2,1)S(1)}, bf16[216,768]{1,0:T(8,128)(2,1)S(1)}, u32[]{:S(2)}, u32[]{:S(2)}) collective-permute-start(bf16[216,768]{1,0:T(8,128)(2,1)S(1)} %pad_maximum_fusion.3), channel_id=1, source_target_pairs={{0,24},{1,25},{2,26},{3,27},{4,28},{5,29},{6,30},{7,31},{8,0},{9,1... | collective-permute-start | bytes 995336 | tf_op jit(solution)/shard_map/ppermute | solution.py:217
  31.0 12.3 %collective-permute-start.6 = (bf16[216,768]{1,0:T(8,128)(2,1)S(1)}, bf16[216,768]{1,0:T(8,128)(2,1)S(1)}, u32[]{:S(2)}, u32[]{:S(2)}) collective-permute-start(bf16[216,768]{1,0:T(8,128)(2,1)S(1)} %pad_maximum_fusion.3), channel_id=1, source_target_pairs={{0,8},{1,9},{2,10},{3,11},{4,12},{5,13},{6,14},{7,15},{8,16},{9,17... | collective-permute-start | bytes 995336 | tf_op jit(solution)/shard_map/ppermute | solution.py:217
  48.1 4.0 %collective-permute-start.11 = (bf16[16,80,768]{2,1,0:T(8,128)(2,1)S(1)}, bf16[16,80,768]{2,1,0:T(8,128)(2,1)S(1)}, u32[]{:S(2)}, u32[]{:S(2)}) collective-permute-start(bf16[16,80,768]{2,1,0:T(8,128)(2,1)S(1)} %constant_dynamic-update-slice_fusion.mine_ref), channel_id=1, source_target_pairs={{0,1},{1,0},{2,3},{3,2},{4,5},{5,4},{6,7},{7,6},{8,9},{9,8},{10,11... | collective-permute-start | bytes 5898248 | tf_op jit(solution)/shard_map/ppermute | solution.py:217
  53.4 19.7 %collective-permute-start.15 = (bf16[5,216,768]{2,1,0:T(8,128)(2,1)}, bf16[5,216,768]{2,1,0:T(8,128)(2,1)}, u32[]{:S(2)}, u32[]{:S(2)}) collective-permute-start(bf16[5,216,768]{2,1,0:T(8,128)(2,1)} %shard_map.323.rest_0_), channel_id=1, source_target_pairs={{0,1},{1,0},{2,3},{3,2},{4,5},{5,4},{6,7},{7,6},{8,9},{9,8},{10,11... | collective-permute-start | bytes 4976648 | tf_op jit(solution)/shard_map/ppermute | solution.py:217
  53.6 18.2 %collective-permute-start.12 = (bf16[216,768]{1,0:T(8,128)(2,1)S(1)}, bf16[216,768]{1,0:T(8,128)(2,1)}, u32[]{:S(2)}, u32[]{:S(2)}) collective-permute-start(bf16[216,768]{1,0:T(8,128)(2,1)S(1)} %pad_maximum_fusion.3), channel_id=1, source_target_pairs={{0,16},{1,17},{2,18},{3,19},{4,20},{5,21},{6,22},{7,23},{8,24},{9,... | collective-permute-start | bytes 995336 | tf_op jit(solution)/shard_map/ppermute | solution.py:217
  54.9 17.2 %collective-permute-start.14 = (bf16[2,216,768]{2,1,0:T(8,128)(2,1)}, bf16[2,216,768]{2,1,0:T(8,128)(2,1)}, u32[]{:S(2)}, u32[]{:S(2)}) collective-permute-start(bf16[2,216,768]{2,1,0:T(8,128)(2,1)} %pad_maximum_fusion.1), channel_id=1, source_target_pairs={{0,4},{1,5},{2,6},{3,7},{4,0},{5,1},{6,2},{7,3},{8,12},{9,13},{10,... | collective-permute-start | bytes 1990664 | tf_op jit(solution)/shard_map/ppermute | solution.py:217
  56.2 16.9 %collective-permute-start.13 = (bf16[2,216,768]{2,1,0:T(8,128)(2,1)}, bf16[2,216,768]{2,1,0:T(8,128)(2,1)}, u32[]{:S(2)}, u32[]{:S(2)}) collective-permute-start(bf16[2,216,768]{2,1,0:T(8,128)(2,1)} %pad_maximum_fusion.1), channel_id=1, source_target_pairs={{0,2},{1,3},{2,0},{3,1},{4,6},{5,7},{6,4},{7,5},{8,10},{9,11},{10,... | collective-permute-start | bytes 1990664 | tf_op jit(solution)/shard_map/ppermute | solution.py:217
  74.8 5.7 %collective-permute-start.16 = (bf16[6,216,768]{2,1,0:T(8,128)(2,1)S(1)}, bf16[6,216,768]{2,1,0:T(8,128)(2,1)S(1)}, u32[]{:S(2)}, u32[]{:S(2)}) collective-permute-start(bf16[6,216,768]{2,1,0:T(8,128)(2,1)S(1)} %pad_maximum_fusion.rest_1_), channel_id=1, source_target_pairs={{0,1},{1,0},{2,3},{3,2},{4,5},{5,4},{6,7},{7,6},{8,9},{9,8},{10,11... | collective-permute-start | bytes 5971976 | tf_op jit(solution)/shard_map/ppermute | solution.py:217
  74.9 19.3 %collective-permute-start.21 = (bf16[216,768]{1,0:T(8,128)(2,1)}, bf16[216,768]{1,0:T(8,128)(2,1)S(1)}, u32[]{:S(2)}, u32[]{:S(2)}) collective-permute-start(bf16[216,768]{1,0:T(8,128)(2,1)} %collective-permute-done.10), channel_id=1, source_target_pairs={{0,24},{1,25},{2,26},{3,27},{4,28},{5,29},{6,30},{7,31},{8,0},{9,1... | collective-permute-start | bytes 995336 | tf_op jit(solution)/shard_map/ppermute | solution.py:217
  78.2 16.0 %collective-permute-start.20 = (bf16[216,768]{1,0:T(8,128)(2,1)}, bf16[216,768]{1,0:T(8,128)(2,1)S(1)}, u32[]{:S(2)}, u32[]{:S(2)}) collective-permute-start(bf16[216,768]{1,0:T(8,128)(2,1)} %collective-permute-done.10), channel_id=1, source_target_pairs={{0,8},{1,9},{2,10},{3,11},{4,12},{5,13},{6,14},{7,15},{8,16},{9,17... | collective-permute-start | bytes 995336 | tf_op jit(solution)/shard_map/ppermute | solution.py:217
  78.5 15.6 %collective-permute-start.19 = (bf16[216,768]{1,0:T(8,128)(2,1)}, bf16[216,768]{1,0:T(8,128)(2,1)S(1)}, u32[]{:S(2)}, u32[]{:S(2)}) collective-permute-start(bf16[216,768]{1,0:T(8,128)(2,1)} %collective-permute-done.12), channel_id=1, source_target_pairs={{0,6},{1,7},{2,4},{3,5},{4,2},{5,3},{6,0},{7,1},{8,14},{9,15},{10,... | collective-permute-start | bytes 995336 | tf_op jit(solution)/shard_map/ppermute | solution.py:217
  80.0 16.5 %collective-permute-start.18 = (bf16[216,768]{1,0:T(8,128)(2,1)}, bf16[216,768]{1,0:T(8,128)(2,1)S(1)}, u32[]{:S(2)}, u32[]{:S(2)}) collective-permute-start(bf16[216,768]{1,0:T(8,128)(2,1)} %collective-permute-done.12), channel_id=1, source_target_pairs={{0,4},{1,5},{2,6},{3,7},{4,0},{5,1},{6,2},{7,3},{8,12},{9,13},{10,... | collective-permute-start | bytes 995336 | tf_op jit(solution)/shard_map/ppermute | solution.py:217
  80.5 16.1 %collective-permute-start.17 = (bf16[216,768]{1,0:T(8,128)(2,1)}, bf16[216,768]{1,0:T(8,128)(2,1)S(1)}, u32[]{:S(2)}, u32[]{:S(2)}) collective-permute-start(bf16[216,768]{1,0:T(8,128)(2,1)} %collective-permute-done.12), channel_id=1, source_target_pairs={{0,2},{1,3},{2,0},{3,1},{4,6},{5,7},{6,4},{7,5},{8,10},{9,11},{10,... | collective-permute-start | bytes 995336 | tf_op jit(solution)/shard_map/ppermute | solution.py:217
  96.7 1.6 collective-permute-start.23
  96.7 2.1 collective-permute-start.22
  97.2 2.1 collective-permute-start.24
  97.2 2.5 collective-permute-start.25
  97.7 2.5 collective-permute-start.26
  152.8 5.2 %collective-permute-start.27 = (bf16[4,4,96,768]{3,2,1,0:T(8,128)(2,1)}, bf16[4,4,96,768]{3,2,1,0:T(8,128)(2,1)}, u32[]{:S(2)}, u32[]{:S(2)}) collective-permute-start(bf16[4,4,96,768]{3,2,1,0:T(8,128)(2,1)} %get-tuple-element.284), channel_id=1, source_target_pairs={{0,1},{1,0},{2,3},{3,2},{4,5},{5,4},{6,7},{7,6},{8,9},{9,8},{10,11... | collective-permute-start | bytes 7077896 | tf_op jit(solution)/shard_map/ppermute | solution.py:217
  161.1 23.6 %collective-permute-start.28 = (bf16[4,96,768]{2,1,0:T(8,128)(2,1)}, bf16[4,96,768]{2,1,0:T(8,128)(2,1)S(1)}, u32[]{:S(2)}, u32[]{:S(2)}) collective-permute-start(bf16[4,96,768]{2,1,0:T(8,128)(2,1)} %get-tuple-element.304), channel_id=1, source_target_pairs={{0,2},{1,3},{2,0},{3,1},{4,6},{5,7},{6,4},{7,5},{8,10},{9,11},{10,... | collective-permute-start | bytes 1769480 | tf_op jit(solution)/shard_map/ppermute | solution.py:217
  161.7 23.1 %collective-permute-start.29 = (bf16[4,96,768]{2,1,0:T(8,128)(2,1)}, bf16[4,96,768]{2,1,0:T(8,128)(2,1)S(1)}, u32[]{:S(2)}, u32[]{:S(2)}) collective-permute-start(bf16[4,96,768]{2,1,0:T(8,128)(2,1)} %get-tuple-element.305), channel_id=1, source_target_pairs={{0,4},{1,5},{2,6},{3,7},{4,0},{5,1},{6,2},{7,3},{8,12},{9,13},{10,... | collective-permute-start | bytes 1769480 | tf_op jit(solution)/shard_map/ppermute | solution.py:217
  163.1 26.7 %collective-permute-start.30 = (bf16[4,96,768]{2,1,0:T(8,128)(2,1)S(1)}, bf16[4,96,768]{2,1,0:T(8,128)(2,1)S(1)}, u32[]{:S(2)}, u32[]{:S(2)}) collective-permute-start(bf16[4,96,768]{2,1,0:T(8,128)(2,1)S(1)} %get-tuple-element.306), channel_id=1, source_target_pairs={{0,6},{1,7},{2,4},{3,5},{4,2},{5,3},{6,0},{7,1},{8,14},{9,15},{10,... | collective-permute-start | bytes 1769480 | tf_op jit(solution)/shard_map/ppermute | solution.py:217
  179.3 11.3 %collective-permute-start.31 = (bf16[4,4,120,768]{3,2,1,0:T(8,128)(2,1)}, bf16[4,4,120,768]{3,2,1,0:T(8,128)(2,1)}, u32[]{:S(2)}, u32[]{:S(2)}) collective-permute-start(bf16[4,4,120,768]{3,2,1,0:T(8,128)(2,1)} %bitcast.37), channel_id=1, source_target_pairs={{0,1},{1,0},{2,3},{3,2},{4,5},{5,4},{6,7},{7,6},{8,9},{9,8},{10,11... | collective-permute-start | bytes 8847368 | tf_op jit(solution)/shard_map/ppermute | solution.py:217
  194.1 26.9 %collective-permute-start.34 = (bf16[4,120,768]{2,1,0:T(8,128)(2,1)}, bf16[4,120,768]{2,1,0:T(8,128)(2,1)S(1)}, u32[]{:S(2)}, u32[]{:S(2)}) collective-permute-start(bf16[4,120,768]{2,1,0:T(8,128)(2,1)} %get-tuple-element.344), channel_id=1, source_target_pairs={{0,2},{1,3},{2,0},{3,1},{4,6},{5,7},{6,4},{7,5},{8,10},{9,11},{10,... | collective-permute-start | bytes 2211848 | tf_op jit(solution)/shard_map/ppermute | solution.py:217
  195.9 33.1 %collective-permute-start.35 = (bf16[4,120,768]{2,1,0:T(8,128)(2,1)}, bf16[4,120,768]{2,1,0:T(8,128)(2,1)S(1)}, u32[]{:S(2)}, u32[]{:S(2)}) collective-permute-start(bf16[4,120,768]{2,1,0:T(8,128)(2,1)} %get-tuple-element.345), channel_id=1, source_target_pairs={{0,4},{1,5},{2,6},{3,7},{4,0},{5,1},{6,2},{7,3},{8,12},{9,13},{10,... | collective-permute-start | bytes 2211848 | tf_op jit(solution)/shard_map/ppermute | solution.py:217
  196.6 33.3 %collective-permute-start.36 = (bf16[4,120,768]{2,1,0:T(8,128)(2,1)}, bf16[4,120,768]{2,1,0:T(8,128)(2,1)S(1)}, u32[]{:S(2)}, u32[]{:S(2)}) collective-permute-start(bf16[4,120,768]{2,1,0:T(8,128)(2,1)} %get-tuple-element.346), channel_id=1, source_target_pairs={{0,6},{1,7},{2,4},{3,5},{4,2},{5,3},{6,0},{7,1},{8,14},{9,15},{10,... | collective-permute-start | bytes 2211848 | tf_op jit(solution)/shard_map/ppermute | solution.py:217
  199.1 9.2 %collective-permute-start.32 = (bf16[96,768]{1,0:T(8,128)(2,1)S(1)}, bf16[96,768]{1,0:T(8,128)(2,1)S(1)}, u32[]{:S(2)}, u32[]{:S(2)}) collective-permute-start(bf16[96,768]{1,0:T(8,128)(2,1)S(1)} %get-tuple-element.330), channel_id=1, source_target_pairs={{0,8},{1,9},{2,10},{3,11},{4,12},{5,13},{6,14},{7,15},{8,16},{9,17... | collective-permute-start | bytes 442376 | tf_op jit(solution)/shard_map/ppermute | solution.py:217
  200.9 7.4 %collective-permute-start.33 = (bf16[96,768]{1,0:T(8,128)(2,1)S(1)}, bf16[96,768]{1,0:T(8,128)(2,1)S(1)}, u32[]{:S(2)}, u32[]{:S(2)}) collective-permute-start(bf16[96,768]{1,0:T(8,128)(2,1)S(1)} %get-tuple-element.331), channel_id=1, source_target_pairs={{0,24},{1,25},{2,26},{3,27},{4,28},{5,29},{6,30},{7,31},{8,0},{9,1... | collective-permute-start | bytes 442376 | tf_op jit(solution)/shard_map/ppermute | solution.py:217
  208.4 12.7 %collective-permute-start.37 = (bf16[96,768]{1,0:T(8,128)(2,1)S(1)}, bf16[96,768]{1,0:T(8,128)(2,1)S(1)}, u32[]{:S(2)}, u32[]{:S(2)}) collective-permute-start(bf16[96,768]{1,0:T(8,128)(2,1)S(1)} %get-tuple-element.348), channel_id=1, source_target_pairs={{0,16},{1,17},{2,18},{3,19},{4,20},{5,21},{6,22},{7,23},{8,24},{9,... | collective-permute-start | bytes 442376 | tf_op jit(solution)/shard_map/ppermute | solution.py:217
  217.5 12.4 %collective-permute-start.38 = (bf16[4,4,80,768]{3,2,1,0:T(8,128)(2,1)}, bf16[4,4,80,768]{3,2,1,0:T(8,128)(2,1)}, u32[]{:S(2)}, u32[]{:S(2)}) collective-permute-start(bf16[4,4,80,768]{3,2,1,0:T(8,128)(2,1)} %get-tuple-element.354), channel_id=1, source_target_pairs={{0,1},{1,0},{2,3},{3,2},{4,5},{5,4},{6,7},{7,6},{8,9},{9,8},{10,11... | collective-permute-start | bytes 5898248 | tf_op jit(solution)/shard_map/ppermute | solution.py:217
  231.8 20.8 %collective-permute-start.39 = (bf16[4,80,768]{2,1,0:T(8,128)(2,1)S(1)}, bf16[4,80,768]{2,1,0:T(8,128)(2,1)S(1)}, u32[]{:S(2)}, u32[]{:S(2)}) collective-permute-start(bf16[4,80,768]{2,1,0:T(8,128)(2,1)S(1)} %get-tuple-element.366), channel_id=1, source_target_pairs={{0,2},{1,3},{2,0},{3,1},{4,6},{5,7},{6,4},{7,5},{8,10},{9,11},{10,... | collective-permute-start | bytes 1474568 | tf_op jit(solution)/shard_map/ppermute | solution.py:217
  232.7 20.0 %collective-permute-start.40 = (bf16[4,80,768]{2,1,0:T(8,128)(2,1)S(1)}, bf16[4,80,768]{2,1,0:T(8,128)(2,1)S(1)}, u32[]{:S(2)}, u32[]{:S(2)}) collective-permute-start(bf16[4,80,768]{2,1,0:T(8,128)(2,1)S(1)} %get-tuple-element.367), channel_id=1, source_target_pairs={{0,4},{1,5},{2,6},{3,7},{4,0},{5,1},{6,2},{7,3},{8,12},{9,13},{10,... | collective-permute-start | bytes 1474568 | tf_op jit(solution)/shard_map/ppermute | solution.py:217
  234.0 19.2 %collective-permute-start.41 = (bf16[4,80,768]{2,1,0:T(8,128)(2,1)S(1)}, bf16[4,80,768]{2,1,0:T(8,128)(2,1)S(1)}, u32[]{:S(2)}, u32[]{:S(2)}) collective-permute-start(bf16[4,80,768]{2,1,0:T(8,128)(2,1)S(1)} %get-tuple-element.368), channel_id=1, source_target_pairs={{0,6},{1,7},{2,4},{3,5},{4,2},{5,3},{6,0},{7,1},{8,14},{9,15},{10,... | collective-permute-start | bytes 1474568 | tf_op jit(solution)/shard_map/ppermute | solution.py:217
  237.0 9.4 %collective-permute-start.42 = (bf16[120,768]{1,0:T(8,128)(2,1)S(1)}, bf16[120,768]{1,0:T(8,128)(2,1)S(1)}, u32[]{:S(2)}, u32[]{:S(2)}) collective-permute-start(bf16[120,768]{1,0:T(8,128)(2,1)S(1)} %get-tuple-element.369), channel_id=1, source_target_pairs={{0,8},{1,9},{2,10},{3,11},{4,12},{5,13},{6,14},{7,15},{8,16},{9,17... | collective-permute-start | bytes 552968 | tf_op jit(solution)/shard_map/ppermute | solution.py:217
  242.3 10.3 %collective-permute-start.43 = (bf16[120,768]{1,0:T(8,128)(2,1)S(1)}, bf16[120,768]{1,0:T(8,128)(2,1)S(1)}, u32[]{:S(2)}, u32[]{:S(2)}) collective-permute-start(bf16[120,768]{1,0:T(8,128)(2,1)S(1)} %get-tuple-element.370), channel_id=1, source_target_pairs={{0,16},{1,17},{2,18},{3,19},{4,20},{5,21},{6,22},{7,23},{8,24},{9,... | collective-permute-start | bytes 552968 | tf_op jit(solution)/shard_map/ppermute | solution.py:217
  246.4 7.0 %collective-permute-start.47 = (bf16[120,768]{1,0:T(8,128)(2,1)S(1)}, bf16[120,768]{1,0:T(8,128)(2,1)S(1)}, u32[]{:S(2)}, u32[]{:S(2)}) collective-permute-start(bf16[120,768]{1,0:T(8,128)(2,1)S(1)} %get-tuple-element.382), channel_id=1, source_target_pairs={{0,24},{1,25},{2,26},{3,27},{4,28},{5,29},{6,30},{7,31},{8,0},{9,1... | collective-permute-start | bytes 552968 | tf_op jit(solution)/shard_map/ppermute | solution.py:217
  255.5 8.1 %collective-permute-start.44 = (bf16[80,768]{1,0:T(8,128)(2,1)S(1)}, bf16[80,768]{1,0:T(8,128)(2,1)S(1)}, u32[]{:S(2)}, u32[]{:S(2)}) collective-permute-start(bf16[80,768]{1,0:T(8,128)(2,1)S(1)} %get-tuple-element.376), channel_id=1, source_target_pairs={{0,8},{1,9},{2,10},{3,11},{4,12},{5,13},{6,14},{7,15},{8,16},{9,17... | collective-permute-start | bytes 368648 | tf_op jit(solution)/shard_map/ppermute | solution.py:217
  258.1 9.0 %collective-permute-start.45 = (bf16[80,768]{1,0:T(8,128)(2,1)S(1)}, bf16[80,768]{1,0:T(8,128)(2,1)S(1)}, u32[]{:S(2)}, u32[]{:S(2)}) collective-permute-start(bf16[80,768]{1,0:T(8,128)(2,1)S(1)} %get-tuple-element.377), channel_id=1, source_target_pairs={{0,16},{1,17},{2,18},{3,19},{4,20},{5,21},{6,22},{7,23},{8,24},{9,... | collective-permute-start | bytes 368648 | tf_op jit(solution)/shard_map/ppermute | solution.py:217
  259.6 7.5 %collective-permute-start.46 = (bf16[80,768]{1,0:T(8,128)(2,1)S(1)}, bf16[80,768]{1,0:T(8,128)(2,1)S(1)}, u32[]{:S(2)}, u32[]{:S(2)}) collective-permute-start(bf16[80,768]{1,0:T(8,128)(2,1)S(1)} %get-tuple-element.378), channel_id=1, source_target_pairs={{0,24},{1,25},{2,26},{3,27},{4,28},{5,29},{6,30},{7,31},{8,0},{9,1... | collective-permute-start | bytes 368648 | tf_op jit(solution)/shard_map/ppermute | solution.py:217
  (49 other events, 394.7 us)

commit v6 on v5

--- a/solution.py
+++ b/solution.py
@@ -420,7 +420,7 @@
         specs + [tile, tile, tile] + [fixed(w) for w in weights] + [fixed(small), fixed(ub)],
         [tile, wide, tile, tile, wide, tile, tile, tile, pl.BlockSpec((8, D), lambda c: (0, 0)), pl.BlockSpec((ff // D, D), lambda c: (0, 0))],
         [act, big, act, act, big, act, shaped((rows, D), F32), act, shaped((8, D), F32), shaped((ff // D, D), F32)],
-        scratch=scratch, vmem=46,
+        scratch=scratch, vmem=48,
         flops=2 * rows * D * (2 * D + 4 * ff), moved=rows * (D * 20 + ff * 4) + D * (D + 2 * ff) * 2,
     )(*place_of, mixed, x, gy, *weights, small, ub)
 
@@ -529,7 +529,7 @@
         functools.partial(wgrad_in_body, far, own), (3,),
         [pl.BlockSpec(memory_space=pltpu.SMEM), full(x), pl.BlockSpec((rows, D), lambda j: (0, j)), full(small), full(ub)],
         specs, outs, scratch=[pltpu.VMEM((3, D, D), F32)],
-     vmem=36,)(at, x, grads, small, ub)
+     vmem=28,)(at, x, grads, small, ub)
 
 
 def pair_sum(keep, other, i):
@@ -560,7 +560,7 @@
     base, *sent = call(
         line_body, (1,), [block] * 5, [part] * far,
         [shaped((rows, D), F32)] + [shaped((rows, D), BF16)] * (far - 1),
-     vmem=16,)(keep, other, *(p[None] for p in near))
+     vmem=10,)(keep, other, *(p[None] for p in near))
     return base, sent
 
 
@@ -644,7 +644,7 @@
     layer_out, hidden, gffn, low, gpre, gattn, g1, gmixed, gtable, gub = ffn_both(
         mixed, tokens, gy, mine + other, table, ub, at, own
     )
-    cuts = (0, 1, 4, chains)
+    cuts = (0, 1, 6, chains)
     keep_d, send_d = wgrad_down(at, hidden, gffn, n)
     gmixed, keep_d, send_d = tie(gmixed, keep_d, send_d)
     other_d = hop(send_d, swap(n, 1))
@@ -683,13 +683,15 @@
     in_grad = input_grad(g1, grads, wq, wk, wv, 2, 4, (in_grad,))
     in_grad, near_i, far_u = tie(in_grad, near_i, far_u)
     base_i, sent_i = line_sum(keep_i, other_i, near_i)
+    sent_i, far_u = tie(sent_i, far_u)
     far_i = far_hops(sent_i, n, (1, 2, 3))
     far_u.update(far_hops(sent_u, n, (3,)))
-    down_own, up_own, in_own = last_sum(base_d, far_d), last_sum(base_u, far_u), last_sum(base_i, far_i)
-
-    gq_w, gk_w, gv_w = (in_own[own * i : own * (i + 1)] for i in range(3))
-    gqb, gvb, gob, gag, gas, gdb, gfg, gfs = (in_own[3 * own + i, :own] for i in range(8))
-    gub = in_own[3 * own, 128 : 128 + wide]
+    down_own, up_own = last_sum(base_d, far_d), last_sum(base_u, far_u)
+    piece = lambda *at: base_i[at] + sum(p[at].astype(F32) for p in far_i.values())
+
+    gq_w, gk_w, gv_w = (piece(slice(own * i, own * (i + 1))) for i in range(3))
+    gqb, gvb, gob, gag, gas, gdb, gfg, gfs = (piece(3 * own + i, slice(0, own)) for i in range(8))
+    gub = piece(3 * own, slice(128, 128 + wide))
     gup = jnp.concatenate([up_own[own * i : own * (i + 1)] for i in range(wide // own)], axis=1)
     go_w = up_own[wide : wide + own]
     return (

time: 270 us -> 268 us (level)
  local copies, waits for them, and re-layouts: 16.1 us -> 11.8 us
    unnamed x101 -> x77, local copies, waits for them, and re-layouts: 12.4 us -> 9.89 us
  transfers between devices with their start and end apart: 48 -> 48, of which waited for: 27 -> 28; matrix products, arithmetic and copies ran while one was open for 3% -> 3% of each run, Pallas kernels for 22% -> 23%
where the time goes in v6:
time: 268 us
  Pallas kernels  115 us (43%)
  waiting for transfers between devices  68 us (25%)
  starting transfers between devices  51.7 us (19%)
  other arithmetic  20.5 us (8%)
  local copies, waits for them, and re-layouts  11.8 us (4%)
    ppermute x48, waiting for transfers between devices, hop(): return lax.ppermute(value, 'fsdp', pairs)  68 us
    ppermute x48, starting transfers between devices, hop(): return lax.ppermute(value, 'fsdp', pairs)  51.7 us
    pallas_call x1, Pallas kernels, ffn_both(): call(body, (rows // tile_rows,), specs + [tile, tile, tile] + [fixed(w) f...  41.3 us
    pallas_call x2, Pallas kernels, attn_fwd(): call(functools.partial(attn_fwd_body, start), (stop - start,), [pl.BlockS...  13.6 us
    pallas_call x3, Pallas kernels, attn_bwd(): call(functools.partial(attn_bwd_body, start), (stop - start,), [pl.BlockS...  12.8 us
    pallas_call x1, Pallas kernels, wgrad_up(): call(functools.partial(wgrad_up_body, far, own), (5,), [pl.BlockSpec(memo...  11.7 us
    pallas_call x1, Pallas kernels, wgrad_down(): call(functools.partial(wgrad_down_body, far, own), (far,), [pl.BlockSpec(...  11.4 us
    unnamed x77, local copies, waits for them, and re-layouts  9.89 us
  transfers between devices with their start and end apart: 48, of which 28 were waited for; matrix products, arithmetic and copies ran while one was open for 3% of the time, Pallas kernels for 23%

profile of v6, /device:TPU:0, one launch (start us, length us, event | category | flops | bytes accessed | tf_op | source)
XLA Modules:
  0.0 267.8 jit_solution(16236274888369840044)
XLA Ops:
  2.5 4.0 %collective-permute-start.10 = (bf16[216,768]{1,0:T(8,128)(2,1)S(1)}, bf16[216,768]{1,0:T(8,128)(2,1)}, u32[]{:S(2)}, u32[]{:S(2)}) collective-permute-start(bf16[216,768]{1,0:T(8,128)(2,1)S(1)} %pad_maximum_fusion.3), channel_id=1, source_target_pairs={{0,6},{1,7},{2,4},{3,5},{4,2},{5,3},{6,0},{7,1},{8,14},{9,15},{10,... | collective-permute-start | bytes 995336 | tf_op jit(solution)/shard_map/ppermute | solution.py:217
  8.1 2.7 collective-permute-start.1
  10.8 1.6 collective-permute-start
  12.4 2.2 collective-permute-start.2
  15.1 5.2 %collective-permute-done.1 = bf16[80,768]{1,0:T(8,128)(2,1)S(1)} collective-permute-done((bf16[80,768]{1,0:T(8,128)(2,1)S(1)}, bf16[80,768]{1,0:T(8,128)(2,1)S(1)}, u32[]{:S(2)}, u32[]{:S(2)}) %collective-permute-start.1) | collective-permute-done | bytes 122912 | tf_op jit(solution)/shard_map/ppermute | solution.py:217
  27.0 4.1 %collective-permute-done.8 = bf16[216,768]{1,0:T(8,128)(2,1)S(1)} collective-permute-done((bf16[216,768]{1,0:T(8,128)(2,1)S(1)}, bf16[216,768]{1,0:T(8,128)(2,1)S(1)}, u32[]{:S(2)}, u32[]{:S(2)}) %collective-permute-start.8) | collective-permute-done | bytes 331808 | tf_op jit(solution)/shard_map/ppermute | solution.py:217
  31.1 4.2 %collective-permute-done.7 = bf16[216,768]{1,0:T(8,128)(2,1)S(1)} collective-permute-done((bf16[216,768]{1,0:T(8,128)(2,1)S(1)}, bf16[216,768]{1,0:T(8,128)(2,1)S(1)}, u32[]{:S(2)}, u32[]{:S(2)}) %collective-permute-start.7) | collective-permute-done | bytes 331808 | tf_op jit(solution)/shard_map/ppermute | solution.py:217
  35.3 8.1 %collective-permute-done.6 = bf16[216,768]{1,0:T(8,128)(2,1)S(1)} collective-permute-done((bf16[216,768]{1,0:T(8,128)(2,1)S(1)}, bf16[216,768]{1,0:T(8,128)(2,1)S(1)}, u32[]{:S(2)}, u32[]{:S(2)}) %collective-permute-start.6) | collective-permute-done | bytes 331808 | tf_op jit(solution)/shard_map/ppermute | solution.py:217
  44.1 3.9 %collective-permute-done.3 = bf16[4,80,768]{2,1,0:T(8,128)(2,1)S(1)} collective-permute-done((bf16[4,80,768]{2,1,0:T(8,128)(2,1)S(1)}, bf16[4,80,768]{2,1,0:T(8,128)(2,1)S(1)}, u32[]{:S(2)}, u32[]{:S(2)}) %collective-permute-start.3) | collective-permute-done | bytes 491552 | tf_op jit(solution)/shard_map/ppermute | solution.py:217
  49.5 2.7 collective-permute-done.11.other_ref
  57.2 3.0 %broadcast_select_fusion.gy_ref = bf16[1120,768]{1,0:T(8,128)(2,1)} fusion(bf16[1120,768]{1,0:T(8,128)(2,1)} %param.21, pred[1120]{0:T(1024)(128)(4,1)S(1)} %broadcast_in_dim.121), kind=kLoop, calls=%fused_computation.1 | loop fusion | flops 860160 | bytes 3441760 | tf_op jit(solution)/shard_map/jit(_where)/select_n | solution.py:610
  60.2 2.6 shard_map.324
  62.9 5.8 %shard_map.325 = (bf16[1120,768]{1,0:T(8,128)(2,1)S(1)}, bf16[1120,768]{1,0:T(8,128)(2,1)S(1)}, bf16[1120,768]{1,0:T(8,128)(2,1)S(1)}, bf16[1120,768]{1,0:T(8,128)(2,1)S(1)}, f32[7,12,160]{2,1,0:T(8,128)S(1)}) custom-call(s32[7]{0:T(128)S(1)} %copy-done.26, bf16[1120,768]{1,0:T(8,128)(2,1)S(1)} %copy-done, bf16[768,768]{1,0:T(8,128)(2,1)S(1)} %bitcast.86, ...), custom_call_target="tpu_custom_call" | custom-call | tf_op jit(solution)/shard_map/pallas_call | solution.py:96
  68.7 3.2 %collective-permute-done.12 = bf16[216,768]{1,0:T(8,128)(2,1)} collective-permute-done((bf16[216,768]{1,0:T(8,128)(2,1)S(1)}, bf16[216,768]{1,0:T(8,128)(2,1)}, u32[]{:S(2)}, u32[]{:S(2)}) %collective-permute-start.12) | collective-permute-done | bytes 331808 | tf_op jit(solution)/shard_map/ppermute | solution.py:217
  73.2 1.7 pad_maximum_fusion.rest_1_
  75.0 3.3 %collective-permute-start.21 = (bf16[216,768]{1,0:T(8,128)(2,1)}, bf16[216,768]{1,0:T(8,128)(2,1)S(1)}, u32[]{:S(2)}, u32[]{:S(2)}) collective-permute-start(bf16[216,768]{1,0:T(8,128)(2,1)} %collective-permute-done.10), channel_id=1, source_target_pairs={{0,24},{1,25},{2,26},{3,27},{4,28},{5,29},{6,30},{7,31},{8,0},{9,1... | collective-permute-start | bytes 995336 | tf_op jit(solution)/shard_map/ppermute | solution.py:217
  82.1 7.8 %shard_map.326 = (bf16[1120,768]{1,0:T(8,128)(2,1)S(1)}, bf16[1120,768]{1,0:T(8,128)(2,1)S(1)}, bf16[1120,768]{1,0:T(8,128)(2,1)S(1)}, bf16[1120,768]{1,0:T(8,128)(2,1)S(1)}, f32[7,12,160]{2,1,0:T(8,128)S(1)}) custom-call(s32[7]{0:T(128)S(1)} %copy-done.26, ...), custom_call_target="tpu_custom_call", output_to_operand_aliasing={{0}: (6, {}), {1}: (7, {}), {2}: (8, {}), {3}: (9, {}), {4}... | custom-call | tf_op jit(solution)/shard_map/pallas_call | solution.py:96
  92.3 1.9 collective-permute-done.21
  94.3 2.4 collective-permute-done.18
  100.3 41.3 %shard_map.327 = (bf16[1120,768]{1,0:T(8,128)(2,1)}, bf16[1120,3072]{1,0:T(8,128)(2,1)}, bf16[1120,768]{1,0:T(8,128)(2,1)}, bf16[1120,768]{1,0:T(8,128)(2,1)}, b...) custom-call(s32[3]{0:T(128)S(1)} %pad_add_fusion.1.at_ref, ...), custom_call_target="tpu_custom_call" | custom-call | tf_op jit(solution)/shard_map/pallas_call | solution.py:418
  141.6 11.4 %shard_map.328 = (bf16[4,4,96,768]{3,2,1,0:T(8,128)(2,1)}, bf16[4,4,96,768]{3,2,1,0:T(8,128)(2,1)}) custom-call(s32[3]{0:T(128)} %copy-done.23, bf16[1120,3072]{1,0:T(8,128)(2,1)} %get-tuple-element.279.hid_ref, bf16[1120,768]{1,0:T(8,128)(2,1)} %get-tuple-element.280.gffn_ref), custom_call_target="tpu_custom_call" | custom-call | tf_op jit(solution)/shard_map/pallas_call | solution.py:458
  156.0 2.1 shard_map.329
  158.2 3.1 %fusion.5 = (bf16[4,96,768]{2,1,0:T(8,128)(2,1)S(1)}, bf16[4,96,768]{2,1,0:T(8,128)(2,1)}, bf16[4,96,768]{2,1,0:T(8,128)(2,1)}) fusion(bf16[4,4,96,768]{3,2,1,0:T(8,128)(2,1)} %collective-permute-done.27.other_ref, bf16[4,4,96,768]{3,2,1,0:T(8,128)(2,1)S(1)} %copy-done.14), kind=kLoop, calls=%fused_computation.17 | loop fusion | flops 3538944 | bytes 5308416 | tf_op jit(solution)/shard_map/convert_element_type | solution.py:540
  163.3 1.5 collective-permute-start.30
  164.8 2.9 %copy-done.18 = bf16[1120,3072]{1,0:T(8,128)(2,1)S(1)} copy-done((bf16[1120,3072]{1,0:T(8,128)(2,1)S(1)}, bf16[1120,3072]{1,0:T(8,128)(2,1)}, u32[]{:S(2)}) %copy-start.18) | copy-done | bytes 6881304
  167.8 11.7 %shard_map.330 = (bf16[4,4,5,24,768]{4,3,2,1,0:T(8,128)(2,1)S(1)}, bf16[4,4,5,24,768]{4,3,2,1,0:T(8,128)(2,1)}) custom-call(s32[3]{0:T(128)S(1)} %copy-done.24, bf16[1120,768]{1,0:T(8,128)(2,1)S(1)} %copy-done.21, bf16[1120,3072]{1,0:T(8,128)(2,1)S(1)} %copy-done.18, bf16[1120,768]{1,0:T(8,128)(2,1)S(1)} %copy-done.12, bf16[1120,768]{1,0:T(8,128)(2,1)S(1)} %copy-done.22), custom_call_target="tpu_custom_call" | custom-call | tf_op jit(solution)/shard_map/pallas_call | solution.py:491
  179.5 8.6 %shard_map.331 = (bf16[1120,2304]{1,0:T(8,128)(2,1)S(1)}, f32[1,768]{1,0:T(1,128)S(1)}, f32[1,768]{1,0:T(1,128)S(1)}) custom-call(s32[7]{0:T(128)S(1)} %copy-done.26, bf16[1120,768]{1,0:T(8,128)(2,1)S(1)} %get-tuple-element.275.q_ref, bf16[1120,768]{1,0:T(8,128)(2,1)S(1)} %get-tuple-element.276.k_ref, ...), custom_call_target="tpu_custom_call", output_to_operand_aliasing={{0}: (6, {})} | custom-call | tf_op jit(solution)/shard_map/pallas_call | solution.py:150
  188.0 2.0 collective-permute-done.30
  190.0 3.5 %fusion.2 = (bf16[4,120,768]{2,1,0:T(8,128)(2,1)S(1)}, bf16[4,120,768]{2,1,0:T(8,128)(2,1)}, bf16[4,120,768]{2,1,0:T(8,128)(2,1)}) fusion(bf16[4,4,120,768]{3,2,1,0:T(8,128)(2,1)} %collective-permute-done.31.other_ref, bf16[4,4,120,768]{3,2,1,0:T(8,128)(2,1)S(1)} %bitcast.98), kind=kLoop, calls=%fused_computation.13 | loop fusion | flops 4423680 | bytes 6635520 | tf_op jit(solution)/shard_map/convert_element_type | solution.py:540
  198.4 1.8 collective-permute-start.32
  200.2 2.1 collective-permute-start.33
  202.3 2.1 shard_map.334
  204.4 2.0 collective-permute-done.32
  208.5 8.7 %shard_map.335 = (bf16[4,4,80,768]{3,2,1,0:T(8,128)(2,1)S(1)}, bf16[4,4,80,768]{3,2,1,0:T(8,128)(2,1)}) custom-call(s32[3]{0:T(128)S(1)} %copy-done.25, bf16[1120,768]{1,0:T(8,128)(2,1)S(1)} %copy-done.1, bf16[1120,2304]{1,0:T(8,128)(2,1)S(1)} %get-tuple-element.338.grad_ref.gq_ref.gk_ref.gv_ref, f32[8,768]{1,0:T(8,128)S(1)} %pad_maximum_fusion.6.small_ref, ...), custom_call_target="tpu_custom_call" | custom-call | tf_op jit(solution)/shard_map/pallas_call | solution.py:528
  217.2 3.5 %shard_map.336.rest_0_ = bf16[1120,768]{1,0:T(8,128)(2,1)} custom-call(f32[1120,768]{1,0:T(8,128)S(1)} %copy-done.13, bf16[1120,2304]{1,0:T(8,128)(2,1)S(1)} %get-tuple-element.338.grad_ref.gq_ref.gk_ref.gv_ref, bf16[1120,2304]{1,0:T(8,128)(2,1)S(1)} %get-tuple-element.338.grad_ref.gq_ref.gk_ref.gv_ref, ...), custom_call_target="tpu_custom_call" | custom-call | tf_op jit(solution)/shard_map/pallas_call | solution.py:594
  220.7 7.7 %collective-permute-done.35 = bf16[4,120,768]{2,1,0:T(8,128)(2,1)S(1)} collective-permute-done((bf16[4,120,768]{2,1,0:T(8,128)(2,1)}, bf16[4,120,768]{2,1,0:T(8,128)(2,1)S(1)}, u32[]{:S(2)}, u32[]{:S(2)}) %collective-permute-start.35) | collective-permute-done | bytes 737312 | tf_op jit(solution)/shard_map/ppermute | solution.py:217
  228.4 1.7 fusion.8
  233.6 1.6 shard_map.338
  235.2 1.8 collective-permute-start.42
  237.0 3.4 %shard_map.339 = bf16[1120,768]{1,0:T(8,128)(2,1)} custom-call(f32[1120,768]{1,0:T(8,128)S(1)} %copy-done.13, bf16[1120,2304]{1,0:T(8,128)(2,1)S(1)} %get-tuple-element.338.grad_ref.gq_ref.gk_ref.gv_ref, bf16[1120,2304]{1,0:T(8,128)(2,1)S(1)} %get-tuple-element.338.grad_ref.gq_ref.gk_ref.gv_ref, ...), custom_call_target="tpu_custom_call", output_to_operand_aliasing={{}: (7, {})} | custom-call | tf_op jit(solution)/shard_map/pallas_call | solution.py:594
  240.4 2.0 collective-permute-start.43
  242.5 2.0 collective-permute-done.42
  246.1 4.7 %collective-permute-done.43 = bf16[120,768]{1,0:T(8,128)(2,1)S(1)} collective-permute-done((bf16[120,768]{1,0:T(8,128)(2,1)S(1)}, bf16[120,768]{1,0:T(8,128)(2,1)S(1)}, u32[]{:S(2)}, u32[]{:S(2)}) %collective-permute-start.43) | collective-permute-done | bytes 184352 | tf_op jit(solution)/shard_map/ppermute | solution.py:217
  250.7 1.6 collective-permute-done.41
  254.4 1.7 collective-permute-start.44
  256.2 2.0 collective-permute-start.45
  259.6 2.9 %collective-permute-done.44 = bf16[80,768]{1,0:T(8,128)(2,1)S(1)} collective-permute-done((bf16[80,768]{1,0:T(8,128)(2,1)S(1)}, bf16[80,768]{1,0:T(8,128)(2,1)S(1)}, u32[]{:S(2)}, u32[]{:S(2)}) %collective-permute-start.44) | collective-permute-done | bytes 122912 | tf_op jit(solution)/shard_map/ppermute | solution.py:217
  262.5 3.0 %collective-permute-done.45 = bf16[80,768]{1,0:T(8,128)(2,1)S(1)} collective-permute-done((bf16[80,768]{1,0:T(8,128)(2,1)S(1)}, bf16[80,768]{1,0:T(8,128)(2,1)S(1)}, u32[]{:S(2)}, u32[]{:S(2)}) %collective-permute-start.45) | collective-permute-done | bytes 122912 | tf_op jit(solution)/shard_map/ppermute | solution.py:217
  (170 shorter events, 52.2 us)
Async XLA Ops:
  2.5 21.4 %collective-permute-start.10 = (bf16[216,768]{1,0:T(8,128)(2,1)S(1)}, bf16[216,768]{1,0:T(8,128)(2,1)}, u32[]{:S(2)}, u32[]{:S(2)}) collective-permute-start(bf16[216,768]{1,0:T(8,128)(2,1)S(1)} %pad_maximum_fusion.3), channel_id=1, source_target_pairs={{0,6},{1,7},{2,4},{3,5},{4,2},{5,3},{6,0},{7,1},{8,14},{9,15},{10,... | collective-permute-start | bytes 995336 | tf_op jit(solution)/shard_map/ppermute | solution.py:217
  8.1 12.2 %collective-permute-start.1 = (bf16[80,768]{1,0:T(8,128)(2,1)S(1)}, bf16[80,768]{1,0:T(8,128)(2,1)S(1)}, u32[]{:S(2)}, u32[]{:S(2)}) collective-permute-start(bf16[80,768]{1,0:T(8,128)(2,1)S(1)} %get-tuple-element.423), channel_id=1, source_target_pairs={{0,16},{1,17},{2,18},{3,19},{4,20},{5,21},{6,22},{7,23},{8,24},{9,... | collective-permute-start | bytes 368648 | tf_op jit(solution)/shard_map/ppermute | solution.py:217
  10.8 10.1 %collective-permute-start = (bf16[80,768]{1,0:T(8,128)(2,1)S(1)}, bf16[80,768]{1,0:T(8,128)(2,1)S(1)}, u32[]{:S(2)}, u32[]{:S(2)}) collective-permute-start(bf16[80,768]{1,0:T(8,128)(2,1)S(1)} %get-tuple-element.423), channel_id=1, source_target_pairs={{0,8},{1,9},{2,10},{3,11},{4,12},{5,13},{6,14},{7,15},{8,16},{9,17... | collective-permute-start | bytes 368648 | tf_op jit(solution)/shard_map/ppermute | solution.py:217
  12.4 8.5 %collective-permute-start.2 = (bf16[80,768]{1,0:T(8,128)(2,1)S(1)}, bf16[80,768]{1,0:T(8,128)(2,1)S(1)}, u32[]{:S(2)}, u32[]{:S(2)}) collective-permute-start(bf16[80,768]{1,0:T(8,128)(2,1)S(1)} %get-tuple-element.423), channel_id=1, source_target_pairs={{0,24},{1,25},{2,26},{3,27},{4,28},{5,29},{6,30},{7,31},{8,0},{9,1... | collective-permute-start | bytes 368648 | tf_op jit(solution)/shard_map/ppermute | solution.py:217
  14.6 10.8 %collective-permute-start.9 = (bf16[216,768]{1,0:T(8,128)(2,1)S(1)}, bf16[216,768]{1,0:T(8,128)(2,1)S(1)}, u32[]{:S(2)}, u32[]{:S(2)}) collective-permute-start(bf16[216,768]{1,0:T(8,128)(2,1)S(1)} %pad_maximum_fusion.3), channel_id=1, source_target_pairs={{0,4},{1,5},{2,6},{3,7},{4,0},{5,1},{6,2},{7,3},{8,12},{9,13},{10,... | collective-permute-start | bytes 995336 | tf_op jit(solution)/shard_map/ppermute | solution.py:217
  20.3 10.7 %collective-permute-start.8 = (bf16[216,768]{1,0:T(8,128)(2,1)S(1)}, bf16[216,768]{1,0:T(8,128)(2,1)S(1)}, u32[]{:S(2)}, u32[]{:S(2)}) collective-permute-start(bf16[216,768]{1,0:T(8,128)(2,1)S(1)} %pad_maximum_fusion.3), channel_id=1, source_target_pairs={{0,2},{1,3},{2,0},{3,1},{4,6},{5,7},{6,4},{7,5},{8,10},{9,11},{10,... | collective-permute-start | bytes 995336 | tf_op jit(solution)/shard_map/ppermute | solution.py:217
  20.9 22.4 %collective-permute-start.5 = (bf16[4,80,768]{2,1,0:T(8,128)(2,1)S(1)}, bf16[4,80,768]{2,1,0:T(8,128)(2,1)S(1)}, u32[]{:S(2)}, u32[]{:S(2)}) collective-permute-start(bf16[4,80,768]{2,1,0:T(8,128)(2,1)S(1)} %pad_maximum_fusion.2), channel_id=1, source_target_pairs={{0,6},{1,7},{2,4},{3,5},{4,2},{5,3},{6,0},{7,1},{8,14},{9,15},{10,... | collective-permute-start | bytes 1474568 | tf_op jit(solution)/shard_map/ppermute | solution.py:217
  22.4 21.7 %collective-permute-start.4 = (bf16[4,80,768]{2,1,0:T(8,128)(2,1)S(1)}, bf16[4,80,768]{2,1,0:T(8,128)(2,1)S(1)}, u32[]{:S(2)}, u32[]{:S(2)}) collective-permute-start(bf16[4,80,768]{2,1,0:T(8,128)(2,1)S(1)} %pad_maximum_fusion.2), channel_id=1, source_target_pairs={{0,4},{1,5},{2,6},{3,7},{4,0},{5,1},{6,2},{7,3},{8,12},{9,13},{10,... | collective-permute-start | bytes 1474568 | tf_op jit(solution)/shard_map/ppermute | solution.py:217
  23.9 24.0 %collective-permute-start.3 = (bf16[4,80,768]{2,1,0:T(8,128)(2,1)S(1)}, bf16[4,80,768]{2,1,0:T(8,128)(2,1)S(1)}, u32[]{:S(2)}, u32[]{:S(2)}) collective-permute-start(bf16[4,80,768]{2,1,0:T(8,128)(2,1)S(1)} %pad_maximum_fusion.2), channel_id=1, source_target_pairs={{0,2},{1,3},{2,0},{3,1},{4,6},{5,7},{6,4},{7,5},{8,10},{9,11},{10,... | collective-permute-start | bytes 1474568 | tf_op jit(solution)/shard_map/ppermute | solution.py:217
  25.5 9.8 %collective-permute-start.7 = (bf16[216,768]{1,0:T(8,128)(2,1)S(1)}, bf16[216,768]{1,0:T(8,128)(2,1)S(1)}, u32[]{:S(2)}, u32[]{:S(2)}) collective-permute-start(bf16[216,768]{1,0:T(8,128)(2,1)S(1)} %pad_maximum_fusion.3), channel_id=1, source_target_pairs={{0,24},{1,25},{2,26},{3,27},{4,28},{5,29},{6,30},{7,31},{8,0},{9,1... | collective-permute-start | bytes 995336 | tf_op jit(solution)/shard_map/ppermute | solution.py:217
  31.0 12.3 %collective-permute-start.6 = (bf16[216,768]{1,0:T(8,128)(2,1)S(1)}, bf16[216,768]{1,0:T(8,128)(2,1)S(1)}, u32[]{:S(2)}, u32[]{:S(2)}) collective-permute-start(bf16[216,768]{1,0:T(8,128)(2,1)S(1)} %pad_maximum_fusion.3), channel_id=1, source_target_pairs={{0,8},{1,9},{2,10},{3,11},{4,12},{5,13},{6,14},{7,15},{8,16},{9,17... | collective-permute-start | bytes 995336 | tf_op jit(solution)/shard_map/ppermute | solution.py:217
  48.1 4.0 %collective-permute-start.11 = (bf16[16,80,768]{2,1,0:T(8,128)(2,1)S(1)}, bf16[16,80,768]{2,1,0:T(8,128)(2,1)S(1)}, u32[]{:S(2)}, u32[]{:S(2)}) collective-permute-start(bf16[16,80,768]{2,1,0:T(8,128)(2,1)S(1)} %constant_dynamic-update-slice_fusion.mine_ref), channel_id=1, source_target_pairs={{0,1},{1,0},{2,3},{3,2},{4,5},{5,4},{6,7},{7,6},{8,9},{9,8},{10,11... | collective-permute-start | bytes 5898248 | tf_op jit(solution)/shard_map/ppermute | solution.py:217
  53.5 19.7 %collective-permute-start.15 = (bf16[5,216,768]{2,1,0:T(8,128)(2,1)}, bf16[5,216,768]{2,1,0:T(8,128)(2,1)}, u32[]{:S(2)}, u32[]{:S(2)}) collective-permute-start(bf16[5,216,768]{2,1,0:T(8,128)(2,1)} %shard_map.323.rest_0_), channel_id=1, source_target_pairs={{0,1},{1,0},{2,3},{3,2},{4,5},{5,4},{6,7},{7,6},{8,9},{9,8},{10,11... | collective-permute-start | bytes 4976648 | tf_op jit(solution)/shard_map/ppermute | solution.py:217
  53.7 18.2 %collective-permute-start.12 = (bf16[216,768]{1,0:T(8,128)(2,1)S(1)}, bf16[216,768]{1,0:T(8,128)(2,1)}, u32[]{:S(2)}, u32[]{:S(2)}) collective-permute-start(bf16[216,768]{1,0:T(8,128)(2,1)S(1)} %pad_maximum_fusion.3), channel_id=1, source_target_pairs={{0,16},{1,17},{2,18},{3,19},{4,20},{5,21},{6,22},{7,23},{8,24},{9,... | collective-permute-start | bytes 995336 | tf_op jit(solution)/shard_map/ppermute | solution.py:217
  55.0 17.2 %collective-permute-start.14 = (bf16[2,216,768]{2,1,0:T(8,128)(2,1)}, bf16[2,216,768]{2,1,0:T(8,128)(2,1)}, u32[]{:S(2)}, u32[]{:S(2)}) collective-permute-start(bf16[2,216,768]{2,1,0:T(8,128)(2,1)} %pad_maximum_fusion.1), channel_id=1, source_target_pairs={{0,4},{1,5},{2,6},{3,7},{4,0},{5,1},{6,2},{7,3},{8,12},{9,13},{10,... | collective-permute-start | bytes 1990664 | tf_op jit(solution)/shard_map/ppermute | solution.py:217
  56.3 16.9 %collective-permute-start.13 = (bf16[2,216,768]{2,1,0:T(8,128)(2,1)}, bf16[2,216,768]{2,1,0:T(8,128)(2,1)}, u32[]{:S(2)}, u32[]{:S(2)}) collective-permute-start(bf16[2,216,768]{2,1,0:T(8,128)(2,1)} %pad_maximum_fusion.1), channel_id=1, source_target_pairs={{0,2},{1,3},{2,0},{3,1},{4,6},{5,7},{6,4},{7,5},{8,10},{9,11},{10,... | collective-permute-start | bytes 1990664 | tf_op jit(solution)/shard_map/ppermute | solution.py:217
  74.9 5.7 %collective-permute-start.16 = (bf16[6,216,768]{2,1,0:T(8,128)(2,1)S(1)}, bf16[6,216,768]{2,1,0:T(8,128)(2,1)S(1)}, u32[]{:S(2)}, u32[]{:S(2)}) collective-permute-start(bf16[6,216,768]{2,1,0:T(8,128)(2,1)S(1)} %pad_maximum_fusion.rest_1_), channel_id=1, source_target_pairs={{0,1},{1,0},{2,3},{3,2},{4,5},{5,4},{6,7},{7,6},{8,9},{9,8},{10,11... | collective-permute-start | bytes 5971976 | tf_op jit(solution)/shard_map/ppermute | solution.py:217
  75.0 19.3 %collective-permute-start.21 = (bf16[216,768]{1,0:T(8,128)(2,1)}, bf16[216,768]{1,0:T(8,128)(2,1)S(1)}, u32[]{:S(2)}, u32[]{:S(2)}) collective-permute-start(bf16[216,768]{1,0:T(8,128)(2,1)} %collective-permute-done.10), channel_id=1, source_target_pairs={{0,24},{1,25},{2,26},{3,27},{4,28},{5,29},{6,30},{7,31},{8,0},{9,1... | collective-permute-start | bytes 995336 | tf_op jit(solution)/shard_map/ppermute | solution.py:217
  78.3 16.0 %collective-permute-start.20 = (bf16[216,768]{1,0:T(8,128)(2,1)}, bf16[216,768]{1,0:T(8,128)(2,1)S(1)}, u32[]{:S(2)}, u32[]{:S(2)}) collective-permute-start(bf16[216,768]{1,0:T(8,128)(2,1)} %collective-permute-done.10), channel_id=1, source_target_pairs={{0,8},{1,9},{2,10},{3,11},{4,12},{5,13},{6,14},{7,15},{8,16},{9,17... | collective-permute-start | bytes 995336 | tf_op jit(solution)/shard_map/ppermute | solution.py:217
  78.6 15.6 %collective-permute-start.19 = (bf16[216,768]{1,0:T(8,128)(2,1)}, bf16[216,768]{1,0:T(8,128)(2,1)S(1)}, u32[]{:S(2)}, u32[]{:S(2)}) collective-permute-start(bf16[216,768]{1,0:T(8,128)(2,1)} %collective-permute-done.12), channel_id=1, source_target_pairs={{0,6},{1,7},{2,4},{3,5},{4,2},{5,3},{6,0},{7,1},{8,14},{9,15},{10,... | collective-permute-start | bytes 995336 | tf_op jit(solution)/shard_map/ppermute | solution.py:217
  80.1 16.5 %collective-permute-start.18 = (bf16[216,768]{1,0:T(8,128)(2,1)}, bf16[216,768]{1,0:T(8,128)(2,1)S(1)}, u32[]{:S(2)}, u32[]{:S(2)}) collective-permute-start(bf16[216,768]{1,0:T(8,128)(2,1)} %collective-permute-done.12), channel_id=1, source_target_pairs={{0,4},{1,5},{2,6},{3,7},{4,0},{5,1},{6,2},{7,3},{8,12},{9,13},{10,... | collective-permute-start | bytes 995336 | tf_op jit(solution)/shard_map/ppermute | solution.py:217
  80.6 16.1 %collective-permute-start.17 = (bf16[216,768]{1,0:T(8,128)(2,1)}, bf16[216,768]{1,0:T(8,128)(2,1)S(1)}, u32[]{:S(2)}, u32[]{:S(2)}) collective-permute-start(bf16[216,768]{1,0:T(8,128)(2,1)} %collective-permute-done.12), channel_id=1, source_target_pairs={{0,2},{1,3},{2,0},{3,1},{4,6},{5,7},{6,4},{7,5},{8,10},{9,11},{10,... | collective-permute-start | bytes 995336 | tf_op jit(solution)/shard_map/ppermute | solution.py:217
  96.7 1.6 collective-permute-start.23
  96.7 2.1 collective-permute-start.22
  97.2 2.1 collective-permute-start.24
  97.2 2.5 collective-permute-start.25
  97.7 2.5 collective-permute-start.26
  153.0 5.2 %collective-permute-start.27 = (bf16[4,4,96,768]{3,2,1,0:T(8,128)(2,1)}, bf16[4,4,96,768]{3,2,1,0:T(8,128)(2,1)}, u32[]{:S(2)}, u32[]{:S(2)}) collective-permute-start(bf16[4,4,96,768]{3,2,1,0:T(8,128)(2,1)} %get-tuple-element.289), channel_id=1, source_target_pairs={{0,1},{1,0},{2,3},{3,2},{4,5},{5,4},{6,7},{7,6},{8,9},{9,8},{10,11... | collective-permute-start | bytes 7077896 | tf_op jit(solution)/shard_map/ppermute | solution.py:217
  161.3 26.7 %collective-permute-start.28 = (bf16[4,96,768]{2,1,0:T(8,128)(2,1)}, bf16[4,96,768]{2,1,0:T(8,128)(2,1)S(1)}, u32[]{:S(2)}, u32[]{:S(2)}) collective-permute-start(bf16[4,96,768]{2,1,0:T(8,128)(2,1)} %get-tuple-element.309), channel_id=1, source_target_pairs={{0,2},{1,3},{2,0},{3,1},{4,6},{5,7},{6,4},{7,5},{8,10},{9,11},{10,... | collective-permute-start | bytes 1769480 | tf_op jit(solution)/shard_map/ppermute | solution.py:217
  161.8 26.2 %collective-permute-start.29 = (bf16[4,96,768]{2,1,0:T(8,128)(2,1)}, bf16[4,96,768]{2,1,0:T(8,128)(2,1)S(1)}, u32[]{:S(2)}, u32[]{:S(2)}) collective-permute-start(bf16[4,96,768]{2,1,0:T(8,128)(2,1)} %get-tuple-element.310), channel_id=1, source_target_pairs={{0,4},{1,5},{2,6},{3,7},{4,0},{5,1},{6,2},{7,3},{8,12},{9,13},{10,... | collective-permute-start | bytes 1769480 | tf_op jit(solution)/shard_map/ppermute | solution.py:217
  163.3 26.7 %collective-permute-start.30 = (bf16[4,96,768]{2,1,0:T(8,128)(2,1)S(1)}, bf16[4,96,768]{2,1,0:T(8,128)(2,1)S(1)}, u32[]{:S(2)}, u32[]{:S(2)}) collective-permute-start(bf16[4,96,768]{2,1,0:T(8,128)(2,1)S(1)} %get-tuple-element.311), channel_id=1, source_target_pairs={{0,6},{1,7},{2,4},{3,5},{4,2},{5,3},{6,0},{7,1},{8,14},{9,15},{10,... | collective-permute-start | bytes 1769480 | tf_op jit(solution)/shard_map/ppermute | solution.py:217
  179.4 10.6 %collective-permute-start.31 = (bf16[4,4,120,768]{3,2,1,0:T(8,128)(2,1)}, bf16[4,4,120,768]{3,2,1,0:T(8,128)(2,1)}, u32[]{:S(2)}, u32[]{:S(2)}) collective-permute-start(bf16[4,4,120,768]{3,2,1,0:T(8,128)(2,1)} %bitcast.37), channel_id=1, source_target_pairs={{0,1},{1,0},{2,3},{3,2},{4,5},{5,4},{6,7},{7,6},{8,9},{9,8},{10,11... | collective-permute-start | bytes 8847368 | tf_op jit(solution)/shard_map/ppermute | solution.py:217
  193.5 27.2 %collective-permute-start.34 = (bf16[4,120,768]{2,1,0:T(8,128)(2,1)}, bf16[4,120,768]{2,1,0:T(8,128)(2,1)S(1)}, u32[]{:S(2)}, u32[]{:S(2)}) collective-permute-start(bf16[4,120,768]{2,1,0:T(8,128)(2,1)} %get-tuple-element.349), channel_id=1, source_target_pairs={{0,2},{1,3},{2,0},{3,1},{4,6},{5,7},{6,4},{7,5},{8,10},{9,11},{10,... | collective-permute-start | bytes 2211848 | tf_op jit(solution)/shard_map/ppermute | solution.py:217
  195.0 33.4 %collective-permute-start.35 = (bf16[4,120,768]{2,1,0:T(8,128)(2,1)}, bf16[4,120,768]{2,1,0:T(8,128)(2,1)S(1)}, u32[]{:S(2)}, u32[]{:S(2)}) collective-permute-start(bf16[4,120,768]{2,1,0:T(8,128)(2,1)} %get-tuple-element.350), channel_id=1, source_target_pairs={{0,4},{1,5},{2,6},{3,7},{4,0},{5,1},{6,2},{7,3},{8,12},{9,13},{10,... | collective-permute-start | bytes 2211848 | tf_op jit(solution)/shard_map/ppermute | solution.py:217
  195.7 32.7 %collective-permute-start.36 = (bf16[4,120,768]{2,1,0:T(8,128)(2,1)S(1)}, bf16[4,120,768]{2,1,0:T(8,128)(2,1)S(1)}, u32[]{:S(2)}, u32[]{:S(2)}) collective-permute-start(bf16[4,120,768]{2,1,0:T(8,128)(2,1)S(1)} %get-tuple-element.351), channel_id=1, source_target_pairs={{0,6},{1,7},{2,4},{3,5},{4,2},{5,3},{6,0},{7,1},{8,14},{9,15},{10,... | collective-permute-start | bytes 2211848 | tf_op jit(solution)/shard_map/ppermute | solution.py:217
  198.4 8.1 %collective-permute-start.32 = (bf16[96,768]{1,0:T(8,128)(2,1)S(1)}, bf16[96,768]{1,0:T(8,128)(2,1)S(1)}, u32[]{:S(2)}, u32[]{:S(2)}) collective-permute-start(bf16[96,768]{1,0:T(8,128)(2,1)S(1)} %get-tuple-element.335), channel_id=1, source_target_pairs={{0,8},{1,9},{2,10},{3,11},{4,12},{5,13},{6,14},{7,15},{8,16},{9,17... | collective-permute-start | bytes 442376 | tf_op jit(solution)/shard_map/ppermute | solution.py:217
  200.2 7.3 %collective-permute-start.33 = (bf16[96,768]{1,0:T(8,128)(2,1)S(1)}, bf16[96,768]{1,0:T(8,128)(2,1)S(1)}, u32[]{:S(2)}, u32[]{:S(2)}) collective-permute-start(bf16[96,768]{1,0:T(8,128)(2,1)S(1)} %get-tuple-element.336), channel_id=1, source_target_pairs={{0,24},{1,25},{2,26},{3,27},{4,28},{5,29},{6,30},{7,31},{8,0},{9,1... | collective-permute-start | bytes 442376 | tf_op jit(solution)/shard_map/ppermute | solution.py:217
  207.5 13.2 %collective-permute-start.37 = (bf16[96,768]{1,0:T(8,128)(2,1)S(1)}, bf16[96,768]{1,0:T(8,128)(2,1)S(1)}, u32[]{:S(2)}, u32[]{:S(2)}) collective-permute-start(bf16[96,768]{1,0:T(8,128)(2,1)S(1)} %get-tuple-element.353), channel_id=1, source_target_pairs={{0,16},{1,17},{2,18},{3,19},{4,20},{5,21},{6,22},{7,23},{8,24},{9,... | collective-permute-start | bytes 442376 | tf_op jit(solution)/shard_map/ppermute | solution.py:217
  217.2 11.2 %collective-permute-start.38 = (bf16[4,4,80,768]{3,2,1,0:T(8,128)(2,1)}, bf16[4,4,80,768]{3,2,1,0:T(8,128)(2,1)}, u32[]{:S(2)}, u32[]{:S(2)}) collective-permute-start(bf16[4,4,80,768]{3,2,1,0:T(8,128)(2,1)} %get-tuple-element.359), channel_id=1, source_target_pairs={{0,1},{1,0},{2,3},{3,2},{4,5},{5,4},{6,7},{7,6},{8,9},{9,8},{10,11... | collective-permute-start | bytes 5898248 | tf_op jit(solution)/shard_map/ppermute | solution.py:217
  230.0 20.7 %collective-permute-start.39 = (bf16[4,80,768]{2,1,0:T(8,128)(2,1)S(1)}, bf16[4,80,768]{2,1,0:T(8,128)(2,1)S(1)}, u32[]{:S(2)}, u32[]{:S(2)}) collective-permute-start(bf16[4,80,768]{2,1,0:T(8,128)(2,1)S(1)} %get-tuple-element.371), channel_id=1, source_target_pairs={{0,2},{1,3},{2,0},{3,1},{4,6},{5,7},{6,4},{7,5},{8,10},{9,11},{10,... | collective-permute-start | bytes 1474568 | tf_op jit(solution)/shard_map/ppermute | solution.py:217
  230.9 19.9 %collective-permute-start.40 = (bf16[4,80,768]{2,1,0:T(8,128)(2,1)S(1)}, bf16[4,80,768]{2,1,0:T(8,128)(2,1)S(1)}, u32[]{:S(2)}, u32[]{:S(2)}) collective-permute-start(bf16[4,80,768]{2,1,0:T(8,128)(2,1)S(1)} %get-tuple-element.372), channel_id=1, source_target_pairs={{0,4},{1,5},{2,6},{3,7},{4,0},{5,1},{6,2},{7,3},{8,12},{9,13},{10,... | collective-permute-start | bytes 1474568 | tf_op jit(solution)/shard_map/ppermute | solution.py:217
  232.2 20.1 %collective-permute-start.41 = (bf16[4,80,768]{2,1,0:T(8,128)(2,1)S(1)}, bf16[4,80,768]{2,1,0:T(8,128)(2,1)S(1)}, u32[]{:S(2)}, u32[]{:S(2)}) collective-permute-start(bf16[4,80,768]{2,1,0:T(8,128)(2,1)S(1)} %get-tuple-element.373), channel_id=1, source_target_pairs={{0,6},{1,7},{2,4},{3,5},{4,2},{5,3},{6,0},{7,1},{8,14},{9,15},{10,... | collective-permute-start | bytes 1474568 | tf_op jit(solution)/shard_map/ppermute | solution.py:217
  235.2 9.3 %collective-permute-start.42 = (bf16[120,768]{1,0:T(8,128)(2,1)S(1)}, bf16[120,768]{1,0:T(8,128)(2,1)S(1)}, u32[]{:S(2)}, u32[]{:S(2)}) collective-permute-start(bf16[120,768]{1,0:T(8,128)(2,1)S(1)} %get-tuple-element.374), channel_id=1, source_target_pairs={{0,8},{1,9},{2,10},{3,11},{4,12},{5,13},{6,14},{7,15},{8,16},{9,17... | collective-permute-start | bytes 552968 | tf_op jit(solution)/shard_map/ppermute | solution.py:217
  240.4 10.3 %collective-permute-start.43 = (bf16[120,768]{1,0:T(8,128)(2,1)S(1)}, bf16[120,768]{1,0:T(8,128)(2,1)S(1)}, u32[]{:S(2)}, u32[]{:S(2)}) collective-permute-start(bf16[120,768]{1,0:T(8,128)(2,1)S(1)} %get-tuple-element.375), channel_id=1, source_target_pairs={{0,16},{1,17},{2,18},{3,19},{4,20},{5,21},{6,22},{7,23},{8,24},{9,... | collective-permute-start | bytes 552968 | tf_op jit(solution)/shard_map/ppermute | solution.py:217
  244.5 9.2 %collective-permute-start.47 = (bf16[120,768]{1,0:T(8,128)(2,1)S(1)}, bf16[120,768]{1,0:T(8,128)(2,1)S(1)}, u32[]{:S(2)}, u32[]{:S(2)}) collective-permute-start(bf16[120,768]{1,0:T(8,128)(2,1)S(1)} %get-tuple-element.392), channel_id=1, source_target_pairs={{0,24},{1,25},{2,26},{3,27},{4,28},{5,29},{6,30},{7,31},{8,0},{9,1... | collective-permute-start | bytes 552968 | tf_op jit(solution)/shard_map/ppermute | solution.py:217
  254.4 8.1 %collective-permute-start.44 = (bf16[80,768]{1,0:T(8,128)(2,1)S(1)}, bf16[80,768]{1,0:T(8,128)(2,1)S(1)}, u32[]{:S(2)}, u32[]{:S(2)}) collective-permute-start(bf16[80,768]{1,0:T(8,128)(2,1)S(1)} %get-tuple-element.386), channel_id=1, source_target_pairs={{0,8},{1,9},{2,10},{3,11},{4,12},{5,13},{6,14},{7,15},{8,16},{9,17... | collective-permute-start | bytes 368648 | tf_op jit(solution)/shard_map/ppermute | solution.py:217
  256.2 9.3 %collective-permute-start.45 = (bf16[80,768]{1,0:T(8,128)(2,1)S(1)}, bf16[80,768]{1,0:T(8,128)(2,1)S(1)}, u32[]{:S(2)}, u32[]{:S(2)}) collective-permute-start(bf16[80,768]{1,0:T(8,128)(2,1)S(1)} %get-tuple-element.387), channel_id=1, source_target_pairs={{0,16},{1,17},{2,18},{3,19},{4,20},{5,21},{6,22},{7,23},{8,24},{9,... | collective-permute-start | bytes 368648 | tf_op jit(solution)/shard_map/ppermute | solution.py:217
  258.2 7.3 %collective-permute-start.46 = (bf16[80,768]{1,0:T(8,128)(2,1)S(1)}, bf16[80,768]{1,0:T(8,128)(2,1)S(1)}, u32[]{:S(2)}, u32[]{:S(2)}) collective-permute-start(bf16[80,768]{1,0:T(8,128)(2,1)S(1)} %get-tuple-element.388), channel_id=1, source_target_pairs={{0,24},{1,25},{2,26},{3,27},{4,28},{5,29},{6,30},{7,31},{8,0},{9,1... | collective-permute-start | bytes 368648 | tf_op jit(solution)/shard_map/ppermute | solution.py:217
  (37 other events, 336.2 us)
